TPU v7x, 32 devices: a whole 2x2x4 slice. The times are simulated.
32 devices in a mesh: groups: 2 (over x), facet: 16 (over z, y, core).
Axes of the slice: x: 2, y: 2, z: 4, core: 2. Of those that a mesh axis runs over, the one named last changes fastest.
Arguments:
- facets: bfloat16 [32, 2, 512, 512], P(('groups', 'facet')), parts along dimension 0, may hold values from -6 to 6
- facet_offsets: int32 [32, 2], P(('groups', 'facet')), parts along dimension 0, may hold values from 0 to 511
- subgrid_offsets: int32 [32, 2], P('groups'), parts along dimension 0, may hold values from 0 to 511
- w_terms: float32 [32], P(('groups', 'facet')), parts along dimension 0, may hold values from 2 to 16
- tile_count: int32 [32], P(('groups', 'facet')), parts along dimension 0, may hold values from 1 to 16, as said below
- tile_offsets: int32 [512, 2], P(('groups', 'facet')), parts along dimension 0, may hold values from 0 to 256
- observed: bfloat16 [512, 2, 128, 128], P(('groups', 'facet')), parts along dimension 0, may hold values from -6 to 6
Outputs:
- residual: bfloat16 [512, 2, 128, 128], P(('groups', 'facet')), parts along dimension 0
- facet_update: bfloat16 [32, 2, 512, 512], P(('groups', 'facet')), parts along dimension 0
There are 2 independent parts, one for each index of `groups`. A program takes and returns all parts, laid end to end along the dimension named above; each array names one. Nothing has to cross between parts.
Inputs may be any that keep to these rules, and one draw needn't show every extreme that they name: `tile_count`: live tile slots of each subgrid; some subgrid has all 16 slots live in every draw.
All inputs are finite; a program needn't handle non-finite values.
Results may differ from a plain program's by a relative error of at most 0.017.
Values may be sent and summed in bfloat16 or wider, within the bound.
No kernel may reach another device: no remote copies, remote signals or barrier semaphores. Data moves between devices by JAX's collectives and lax.ppermute only.
A program may use at most 64 MiB of HBM per device.

v0:
```python
import math

import jax
import jax.numpy as jnp
from jax import lax
from jax.sharding import PartitionSpec as P

F = 512
M = 128
SG = 512
TV = 128


TWO_PI = 2.0 * math.pi


def basis_tables():
    index_f = jnp.arange(F, dtype=jnp.int32)
    product = index_f[:, None] * index_f[None, :] % F
    angle = -TWO_PI * product.astype(jnp.float32) / F
    scale = 1.0 / math.sqrt(F)
    return (
        (jnp.cos(angle) * scale).astype(jnp.bfloat16),
        (jnp.sin(angle) * scale).astype(jnp.bfloat16),
    )


def padding_tables(facet_count):
    rows = jnp.arange(SG, dtype=jnp.int32)
    columns = jnp.arange(M, dtype=jnp.int32)
    product = rows[:, None] * columns[None, :] % SG
    angle = TWO_PI * product.astype(jnp.float32) / SG
    scale = (M * math.sqrt(facet_count)) ** (-0.5)
    return (
        (jnp.cos(angle) * scale).astype(jnp.bfloat16),
        (jnp.sin(angle) * scale).astype(jnp.bfloat16),
    )


def taper_square():
    position = jnp.arange(M, dtype=jnp.float32)
    taper = 0.6 + 0.4 * jnp.sin(math.pi * (position + 0.5) / M)
    return taper[:, None] * taper[None, :]


def kernel_table():
    rows = jnp.arange(TV, dtype=jnp.float32)[:, None]
    columns = jnp.arange(2 * TV, dtype=jnp.float32)[None, :]
    distance = columns - 2.0 * rows - 1.0
    value = 0.75 * jnp.exp(-(distance / 1.5) * (distance / 1.5))
    return jnp.where(jnp.abs(distance) <= 4.0, value, jnp.zeros_like(value)).astype(jnp.bfloat16)


def facet_phase(offset):
    index_m = jnp.arange(M, dtype=jnp.int32)
    total = ((index_m * offset[0])[:, None] + (index_m * offset[1])[None, :]) % F
    angle = TWO_PI * total.astype(jnp.float32) / F
    return (jnp.cos(angle), jnp.sin(angle))


def screen_table(w_value):
    centred = jnp.arange(SG, dtype=jnp.float32) - SG / 2.0
    radius = (centred[:, None] * centred[:, None] + centred[None, :] * centred[None, :]) / (SG * SG)
    angle = TWO_PI * w_value * (jnp.sqrt(1.0 + radius) - 1.0)
    return (jnp.cos(angle), jnp.sin(angle))


def matmul(left, right):
    return jnp.dot(left, right, preferred_element_type=jnp.float32)


def complex_dot(left_real, left_imag, right_real, right_imag):
    real_part = matmul(left_real, right_real) - matmul(left_imag, right_imag)
    imag_part = matmul(left_real, right_imag) + matmul(left_imag, right_real)
    return (real_part, imag_part)


def facet_spectrum(facet, basis_real, basis_imag):
    half_real, half_imag = complex_dot(facet[0], facet[1], basis_real.T, basis_imag.T)
    return complex_dot(
        basis_real, basis_imag, half_real.astype(jnp.bfloat16), half_imag.astype(jnp.bfloat16)
    )


def extract(spectrum_real, spectrum_imag, offsets, phase_cos, phase_sin, taper2):
    stacked = jnp.stack([spectrum_real, spectrum_imag])
    padded = jnp.concatenate([stacked, stacked[:, :M, :]], axis=1)
    padded = jnp.concatenate([padded, padded[:, :, :M]], axis=2)
    zero = jnp.zeros((), jnp.int32)

    def window(offset):
        return lax.dynamic_slice(padded, (zero, offset[0], offset[1]), (2, M, M))

    windows = jax.vmap(window)(offsets)
    real_part = taper2 * (phase_cos * windows[:, 0] - phase_sin * windows[:, 1])
    imag_part = taper2 * (phase_cos * windows[:, 1] + phase_sin * windows[:, 0])
    return jnp.stack([real_part, imag_part], axis=1).astype(jnp.bfloat16)


def subgrid_model(summed, pad_real, pad_imag, screen_cos, screen_sin):
    inner_real, inner_imag = complex_dot(pad_real, pad_imag, summed[0], summed[1])
    image_real, image_imag = complex_dot(
        inner_real.astype(jnp.bfloat16), inner_imag.astype(jnp.bfloat16), pad_real.T, pad_imag.T
    )
    model_real = screen_cos * image_real - screen_sin * image_imag
    model_imag = screen_cos * image_imag + screen_sin * image_real
    return jnp.stack([model_real, model_imag]).astype(jnp.bfloat16)


def tile_terms(model, observed_tile, offset, kernel):
    zero = jnp.zeros((), jnp.int32)
    window = lax.dynamic_slice(model, (zero, offset[0], offset[1]), (2, 2 * TV, 2 * TV))
    left = jnp.einsum("jq,cqk->cjk", kernel, window, preferred_element_type=jnp.float32).astype(
        jnp.bfloat16
    )
    predicted = jnp.einsum("cjk,lk->cjl", left, kernel, preferred_element_type=jnp.float32)
    residual = (observed_tile.astype(jnp.float32) - predicted).astype(jnp.bfloat16)
    back = jnp.einsum("cjl,lk->cjk", residual, kernel, preferred_element_type=jnp.float32).astype(
        jnp.bfloat16
    )
    spread = jnp.einsum("jq,cjk->cqk", kernel, back, preferred_element_type=jnp.float32)
    return (residual, spread)


def add_window(adjoint, spread, offset):
    zero = jnp.zeros((), jnp.int32)
    start = (zero, offset[0], offset[1])
    current = lax.dynamic_slice(adjoint, start, spread.shape)
    return lax.dynamic_update_slice(adjoint, current + spread, start)


def back_coefficients(adjoint, pad_real, pad_imag, screen_cos, screen_sin):
    screened_real = (screen_cos * adjoint[0] + screen_sin * adjoint[1]).astype(jnp.bfloat16)
    screened_imag = (screen_cos * adjoint[1] - screen_sin * adjoint[0]).astype(jnp.bfloat16)
    reduced_real = (matmul(pad_real.T, screened_real) + matmul(pad_imag.T, screened_imag)).astype(
        jnp.bfloat16
    )
    reduced_imag = (matmul(pad_real.T, screened_imag) - matmul(pad_imag.T, screened_real)).astype(
        jnp.bfloat16
    )
    coef_real = matmul(reduced_real, pad_real) + matmul(reduced_imag, pad_imag)
    coef_imag = matmul(reduced_imag, pad_real) - matmul(reduced_real, pad_imag)
    return jnp.stack([coef_real, coef_imag]).astype(jnp.bfloat16)


def facet_back(back_spectrum, basis_real, basis_imag):
    half_real = (
        matmul(basis_real, back_spectrum[0]) + matmul(basis_imag, back_spectrum[1])
    ).astype(jnp.bfloat16)
    half_imag = (
        matmul(basis_real, back_spectrum[1]) - matmul(basis_imag, back_spectrum[0])
    ).astype(jnp.bfloat16)
    update_real = matmul(half_real, basis_real) + matmul(half_imag, basis_imag)
    update_imag = matmul(half_imag, basis_real) - matmul(half_real, basis_imag)
    return jnp.stack([update_real, update_imag]).astype(jnp.bfloat16)


def process_tiles(model, observed, tile_offsets, kernel, lower, upper):
    slots = observed.shape[0]

    def tile_step(slot, carry):
        residual_buf, adjoint = carry
        residual, spread = tile_terms(model, observed[slot], tile_offsets[slot], kernel)
        residual_buf = lax.dynamic_update_index_in_dim(residual_buf, residual, slot, 0)
        return (residual_buf, add_window(adjoint, spread, tile_offsets[slot]))

    start = (jnp.zeros((slots, 2, TV, TV), jnp.bfloat16), jnp.zeros((2, SG, SG), jnp.float32))
    return lax.fori_loop(lower, upper, tile_step, start)


def per_device(facets, facet_offsets, subgrid_offsets, w_terms, tile_count, tile_offsets, observed):
    facet_count = lax.axis_size("facet")
    basis_real, basis_imag = basis_tables()
    pad_real, pad_imag = padding_tables(facet_count)
    taper2 = taper_square()
    kernel = kernel_table()
    spectrum_real, spectrum_imag = facet_spectrum(facets[0], basis_real, basis_imag)
    phase_cos, phase_sin = facet_phase(facet_offsets[0])
    contributions = extract(
        spectrum_real, spectrum_imag, subgrid_offsets, phase_cos, phase_sin, taper2
    )
    summed = lax.psum_scatter(
        contributions.astype(jnp.float32), "facet", scatter_dimension=0, tiled=True
    )[0]
    screen_cos, screen_sin = screen_table(w_terms[0])
    model = subgrid_model(summed.astype(jnp.bfloat16), pad_real, pad_imag, screen_cos, screen_sin)
    count = tile_count[0]
    lowest = jnp.zeros((), jnp.int32)
    residual, adjoint = process_tiles(model, observed, tile_offsets, kernel, lowest, count)
    coefficient = back_coefficients(adjoint, pad_real, pad_imag, screen_cos, screen_sin)
    empty = jnp.zeros((2, F + M, F + M), jnp.float32)
    piece = lax.all_gather(coefficient[None], "facet", axis=0, tiled=True)

    def put(index, current):
        offset = subgrid_offsets[index]
        values = piece[index].astype(jnp.float32)
        values_real = taper2 * (phase_cos * values[0] + phase_sin * values[1])
        values_imag = taper2 * (phase_cos * values[1] - phase_sin * values[0])
        return add_window(current, jnp.stack([values_real, values_imag]), offset)

    buffer = lax.fori_loop(0, piece.shape[0], put, empty)
    folded = buffer[:, :F, :].at[:, :M, :].add(buffer[:, F:, :])
    folded = folded[:, :, :F].at[:, :, :M].add(folded[:, :, F:])
    update = facet_back(folded.astype(jnp.bfloat16), basis_real, basis_imag)
    return (residual, update[None])


def solution(mesh):
    placed = (
        P(("groups", "facet"), None, None, None),
        P(("groups", "facet"), None),
        P("groups", None),
        P(("groups", "facet")),
        P(("groups", "facet")),
        P(("groups", "facet"), None),
        P(("groups", "facet"), None, None, None),
    )
    return jax.shard_map(
        per_device,
        mesh=mesh,
        in_specs=placed,
        out_specs=(
            P(("groups", "facet"), None, None, None),
            P(("groups", "facet"), None, None, None),
        ),
        check_vma=False,
    )
```

profile of v0, /device:TPU:1, one launch (start us, length us, event | category | flops | bytes accessed | tf_op | source)
XLA Modules:
  0.0 676.3 jit_solution(7182427111298475314)
XLA Ops:
  7.2 5.1 fusion.99
  12.4 4.0 fusion.101
  16.4 4.4 fusion.69
  20.8 4.0 fusion.107
  24.7 4.6 fusion.68
  33.3 4.1 fusion.66
  37.4 4.3 fusion.67
  42.4 42.2 %while.33 = (s32[]{:T(128)}, f32[2,640,640]{2,1,0:T(8,128)S(1)}, s32[16,3]{0,1:T(4,128)S(1)}, f32[16,2,128,128]{3,2,1,0:T(8,128)}, s32[]{:T(128)}) while((s32[]{:T(128)}, f32[2,640,640]{2,1,0:T(8,128)S(1)}, s32[16,3]{0,1:T(4,128)S(1)}, f32[16,2,128,128]{3,2,1,0:T(8,128)}, s32[]{:T(128)}) %tuple.101), condition=%wide.while_cond.2, body=%wide.while_body.2.sunk | while | flops 2 | bytes 263785 | solution.py:92
  91.1 61.5 %reduce-scatter.2.cloned.1.call-done = f32[1,2,128,128]{3,2,1,0:T(8,128)} async-done(((f32[16,2,128,128]{3,2,1,0:T(8,128)}), f32[1,2,128,128]{3,2,1,0:T(8,128)}) %reduce-scatter.2.cloned.1.call-update) | async-done | bytes 131088 | tf_op jit(solution)/shard_map/reduce_scatter | solution.py:182
  162.3 5.7 fusion.109
  170.5 67.4 %while.34 = (s32[]{:T(128)}, bf16[16,2,128,128]{3,2,1,0:T(8,128)(2,1)}, f32[2,512,512]{2,1,0:T(8,128)S(1)}, s32[]{:T(128)}, bf16[16,2,128,128]{3,2,1,0:T(8,128)(...) while((s32[]{:T(128)}, ...), condition=%wide.region_2.3_spmd.clone.clone, body=%wide.region_1.2_spmd.clone.clone.sunk | while | flops 102334472 | bytes 5768983 | solution.py:168
  178.8 8.8 %dynamic_update_slice.26 = f32[2,512,512]{2,1,0:T(8,128)S(1)} dynamic-update-slice(f32[2,512,512]{2,1,0:T(8,128)S(1)} %get-tuple-element.556, f32[2,256,256]{2,1,0:T(8,128)S(1)} %copy.19, s32[]{:T(128)} %constant.166.clone.1..sunk, s32[]{:T(128)S(6)} %select_n.283, s32[]{:T(128)S(6)} %select_n.284) | dynamic-update-slice | bytes 1048580 | tf_op jit(solution)/shard_map/while/body/dynamic_update_slice | solution.py:129
  196.0 7.7 %dynamic_update_slice.26 = f32[2,512,512]{2,1,0:T(8,128)S(1)} dynamic-update-slice(f32[2,512,512]{2,1,0:T(8,128)S(1)} %get-tuple-element.556, f32[2,256,256]{2,1,0:T(8,128)S(1)} %copy.19, s32[]{:T(128)} %constant.166.clone.1..sunk, s32[]{:T(128)S(6)} %select_n.283, s32[]{:T(128)S(6)} %select_n.284) | dynamic-update-slice | bytes 1048580 | tf_op jit(solution)/shard_map/while/body/dynamic_update_slice | solution.py:129
  212.0 8.8 %dynamic_update_slice.26 = f32[2,512,512]{2,1,0:T(8,128)S(1)} dynamic-update-slice(f32[2,512,512]{2,1,0:T(8,128)S(1)} %get-tuple-element.556, f32[2,256,256]{2,1,0:T(8,128)S(1)} %copy.19, s32[]{:T(128)} %constant.166.clone.1..sunk, s32[]{:T(128)S(6)} %select_n.283, s32[]{:T(128)S(6)} %select_n.284) | dynamic-update-slice | bytes 1048580 | tf_op jit(solution)/shard_map/while/body/dynamic_update_slice | solution.py:129
  229.2 8.1 %dynamic_update_slice.26 = f32[2,512,512]{2,1,0:T(8,128)S(1)} dynamic-update-slice(f32[2,512,512]{2,1,0:T(8,128)S(1)} %get-tuple-element.556, f32[2,256,256]{2,1,0:T(8,128)S(1)} %copy.19, s32[]{:T(128)} %constant.166.clone.1..sunk, s32[]{:T(128)S(6)} %select_n.283, s32[]{:T(128)S(6)} %select_n.284) | dynamic-update-slice | bytes 1048580 | tf_op jit(solution)/shard_map/while/body/dynamic_update_slice | solution.py:129
  237.9 5.4 fusion.88
  253.4 246.2 %all-gather.2.cloned.1.call-done = bf16[16,2,128,128]{3,2,1,0:T(8,128)(2,1)} async-done(((bf16[1,2,128,128]{3,2,1,0:T(8,128)(2,1)}), bf16[16,2,128,128]{3,2,1,0:T(8,128)(2,1)}) %all-gather.2.cloned.1.call-update) | async-done | bytes 1048592 | tf_op jit(solution)/shard_map/all_gather | solution.py:192
  499.8 131.6 %while.35 = (s32[]{:T(128)}, f32[2,640,640]{2,1,0:T(8,128)S(1)}, s32[16,2]{0,1:T(2,128)S(1)}, bf16[16,2,128,128]{3,2,1,0:T(8,128)(2,1)}, f32[128]{0:T(128)S(1)},...) while((s32[]{:T(128)}, f32[2,640,640]{2,1,0:T(8,128)S(1)}, ...), condition=%wide.region_4.5_spmd.clone.clone.clone, body=%wide.region_3.4_spmd.clone.clone.clone.sunk | while | flops 475144 | bytes 1116381 | solution.py:201
  639.8 4.2 fusion.70
  644.0 5.0 fusion.105
  649.1 4.2 fusion.71
  653.3 4.8 fusion.103
  658.1 5.0 fusion.75
  663.1 5.0 fusion.74
  (228 shorter events, 169.3 us)
Async XLA Ops:
  7.2 5.2 copy-start.3
  7.2 145.4 %reduce-scatter.2.cloned.1.call-start = ((), (), s32[]{:S(2)}) async-start(), calls=%async_computation.1 | async-start | bytes 2228224 | tf_op jit(solution)/shard_map/reduce_scatter | solution.py:182
  41.7 0.7 copy-start
  41.7 42.9 %copy-start.2 = (s32[1,2]{1,0:T(1,128)S(1)}, s32[1,2]{1,0:T(1,128)}, u32[]{:S(2)}) copy-start(s32[1,2]{1,0:T(1,128)} %param.16) | copy-start | bytes 28
  90.3 409.3 %all-gather.2.cloned.1.call-start = ((), (), s32[]{:S(2)}) async-start(), calls=%async_computation.2 | async-start | bytes 1114112 | tf_op jit(solution)/shard_map/all_gather | solution.py:192
  167.9 2.5 copy-start.1
Sparse Core Ops, SparseCore 0:
  90.4 62.0 reduce-scatter.1
  253.5 246.0 all-gather.1
where the time goes:
time: 688 us; the launch traced here: 676 us
  waiting for transfers between devices  308 us (45%)
  local copies, waits for them, and re-layouts  132 us (19%)
  matrix products  105 us (15%)
  loops' own time  80.9 us (12%)
  other arithmetic  36 us (5%)
  between operations  15.2 us (2%)
    all_gather x1, waiting for transfers between devices, per_device(): piece = lax.all_gather(coefficient[None], 'facet', axis=0, tiled=True)  246 us
    dot_general x32, matrix products, matmul(): return jnp.dot(left, right, preferred_element_type=jnp.float32)  94.4 us
    dynamic_update_slice x24, local copies, waits for them, and re-layouts, add_window(): return lax.dynamic_update_slice(adjoint, current + spread, start)  72.4 us
    another operation x1, loops' own time, per_device(): buffer = lax.fori_loop(0, piece.shape[0], put, empty)  62.4 us
    reduce_scatter x1, waiting for transfers between devices, per_device(): lax.psum_scatter(contributions.astype(jnp.float32), 'facet', scatter_dime...  61.5 us
    gather x48, local copies, waits for them, and re-layouts  42.2 us
    another operation x1, loops' own time, process_tiles(): return lax.fori_loop(lower, upper, tile_step, start)  18.5 us
  transfers between devices with their start and end apart: 2, of which 2 were waited for; matrix products, arithmetic and copies ran while one was open for 0% of the time, Pallas kernels for 0%

commit v1 on v0

v1 whole, which is shorter than its diff:
```python
import functools
import math

import jax
import jax.numpy as jnp
import ml_dtypes
import numpy as np
from jax import lax
from jax.experimental import pallas as pl
from jax.experimental.pallas import tpu as pltpu
from jax.sharding import PartitionSpec as P

F = 512
M = 128
SG = 512
TV = 128
BF = jnp.bfloat16
F32 = jnp.float32
TWO_PI = 2.0 * math.pi
VMEM_LIMIT = 56 * 1024 * 1024


def basis_tables():
    index = np.arange(F, dtype=np.int64)
    angle = -TWO_PI * ((index[:, None] * index[None, :]) % F) / F
    table = np.stack([np.cos(angle), np.sin(angle)]) / math.sqrt(F)
    return table.astype(ml_dtypes.bfloat16)


def padding_tables(facet_count):
    product = (np.arange(SG)[:, None] * np.arange(M)[None, :]) % SG
    angle = TWO_PI * product / SG
    scale = (M * math.sqrt(facet_count)) ** (-0.5)
    table = np.stack([np.cos(angle), np.sin(angle)]) * scale
    return table.astype(ml_dtypes.bfloat16)


def kernel_table():
    rows = np.arange(TV, dtype=np.float64)[:, None]
    columns = np.arange(2 * TV, dtype=np.float64)[None, :]
    distance = columns - 2.0 * rows - 1.0
    value = 0.75 * np.exp(-((distance / 1.5) ** 2))
    return np.where(np.abs(distance) <= 4.0, value, 0.0).astype(ml_dtypes.bfloat16)


def taper_square():
    position = np.arange(M, dtype=np.float64)
    taper = 0.6 + 0.4 * np.sin(math.pi * (position + 0.5) / M)
    return (taper[:, None] * taper[None, :]).astype(np.float32)


def turn_polynomials():
    nodes = 0.5 * np.cos(math.pi * (np.arange(400) + 0.5) / 800)
    square = nodes * nodes
    powers = np.stack([square**k for k in range(8)], axis=1)
    cos_c = np.linalg.lstsq(powers, np.cos(TWO_PI * nodes), rcond=None)[0]
    sin_c = np.linalg.lstsq(powers, np.sin(TWO_PI * nodes) / nodes, rcond=None)[0]
    return [float(c) for c in cos_c], [float(c) for c in sin_c]


COS_C, SIN_C = turn_polynomials()


def cos_sin_turns(turns):
    rest = turns - jnp.floor(turns + 0.5)
    square = rest * rest
    cos_v = jnp.full_like(square, COS_C[7])
    sin_v = jnp.full_like(square, SIN_C[7])
    for k in range(6, -1, -1):
        cos_v = cos_v * square + COS_C[k]
        sin_v = sin_v * square + SIN_C[k]
    return cos_v, sin_v * rest


def dot(left, right):
    return jnp.dot(left, right, preferred_element_type=F32)


def dot_nt(left, right):
    return lax.dot_general(left, right, (((1,), (1,)), ((), ())), preferred_element_type=F32)


def phase_taper(fo_ref, taper_ref):
    rows = lax.broadcasted_iota(jnp.int32, (M, M), 0)
    columns = lax.broadcasted_iota(jnp.int32, (M, M), 1)
    total = (rows * fo_ref[0, 0] + columns * fo_ref[0, 1]) & (F - 1)
    cos_v, sin_v = cos_sin_turns(total.astype(F32) * (1.0 / F))
    taper2 = taper_ref[...]
    return cos_v * taper2, sin_v * taper2


def forward_kernel(stages, me_ref, fo_ref, so_ref, facet_ref, basis_ref, taper_ref, *rest):
    outs, (half_ref, spec_ref) = rest[: len(stages)], rest[len(stages) :]
    br, bi = basis_ref[0], basis_ref[1]
    fr, fi = facet_ref[0, 0], facet_ref[0, 1]
    half_ref[0] = (dot(fr, br) - dot(fi, bi)).astype(BF)
    half_ref[1] = (dot(fr, bi) + dot(fi, br)).astype(BF)
    hr, hi = half_ref[0], half_ref[1]
    spectrum = (dot(br, hr) - dot(bi, hi), dot(br, hi) + dot(bi, hr))
    columns = F // M
    for plane in range(2):
        for c in range(columns):
            part = spectrum[plane][:, c * M : (c + 1) * M]
            spec_ref[plane, c, :F] = part
            spec_ref[plane, c, F:] = part[:M]
            if c == 0:
                spec_ref[plane, columns, :F] = part
                spec_ref[plane, columns, F:] = part[:M]
    pc, ps = phase_taper(fo_ref, taper_ref)
    me = me_ref[0]

    def block(out_ref, item, j):
        owner = j ^ me
        sx, sy = so_ref[owner, 0], so_ref[owner, 1]
        lane = sy // M
        shift = (2 * M - (sy & (M - 1))) & (2 * M - 1)
        parts = []
        for plane in range(2):
            left = spec_ref[plane, lane, pl.ds(sx, M), :]
            right = spec_ref[plane, lane + 1, pl.ds(sx, M), :]
            wide = jnp.concatenate([left, right], axis=1)
            parts.append(pltpu.roll(wide, shift, 1)[:, :M])
        wr, wi = parts
        out_ref[item, 0] = (pc * wr - ps * wi).astype(BF)
        out_ref[item, 1] = (pc * wi + ps * wr).astype(BF)

    for out_ref, (count, step, first) in zip(outs, stages):
        if count == 1:
            block(out_ref, 0, first)
        else:

            def body(item, carry, out_ref=out_ref, step=step, first=first):
                block(out_ref, item, item * step + first)
                return carry

            lax.fori_loop(0, count, body, 0)


def subgrid_kernel(
    parts, w_ref, tc_ref, to_ref, *rest
):
    sums = rest[:parts]
    (obs_ref, pad_ref, padt_ref, kern_ref, kt_ref, res_ref, coef_ref) = rest[parts : parts + 7]
    (screen_ref, model_ref, kvt_ref, rows_ref, z_ref) = rest[parts + 7 :]
    slots = obs_ref.shape[0]
    count = tc_ref[0]
    w = w_ref[0]

    row = lax.broadcasted_iota(jnp.int32, (SG, 1), 0).astype(F32) - SG / 2.0
    column = lax.broadcasted_iota(jnp.int32, (1, SG), 1).astype(F32) - SG / 2.0
    row2 = row * row * (1.0 / (SG * SG)) + 1.0
    column2 = column * column * (1.0 / (SG * SG))
    cos_v, sin_v = cos_sin_turns((jnp.sqrt(row2 + column2) - 1.0) * w)
    screen_ref[0] = cos_v
    screen_ref[1] = sin_v

    for t in range(slots):
        band = kt_ref[pl.ds(2 * TV - to_ref[t, 1], SG), :]
        kvt_ref[:, t * TV : (t + 1) * TV] = band.astype(BF)

    def total(plane):
        value = sums[0][0, plane].astype(F32)
        for ref in sums[1:]:
            value = value + ref[0, plane].astype(F32)
        return value.astype(BF)

    sr, si = total(0), total(1)
    pr, pi = pad_ref[0], pad_ref[1]
    inner_r = (dot(pr, sr) - dot(pi, si)).astype(BF)
    inner_i = (dot(pr, si) + dot(pi, sr)).astype(BF)
    tr, ti = padt_ref[0], padt_ref[1]
    image_r = dot(inner_r, tr) - dot(inner_i, ti)
    image_i = dot(inner_r, ti) + dot(inner_i, tr)
    sc, ss = screen_ref[0], screen_ref[1]
    model_ref[:SG] = (sc * image_r - ss * image_i).astype(BF)
    model_ref[SG:] = (sc * image_i + ss * image_r).astype(BF)

    model = model_ref[...]
    kern = kern_ref[...]
    for t0 in range(0, slots, 2):
        pair = dot(model, kvt_ref[:, t0 * TV : (t0 + 2) * TV])
        for t in (t0, t0 + 1):
            rows_ref[t % rows_ref.shape[0]] = pair[:, (t - t0) * TV : (t - t0 + 1) * TV]
        for t in (t0, t0 + 1):
            slot = t % rows_ref.shape[0]
            ou = to_ref[t, 0]
            wr = rows_ref[slot, pl.ds(ou, 2 * TV), :]
            wi = rows_ref[slot, pl.ds(SG + ou, 2 * TV), :]
            window = jnp.concatenate([wr.astype(BF), wi.astype(BF)], axis=1)
            predicted = dot(kern, window)
            live = count > t
            res = []
            for plane in range(2):
                value = obs_ref[t, plane].astype(F32) - predicted[:, plane * TV : (plane + 1) * TV]
                res.append(jnp.where(live, value, 0.0).astype(BF))
                res_ref[t, plane] = res[plane]
            band = kt_ref[pl.ds(2 * TV - ou, SG), :].astype(BF)
            z = dot(band, jnp.concatenate(res, axis=1)).astype(BF)
            z_ref[:SG, t * TV : (t + 1) * TV] = z[:, :TV]
            z_ref[SG:, t * TV : (t + 1) * TV] = z[:, TV:]

    kvt = kvt_ref[...]
    ar = dot_nt(z_ref[:SG], kvt)
    ai = dot_nt(z_ref[SG:], kvt)
    screened_r = (sc * ar + ss * ai).astype(BF)
    screened_i = (sc * ai - ss * ar).astype(BF)
    reduced_r = (dot(tr, screened_r) + dot(ti, screened_i)).astype(BF)
    reduced_i = (dot(tr, screened_i) - dot(ti, screened_r)).astype(BF)
    coef_ref[0, 0] = (dot(reduced_r, pr) + dot(reduced_i, pi)).astype(BF)
    coef_ref[0, 1] = (dot(reduced_i, pr) - dot(reduced_r, pi)).astype(BF)


def backward_kernel(pieces, me_ref, fo_ref, so_ref, basis_ref, taper_ref, *rest):
    ins = rest[: len(pieces)]
    out_ref, grid_ref, half_ref = rest[len(pieces) :]
    grid_ref[...] = jnp.zeros_like(grid_ref)
    pc, ps = phase_taper(fo_ref, taper_ref)
    me = me_ref[0]
    blank = jnp.zeros((M, M), F32)

    def block(in_ref, item, j):
        owner = j ^ me
        sx, sy = so_ref[owner, 0], so_ref[owner, 1]
        lane = sy // M
        shift = sy & (M - 1)
        cr, ci = in_ref[item, 0].astype(F32), in_ref[item, 1].astype(F32)
        values = (pc * cr + ps * ci, pc * ci - ps * cr)
        for plane in range(2):
            wide = pltpu.roll(jnp.concatenate([values[plane], blank], axis=1), shift, 1)
            grid_ref[plane, lane, pl.ds(sx, M), :] += wide[:, :M]
            grid_ref[plane, lane + 1, pl.ds(sx, M), :] += wide[:, M:]

    for in_ref, (count, step, first) in zip(ins, pieces):
        if count == 1:
            block(in_ref, 0, first)
        else:

            def body(item, carry, in_ref=in_ref, step=step, first=first):
                block(in_ref, item, item * step + first)
                return carry

            lax.fori_loop(0, count, body, 0)

    columns = F // M
    folded = []
    for plane in range(2):
        grid_ref[plane, 0] += grid_ref[plane, columns]
        for c in range(columns):
            grid_ref[plane, c, :M] += grid_ref[plane, c, F:]
        strips = [grid_ref[plane, c, :F].astype(BF) for c in range(columns)]
        folded.append(jnp.concatenate(strips, axis=1))
    sr, si = folded
    br, bi = basis_ref[0], basis_ref[1]
    half_ref[0] = (dot(br, sr) + dot(bi, si)).astype(BF)
    half_ref[1] = (dot(br, si) - dot(bi, sr)).astype(BF)
    hr, hi = half_ref[0], half_ref[1]
    out_ref[0, 0] = (dot(hr, br) + dot(hi, bi)).astype(BF)
    out_ref[0, 1] = (dot(hi, br) - dot(hr, bi)).astype(BF)


SMEM = pl.BlockSpec(memory_space=pltpu.SMEM)
VMEM = pl.BlockSpec(memory_space=pltpu.VMEM)
PARAMS = pltpu.CompilerParams(vmem_limit_bytes=VMEM_LIMIT)


def blocks(count):
    return jax.ShapeDtypeStruct((count, 2, M, M), BF)


def exchange(value, bit, n):
    return lax.ppermute(value, "facet", [(i, i ^ bit) for i in range(n)])


def per_device(facets, facet_offsets, subgrid_offsets, w_terms, tile_count, tile_offsets, observed):
    n = lax.axis_size("facet")
    bits = [1 << k for k in range(n.bit_length() - 1)]
    me = lax.axis_index("facet").astype(jnp.int32).reshape(1)
    basis = jnp.asarray(basis_tables())
    taper2 = jnp.asarray(taper_square())
    pad_np = padding_tables(n)
    kern_np = kernel_table()
    kt_np = np.zeros((6 * TV, TV), np.float32)
    kt_np[2 * TV : 4 * TV] = kern_np.astype(np.float32).T

    stages = [(n // (2 * b), 2 * b, b) for b in bits] + [(1, 1, 0)]
    own = pl.pallas_call(
        functools.partial(forward_kernel, stages),
        out_shape=[blocks(count) for count, _, _ in stages],
        in_specs=[SMEM] * 3 + [VMEM] * 3,
        out_specs=[VMEM] * len(stages),
        scratch_shapes=[
            pltpu.VMEM((2, F, F), BF),
            pltpu.VMEM((2, F // M + 1, F + M, M), F32),
        ],
        compiler_params=PARAMS,
        name="forward",
    )(me, facet_offsets, subgrid_offsets, facets, basis, taper2)

    arrived = []
    for k, b in enumerate(bits):
        send = own[k]
        if k:
            total = send.astype(F32)
            for i, got in enumerate(arrived):
                skip = b >> (i + 1)
                pick = got.reshape((got.shape[0] // (2 * skip), 2 * skip) + got.shape[1:])[:, skip]
                total = total + pick.astype(F32)
            send = total.astype(BF)
        arrived.append(exchange(send, b, n))
    sums = [own[-1]] + [got[:1] for got in arrived]

    residual, coefficient = pl.pallas_call(
        functools.partial(subgrid_kernel, len(sums)),
        out_shape=[
            jax.ShapeDtypeStruct(observed.shape, BF),
            blocks(1),
        ],
        in_specs=[SMEM] * 3 + [VMEM] * (len(sums) + 5),
        out_specs=[VMEM] * 2,
        scratch_shapes=[
            pltpu.VMEM((2, SG, SG), F32),
            pltpu.VMEM((2 * SG, SG), BF),
            pltpu.VMEM((SG, observed.shape[0] * TV), BF),
            pltpu.VMEM((8, 2 * SG, TV), F32),
            pltpu.VMEM((2 * SG, observed.shape[0] * TV), BF),
        ],
        compiler_params=PARAMS,
        name="subgrid",
    )(
        w_terms,
        tile_count,
        tile_offsets,
        *sums,
        observed,
        jnp.asarray(pad_np),
        jnp.asarray(pad_np.transpose(0, 2, 1)),
        jnp.asarray(kern_np),
        jnp.asarray(kt_np),
    )

    gathered = coefficient
    held = [coefficient]
    pieces = [(1, 1, 0)]
    for b in reversed(bits):
        got = exchange(gathered, b, n)
        held.append(got)
        pieces.append((got.shape[0], 2 * b, b))
        if b > 1:
            gathered = jnp.stack([gathered, got], axis=1).reshape((-1,) + got.shape[1:])

    update = pl.pallas_call(
        functools.partial(backward_kernel, pieces),
        out_shape=jax.ShapeDtypeStruct(facets.shape, BF),
        in_specs=[SMEM] * 3 + [VMEM] * (2 + len(held)),
        out_specs=VMEM,
        scratch_shapes=[
            pltpu.VMEM((2, F // M + 1, F + M, M), F32),
            pltpu.VMEM((2, F, F), BF),
        ],
        compiler_params=PARAMS,
        name="backward",
    )(me, facet_offsets, subgrid_offsets, basis, taper2, *held)
    return (residual, update)


def solution(mesh):
    placed = (
        P(("groups", "facet"), None, None, None),
        P(("groups", "facet"), None),
        P("groups", None),
        P(("groups", "facet")),
        P(("groups", "facet")),
        P(("groups", "facet"), None),
        P(("groups", "facet"), None, None, None),
    )
    return jax.shard_map(
        per_device,
        mesh=mesh,
        in_specs=placed,
        out_specs=(
            P(("groups", "facet"), None, None, None),
            P(("groups", "facet"), None, None, None),
        ),
        check_vma=False,
    )
```

time: 688 us -> 81.7 us (0.12); the launches traced: 676 us -> 81.1 us
  waiting for transfers between devices: 308 us -> 23.1 us
  local copies, waits for them, and re-layouts: 132 us -> 6.67 us
  matrix products: 105 us -> 0 us
  loops' own time: 80.9 us -> 0 us
  other arithmetic: 36 us -> 2.11 us
  Pallas kernels: 0 us -> 31.9 us
  starting transfers between devices: 0.08 us -> 15.2 us
  between operations: 15.2 us -> 2.02 us
    all_gather x1 -> x0, waiting for transfers between devices: 246 us -> none  [per_device(): piece = lax.all_gather(coefficient[None], 'facet', axis=0, tiled=True)]
    dot_general x40 -> x0, matrix products: 105 us -> none  [the longest x32 94.4 us: matmul(): return jnp.dot(left, right, preferred_element_type=jnp.float32)]
    another operation x3 -> x0, loops' own time: 80.9 us -> none  [the longest x1 62.4 us: per_device(): buffer = lax.fori_loop(0, piece.shape[0], put, empty)]
    dynamic_update_slice x24 -> x0, local copies, waits for them, and re-layouts: 72.4 us -> none  [add_window(): return lax.dynamic_update_slice(adjoint, current + spread, start)]
    reduce_scatter x1 -> x0, waiting for transfers between devices: 61.5 us -> none  [per_device(): lax.psum_scatter(contributions.astype(jnp.float32), 'facet', scatter_dime...]
    gather x48 -> x0, local copies, waits for them, and re-layouts: 42.2 us -> none
    pallas_call x0 -> x3, Pallas kernels: none -> 31.9 us  [the longest x1 17.9 us: per_device(): pl.pallas_call(functools.partial(subgrid_kernel, len(sums)), out_shape=[j...]
    ppermute x0 -> x8, waiting for transfers between devices: none -> 23.1 us  [exchange(): return lax.ppermute(value, 'facet', [(i, i ^ bit) for i in range(n)])]
  transfers between devices with their start and end apart: 2 -> 8, of which waited for: 2 -> 7; matrix products, arithmetic and copies ran while one was open for 0% -> 3% of each run, Pallas kernels for 0% -> 0%
where the time goes in v1:
time: 81.7 us; the launch traced here: 81.1 us
  Pallas kernels  31.9 us (39%)
  waiting for transfers between devices  23.1 us (28%)
  starting transfers between devices  15.2 us (19%)
  local copies, waits for them, and re-layouts  6.67 us (8%)
  other arithmetic  2.11 us (3%)
  between operations  2.02 us (2%)
    ppermute x8, waiting for transfers between devices, exchange(): return lax.ppermute(value, 'facet', [(i, i ^ bit) for i in range(n)])  23.1 us
    pallas_call x1, Pallas kernels, per_device(): pl.pallas_call(functools.partial(subgrid_kernel, len(sums)), out_shape=[j...  17.9 us
    ppermute x8, starting transfers between devices, exchange(): return lax.ppermute(value, 'facet', [(i, i ^ bit) for i in range(n)])  15.2 us
    pallas_call x1, Pallas kernels, per_device(): pl.pallas_call(functools.partial(backward_kernel, pieces), out_shape=jax....  7.08 us
    pallas_call x1, Pallas kernels, per_device(): pl.pallas_call(functools.partial(forward_kernel, stages), out_shape=[bloc...  6.97 us
    unnamed x20, local copies, waits for them, and re-layouts  4.72 us
    slice x3, local copies, waits for them, and re-layouts, per_device(): sums = [own[-1]] + [got[:1] for got in arrived]  1.89 us
  transfers between devices with their start and end apart: 8, of which 7 were waited for; matrix products, arithmetic and copies ran while one was open for 3% of the time, Pallas kernels for 0%

profile of v1, /device:TPU:1, one launch (start us, length us, event | category | flops | bytes accessed | tf_op | source)
XLA Modules:
  0.0 81.1 jit_solution(13920737137128080460)
XLA Ops:
  0.6 0.7 copy-done.7
  1.3 0.7 copy.21.so_ref
  2.0 7.0 %forward.1 = (bf16[8,2,128,128]{3,2,1,0:T(8,128)(2,1)}, bf16[4,2,128,128]{3,2,1,0:T(8,128)(2,1)}, bf16[2,2,128,128]{3,2,1,0:T(8,128)(2,1)}, bf16[1,2,128,128]{3,2,1,0:T(8,128)(2,1)}, bf16[1,2,128,128]{3,2,1,0:T(8,128)(2,1)}) custom-call(s32[1]{0:T(128)} %bitcast.me_ref, s32[1,2]{1,0:T(1,128)} %fo_ref.3, s32[16,2]{1,0:T(8,128)} %copy.21.so_ref, ...), custom_call_target="tpu_custom_call" | custom-call | tf_op jit(solution)/shard_map/forward/pallas_call | solution.py:286
  9.0 2.1 %collective-permute-done = bf16[8,2,128,128]{3,2,1,0:T(8,128)(2,1)S(1)} collective-permute-done((bf16[8,2,128,128]{3,2,1,0:T(8,128)(2,1)}, bf16[8,2,128,128]{3,2,1,0:T(8,128)(2,1)S(1)}, u32[]{:S(2)}, u32[]{:S(2)}) %collective-permute-start) | collective-permute-done | bytes 524320 | tf_op jit(solution)/shard_map/ppermute | solution.py:271
  11.1 1.1 %fusion = bf16[4,2,128,128]{3,2,1,0:T(8,128)(2,1)S(1)} fusion(bf16[4,2,128,128]{3,2,1,0:T(8,128)(2,1)} %get-tuple-element.11, bf16[4,2,2,128,128]{4,3,2,1,0:T(8,128)(2,1)S(1)} %bitcast.57), kind=kLoop, calls=%fused_computation.2 | loop fusion | flops 524288 | bytes 786432 | tf_op jit(solution)/shard_map/convert_element_type | solution.py:308
  12.1 2.4 %collective-permute-start.1 = (bf16[4,2,128,128]{3,2,1,0:T(8,128)(2,1)S(1)}, bf16[4,2,128,128]{3,2,1,0:T(8,128)(2,1)S(1)}, u32[]{:S(2)}, u32[]{:S(2)}) collective-permute-start(bf16[4,2,128,128]{3,2,1,0:T(8,128)(2,1)S(1)} %fusion), channel_id=1, source_target_pairs={{0,2},{1,3},{2,0},{3,1},{4,6},{5,7},{6,4},{7,5},{8,10},{9,11},{10,... | collective-permute-start | bytes 786440 | tf_op jit(solution)/shard_map/ppermute | solution.py:271
  14.6 6.4 %collective-permute-done.1 = bf16[4,2,128,128]{3,2,1,0:T(8,128)(2,1)S(1)} collective-permute-done((bf16[4,2,128,128]{3,2,1,0:T(8,128)(2,1)S(1)}, bf16[4,2,128,128]{3,2,1,0:T(8,128)(2,1)S(1)}, u32[]{:S(2)}, u32[]{:S(2)}) %collective-permute-start.1) | collective-permute-done | bytes 262176 | tf_op jit(solution)/shard_map/ppermute | solution.py:271
  21.0 1.3 %collective-permute-start.2 = (bf16[2,2,128,128]{3,2,1,0:T(8,128)(2,1)S(1)}, bf16[2,2,128,128]{3,2,1,0:T(8,128)(2,1)S(1)}, u32[]{:S(2)}, u32[]{:S(2)}) collective-permute-start(bf16[2,2,128,128]{3,2,1,0:T(8,128)(2,1)S(1)} %fusion.1), channel_id=1, source_target_pairs={{0,4},{1,5},{2,6},{3,7},{4,0},{5,1},{6,2},{7,3},{8,12},{9,13},{10,... | collective-permute-start | bytes 393224 | tf_op jit(solution)/shard_map/ppermute | solution.py:271
  22.3 2.9 %collective-permute-done.2 = bf16[2,2,128,128]{3,2,1,0:T(8,128)(2,1)S(1)} collective-permute-done((bf16[2,2,128,128]{3,2,1,0:T(8,128)(2,1)S(1)}, bf16[2,2,128,128]{3,2,1,0:T(8,128)(2,1)S(1)}, u32[]{:S(2)}, u32[]{:S(2)}) %collective-permute-start.2) | collective-permute-done | bytes 131104 | tf_op jit(solution)/shard_map/ppermute | solution.py:271
  25.3 2.0 %collective-permute-start.3 = (bf16[1,2,128,128]{3,2,1,0:T(8,128)(2,1)S(1)}, bf16[1,2,128,128]{3,2,1,0:T(8,128)(2,1)S(1)}, u32[]{:S(2)}, u32[]{:S(2)}) collective-permute-start(bf16[1,2,128,128]{3,2,1,0:T(8,128)(2,1)S(1)} %fusion.2), channel_id=1, source_target_pairs={{0,8},{1,9},{2,10},{3,11},{4,12},{5,13},{6,14},{7,15},{8,0},{9,1},... | collective-permute-start | bytes 196616 | tf_op jit(solution)/shard_map/ppermute | solution.py:271
  28.6 0.7 copy.25.to_ref
  29.2 0.6 slice.36.rest_1_
  31.8 17.9 %subgrid.1 = (bf16[16,2,128,128]{3,2,1,0:T(8,128)(2,1)}, bf16[1,2,128,128]{3,2,1,0:T(8,128)(2,1)}) custom-call(f32[1]{0:T(128)S(6)} %copy.33.w_ref, s32[1]{0:T(128)S(6)} %copy.34.tc_ref, s32[16,2]{1,0:T(8,128)} %copy.25.to_ref, bf16[1,2,128,128]{3,2,1,0:T(8,128)(2,1)} %get-tuple-element.9.rest_0_, bf16[1,2,128,128]{3,2,1,0:T(8,128)(2,1)} %slice.36.rest_1_, ...), custom_call_target="tpu_custom_call" | custom-call | tf_op jit(solution)/shard_map/subgrid/pallas_call | solution.py:312
  50.1 3.7 %collective-permute-done.4.rest_1_ = bf16[1,2,128,128]{3,2,1,0:T(8,128)(2,1)S(1)} collective-permute-done((bf16[1,2,128,128]{3,2,1,0:T(8,128)(2,1)}, bf16[1,2,128,128]{3,2,1,0:T(8,128)(2,1)S(1)}, u32[]{:S(2)}, u32[]{:S(2)}) %collective-permute-start.4) | collective-permute-done | bytes 65568 | tf_op jit(solution)/shard_map/ppermute | solution.py:271
  53.8 0.9 %fusion.3 = (bf16[2,1,2,128,128]{4,3,2,0,1:T(8,128)(2,1)S(1)}, bf16[2,2,128,128]{3,2,1,0:T(8,128)(2,1)S(1)}) fusion(bf16[1,1,2,128,128]{4,3,2,1,0:T(8,128)(2,1)S(1)} %bitcast.63, bf16[1,1,2,128,128]{4,3,2,1,0:T(8,128)(2,1)} %bitcast.62), kind=kLoop, calls=%fused_computation.15 | loop fusion | flops 65536 | bytes 393216 | tf_op jit(solution)/shard_map/stack;reshape | solution.py:349
  54.7 1.4 %collective-permute-start.5 = (bf16[2,2,128,128]{3,2,1,0:T(8,128)(2,1)S(1)}, bf16[2,2,128,128]{3,2,1,0:T(8,128)(2,1)S(1)}, u32[]{:S(2)}, u32[]{:S(2)}) collective-permute-start(bf16[2,2,128,128]{3,2,1,0:T(8,128)(2,1)S(1)} %get-tuple-element.17), channel_id=1, source_target_pairs={{0,4},{1,5},{2,6},{3,7},{4,0},{5,1},{6,2},{7,3},{8,12},{9,13},{10,... | collective-permute-start | bytes 393224 | tf_op jit(solution)/shard_map/ppermute | solution.py:271
  56.1 2.5 %collective-permute-done.5.rest_2_ = bf16[2,2,128,128]{3,2,1,0:T(8,128)(2,1)S(1)} collective-permute-done((bf16[2,2,128,128]{3,2,1,0:T(8,128)(2,1)S(1)}, bf16[2,2,128,128]{3,2,1,0:T(8,128)(2,1)S(1)}, u32[]{:S(2)}, u32[]{:S(2)}) %collective-permute-start.5) | collective-permute-done | bytes 131104 | tf_op jit(solution)/shard_map/ppermute | solution.py:271
  59.3 1.5 %collective-permute-start.6 = (bf16[4,2,128,128]{3,2,1,0:T(8,128)(2,1)S(1)}, bf16[4,2,128,128]{3,2,1,0:T(8,128)(2,1)S(1)}, u32[]{:S(2)}, u32[]{:S(2)}) collective-permute-start(bf16[4,2,128,128]{3,2,1,0:T(8,128)(2,1)S(1)} %bitcast.55), channel_id=1, source_target_pairs={{0,2},{1,3},{2,0},{3,1},{4,6},{5,7},{6,4},{7,5},{8,10},{9,11},{10,... | collective-permute-start | bytes 786440 | tf_op jit(solution)/shard_map/ppermute | solution.py:271
  60.8 4.0 %collective-permute-done.6.rest_3_ = bf16[4,2,128,128]{3,2,1,0:T(8,128)(2,1)S(1)} collective-permute-done((bf16[4,2,128,128]{3,2,1,0:T(8,128)(2,1)S(1)}, bf16[4,2,128,128]{3,2,1,0:T(8,128)(2,1)S(1)}, u32[]{:S(2)}, u32[]{:S(2)}) %collective-permute-start.6) | collective-permute-done | bytes 262176 | tf_op jit(solution)/shard_map/ppermute | solution.py:271
  64.8 0.6 copy-done
  65.5 6.2 %collective-permute-start.7 = (bf16[8,2,128,128]{3,2,1,0:T(8,128)(2,1)S(1)}, bf16[8,2,128,128]{3,2,1,0:T(8,128)(2,1)S(1)}, u32[]{:S(2)}, u32[]{:S(2)}) collective-permute-start(bf16[8,2,128,128]{3,2,1,0:T(8,128)(2,1)S(1)} %bitcast.60), channel_id=1, source_target_pairs={{0,1},{1,0},{2,3},{3,2},{4,5},{5,4},{6,7},{7,6},{8,9},{9,8},{10,11... | collective-permute-start | bytes 1572872 | tf_op jit(solution)/shard_map/ppermute | solution.py:271
  71.7 1.5 %collective-permute-done.7.rest_4_ = bf16[8,2,128,128]{3,2,1,0:T(8,128)(2,1)S(1)} collective-permute-done((bf16[8,2,128,128]{3,2,1,0:T(8,128)(2,1)S(1)}, bf16[8,2,128,128]{3,2,1,0:T(8,128)(2,1)S(1)}, u32[]{:S(2)}, u32[]{:S(2)}) %collective-permute-start.7) | collective-permute-done | bytes 524320 | tf_op jit(solution)/shard_map/ppermute | solution.py:271
  73.2 0.8 copy-done.2
  74.0 7.1 %backward.1 = bf16[1,2,512,512]{3,2,1,0:T(8,128)(2,1)} custom-call(s32[1]{0:T(128)} %bitcast.me_ref, s32[1,2]{1,0:T(1,128)} %fo_ref.3, s32[16,2]{1,0:T(8,128)} %copy.21.so_ref, bf16[2,512,512]{2,1,0:T(8,128)(2,1)} %constant.16.clone.basis_ref, f32[128,128]{1,0:T(8,128)} %constant.17.clone.taper_ref, bf16[1,2,128,128]{3,2,1,0:T(8,128)(2,1)} %get-tuple-element.15.rest_0_, ...), custom_call_target="tpu_custom_call" | custom-call | tf_op jit(solution)/shard_map/backward/pallas_call | solution.py:351
  (26 shorter events, 3.3 us)
Async XLA Ops:
  0.6 0.7 copy-start.7
  9.0 2.1 %collective-permute-start = (bf16[8,2,128,128]{3,2,1,0:T(8,128)(2,1)}, bf16[8,2,128,128]{3,2,1,0:T(8,128)(2,1)S(1)}, u32[]{:S(2)}, u32[]{:S(2)}) collective-permute-start(bf16[8,2,128,128]{3,2,1,0:T(8,128)(2,1)} %get-tuple-element.10), channel_id=1, source_target_pairs={{0,1},{1,0},{2,3},{3,2},{4,5},{5,4},{6,7},{7,6},{8,9},{9,8},{10,11... | collective-permute-start | bytes 1572872 | tf_op jit(solution)/shard_map/ppermute | solution.py:271
  11.1 9.9 %copy-start.4 = (bf16[2,2,128,128]{3,2,1,0:T(8,128)(2,1)S(1)}, bf16[2,2,128,128]{3,2,1,0:T(8,128)(2,1)}, u32[]{:S(2)}) copy-start(bf16[2,2,128,128]{3,2,1,0:T(8,128)(2,1)} %get-tuple-element.12) | copy-start | bytes 393220
  12.1 8.8 %collective-permute-start.1 = (bf16[4,2,128,128]{3,2,1,0:T(8,128)(2,1)S(1)}, bf16[4,2,128,128]{3,2,1,0:T(8,128)(2,1)S(1)}, u32[]{:S(2)}, u32[]{:S(2)}) collective-permute-start(bf16[4,2,128,128]{3,2,1,0:T(8,128)(2,1)S(1)} %fusion), channel_id=1, source_target_pairs={{0,2},{1,3},{2,0},{3,1},{4,6},{5,7},{6,4},{7,5},{8,10},{9,11},{10,... | collective-permute-start | bytes 786440 | tf_op jit(solution)/shard_map/ppermute | solution.py:271
  21.0 4.3 %copy-start.5 = (bf16[1,2,128,128]{3,2,1,0:T(8,128)(2,1)S(1)}, bf16[1,2,128,128]{3,2,1,0:T(8,128)(2,1)}, u32[]{:S(2)}) copy-start(bf16[1,2,128,128]{3,2,1,0:T(8,128)(2,1)} %get-tuple-element.13) | copy-start | bytes 196612
  21.0 4.2 %collective-permute-start.2 = (bf16[2,2,128,128]{3,2,1,0:T(8,128)(2,1)S(1)}, bf16[2,2,128,128]{3,2,1,0:T(8,128)(2,1)S(1)}, u32[]{:S(2)}, u32[]{:S(2)}) collective-permute-start(bf16[2,2,128,128]{3,2,1,0:T(8,128)(2,1)S(1)} %fusion.1), channel_id=1, source_target_pairs={{0,4},{1,5},{2,6},{3,7},{4,0},{5,1},{6,2},{7,3},{8,12},{9,13},{10,... | collective-permute-start | bytes 393224 | tf_op jit(solution)/shard_map/ppermute | solution.py:271
  25.3 5.9 %collective-permute-start.3 = (bf16[1,2,128,128]{3,2,1,0:T(8,128)(2,1)S(1)}, bf16[1,2,128,128]{3,2,1,0:T(8,128)(2,1)S(1)}, u32[]{:S(2)}, u32[]{:S(2)}) collective-permute-start(bf16[1,2,128,128]{3,2,1,0:T(8,128)(2,1)S(1)} %fusion.2), channel_id=1, source_target_pairs={{0,8},{1,9},{2,10},{3,11},{4,12},{5,13},{6,14},{7,15},{8,0},{9,1},... | collective-permute-start | bytes 196616 | tf_op jit(solution)/shard_map/ppermute | solution.py:271
  27.9 0.7 copy-start.8
  31.1 0.6 copy-start.6
  49.6 4.2 %collective-permute-start.4 = (bf16[1,2,128,128]{3,2,1,0:T(8,128)(2,1)}, bf16[1,2,128,128]{3,2,1,0:T(8,128)(2,1)S(1)}, u32[]{:S(2)}, u32[]{:S(2)}) collective-permute-start(bf16[1,2,128,128]{3,2,1,0:T(8,128)(2,1)} %get-tuple-element.15.rest_0_), channel_id=1, source_target_pairs={{0,8},{1,9},{2,10},{3,11},{4,12},{5,13},{6,14},{7,15},{8,0},{9,1},... | collective-permute-start | bytes 196616 | tf_op jit(solution)/shard_map/ppermute | solution.py:271
  53.8 0.9 %copy-start.3 = (bf16[1,2,128,128]{3,2,1,0:T(8,128)(2,1)}, bf16[1,2,128,128]{3,2,1,0:T(8,128)(2,1)S(1)}, u32[]{:S(2)}) copy-start(bf16[1,2,128,128]{3,2,1,0:T(8,128)(2,1)S(1)} %collective-permute-done.4.rest_1_) | copy-start | bytes 196612
  54.7 3.9 %collective-permute-start.5 = (bf16[2,2,128,128]{3,2,1,0:T(8,128)(2,1)S(1)}, bf16[2,2,128,128]{3,2,1,0:T(8,128)(2,1)S(1)}, u32[]{:S(2)}, u32[]{:S(2)}) collective-permute-start(bf16[2,2,128,128]{3,2,1,0:T(8,128)(2,1)S(1)} %get-tuple-element.17), channel_id=1, source_target_pairs={{0,4},{1,5},{2,6},{3,7},{4,0},{5,1},{6,2},{7,3},{8,12},{9,13},{10,... | collective-permute-start | bytes 393224 | tf_op jit(solution)/shard_map/ppermute | solution.py:271
  58.6 0.6 copy-start.1
  59.3 5.5 %collective-permute-start.6 = (bf16[4,2,128,128]{3,2,1,0:T(8,128)(2,1)S(1)}, bf16[4,2,128,128]{3,2,1,0:T(8,128)(2,1)S(1)}, u32[]{:S(2)}, u32[]{:S(2)}) collective-permute-start(bf16[4,2,128,128]{3,2,1,0:T(8,128)(2,1)S(1)} %bitcast.55), channel_id=1, source_target_pairs={{0,2},{1,3},{2,0},{3,1},{4,6},{5,7},{6,4},{7,5},{8,10},{9,11},{10,... | collective-permute-start | bytes 786440 | tf_op jit(solution)/shard_map/ppermute | solution.py:271
  64.8 0.7 copy-start
  65.5 7.7 %collective-permute-start.7 = (bf16[8,2,128,128]{3,2,1,0:T(8,128)(2,1)S(1)}, bf16[8,2,128,128]{3,2,1,0:T(8,128)(2,1)S(1)}, u32[]{:S(2)}, u32[]{:S(2)}) collective-permute-start(bf16[8,2,128,128]{3,2,1,0:T(8,128)(2,1)S(1)} %bitcast.60), channel_id=1, source_target_pairs={{0,1},{1,0},{2,3},{3,2},{4,5},{5,4},{6,7},{7,6},{8,9},{9,8},{10,11... | collective-permute-start | bytes 1572872 | tf_op jit(solution)/shard_map/ppermute | solution.py:271
  73.2 0.8 copy-start.2

commit v2 on v1

--- a/solution.py
+++ b/solution.py
@@ -17,7 +17,6 @@
 BF = jnp.bfloat16
 F32 = jnp.float32
 TWO_PI = 2.0 * math.pi
-VMEM_LIMIT = 56 * 1024 * 1024
 
 
 def basis_tables():
@@ -76,10 +75,6 @@
     return jnp.dot(left, right, preferred_element_type=F32)
 
 
-def dot_nt(left, right):
-    return lax.dot_general(left, right, (((1,), (1,)), ((), ())), preferred_element_type=F32)
-
-
 def phase_taper(fo_ref, taper_ref):
     rows = lax.broadcasted_iota(jnp.int32, (M, M), 0)
     columns = lax.broadcasted_iota(jnp.int32, (M, M), 1)
@@ -89,8 +84,8 @@
     return cos_v * taper2, sin_v * taper2
 
 
-def forward_kernel(stages, me_ref, fo_ref, so_ref, facet_ref, basis_ref, taper_ref, *rest):
-    outs, (half_ref, spec_ref) = rest[: len(stages)], rest[len(stages) :]
+def forward_kernel(sends, me_ref, fo_ref, so_ref, facet_ref, basis_ref, taper_ref, *rest):
+    outs, (half_ref, spec_ref) = rest[: len(sends)], rest[len(sends) :]
     br, bi = basis_ref[0], basis_ref[1]
     fr, fi = facet_ref[0, 0], facet_ref[0, 1]
     half_ref[0] = (dot(fr, br) - dot(fi, bi)).astype(BF)
@@ -111,7 +106,7 @@
 
     def block(out_ref, item, j):
         owner = j ^ me
-        sx, sy = so_ref[owner, 0], so_ref[owner, 1]
+        sx, sy = so_ref[0, owner], so_ref[1, owner]
         lane = sy // M
         shift = (2 * M - (sy & (M - 1))) & (2 * M - 1)
         parts = []
@@ -124,28 +119,27 @@
         out_ref[item, 0] = (pc * wr - ps * wi).astype(BF)
         out_ref[item, 1] = (pc * wi + ps * wr).astype(BF)
 
-    for out_ref, (count, step, first) in zip(outs, stages):
-        if count == 1:
-            block(out_ref, 0, first)
-        else:
-
-            def body(item, carry, out_ref=out_ref, step=step, first=first):
-                block(out_ref, item, item * step + first)
-                return carry
-
-            lax.fori_loop(0, count, body, 0)
-
-
-def subgrid_kernel(
-    parts, w_ref, tc_ref, to_ref, *rest
-):
-    sums = rest[:parts]
-    (obs_ref, pad_ref, padt_ref, kern_ref, kt_ref, res_ref, coef_ref) = rest[parts : parts + 7]
-    (screen_ref, model_ref, kvt_ref, rows_ref, z_ref) = rest[parts + 7 :]
-    slots = obs_ref.shape[0]
-    count = tc_ref[0]
+    for out_ref, js in zip(outs, sends):
+        for_blocks(block, out_ref, js)
+
+
+def for_blocks(block, ref, js):
+    step = js[1] - js[0] if len(js) > 1 else 1
+    if len(js) > 1 and js == list(range(js[0], js[0] + step * len(js), step)):
+
+        def body(item, carry):
+            block(ref, item, item * step + js[0])
+            return carry
+
+        lax.fori_loop(0, len(js), body, 0)
+    else:
+        for item, j in enumerate(js):
+            block(ref, item, j)
+
+
+def prepare_kernel(w_ref, to_ref, kt_ref, kwide_ref, screen_ref, kvt_ref, kv_ref, kut_ref):
+    slots = kut_ref.shape[0]
     w = w_ref[0]
-
     row = lax.broadcasted_iota(jnp.int32, (SG, 1), 0).astype(F32) - SG / 2.0
     column = lax.broadcasted_iota(jnp.int32, (1, SG), 1).astype(F32) - SG / 2.0
     row2 = row * row * (1.0 / (SG * SG)) + 1.0
@@ -153,15 +147,26 @@
     cos_v, sin_v = cos_sin_turns((jnp.sqrt(row2 + column2) - 1.0) * w)
     screen_ref[0] = cos_v
     screen_ref[1] = sin_v
-
     for t in range(slots):
-        band = kt_ref[pl.ds(2 * TV - to_ref[t, 1], SG), :]
-        kvt_ref[:, t * TV : (t + 1) * TV] = band.astype(BF)
+        ou, ov = to_ref[0, t], to_ref[1, t]
+        kut_ref[t] = kt_ref[pl.ds(2 * TV - ou, SG), :].astype(BF)
+        kvt_ref[:, t * TV : (t + 1) * TV] = kt_ref[pl.ds(2 * TV - ov, SG), :].astype(BF)
+        kv_ref[t * TV : (t + 1) * TV] = pltpu.roll(kwide_ref[...], ov, 1).astype(BF)
+
+
+def subgrid_kernel(picks, tc_ref, to_ref, *rest):
+    parts = len(picks)
+    sums = rest[:parts]
+    (obs_ref, pad_ref, padt_ref, kern_ref) = rest[parts : parts + 4]
+    (screen_ref, kvt_ref, kv_ref, kut_ref) = rest[parts + 4 : parts + 8]
+    (res_ref, coef_ref, model_ref, rows_ref, z_ref) = rest[parts + 8 :]
+    slots = obs_ref.shape[0]
+    count = tc_ref[0]
 
     def total(plane):
-        value = sums[0][0, plane].astype(F32)
-        for ref in sums[1:]:
-            value = value + ref[0, plane].astype(F32)
+        value = sums[0][picks[0], plane].astype(F32)
+        for ref, item in zip(sums[1:], picks[1:]):
+            value = value + ref[item, plane].astype(F32)
         return value.astype(BF)
 
     sr, si = total(0), total(1)
@@ -183,7 +188,7 @@
             rows_ref[t % rows_ref.shape[0]] = pair[:, (t - t0) * TV : (t - t0 + 1) * TV]
         for t in (t0, t0 + 1):
             slot = t % rows_ref.shape[0]
-            ou = to_ref[t, 0]
+            ou = to_ref[0, t]
             wr = rows_ref[slot, pl.ds(ou, 2 * TV), :]
             wi = rows_ref[slot, pl.ds(SG + ou, 2 * TV), :]
             window = jnp.concatenate([wr.astype(BF), wi.astype(BF)], axis=1)
@@ -194,14 +199,13 @@
                 value = obs_ref[t, plane].astype(F32) - predicted[:, plane * TV : (plane + 1) * TV]
                 res.append(jnp.where(live, value, 0.0).astype(BF))
                 res_ref[t, plane] = res[plane]
-            band = kt_ref[pl.ds(2 * TV - ou, SG), :].astype(BF)
-            z = dot(band, jnp.concatenate(res, axis=1)).astype(BF)
+            z = dot(kut_ref[t], jnp.concatenate(res, axis=1)).astype(BF)
             z_ref[:SG, t * TV : (t + 1) * TV] = z[:, :TV]
             z_ref[SG:, t * TV : (t + 1) * TV] = z[:, TV:]
 
-    kvt = kvt_ref[...]
-    ar = dot_nt(z_ref[:SG], kvt)
-    ai = dot_nt(z_ref[SG:], kvt)
+    kv = kv_ref[...]
+    ar = dot(z_ref[:SG], kv)
+    ai = dot(z_ref[SG:], kv)
     screened_r = (sc * ar + ss * ai).astype(BF)
     screened_i = (sc * ai - ss * ar).astype(BF)
     reduced_r = (dot(tr, screened_r) + dot(ti, screened_i)).astype(BF)
@@ -220,7 +224,7 @@
 
     def block(in_ref, item, j):
         owner = j ^ me
-        sx, sy = so_ref[owner, 0], so_ref[owner, 1]
+        sx, sy = so_ref[0, owner], so_ref[1, owner]
         lane = sy // M
         shift = sy & (M - 1)
         cr, ci = in_ref[item, 0].astype(F32), in_ref[item, 1].astype(F32)
@@ -230,16 +234,8 @@
             grid_ref[plane, lane, pl.ds(sx, M), :] += wide[:, :M]
             grid_ref[plane, lane + 1, pl.ds(sx, M), :] += wide[:, M:]
 
-    for in_ref, (count, step, first) in zip(ins, pieces):
-        if count == 1:
-            block(in_ref, 0, first)
-        else:
-
-            def body(item, carry, in_ref=in_ref, step=step, first=first):
-                block(in_ref, item, item * step + first)
-                return carry
-
-            lax.fori_loop(0, count, body, 0)
+    for in_ref, js in zip(ins, pieces):
+        for_blocks(block, in_ref, js)
 
     columns = F // M
     folded = []
@@ -260,106 +256,164 @@
 
 SMEM = pl.BlockSpec(memory_space=pltpu.SMEM)
 VMEM = pl.BlockSpec(memory_space=pltpu.VMEM)
-PARAMS = pltpu.CompilerParams(vmem_limit_bytes=VMEM_LIMIT)
-
-
-def blocks(count):
-    return jax.ShapeDtypeStruct((count, 2, M, M), BF)
-
-
-def exchange(value, bit, n):
-    return lax.ppermute(value, "facet", [(i, i ^ bit) for i in range(n)])
+
+
+def params(mib):
+    return pltpu.CompilerParams(vmem_limit_bytes=mib * 1024 * 1024)
+
+
+def near(value):
+    return pltpu.with_memory_space_constraint(value, pltpu.VMEM)
+
+
+def held(shape, dtype=BF):
+    return pltpu.VMEM(shape, dtype)
+
+
+def exchange(value, mask, n):
+    return lax.ppermute(value, "facet", [(i, i ^ mask) for i in range(n)])
+
+
+def digit_levels(n):
+    levels, base = [], 1
+    while base < n:
+        radix = 2 if base < 4 or n // base < 4 else 4
+        levels.append((base, radix))
+        base *= radix
+    return levels
+
+
+def reduce_sends(n):
+    levels = digit_levels(n)
+    sends = []
+    for k, (base, radix) in enumerate(levels):
+        for g in range(1, radix):
+            js = [j for j in range(0, n, base) if (j // base) % radix == g]
+            if k + 1 < len(levels):
+                after, width = levels[k + 1]
+                groups = [[j for j in js if (j // after) % width], [j for j in js if not (j // after) % width]]
+            else:
+                groups = [js]
+            sends += [(group, g * base) for group in groups if group]
+    return sends
+
+
+def pick(value, items):
+    step = items[1] - items[0] if len(items) > 1 else 1
+    if items == list(range(items[0], items[0] + step * len(items), step)):
+        if len(items) == value.shape[0]:
+            return value
+        return lax.slice_in_dim(value, items[0], items[-1] + 1, step)
+    return jnp.concatenate([value[i : i + 1] for i in items])
 
 
 def per_device(facets, facet_offsets, subgrid_offsets, w_terms, tile_count, tile_offsets, observed):
     n = lax.axis_size("facet")
-    bits = [1 << k for k in range(n.bit_length() - 1)]
+    slots = observed.shape[0]
     me = lax.axis_index("facet").astype(jnp.int32).reshape(1)
-    basis = jnp.asarray(basis_tables())
-    taper2 = jnp.asarray(taper_square())
+    corners = subgrid_offsets.T
+    tile_corners = tile_offsets.T
+    basis = near(jnp.asarray(basis_tables()))
+    taper2 = near(jnp.asarray(taper_square()))
     pad_np = padding_tables(n)
     kern_np = kernel_table()
     kt_np = np.zeros((6 * TV, TV), np.float32)
     kt_np[2 * TV : 4 * TV] = kern_np.astype(np.float32).T
-
-    stages = [(n // (2 * b), 2 * b, b) for b in bits] + [(1, 1, 0)]
+    kwide_np = np.zeros((TV, SG), np.float32)
+    kwide_np[:, : 2 * TV] = kern_np.astype(np.float32)
+
+    sends = reduce_sends(n)
     own = pl.pallas_call(
-        functools.partial(forward_kernel, stages),
-        out_shape=[blocks(count) for count, _, _ in stages],
+        functools.partial(forward_kernel, [js for js, _ in sends] + [[0]]),
+        out_shape=[held((len(js), 2, M, M)) for js, _ in sends] + [held((1, 2, M, M))],
         in_specs=[SMEM] * 3 + [VMEM] * 3,
-        out_specs=[VMEM] * len(stages),
+        out_specs=[VMEM] * (len(sends) + 1),
         scratch_shapes=[
             pltpu.VMEM((2, F, F), BF),
             pltpu.VMEM((2, F // M + 1, F + M, M), F32),
         ],
-        compiler_params=PARAMS,
+        compiler_params=params(16),
         name="forward",
-    )(me, facet_offsets, subgrid_offsets, facets, basis, taper2)
+    )(me, facet_offsets, corners, facets, basis, taper2)
+
+    screen, kvt, kv, kut = pl.pallas_call(
+        prepare_kernel,
+        out_shape=[
+            held((2, SG, SG), F32),
+            held((SG, slots * TV)),
+            held((slots * TV, SG)),
+            held((slots, SG, TV)),
+        ],
+        in_specs=[SMEM] * 2 + [VMEM] * 2,
+        out_specs=[VMEM] * 4,
+        compiler_params=params(8),
+        name="prepare",
+    )(w_terms, tile_corners, jnp.asarray(kt_np), jnp.asarray(kwide_np))
 
     arrived = []
-    for k, b in enumerate(bits):
-        send = own[k]
-        if k:
-            total = send.astype(F32)
-            for i, got in enumerate(arrived):
-                skip = b >> (i + 1)
-                pick = got.reshape((got.shape[0] // (2 * skip), 2 * skip) + got.shape[1:])[:, skip]
-                total = total + pick.astype(F32)
-            send = total.astype(BF)
-        arrived.append(exchange(send, b, n))
-    sums = [own[-1]] + [got[:1] for got in arrived]
+    for (js, mask), value in zip(sends, own):
+        terms = []
+        for got_js, got in arrived:
+            if set(js) <= set(got_js):
+                terms.append(pick(got, [got_js.index(j) for j in js]))
+            else:
+                assert not set(js) & set(got_js)
+        if terms:
+            total = value.astype(F32)
+            for term in terms:
+                total = total + term.astype(F32)
+            value = total.astype(BF)
+        arrived.append(([j ^ mask for j in js], exchange(value, mask, n)))
+    last = [(js, got) for js, got in arrived if 0 in js]
 
     residual, coefficient = pl.pallas_call(
-        functools.partial(subgrid_kernel, len(sums)),
-        out_shape=[
-            jax.ShapeDtypeStruct(observed.shape, BF),
-            blocks(1),
-        ],
-        in_specs=[SMEM] * 3 + [VMEM] * (len(sums) + 5),
+        functools.partial(subgrid_kernel, [0] + [js.index(0) for js, _ in last]),
+        out_shape=[held(observed.shape), held((1, 2, M, M))],
+        in_specs=[SMEM] * 2 + [VMEM] * (len(last) + 9),
         out_specs=[VMEM] * 2,
         scratch_shapes=[
-            pltpu.VMEM((2, SG, SG), F32),
             pltpu.VMEM((2 * SG, SG), BF),
-            pltpu.VMEM((SG, observed.shape[0] * TV), BF),
             pltpu.VMEM((8, 2 * SG, TV), F32),
-            pltpu.VMEM((2 * SG, observed.shape[0] * TV), BF),
+            pltpu.VMEM((2 * SG, slots * TV), BF),
         ],
-        compiler_params=PARAMS,
+        compiler_params=params(24),
         name="subgrid",
     )(
-        w_terms,
         tile_count,
-        tile_offsets,
-        *sums,
-        observed,
-        jnp.asarray(pad_np),
-        jnp.asarray(pad_np.transpose(0, 2, 1)),
-        jnp.asarray(kern_np),
-        jnp.asarray(kt_np),
+        tile_corners,
+        near(own[-1]),
+        *[near(got) for _, got in last],
+        near(observed),
+        near(jnp.asarray(pad_np)),
+        near(jnp.asarray(pad_np.transpose(0, 2, 1))),
+        near(jnp.asarray(kern_np)),
+        near(screen),
+        near(kvt),
+        near(kv),
+        near(kut),
     )
 
-    gathered = coefficient
-    held = [coefficient]
-    pieces = [(1, 1, 0)]
-    for b in reversed(bits):
-        got = exchange(gathered, b, n)
-        held.append(got)
-        pieces.append((got.shape[0], 2 * b, b))
-        if b > 1:
-            gathered = jnp.stack([gathered, got], axis=1).reshape((-1,) + got.shape[1:])
+    pieces = [([0], coefficient)]
+    for base, radix in reversed(digit_levels(n)):
+        more = []
+        for js, value in pieces:
+            got = [exchange(value, g * base, n) for g in range(1, radix)]
+            got_js = [j ^ (g * base) for g in range(1, radix) for j in js]
+            more.append((got_js, got[0] if radix == 2 else jnp.concatenate(got)))
+        pieces += more
 
     update = pl.pallas_call(
-        functools.partial(backward_kernel, pieces),
+        functools.partial(backward_kernel, [js for js, _ in pieces]),
         out_shape=jax.ShapeDtypeStruct(facets.shape, BF),
-        in_specs=[SMEM] * 3 + [VMEM] * (2 + len(held)),
+        in_specs=[SMEM] * 3 + [VMEM] * (2 + len(pieces)),
         out_specs=VMEM,
         scratch_shapes=[
             pltpu.VMEM((2, F // M + 1, F + M, M), F32),
             pltpu.VMEM((2, F, F), BF),
         ],
-        compiler_params=PARAMS,
+        compiler_params=params(16),
         name="backward",
-    )(me, facet_offsets, subgrid_offsets, basis, taper2, *held)
+    )(me, facet_offsets, corners, basis, taper2, *[near(value) for _, value in pieces])
     return (residual, update)
 
 

time: 81.7 us -> 74.9 us (0.917)
  waiting for transfers between devices: 23.1 us -> 12.8 us
  starting transfers between devices: 15.2 us -> 22.3 us
  other arithmetic: 2.11 us -> 0.16 us
  local copies, waits for them, and re-layouts: 6.67 us -> 5.68 us
    ppermute x8 -> x16, waiting for transfers between devices: 23.1 us -> 12.8 us  [exchange(): return lax.ppermute(value, 'facet', [(i, i ^ mask) for i in range(n)])]
    ppermute x8 -> x16, starting transfers between devices: 15.2 us -> 22.3 us  [exchange(): return lax.ppermute(value, 'facet', [(i, i ^ mask) for i in range(n)])]
    slice x3 -> x0, local copies, waits for them, and re-layouts: 1.89 us -> none  [per_device(): sums = [own[-1]] + [got[:1] for got in arrived]]
    convert_element_type x3, other arithmetic: 1.15 us -> 0.16 us  [per_device(): value = total.astype(BF)]
    another operation x3 -> x0, other arithmetic: 0.96 us -> none  [per_device(): gathered = jnp.stack([gathered, got], axis=1).reshape((-1,) + got.shape[1:])]
    unnamed x20 -> x35, local copies, waits for them, and re-layouts: 4.72 us -> 5.66 us
    pallas_call x3 -> x4, Pallas kernels: 31.9 us -> 31.3 us  [the longest x1 14.9 us: per_device(): pl.pallas_call(functools.partial(subgrid_kernel, [0] + [js.index(0) for j...]
  transfers between devices with their start and end apart: 8 -> 16, of which waited for: 7 -> 4; matrix products, arithmetic and copies ran while one was open for 3% -> 2% of each run, Pallas kernels for 0% -> 7%
where the time goes in v2:
time: 74.9 us; the launch traced here: 74.4 us
  Pallas kernels  31.3 us (42%)
  starting transfers between devices  22.3 us (30%)
  waiting for transfers between devices  12.8 us (17%)
  local copies, waits for them, and re-layouts  5.68 us (8%)
  between operations  2.2 us (3%)
    ppermute x16, starting transfers between devices, exchange(): return lax.ppermute(value, 'facet', [(i, i ^ mask) for i in range(n)])  22.3 us
    pallas_call x1, Pallas kernels, per_device(): pl.pallas_call(functools.partial(subgrid_kernel, [0] + [js.index(0) for j...  14.9 us
    ppermute x16, waiting for transfers between devices, exchange(): return lax.ppermute(value, 'facet', [(i, i ^ mask) for i in range(n)])  12.8 us
    pallas_call x1, Pallas kernels, per_device(): pl.pallas_call(functools.partial(backward_kernel, [js for js, _ in pieces...  6.25 us
    unnamed x35, local copies, waits for them, and re-layouts  5.66 us
    pallas_call x1, Pallas kernels, per_device(): pl.pallas_call(prepare_kernel, out_shape=[held((2, SG, SG), F32), held((S...  5.1 us
    pallas_call x1, Pallas kernels, per_device(): pl.pallas_call(functools.partial(forward_kernel, [js for js, _ in sends]...  5.05 us
  transfers between devices with their start and end apart: 16, of which 4 were waited for; matrix products, arithmetic and copies ran while one was open for 2% of the time, Pallas kernels for 7%

profile of v2, /device:TPU:1, one launch (start us, length us, event | category | flops | bytes accessed | tf_op | source)
XLA Modules:
  0.0 74.4 jit_solution(15596077459148323134)
XLA Ops:
  0.7 1.2 %copy-done = bf16[2,512,512]{2,1,0:T(8,128)(2,1)S(1)} copy-done((bf16[2,512,512]{2,1,0:T(8,128)(2,1)S(1)}, bf16[2,512,512]{2,1,0:T(8,128)(2,1)}, u32[]{:S(2)}) %copy-start) | copy-done | bytes 1048600
  1.9 1.2 %copy-done.2 = bf16[1,2,512,512]{3,2,1,0:T(8,128)(2,1)S(1)} copy-done((bf16[1,2,512,512]{3,2,1,0:T(8,128)(2,1)S(1)}, bf16[1,2,512,512]{3,2,1,0:T(8,128)(2,1)}, u32[]{:S(2)}) %copy-start.2) | copy-done | bytes 1048600
  3.1 0.8 %copy-done.7 = f32[128,128]{1,0:T(8,128)S(1)} copy-done((f32[128,128]{1,0:T(8,128)S(1)}, f32[128,128]{1,0:T(8,128)}, u32[]{:S(2)}) %copy-start.7) | copy-done | bytes 65560
  3.9 0.7 copy-done.11
  4.6 0.7 copy-done.14
  5.3 5.0 %forward.1 = (bf16[4,2,128,128]{3,2,1,0:T(8,128)(2,1)S(1)}, bf16[4,2,128,128]{3,2,1,0:T(8,128)(2,1)S(1)}, bf16[3,2,128,128]{3,2,1,0:T(8,128)(2,1)S(1)}, bf16[1,2...) custom-call(s32[1]{0:T(128)} %bitcast.1.me_ref, ...), custom_call_target="tpu_custom_call" | custom-call | tf_op jit(solution)/shard_map/forward/pallas_call | solution.py:326
  10.5 0.5 collective-permute-start
  10.9 1.0 %collective-permute-done.1 = bf16[4,2,128,128]{3,2,1,0:T(8,128)(2,1)S(1)} collective-permute-done((bf16[4,2,128,128]{3,2,1,0:T(8,128)(2,1)S(1)}, bf16[4,2,128,128]{3,2,1,0:T(8,128)(2,1)S(1)}, u32[]{:S(2)}, u32[]{:S(2)}) %collective-permute-start.1) | collective-permute-done | bytes 262176 | tf_op jit(solution)/shard_map/ppermute | solution.py:274
  12.0 2.4 %collective-permute-start.3 = (bf16[3,2,128,128]{3,2,1,0:T(8,128)(2,1)S(1)}, bf16[3,2,128,128]{3,2,1,0:T(8,128)(2,1)S(1)}, u32[]{:S(2)}, u32[]{:S(2)}) collective-permute-start(bf16[3,2,128,128]{3,2,1,0:T(8,128)(2,1)S(1)} %add_convert_fusion), channel_id=1, source_target_pairs={{0,2},{1,3},{2,0},{3,1},{4,6},{5,7},{6,4},{7,5},{8,10},{9,11},{10,... | collective-permute-start | bytes 589832 | tf_op jit(solution)/shard_map/ppermute | solution.py:274
  14.6 4.9 %collective-permute-done.3 = bf16[3,2,128,128]{3,2,1,0:T(8,128)(2,1)S(1)} collective-permute-done((bf16[3,2,128,128]{3,2,1,0:T(8,128)(2,1)S(1)}, bf16[3,2,128,128]{3,2,1,0:T(8,128)(2,1)S(1)}, u32[]{:S(2)}, u32[]{:S(2)}) %collective-permute-start.3) | collective-permute-done | bytes 196640 | tf_op jit(solution)/shard_map/ppermute | solution.py:274
  19.5 3.3 %collective-permute-start.6 = (bf16[1,2,128,128]{3,2,1,0:T(8,128)(2,1)S(1)}, bf16[1,2,128,128]{3,2,1,0:T(8,128)(2,1)S(1)}, u32[]{:S(2)}, u32[]{:S(2)}) collective-permute-start(bf16[1,2,128,128]{3,2,1,0:T(8,128)(2,1)S(1)} %get-tuple-element.30), channel_id=1, source_target_pairs={{0,12},{1,13},{2,14},{3,15},{4,8},{5,9},{6,10},{7,11},{8,4},{9,5},... | collective-permute-start | bytes 196616 | tf_op jit(solution)/shard_map/ppermute | solution.py:274
  24.5 5.1 %prepare.1 = (f32[2,512,512]{2,1,0:T(8,128)S(1)}, bf16[512,2048]{1,0:T(8,128)(2,1)S(1)}, bf16[2048,512]{1,0:T(8,128)(2,1)S(1)}, bf16[16,512,128]{2,1,0:T(8,128)(2,1)S(1)}) custom-call(f32[1]{0:T(128)S(6)} %copy.19.w_ref, s32[2,16]{1,0:T(2,128)S(1)} %bitcast.5, f32[768,128]{1,0:T(8,128)S(1)} %copy-done.4, f32[128,512]{1,0:T(8,128)S(1)} %copy-done.9), custom_call_target="tpu_custom_call" | custom-call | tf_op jit(solution)/shard_map/prepare/pallas_call | solution.py:339
  29.7 14.9 %subgrid.1 = (bf16[16,2,128,128]{3,2,1,0:T(8,128)(2,1)S(1)}, bf16[1,2,128,128]{3,2,1,0:T(8,128)(2,1)S(1)}) custom-call(s32[1]{0:T(128)S(6)} %copy.20.tc_ref, s32[2,16]{1,0:T(2,128)S(1)} %bitcast.6, bf16[1,2,128,128]{3,2,1,0:T(8,128)(2,1)S(1)} %get-tuple-element.16.rest_0_, bf16[4,2,128,128]{3,2,1,0:T(8,128)(2,1)S(1)} %collective-permute-done.rest_1_, ...), custom_call_target="tpu_custom_call" | custom-call | tf_op jit(solution)/shard_map/subgrid/pallas_call | solution.py:369
  44.6 1.2 %collective-permute-start.7 = (bf16[1,2,128,128]{3,2,1,0:T(8,128)(2,1)S(1)}, bf16[1,2,128,128]{3,2,1,0:T(8,128)(2,1)S(1)}, u32[]{:S(2)}, u32[]{:S(2)}) collective-permute-start(bf16[1,2,128,128]{3,2,1,0:T(8,128)(2,1)S(1)} %get-tuple-element.29.rest_0_), channel_id=1, source_target_pairs={{0,4},{1,5},{2,6},{3,7},{4,0},{5,1},{6,2},{7,3},{8,12},{9,13},{10,... | collective-permute-start | bytes 196616 | tf_op jit(solution)/shard_map/ppermute | solution.py:274
  45.8 2.2 %collective-permute-start.9 = (bf16[1,2,128,128]{3,2,1,0:T(8,128)(2,1)S(1)}, bf16[1,2,128,128]{3,2,1,0:T(8,128)(2,1)S(1)}, u32[]{:S(2)}, u32[]{:S(2)}) collective-permute-start(bf16[1,2,128,128]{3,2,1,0:T(8,128)(2,1)S(1)} %get-tuple-element.29.rest_0_), channel_id=1, source_target_pairs={{0,12},{1,13},{2,14},{3,15},{4,8},{5,9},{6,10},{7,11},{8,4},{9,5},... | collective-permute-start | bytes 196616 | tf_op jit(solution)/shard_map/ppermute | solution.py:274
  48.2 4.7 %collective-permute-done.8 = bf16[1,2,128,128]{3,2,1,0:T(8,128)(2,1)S(1)} collective-permute-done((bf16[1,2,128,128]{3,2,1,0:T(8,128)(2,1)S(1)}, bf16[1,2,128,128]{3,2,1,0:T(8,128)(2,1)S(1)}, u32[]{:S(2)}, u32[]{:S(2)}) %collective-permute-start.8) | collective-permute-done | bytes 65568 | tf_op jit(solution)/shard_map/ppermute | solution.py:274
  53.0 1.3 %collective-permute-start.11 = (bf16[3,2,128,128]{3,2,1,0:T(8,128)(2,1)S(1)}, bf16[3,2,128,128]{3,2,1,0:T(8,128)(2,1)S(1)}, u32[]{:S(2)}, u32[]{:S(2)}) collective-permute-start(bf16[3,2,128,128]{3,2,1,0:T(8,128)(2,1)S(1)} %constant_dynamic-update-slice_fusion.rest_1_), channel_id=1, source_target_pairs={{0,2},{1,3},{2,0},{3,1},{4,6},{5,7},{6,4},{7,5},{8,10},{9,11},{10,... | collective-permute-start | bytes 589832 | tf_op jit(solution)/shard_map/ppermute | solution.py:274
  54.2 4.2 %collective-permute-start.13 = (bf16[3,2,128,128]{3,2,1,0:T(8,128)(2,1)S(1)}, bf16[3,2,128,128]{3,2,1,0:T(8,128)(2,1)S(1)}, u32[]{:S(2)}, u32[]{:S(2)}) collective-permute-start(bf16[3,2,128,128]{3,2,1,0:T(8,128)(2,1)S(1)} %constant_dynamic-update-slice_fusion.rest_1_), channel_id=1, source_target_pairs={{0,1},{1,0},{2,3},{3,2},{4,5},{5,4},{6,7},{7,6},{8,9},{9,8},{10,11... | collective-permute-start | bytes 589832 | tf_op jit(solution)/shard_map/ppermute | solution.py:274
  58.5 4.2 %collective-permute-start.15 = (bf16[3,2,128,128]{3,2,1,0:T(8,128)(2,1)S(1)}, bf16[3,2,128,128]{3,2,1,0:T(8,128)(2,1)S(1)}, u32[]{:S(2)}, u32[]{:S(2)}) collective-permute-start(bf16[3,2,128,128]{3,2,1,0:T(8,128)(2,1)S(1)} %collective-permute-done.11.rest_3_), channel_id=1, source_target_pairs={{0,1},{1,0},{2,3},{3,2},{4,5},{5,4},{6,7},{7,6},{8,9},{9,8},{10,11... | collective-permute-start | bytes 589832 | tf_op jit(solution)/shard_map/ppermute | solution.py:274
  62.6 1.2 %collective-permute-start.10 = (bf16[1,2,128,128]{3,2,1,0:T(8,128)(2,1)S(1)}, bf16[1,2,128,128]{3,2,1,0:T(8,128)(2,1)S(1)}, u32[]{:S(2)}, u32[]{:S(2)}) collective-permute-start(bf16[1,2,128,128]{3,2,1,0:T(8,128)(2,1)S(1)} %get-tuple-element.29.rest_0_), channel_id=1, source_target_pairs={{0,2},{1,3},{2,0},{3,1},{4,6},{5,7},{6,4},{7,5},{8,10},{9,11},{10,... | collective-permute-start | bytes 196616 | tf_op jit(solution)/shard_map/ppermute | solution.py:274
  64.2 2.2 %collective-permute-done.10.rest_2_ = bf16[1,2,128,128]{3,2,1,0:T(8,128)(2,1)S(1)} collective-permute-done((bf16[1,2,128,128]{3,2,1,0:T(8,128)(2,1)S(1)}, bf16[1,2,128,128]{3,2,1,0:T(8,128)(2,1)S(1)}, u32[]{:S(2)}, u32[]{:S(2)}) %collective-permute-start.10) | collective-permute-done | bytes 65568 | tf_op jit(solution)/shard_map/ppermute | solution.py:274
  66.4 0.8 %collective-permute-start.14 = (bf16[1,2,128,128]{3,2,1,0:T(8,128)(2,1)S(1)}, bf16[1,2,128,128]{3,2,1,0:T(8,128)(2,1)S(1)}, u32[]{:S(2)}, u32[]{:S(2)}) collective-permute-start(bf16[1,2,128,128]{3,2,1,0:T(8,128)(2,1)S(1)} %collective-permute-done.10.rest_2_), channel_id=1, source_target_pairs={{0,1},{1,0},{2,3},{3,2},{4,5},{5,4},{6,7},{7,6},{8,9},{9,8},{10,11... | collective-permute-start | bytes 196616 | tf_op jit(solution)/shard_map/ppermute | solution.py:274
  67.2 1.0 %copy.18 = bf16[16,2,128,128]{3,2,1,0:T(8,128)(2,1)} copy(bf16[16,2,128,128]{3,2,1,0:T(8,128)(2,1)S(1)} %get-tuple-element.33) | data formatting | bytes 2097152
  68.2 6.3 %backward.1 = bf16[1,2,512,512]{3,2,1,0:T(8,128)(2,1)} custom-call(s32[1]{0:T(128)} %bitcast.1.me_ref, s32[1,2]{1,0:T(1,128)S(1)} %copy-done.15, s32[2,16]{1,0:T(2,128)S(1)} %bitcast.4, bf16[2,512,512]{2,1,0:T(8,128)(2,1)S(1)} %copy-done.1, f32[128,128]{1,0:T(8,128)S(1)} %copy-done.8, bf16[1,2,128,128]{3,2,1,0:T(8,128)(2,1)S(1)} %get-tuple-element.29.rest_0_, ...), custom_call_target="tpu_custom_call" | custom-call | tf_op jit(solution)/shard_map/backward/pallas_call | solution.py:405
  (51 shorter events, 1.4 us)
Async XLA Ops:
  0.6 23.8 %copy-start.13 = (s32[16,2]{0,1:T(2,128)S(1)}, s32[16,2]{0,1:T(2,128)}, u32[]{:S(2)}) copy-start(s32[16,2]{0,1:T(2,128)} %param.19) | copy-start | bytes 388
  5.3 24.4 %copy-start.3 = (bf16[16,2,128,128]{3,2,1,0:T(8,128)(2,1)S(1)}, bf16[16,2,128,128]{3,2,1,0:T(8,128)(2,1)}, u32[]{:S(2)}) copy-start(bf16[16,2,128,128]{3,2,1,0:T(8,128)(2,1)} %rest_6_.1) | copy-start | bytes 3145732
  5.3 24.4 %copy-start.5 = (bf16[2,128,512]{2,1,0:T(8,128)(2,1)S(1)}, bf16[2,128,512]{2,1,0:T(8,128)(2,1)}, u32[]{:S(2)}) copy-start(bf16[2,128,512]{2,1,0:T(8,128)(2,1)} %constant.23.clone.rest_8_) | copy-start | bytes 786436
  5.3 24.4 %copy-start.6 = (bf16[2,512,128]{2,1,0:T(8,128)(2,1)S(1)}, bf16[2,512,128]{2,1,0:T(8,128)(2,1)}, u32[]{:S(2)}) copy-start(bf16[2,512,128]{2,1,0:T(8,128)(2,1)} %constant.22.clone.rest_7_) | copy-start | bytes 786436
  5.3 24.4 %copy-start.10 = (bf16[128,256]{1,0:T(8,128)(2,1)S(1)}, bf16[128,256]{1,0:T(8,128)(2,1)}, u32[]{:S(2)}) copy-start(bf16[128,256]{1,0:T(8,128)(2,1)} %constant.24.clone.rest_9_) | copy-start | bytes 196612
  10.4 1.6 %collective-permute-start.1 = (bf16[4,2,128,128]{3,2,1,0:T(8,128)(2,1)S(1)}, bf16[4,2,128,128]{3,2,1,0:T(8,128)(2,1)S(1)}, u32[]{:S(2)}, u32[]{:S(2)}) collective-permute-start(bf16[4,2,128,128]{3,2,1,0:T(8,128)(2,1)S(1)} %get-tuple-element.19), channel_id=1, source_target_pairs={{0,1},{1,0},{2,3},{3,2},{4,5},{5,4},{6,7},{7,6},{8,9},{9,8},{10,11... | collective-permute-start | bytes 786440 | tf_op jit(solution)/shard_map/ppermute | solution.py:274
  10.5 4.1 %collective-permute-start = (bf16[4,2,128,128]{3,2,1,0:T(8,128)(2,1)S(1)}, bf16[4,2,128,128]{3,2,1,0:T(8,128)(2,1)S(1)}, u32[]{:S(2)}, u32[]{:S(2)}) collective-permute-start(bf16[4,2,128,128]{3,2,1,0:T(8,128)(2,1)S(1)} %get-tuple-element.17), channel_id=1, source_target_pairs={{0,1},{1,0},{2,3},{3,2},{4,5},{5,4},{6,7},{7,6},{8,9},{9,8},{10,11... | collective-permute-start | bytes 786440 | tf_op jit(solution)/shard_map/ppermute | solution.py:274
  12.0 7.4 %collective-permute-start.3 = (bf16[3,2,128,128]{3,2,1,0:T(8,128)(2,1)S(1)}, bf16[3,2,128,128]{3,2,1,0:T(8,128)(2,1)S(1)}, u32[]{:S(2)}, u32[]{:S(2)}) collective-permute-start(bf16[3,2,128,128]{3,2,1,0:T(8,128)(2,1)S(1)} %add_convert_fusion), channel_id=1, source_target_pairs={{0,2},{1,3},{2,0},{3,1},{4,6},{5,7},{6,4},{7,5},{8,10},{9,11},{10,... | collective-permute-start | bytes 589832 | tf_op jit(solution)/shard_map/ppermute | solution.py:274
  14.5 15.1 %collective-permute-start.2 = (bf16[1,2,128,128]{3,2,1,0:T(8,128)(2,1)S(1)}, bf16[1,2,128,128]{3,2,1,0:T(8,128)(2,1)S(1)}, u32[]{:S(2)}, u32[]{:S(2)}) collective-permute-start(bf16[1,2,128,128]{3,2,1,0:T(8,128)(2,1)S(1)} %add_convert_fusion.4), channel_id=1, source_target_pairs={{0,2},{1,3},{2,0},{3,1},{4,6},{5,7},{6,4},{7,5},{8,10},{9,11},{10,... | collective-permute-start | bytes 196616 | tf_op jit(solution)/shard_map/ppermute | solution.py:274
  19.5 10.1 %collective-permute-start.6 = (bf16[1,2,128,128]{3,2,1,0:T(8,128)(2,1)S(1)}, bf16[1,2,128,128]{3,2,1,0:T(8,128)(2,1)S(1)}, u32[]{:S(2)}, u32[]{:S(2)}) collective-permute-start(bf16[1,2,128,128]{3,2,1,0:T(8,128)(2,1)S(1)} %get-tuple-element.30), channel_id=1, source_target_pairs={{0,12},{1,13},{2,14},{3,15},{4,8},{5,9},{6,10},{7,11},{8,4},{9,5},... | collective-permute-start | bytes 196616 | tf_op jit(solution)/shard_map/ppermute | solution.py:274
  22.8 6.8 %collective-permute-start.5 = (bf16[1,2,128,128]{3,2,1,0:T(8,128)(2,1)S(1)}, bf16[1,2,128,128]{3,2,1,0:T(8,128)(2,1)S(1)}, u32[]{:S(2)}, u32[]{:S(2)}) collective-permute-start(bf16[1,2,128,128]{3,2,1,0:T(8,128)(2,1)S(1)} %get-tuple-element.31), channel_id=1, source_target_pairs={{0,8},{1,9},{2,10},{3,11},{4,12},{5,13},{6,14},{7,15},{8,0},{9,1},... | collective-permute-start | bytes 196616 | tf_op jit(solution)/shard_map/ppermute | solution.py:274
  22.8 6.8 %collective-permute-start.4 = (bf16[1,2,128,128]{3,2,1,0:T(8,128)(2,1)S(1)}, bf16[1,2,128,128]{3,2,1,0:T(8,128)(2,1)S(1)}, u32[]{:S(2)}, u32[]{:S(2)}) collective-permute-start(bf16[1,2,128,128]{3,2,1,0:T(8,128)(2,1)S(1)} %get-tuple-element.32), channel_id=1, source_target_pairs={{0,4},{1,5},{2,6},{3,7},{4,0},{5,1},{6,2},{7,3},{8,12},{9,13},{10,... | collective-permute-start | bytes 196616 | tf_op jit(solution)/shard_map/ppermute | solution.py:274
  44.6 23.6 %copy-start.1 = (bf16[2,512,512]{2,1,0:T(8,128)(2,1)S(1)}, bf16[2,512,512]{2,1,0:T(8,128)(2,1)}, u32[]{:S(2)}) copy-start(bf16[2,512,512]{2,1,0:T(8,128)(2,1)} %constant.18.clone.basis_ref) | copy-start | bytes 3145732
  44.6 23.6 %copy-start.8 = (f32[128,128]{1,0:T(8,128)S(1)}, f32[128,128]{1,0:T(8,128)}, u32[]{:S(2)}) copy-start(f32[128,128]{1,0:T(8,128)} %constant.19.clone.taper_ref) | copy-start | bytes 196612
  44.6 23.6 %copy-start.12 = (s32[16,2]{0,1:T(2,128)S(1)}, s32[16,2]{0,1:T(2,128)}, u32[]{:S(2)}) copy-start(s32[16,2]{0,1:T(2,128)} %param.16) | copy-start | bytes 388
  44.6 3.6 %collective-permute-start.7 = (bf16[1,2,128,128]{3,2,1,0:T(8,128)(2,1)S(1)}, bf16[1,2,128,128]{3,2,1,0:T(8,128)(2,1)S(1)}, u32[]{:S(2)}, u32[]{:S(2)}) collective-permute-start(bf16[1,2,128,128]{3,2,1,0:T(8,128)(2,1)S(1)} %get-tuple-element.29.rest_0_), channel_id=1, source_target_pairs={{0,4},{1,5},{2,6},{3,7},{4,0},{5,1},{6,2},{7,3},{8,12},{9,13},{10,... | collective-permute-start | bytes 196616 | tf_op jit(solution)/shard_map/ppermute | solution.py:274
  45.8 7.1 %collective-permute-start.9 = (bf16[1,2,128,128]{3,2,1,0:T(8,128)(2,1)S(1)}, bf16[1,2,128,128]{3,2,1,0:T(8,128)(2,1)S(1)}, u32[]{:S(2)}, u32[]{:S(2)}) collective-permute-start(bf16[1,2,128,128]{3,2,1,0:T(8,128)(2,1)S(1)} %get-tuple-element.29.rest_0_), channel_id=1, source_target_pairs={{0,12},{1,13},{2,14},{3,15},{4,8},{5,9},{6,10},{7,11},{8,4},{9,5},... | collective-permute-start | bytes 196616 | tf_op jit(solution)/shard_map/ppermute | solution.py:274
  48.0 4.9 %collective-permute-start.8 = (bf16[1,2,128,128]{3,2,1,0:T(8,128)(2,1)S(1)}, bf16[1,2,128,128]{3,2,1,0:T(8,128)(2,1)S(1)}, u32[]{:S(2)}, u32[]{:S(2)}) collective-permute-start(bf16[1,2,128,128]{3,2,1,0:T(8,128)(2,1)S(1)} %get-tuple-element.29.rest_0_), channel_id=1, source_target_pairs={{0,8},{1,9},{2,10},{3,11},{4,12},{5,13},{6,14},{7,15},{8,0},{9,1},... | collective-permute-start | bytes 196616 | tf_op jit(solution)/shard_map/ppermute | solution.py:274
  53.0 5.5 %collective-permute-start.11 = (bf16[3,2,128,128]{3,2,1,0:T(8,128)(2,1)S(1)}, bf16[3,2,128,128]{3,2,1,0:T(8,128)(2,1)S(1)}, u32[]{:S(2)}, u32[]{:S(2)}) collective-permute-start(bf16[3,2,128,128]{3,2,1,0:T(8,128)(2,1)S(1)} %constant_dynamic-update-slice_fusion.rest_1_), channel_id=1, source_target_pairs={{0,2},{1,3},{2,0},{3,1},{4,6},{5,7},{6,4},{7,5},{8,10},{9,11},{10,... | collective-permute-start | bytes 589832 | tf_op jit(solution)/shard_map/ppermute | solution.py:274
  54.2 13.9 %collective-permute-start.13 = (bf16[3,2,128,128]{3,2,1,0:T(8,128)(2,1)S(1)}, bf16[3,2,128,128]{3,2,1,0:T(8,128)(2,1)S(1)}, u32[]{:S(2)}, u32[]{:S(2)}) collective-permute-start(bf16[3,2,128,128]{3,2,1,0:T(8,128)(2,1)S(1)} %constant_dynamic-update-slice_fusion.rest_1_), channel_id=1, source_target_pairs={{0,1},{1,0},{2,3},{3,2},{4,5},{5,4},{6,7},{7,6},{8,9},{9,8},{10,11... | collective-permute-start | bytes 589832 | tf_op jit(solution)/shard_map/ppermute | solution.py:274
  58.5 9.6 %collective-permute-start.15 = (bf16[3,2,128,128]{3,2,1,0:T(8,128)(2,1)S(1)}, bf16[3,2,128,128]{3,2,1,0:T(8,128)(2,1)S(1)}, u32[]{:S(2)}, u32[]{:S(2)}) collective-permute-start(bf16[3,2,128,128]{3,2,1,0:T(8,128)(2,1)S(1)} %collective-permute-done.11.rest_3_), channel_id=1, source_target_pairs={{0,1},{1,0},{2,3},{3,2},{4,5},{5,4},{6,7},{7,6},{8,9},{9,8},{10,11... | collective-permute-start | bytes 589832 | tf_op jit(solution)/shard_map/ppermute | solution.py:274
  62.6 3.7 %collective-permute-start.10 = (bf16[1,2,128,128]{3,2,1,0:T(8,128)(2,1)S(1)}, bf16[1,2,128,128]{3,2,1,0:T(8,128)(2,1)S(1)}, u32[]{:S(2)}, u32[]{:S(2)}) collective-permute-start(bf16[1,2,128,128]{3,2,1,0:T(8,128)(2,1)S(1)} %get-tuple-element.29.rest_0_), channel_id=1, source_target_pairs={{0,2},{1,3},{2,0},{3,1},{4,6},{5,7},{6,4},{7,5},{8,10},{9,11},{10,... | collective-permute-start | bytes 196616 | tf_op jit(solution)/shard_map/ppermute | solution.py:274
  63.9 4.2 %collective-permute-start.12 = (bf16[1,2,128,128]{3,2,1,0:T(8,128)(2,1)S(1)}, bf16[1,2,128,128]{3,2,1,0:T(8,128)(2,1)S(1)}, u32[]{:S(2)}, u32[]{:S(2)}) collective-permute-start(bf16[1,2,128,128]{3,2,1,0:T(8,128)(2,1)S(1)} %get-tuple-element.29.rest_0_), channel_id=1, source_target_pairs={{0,1},{1,0},{2,3},{3,2},{4,5},{5,4},{6,7},{7,6},{8,9},{9,8},{10,11... | collective-permute-start | bytes 196616 | tf_op jit(solution)/shard_map/ppermute | solution.py:274
  66.4 1.8 %collective-permute-start.14 = (bf16[1,2,128,128]{3,2,1,0:T(8,128)(2,1)S(1)}, bf16[1,2,128,128]{3,2,1,0:T(8,128)(2,1)S(1)}, u32[]{:S(2)}, u32[]{:S(2)}) collective-permute-start(bf16[1,2,128,128]{3,2,1,0:T(8,128)(2,1)S(1)} %collective-permute-done.10.rest_2_), channel_id=1, source_target_pairs={{0,1},{1,0},{2,3},{3,2},{4,5},{5,4},{6,7},{7,6},{8,9},{9,8},{10,11... | collective-permute-start | bytes 196616 | tf_op jit(solution)/shard_map/ppermute | solution.py:274
  (8 other events, 66.6 us)

commit v3 on v2

v3 whole, which is shorter than its diff:
```python
import functools
import math

import jax
import jax.numpy as jnp
import ml_dtypes
import numpy as np
from jax import lax
from jax.experimental import pallas as pl
from jax.experimental.pallas import tpu as pltpu
from jax.sharding import PartitionSpec as P

F = 512
M = 128
SG = 512
TV = 128
BF = jnp.bfloat16
F32 = jnp.float32
TWO_PI = 2.0 * math.pi


def basis_tables():
    index = np.arange(F, dtype=np.int64)
    angle = -TWO_PI * ((index[:, None] * index[None, :]) % F) / F
    table = np.stack([np.cos(angle), np.sin(angle)]) / math.sqrt(F)
    return table.astype(ml_dtypes.bfloat16)


def padding_tables(facet_count):
    product = (np.arange(SG)[:, None] * np.arange(M)[None, :]) % SG
    angle = TWO_PI * product / SG
    scale = (M * math.sqrt(facet_count)) ** (-0.5)
    table = np.stack([np.cos(angle), np.sin(angle)]) * scale
    return table.astype(ml_dtypes.bfloat16)


def kernel_table():
    rows = np.arange(TV, dtype=np.float64)[:, None]
    columns = np.arange(2 * TV, dtype=np.float64)[None, :]
    distance = columns - 2.0 * rows - 1.0
    value = 0.75 * np.exp(-((distance / 1.5) ** 2))
    return np.where(np.abs(distance) <= 4.0, value, 0.0).astype(ml_dtypes.bfloat16)


def taper_square():
    position = np.arange(M, dtype=np.float64)
    taper = 0.6 + 0.4 * np.sin(math.pi * (position + 0.5) / M)
    return (taper[:, None] * taper[None, :]).astype(np.float32)


def turn_polynomials():
    nodes = 0.5 * np.cos(math.pi * (np.arange(400) + 0.5) / 800)
    square = nodes * nodes
    powers = np.stack([square**k for k in range(8)], axis=1)
    cos_c = np.linalg.lstsq(powers, np.cos(TWO_PI * nodes), rcond=None)[0]
    sin_c = np.linalg.lstsq(powers, np.sin(TWO_PI * nodes) / nodes, rcond=None)[0]
    return [float(c) for c in cos_c], [float(c) for c in sin_c]


COS_C, SIN_C = turn_polynomials()


def cos_sin_turns(turns):
    rest = turns - jnp.floor(turns + 0.5)
    square = rest * rest
    cos_v = jnp.full_like(square, COS_C[7])
    sin_v = jnp.full_like(square, SIN_C[7])
    for k in range(6, -1, -1):
        cos_v = cos_v * square + COS_C[k]
        sin_v = sin_v * square + SIN_C[k]
    return cos_v, sin_v * rest


def dot(left, right):
    return jnp.dot(left, right, preferred_element_type=F32)


def mul_left(left_r, left_i, right_r, right_i):
    left = jnp.concatenate([left_r, left_i], axis=1)
    real = dot(left, jnp.concatenate([right_r, -right_i], axis=0))
    imag = dot(left, jnp.concatenate([right_i, right_r], axis=0))
    return real, imag


def mul_right(left_r, left_i, right_r, right_i):
    right = jnp.concatenate([right_r, right_i], axis=0)
    real = dot(jnp.concatenate([left_r, -left_i], axis=1), right)
    imag = dot(jnp.concatenate([left_i, left_r], axis=1), right)
    return real, imag


def phase_taper(fo_ref):
    rows = lax.broadcasted_iota(jnp.int32, (M, M), 0)
    columns = lax.broadcasted_iota(jnp.int32, (M, M), 1)
    total = (rows * fo_ref[0, 0] + columns * fo_ref[0, 1]) & (F - 1)
    cos_v, sin_v = cos_sin_turns(total.astype(F32) * (1.0 / F))
    row = lax.broadcasted_iota(jnp.int32, (M, 1), 0).astype(F32)
    column = lax.broadcasted_iota(jnp.int32, (1, M), 1).astype(F32)
    _, row_sin = cos_sin_turns((row + 0.5) * (0.5 / M))
    _, column_sin = cos_sin_turns((column + 0.5) * (0.5 / M))
    taper2 = (0.6 + 0.4 * row_sin) * (0.6 + 0.4 * column_sin)
    return cos_v * taper2, sin_v * taper2


def owner_of(j, me):
    return (j & ~3) | ((j ^ me) & 3)


def forward_kernel(sends, me_ref, fo_ref, so_ref, facet_ref, basis_ref, *rest):
    outs, (facet_buf, basis_buf, spec_ref, sems) = rest[: len(sends)], rest[len(sends) :]
    copies = []
    for k in range(2):
        copies.append(pltpu.make_async_copy(basis_ref.at[k], basis_buf.at[k], sems.at[2 * k]))
        copies.append(pltpu.make_async_copy(facet_ref.at[0, k], facet_buf.at[k], sems.at[2 * k + 1]))
    for copy in copies:
        copy.start()
    pc, ps = phase_taper(fo_ref)
    for copy in copies:
        copy.wait()
    br, bi = basis_buf[0], basis_buf[1]
    hr, hi = mul_left(facet_buf[0], facet_buf[1], br, bi)
    spectrum = mul_right(br, bi, hr.astype(BF), hi.astype(BF))
    columns = F // M
    for plane in range(2):
        for c in range(columns):
            part = spectrum[plane][:, c * M : (c + 1) * M]
            spec_ref[plane, c, :F] = part
            spec_ref[plane, c, F:] = part[:M]
            if c == 0:
                spec_ref[plane, columns, :F] = part
                spec_ref[plane, columns, F:] = part[:M]
    me = me_ref[0]

    def block(out_ref, item, j):
        owner = owner_of(j, me)
        sx, sy = so_ref[0, owner], so_ref[1, owner]
        lane = sy // M
        shift = (2 * M - (sy & (M - 1))) & (2 * M - 1)
        parts = []
        for plane in range(2):
            left = spec_ref[plane, lane, pl.ds(sx, M), :]
            right = spec_ref[plane, lane + 1, pl.ds(sx, M), :]
            wide = jnp.concatenate([left, right], axis=1)
            parts.append(pltpu.roll(wide, shift, 1)[:, :M])
        wr, wi = parts
        out_ref[item, 0] = (pc * wr - ps * wi).astype(BF)
        out_ref[item, 1] = (pc * wi + ps * wr).astype(BF)

    for out_ref, js in zip(outs, sends):
        for_blocks(block, out_ref, js)


def for_blocks(block, ref, js):
    step = js[1] - js[0] if len(js) > 1 else 1
    if len(js) > 1 and js == list(range(js[0], js[0] + step * len(js), step)):

        def body(item, carry):
            block(ref, item, item * step + js[0])
            return carry

        lax.fori_loop(0, len(js), body, 0)
    else:
        for item, j in enumerate(js):
            block(ref, item, j)


def prepare_kernel(w_ref, to_ref, kt_ref, kwide_ref, screen_ref, kvt_ref, kv_ref, kut_ref):
    slots = kut_ref.shape[0]
    w = w_ref[0]
    row = lax.broadcasted_iota(jnp.int32, (SG, 1), 0).astype(F32) - SG / 2.0
    column = lax.broadcasted_iota(jnp.int32, (1, SG), 1).astype(F32) - SG / 2.0
    row2 = row * row * (1.0 / (SG * SG)) + 1.0
    column2 = column * column * (1.0 / (SG * SG))
    cos_v, sin_v = cos_sin_turns((jnp.sqrt(row2 + column2) - 1.0) * w)
    screen_ref[0] = cos_v
    screen_ref[1] = sin_v
    for t in range(slots):
        ou, ov = to_ref[0, t], to_ref[1, t]
        kut_ref[t] = kt_ref[pl.ds(2 * TV - ou, SG), :].astype(BF)
        kvt_ref[:, t * TV : (t + 1) * TV] = kt_ref[pl.ds(2 * TV - ov, SG), :].astype(BF)
        kv_ref[t * TV : (t + 1) * TV] = pltpu.roll(kwide_ref[...], ov, 1).astype(BF)


def subgrid_kernel(tc_ref, to_ref, got_ref, obs_ref, pad_ref, padt_ref, kern_ref, *rest):
    (screen_ref, kvt_ref, kv_ref, kut_ref) = rest[:4]
    (out_ref, coef_ref, model_ref, rows_ref, z_ref, res_ref, sems) = rest[4:]
    slots = obs_ref.shape[0]
    count = tc_ref[0]

    def total(plane):
        value = got_ref[0, plane].astype(F32)
        for item in range(1, got_ref.shape[0]):
            value = value + got_ref[item, plane].astype(F32)
        return value.astype(BF)

    pr, pi = pad_ref[0], pad_ref[1]
    inner_r, inner_i = mul_right(pr, pi, total(0), total(1))
    tr, ti = padt_ref[0], padt_ref[1]
    image_r, image_i = mul_left(inner_r.astype(BF), inner_i.astype(BF), tr, ti)
    sc, ss = screen_ref[0], screen_ref[1]
    model_ref[:SG] = (sc * image_r - ss * image_i).astype(BF)
    model_ref[SG:] = (sc * image_i + ss * image_r).astype(BF)

    model = model_ref[...]
    kern = kern_ref[...]
    copies = []
    for t0 in range(0, slots, 2):
        pair = dot(model, kvt_ref[:, t0 * TV : (t0 + 2) * TV])
        for t in (t0, t0 + 1):
            rows_ref[t % rows_ref.shape[0]] = pair[:, (t - t0) * TV : (t - t0 + 1) * TV]
        for t in (t0, t0 + 1):
            slot = t % rows_ref.shape[0]
            ou = to_ref[0, t]
            wr = rows_ref[slot, pl.ds(ou, 2 * TV), :]
            wi = rows_ref[slot, pl.ds(SG + ou, 2 * TV), :]
            window = jnp.concatenate([wr.astype(BF), wi.astype(BF)], axis=1)
            predicted = dot(kern, window)
            live = count > t
            res = []
            for plane in range(2):
                value = obs_ref[t, plane].astype(F32) - predicted[:, plane * TV : (plane + 1) * TV]
                res.append(jnp.where(live, value, 0.0).astype(BF))
                res_ref[t, plane] = res[plane]
            z = dot(kut_ref[t], jnp.concatenate(res, axis=1)).astype(BF)
            z_ref[:SG, t * TV : (t + 1) * TV] = z[:, :TV]
            z_ref[SG:, t * TV : (t + 1) * TV] = z[:, TV:]
        if t0 % 4 == 2:
            copies.append(
                pltpu.make_async_copy(
                    res_ref.at[pl.ds(t0 - 2, 4)], out_ref.at[pl.ds(t0 - 2, 4)], sems.at[t0 // 4]
                )
            )
            copies[-1].start()

    kv = kv_ref[...]
    ar = dot(z_ref[:SG], kv)
    ai = dot(z_ref[SG:], kv)
    screened_r = (sc * ar + ss * ai).astype(BF)
    screened_i = (sc * ai - ss * ar).astype(BF)
    reduced_r, reduced_i = mul_right(tr, -ti, screened_r, screened_i)
    coef_r, coef_i = mul_left(reduced_r.astype(BF), reduced_i.astype(BF), pr, -pi)
    for item in range(coef_ref.shape[0]):
        coef_ref[item, 0] = coef_r.astype(BF)
        coef_ref[item, 1] = coef_i.astype(BF)
    for copy in copies:
        copy.wait()


def grid_blocks(pieces, refs, me_ref, fo_ref, so_ref, grid_ref):
    pc, ps = phase_taper(fo_ref)
    me = me_ref[0]
    blank = jnp.zeros((M, M), F32)

    def block(in_ref, item, j):
        owner = owner_of(j, me)
        sx, sy = so_ref[0, owner], so_ref[1, owner]
        lane = sy // M
        shift = sy & (M - 1)
        cr, ci = in_ref[item, 0].astype(F32), in_ref[item, 1].astype(F32)
        values = (pc * cr + ps * ci, pc * ci - ps * cr)
        for plane in range(2):
            wide = pltpu.roll(jnp.concatenate([values[plane], blank], axis=1), shift, 1)
            grid_ref[plane, lane, pl.ds(sx, M), :] += wide[:, :M]
            grid_ref[plane, lane + 1, pl.ds(sx, M), :] += wide[:, M:]

    for in_ref, js in zip(refs, pieces):
        for_blocks(block, in_ref, js)


def first_grid_kernel(pieces, me_ref, fo_ref, so_ref, *rest):
    grid_ref = rest[-1]
    grid_ref[...] = jnp.zeros_like(grid_ref)
    grid_blocks(pieces, rest[:-1], me_ref, fo_ref, so_ref, grid_ref)


def next_grid_kernel(pieces, me_ref, fo_ref, so_ref, *rest):
    rest[-1][...] = rest[-2][...]
    grid_blocks(pieces, rest[:-2], me_ref, fo_ref, so_ref, rest[-1])


def backward_kernel(pieces, me_ref, fo_ref, so_ref, basis_ref, *rest):
    grid_ref, out_ref, _, out_buf, sems = rest[-5:]
    grid_blocks(pieces, rest[: len(pieces)], me_ref, fo_ref, so_ref, grid_ref)
    columns = F // M
    folded = []
    for plane in range(2):
        strips = []
        for c in range(columns):
            strip = grid_ref[plane, c]
            if c == 0:
                strip = strip + grid_ref[plane, columns]
            top = strip[:M] + strip[F:]
            strips.append(jnp.concatenate([top.astype(BF), strip[M:F].astype(BF)], axis=0))
        folded.append(jnp.concatenate(strips, axis=1))
    br, bi = basis_ref[0], basis_ref[1]
    hr, hi = mul_right(br, -bi, *folded)
    hr, hi = hr.astype(BF), hi.astype(BF)
    half = F // 2
    copies = []
    for k in range(2):
        rows = slice(k * half, (k + 1) * half)
        real, imag = mul_left(hr[rows], hi[rows], br, -bi)
        for plane, value in enumerate((real, imag)):
            out_buf[plane, rows] = value.astype(BF)
            copy = pltpu.make_async_copy(
                out_buf.at[plane, pl.ds(k * half, half)],
                out_ref.at[0, plane, pl.ds(k * half, half)],
                sems.at[2 * k + plane],
            )
            copy.start()
            copies.append(copy)
    for copy in copies:
        copy.wait()


SMEM = pl.BlockSpec(memory_space=pltpu.SMEM)
VMEM = pl.BlockSpec(memory_space=pltpu.VMEM)
ANY = pl.BlockSpec(memory_space=pl.ANY)


def params(mib):
    return pltpu.CompilerParams(vmem_limit_bytes=mib * 1024 * 1024)


def near(value):
    return pltpu.with_memory_space_constraint(value, pltpu.VMEM)


def far(value):
    return pltpu.with_memory_space_constraint(value, pltpu.HBM)


def held(shape, dtype=BF):
    return pltpu.VMEM(shape, dtype)


def exchange(value, mask, n):
    return lax.ppermute(value, "facet", [(i, i ^ mask) for i in range(n)])


def per_device(facets, facet_offsets, subgrid_offsets, w_terms, tile_count, tile_offsets, observed):
    n = lax.axis_size("facet")
    far_n = n // 4
    slots = observed.shape[0]
    me = lax.axis_index("facet").astype(jnp.int32).reshape(1)
    corners = far(subgrid_offsets.T)
    tile_corners = tile_offsets.T
    facet_offsets = far(facet_offsets)
    basis = jnp.asarray(basis_tables())
    pad_np = padding_tables(n)
    kern_np = kernel_table()
    kt_np = np.zeros((6 * TV, TV), np.float32)
    kt_np[2 * TV : 4 * TV] = kern_np.astype(np.float32).T
    kwide_np = np.zeros((TV, SG), np.float32)
    kwide_np[:, : 2 * TV] = kern_np.astype(np.float32)
    columns = [[high * 4 + low for high in range(far_n)] for low in range(4)]
    quarter = [[high * 4 + low for high in range(far_n)] for low in range(4)]

    own0, own1, own2, own3 = pl.pallas_call(
        functools.partial(forward_kernel, quarter),
        out_shape=[held((far_n, 2, M, M))] * 4,
        in_specs=[SMEM] * 3 + [ANY] * 2,
        out_specs=[VMEM] * 4,
        scratch_shapes=[
            pltpu.VMEM((2, F, F), BF),
            pltpu.VMEM((2, F, F), BF),
            pltpu.VMEM((2, F // M + 1, F + M, M), F32),
            pltpu.SemaphoreType.DMA((4,)),
        ],
        compiler_params=params(16),
        name="forward",
    )(me, facet_offsets, corners, far(facets), far(basis))

    screen, kvt, kv, kut = pl.pallas_call(
        prepare_kernel,
        out_shape=[
            held((2, SG, SG), F32),
            held((SG, slots * TV)),
            held((slots * TV, SG)),
            held((slots, SG, TV)),
        ],
        in_specs=[SMEM] * 2 + [VMEM] * 2,
        out_specs=[VMEM] * 4,
        compiler_params=params(8),
        name="prepare",
    )(w_terms, tile_corners, jnp.asarray(kt_np), jnp.asarray(kwide_np))

    def plus(*terms):
        return sum(term.astype(F32) for term in terms).astype(BF)

    def spread(value):
        return lax.all_to_all(value, "facet", 0, 0, axis_index_groups=columns, tiled=True)

    got3 = exchange(own3, 1, n)
    got1 = exchange(own1, 1, n)
    got2 = exchange(plus(own2, got3), 2, n)
    got = spread(plus(own0, got1, got2))

    residual, coefficients = pl.pallas_call(
        subgrid_kernel,
        out_shape=[pltpu.HBM(observed.shape, BF), held((far_n, 2, M, M))],
        in_specs=[SMEM] * 2 + [VMEM] * 9,
        out_specs=[ANY, VMEM],
        scratch_shapes=[
            pltpu.VMEM((2 * SG, SG), BF),
            pltpu.VMEM((8, 2 * SG, TV), F32),
            pltpu.VMEM((2 * SG, slots * TV), BF),
            pltpu.VMEM(observed.shape, BF),
            pltpu.SemaphoreType.DMA((slots // 4,)),
        ],
        compiler_params=params(24),
        name="subgrid",
    )(
        tile_count,
        tile_corners,
        near(got),
        near(observed),
        near(jnp.asarray(pad_np)),
        near(jnp.asarray(pad_np.transpose(0, 2, 1))),
        near(jnp.asarray(kern_np)),
        near(screen),
        near(kvt),
        near(kv),
        near(kut),
    )

    all0 = spread(coefficients)
    all2 = exchange(all0, 2, n)
    all1 = exchange(all0, 1, n)
    all3 = exchange(all2, 1, n)
    grid_shape = (2, F // M + 1, F + M, M)
    grid = pl.pallas_call(
        functools.partial(first_grid_kernel, quarter[:1]),
        out_shape=held(grid_shape, F32),
        in_specs=[SMEM] * 3 + [VMEM],
        out_specs=VMEM,
        compiler_params=params(8),
        name="grid_first",
    )(me, facet_offsets, corners, near(all0))
    grid = pl.pallas_call(
        functools.partial(next_grid_kernel, quarter[1:3]),
        out_shape=held(grid_shape, F32),
        in_specs=[SMEM] * 3 + [VMEM] * 3,
        out_specs=VMEM,
        compiler_params=params(8),
        name="grid_next",
    )(me, facet_offsets, corners, near(all1), near(all2), near(grid))
    update = pl.pallas_call(
        functools.partial(backward_kernel, quarter[3:]),
        out_shape=[pltpu.HBM(facets.shape, BF), held(grid_shape, F32)],
        in_specs=[SMEM] * 3 + [VMEM] * 3,
        out_specs=[ANY, VMEM],
        input_output_aliases={5: 1},
        scratch_shapes=[
            pltpu.VMEM((2, F, F), BF),
            pltpu.SemaphoreType.DMA((4,)),
        ],
        compiler_params=params(16),
        name="backward",
    )(me, facet_offsets, corners, near(basis), near(all3), near(grid))[0]
    return (residual, update)


def solution(mesh):
    placed = (
        P(("groups", "facet"), None, None, None),
        P(("groups", "facet"), None),
        P("groups", None),
        P(("groups", "facet")),
        P(("groups", "facet")),
        P(("groups", "facet"), None),
        P(("groups", "facet"), None, None, None),
    )
    return jax.shard_map(
        per_device,
        mesh=mesh,
        in_specs=placed,
        out_specs=(
            P(("groups", "facet"), None, None, None),
            P(("groups", "facet"), None, None, None),
        ),
        check_vma=False,
    )
```

time: 74.9 us -> 86.8 us (1.16)
  blocking collectives: 0 us -> 10.4 us
  local copies, waits for them, and re-layouts: 5.68 us -> 12.6 us
  waiting for transfers between devices: 12.8 us -> 7.41 us
  starting transfers between devices: 22.3 us -> 17.7 us
  Pallas kernels: 31.3 us -> 35 us
    all_to_all x0 -> x1, blocking collectives: none -> 10.4 us  [spread(): lax.all_to_all(value, 'facet', 0, 0, axis_index_groups=columns, tiled=True)]
    ppermute x16 -> x6, starting transfers between devices: 22.3 us -> 13.2 us  [exchange(): return lax.ppermute(value, 'facet', [(i, i ^ mask) for i in range(n)])]
    unnamed x35 -> x28, local copies, waits for them, and re-layouts: 5.66 us -> 12.6 us
    ppermute x16 -> x6, waiting for transfers between devices: 12.8 us -> 7.41 us  [exchange(): return lax.ppermute(value, 'facet', [(i, i ^ mask) for i in range(n)])]
    all_to_all x0 -> x1, starting transfers between devices: none -> 4.49 us  [spread(): lax.all_to_all(value, 'facet', 0, 0, axis_index_groups=columns, tiled=True)]
    pallas_call x3 -> x5, Pallas kernels: 26.2 us -> 29.9 us  [the longest x1 14.5 us: per_device(): pl.pallas_call(subgrid_kernel, out_shape=[pltpu.HBM(observed.shape, BF),...]
  transfers between devices with their start and end apart: 16 -> 7, of which waited for: 4 -> 2; matrix products, arithmetic and copies ran while one was open for 2% -> 0% of each run, Pallas kernels for 7% -> 10%
where the time goes in v3:
time: 86.8 us; the launch traced here: 86.3 us
  Pallas kernels  35 us (40%)
  starting transfers between devices  17.7 us (20%)
  local copies, waits for them, and re-layouts  12.6 us (15%)
  blocking collectives  10.4 us (12%)
  waiting for transfers between devices  7.41 us (9%)
  between operations  2.26 us (3%)
  other arithmetic  0.88 us (1%)
    pallas_call x1, Pallas kernels, per_device(): pl.pallas_call(subgrid_kernel, out_shape=[pltpu.HBM(observed.shape, BF),...  14.5 us
    ppermute x6, starting transfers between devices, exchange(): return lax.ppermute(value, 'facet', [(i, i ^ mask) for i in range(n)])  13.2 us
    unnamed x28, local copies, waits for them, and re-layouts  12.6 us
    all_to_all x1, blocking collectives, spread(): lax.all_to_all(value, 'facet', 0, 0, axis_index_groups=columns, tiled=True)  10.4 us
    ppermute x6, waiting for transfers between devices, exchange(): return lax.ppermute(value, 'facet', [(i, i ^ mask) for i in range(n)])  7.41 us
    pallas_call x1, Pallas kernels, per_device(): pl.pallas_call(functools.partial(forward_kernel, quarter), out_shape=[hel...  7.18 us
    pallas_call x1, Pallas kernels, per_device(): pl.pallas_call(prepare_kernel, out_shape=[held((2, SG, SG), F32), held((S...  5.09 us
    all_to_all x1, starting transfers between devices, spread(): lax.all_to_all(value, 'facet', 0, 0, axis_index_groups=columns, tiled=True)  4.49 us
  transfers between devices with their start and end apart: 7, of which 2 were waited for; matrix products, arithmetic and copies ran while one was open for 0% of the time, Pallas kernels for 10%

profile of v3, /device:TPU:1, one launch (start us, length us, event | category | flops | bytes accessed | tf_op | source)
XLA Modules:
  0.0 86.3 jit_solution(6689822747468447983)
XLA Ops:
  0.7 7.2 %forward.1 = (bf16[4,2,128,128]{3,2,1,0:T(8,128)(2,1)S(1)}, bf16[4,2,128,128]{3,2,1,0:T(8,128)(2,1)S(1)}, bf16[4,2,128,128]{3,2,1,0:T(8,128)(2,1)S(1)}, bf16[4,2,128,128]{3,2,1,0:T(8,128)(2,1)S(1)}) custom-call(s32[1]{0:T(128)} %bitcast.1.me_ref, s32[1,2]{1,0:T(1,128)} %fo_ref.7, s32[2,16]{1,0:T(2,128)} %bitcast.5, bf16[1,2,512,512]{3,2,1,0:T(8,128)(2,1)} %facet_ref.1, ...), custom_call_target="tpu_custom_call" | custom-call | tf_op jit(solution)/shard_map/forward/pallas_call | solution.py:359
  8.4 1.0 %collective-permute-done.1 = bf16[4,2,128,128]{3,2,1,0:T(8,128)(2,1)S(1)} collective-permute-done((bf16[4,2,128,128]{3,2,1,0:T(8,128)(2,1)S(1)}, bf16[4,2,128,128]{3,2,1,0:T(8,128)(2,1)S(1)}, u32[]{:S(2)}, u32[]{:S(2)}) %collective-permute-start.1) | collective-permute-done | bytes 262176 | tf_op jit(solution)/shard_map/ppermute | solution.py:338
  9.5 2.4 %collective-permute-start.2 = (bf16[4,2,128,128]{3,2,1,0:T(8,128)(2,1)S(1)}, bf16[4,2,128,128]{3,2,1,0:T(8,128)(2,1)S(1)}, u32[]{:S(2)}, u32[]{:S(2)}) collective-permute-start(bf16[4,2,128,128]{3,2,1,0:T(8,128)(2,1)S(1)} %add_convert_fusion.1), channel_id=1, source_target_pairs={{0,2},{1,3},{2,0},{3,1},{4,6},{5,7},{6,4},{7,5},{8,10},{9,11},{10,... | collective-permute-start | bytes 786440 | tf_op jit(solution)/shard_map/ppermute | solution.py:338
  12.0 6.4 %collective-permute-done.2 = bf16[4,2,128,128]{3,2,1,0:T(8,128)(2,1)S(1)} collective-permute-done((bf16[4,2,128,128]{3,2,1,0:T(8,128)(2,1)S(1)}, bf16[4,2,128,128]{3,2,1,0:T(8,128)(2,1)S(1)}, u32[]{:S(2)}, u32[]{:S(2)}) %collective-permute-start.2) | collective-permute-done | bytes 262176 | tf_op jit(solution)/shard_map/ppermute | solution.py:338
  19.2 4.5 %all-to-all-start = ((bf16[4,2,128,128]{3,2,1,0:T(8,128)(2,1)}), bf16[4,2,128,128]{3,2,1,0:T(8,128)(2,1)S(1)}, u32[]{:S(2)}, u32[]{:S(2)}) async-start(bf16[4,2,128,128]{3,2,1,0:T(8,128)(2,1)} %add_convert_fusion), calls=%async_computation | async-start | bytes 524288 | tf_op jit(solution)/shard_map/all_to_all | solution.py:392
  25.0 1.0 %copy-done.8 = f32[768,128]{1,0:T(8,128)S(1)} copy-done((f32[768,128]{1,0:T(8,128)S(1)}, f32[768,128]{1,0:T(8,128)}, u32[]{:S(2)}) %copy-start.8) | copy-done | bytes 393240
  26.0 0.9 %copy-done.11 = f32[128,512]{1,0:T(8,128)S(1)} copy-done((f32[128,512]{1,0:T(8,128)S(1)}, f32[128,512]{1,0:T(8,128)}, u32[]{:S(2)}) %copy-start.11) | copy-done | bytes 262168
  26.9 5.1 %prepare.1 = (f32[2,512,512]{2,1,0:T(8,128)S(1)}, bf16[512,2048]{1,0:T(8,128)(2,1)S(1)}, bf16[2048,512]{1,0:T(8,128)(2,1)S(1)}, bf16[16,512,128]{2,1,0:T(8,128)(2,1)S(1)}) custom-call(f32[1]{0:T(128)S(6)} %copy.17.w_ref, s32[2,16]{1,0:T(2,128)S(1)} %bitcast.3, f32[768,128]{1,0:T(8,128)S(1)} %copy-done.8, f32[128,512]{1,0:T(8,128)S(1)} %copy-done.11), custom_call_target="tpu_custom_call" | custom-call | tf_op jit(solution)/shard_map/prepare/pallas_call | solution.py:374
  32.0 1.3 %copy-done.1 = bf16[512,2048]{1,0:T(8,128)(2,1)} copy-done((bf16[512,2048]{1,0:T(8,128)(2,1)}, bf16[512,2048]{1,0:T(8,128)(2,1)S(1)}, u32[]{:S(2)}) %copy-start.1) | copy-done | bytes 2097176
  33.3 1.3 %copy-done.3 = bf16[2048,512]{1,0:T(8,128)(2,1)} copy-done((bf16[2048,512]{1,0:T(8,128)(2,1)}, bf16[2048,512]{1,0:T(8,128)(2,1)S(1)}, u32[]{:S(2)}) %copy-start.3) | copy-done | bytes 2097176
  34.6 1.3 %copy-done.5 = bf16[16,512,128]{2,1,0:T(8,128)(2,1)} copy-done((bf16[16,512,128]{2,1,0:T(8,128)(2,1)}, bf16[16,512,128]{2,1,0:T(8,128)(2,1)S(1)}, u32[]{:S(2)}) %copy-start.5) | copy-done | bytes 2097176
  36.0 1.6 %copy-done.2 = bf16[512,2048]{1,0:T(8,128)(2,1)S(1)} copy-done((bf16[512,2048]{1,0:T(8,128)(2,1)S(1)}, bf16[512,2048]{1,0:T(8,128)(2,1)}, u32[]{:S(2)}) %copy-start.2) | copy-done | bytes 2097176
  37.6 1.6 %copy-done.4 = bf16[2048,512]{1,0:T(8,128)(2,1)S(1)} copy-done((bf16[2048,512]{1,0:T(8,128)(2,1)S(1)}, bf16[2048,512]{1,0:T(8,128)(2,1)}, u32[]{:S(2)}) %copy-start.4) | copy-done | bytes 2097176
  39.2 1.6 %copy-done.6 = bf16[16,512,128]{2,1,0:T(8,128)(2,1)S(1)} copy-done((bf16[16,512,128]{2,1,0:T(8,128)(2,1)S(1)}, bf16[16,512,128]{2,1,0:T(8,128)(2,1)}, u32[]{:S(2)}) %copy-start.6) | copy-done | bytes 2097176
  40.8 0.9 %copy-done.9 = bf16[2,128,512]{2,1,0:T(8,128)(2,1)S(1)} copy-done((bf16[2,128,512]{2,1,0:T(8,128)(2,1)S(1)}, bf16[2,128,512]{2,1,0:T(8,128)(2,1)}, u32[]{:S(2)}) %copy-start.9) | copy-done | bytes 262168
  41.7 0.9 %copy-done.10 = bf16[2,512,128]{2,1,0:T(8,128)(2,1)S(1)} copy-done((bf16[2,512,128]{2,1,0:T(8,128)(2,1)S(1)}, bf16[2,512,128]{2,1,0:T(8,128)(2,1)}, u32[]{:S(2)}) %copy-start.10) | copy-done | bytes 262168
  42.7 14.5 %subgrid.1 = (bf16[16,2,128,128]{3,2,1,0:T(8,128)(2,1)}, bf16[4,2,128,128]{3,2,1,0:T(8,128)(2,1)S(1)}) custom-call(s32[1]{0:T(128)S(6)} %copy.18.tc_ref, s32[2,16]{1,0:T(2,128)S(1)} %bitcast.4, bf16[4,2,128,128]{3,2,1,0:T(8,128)(2,1)S(1)} %all-to-all-done.got_ref, bf16[16,2,128,128]{3,2,1,0:T(8,128)(2,1)S(1)} %copy-done.7, ...), custom_call_target="tpu_custom_call" | custom-call | tf_op jit(solution)/shard_map/subgrid/pallas_call | solution.py:399
  57.2 10.4 %all_to_all.10.rest_0_ = bf16[4,2,128,128]{3,2,1,0:T(8,128)(2,1)S(1)} all-to-all(bf16[4,2,128,128]{3,2,1,0:T(8,128)(2,1)S(1)} %get-tuple-element.22), channel_id=1, replica_groups={{0,4,8,12},{1,5,9,13},{2,6,10,14},{3,7,11,15},{16,20,24,28},{17,21,25,2..., dimensions={0} | all-to-all | bytes 524288 | tf_op jit(solution)/shard_map/all_to_all | solution.py:392
  67.6 1.2 %collective-permute-start.3 = (bf16[4,2,128,128]{3,2,1,0:T(8,128)(2,1)S(1)}, bf16[4,2,128,128]{3,2,1,0:T(8,128)(2,1)S(1)}, u32[]{:S(2)}, u32[]{:S(2)}) collective-permute-start(bf16[4,2,128,128]{3,2,1,0:T(8,128)(2,1)S(1)} %all_to_all.10.rest_0_), channel_id=1, source_target_pairs={{0,2},{1,3},{2,0},{3,1},{4,6},{5,7},{6,4},{7,5},{8,10},{9,11},{10,... | collective-permute-start | bytes 786440 | tf_op jit(solution)/shard_map/ppermute | solution.py:338
  68.9 4.1 %collective-permute-start.5 = (bf16[4,2,128,128]{3,2,1,0:T(8,128)(2,1)S(1)}, bf16[4,2,128,128]{3,2,1,0:T(8,128)(2,1)S(1)}, u32[]{:S(2)}, u32[]{:S(2)}) collective-permute-start(bf16[4,2,128,128]{3,2,1,0:T(8,128)(2,1)S(1)} %all_to_all.10.rest_0_), channel_id=1, source_target_pairs={{0,1},{1,0},{2,3},{3,2},{4,5},{5,4},{6,7},{7,6},{8,9},{9,8},{10,11... | collective-permute-start | bytes 786440 | tf_op jit(solution)/shard_map/ppermute | solution.py:338
  72.9 4.9 %collective-permute-start.4 = (bf16[4,2,128,128]{3,2,1,0:T(8,128)(2,1)S(1)}, bf16[4,2,128,128]{3,2,1,0:T(8,128)(2,1)S(1)}, u32[]{:S(2)}, u32[]{:S(2)}) collective-permute-start(bf16[4,2,128,128]{3,2,1,0:T(8,128)(2,1)S(1)} %collective-permute-done.3.rest_1_), channel_id=1, source_target_pairs={{0,1},{1,0},{2,3},{3,2},{4,5},{5,4},{6,7},{7,6},{8,9},{9,8},{10,11... | collective-permute-start | bytes 786440 | tf_op jit(solution)/shard_map/ppermute | solution.py:338
  77.8 1.6 %grid_first.1.rest_2_ = f32[2,5,640,128]{3,2,1,0:T(8,128)S(1)} custom-call(s32[1]{0:T(128)} %bitcast.1.me_ref, s32[1,2]{1,0:T(1,128)} %fo_ref.7, s32[2,16]{1,0:T(2,128)} %bitcast.6, bf16[4,2,128,128]{3,2,1,0:T(8,128)(2,1)S(1)} %all_to_all.10.rest_0_), custom_call_target="tpu_custom_call" | custom-call | tf_op jit(solution)/shard_map/grid_first/pallas_call | solution.py:432
  79.4 2.2 %grid_next.1.rest_1_ = f32[2,5,640,128]{3,2,1,0:T(8,128)S(1)} custom-call(s32[1]{0:T(128)} %bitcast.1.me_ref, s32[1,2]{1,0:T(1,128)} %fo_ref.7, s32[2,16]{1,0:T(2,128)} %bitcast.7, bf16[4,2,128,128]{3,2,1,0:T(8,128)(2,1)S(1)} %collective-permute-done.5.rest_0_, bf16[4,2,128,128]{3,2,1,0:T(8,128)(2,1)S(1)} %collective-permute-done.3.rest_1_, ...), custom_call_target="tpu_custom_call" | custom-call | tf_op jit(solution)/shard_map/grid_next/pallas_call | solution.py:440
  81.6 4.5 %backward.1 = (bf16[1,2,512,512]{3,2,1,0:T(8,128)(2,1)}, f32[2,5,640,128]{3,2,1,0:T(8,128)S(1)}) custom-call(s32[1]{0:T(128)} %bitcast.1.me_ref, s32[1,2]{1,0:T(1,128)} %fo_ref.7, s32[2,16]{1,0:T(2,128)} %bitcast.8, bf16[2,512,512]{2,1,0:T(8,128)(2,1)S(1)} %copy-done, ...), custom_call_target="tpu_custom_call", output_to_operand_aliasing={{1}: (5, {})} | custom-call | tf_op jit(solution)/shard_map/backward/pallas_call | solution.py:448
  (27 shorter events, 1.5 us)
Async XLA Ops:
  0.6 24.3 %copy-start.13 = (s32[16,2]{0,1:T(2,128)S(1)}, s32[16,2]{0,1:T(2,128)}, u32[]{:S(2)}) copy-start(s32[16,2]{0,1:T(2,128)} %param.18) | copy-start | bytes 388
  0.6 35.4 %copy-start.7 = (bf16[16,2,128,128]{3,2,1,0:T(8,128)(2,1)S(1)}, bf16[16,2,128,128]{3,2,1,0:T(8,128)(2,1)}, u32[]{:S(2)}) copy-start(bf16[16,2,128,128]{3,2,1,0:T(8,128)(2,1)} %obs_ref.1) | copy-start | bytes 3145732
  0.7 35.3 %copy-start.12 = (bf16[128,256]{1,0:T(8,128)(2,1)S(1)}, bf16[128,256]{1,0:T(8,128)(2,1)}, u32[]{:S(2)}) copy-start(bf16[128,256]{1,0:T(8,128)(2,1)} %constant.21.clone.kern_ref) | copy-start | bytes 196612
  7.9 1.6 %collective-permute-start.1 = (bf16[4,2,128,128]{3,2,1,0:T(8,128)(2,1)S(1)}, bf16[4,2,128,128]{3,2,1,0:T(8,128)(2,1)S(1)}, u32[]{:S(2)}, u32[]{:S(2)}) collective-permute-start(bf16[4,2,128,128]{3,2,1,0:T(8,128)(2,1)S(1)} %get-tuple-element.16), channel_id=1, source_target_pairs={{0,1},{1,0},{2,3},{3,2},{4,5},{5,4},{6,7},{7,6},{8,9},{9,8},{10,11... | collective-permute-start | bytes 786440 | tf_op jit(solution)/shard_map/ppermute | solution.py:338
  8.0 4.0 %collective-permute-start = (bf16[4,2,128,128]{3,2,1,0:T(8,128)(2,1)S(1)}, bf16[4,2,128,128]{3,2,1,0:T(8,128)(2,1)S(1)}, u32[]{:S(2)}, u32[]{:S(2)}) collective-permute-start(bf16[4,2,128,128]{3,2,1,0:T(8,128)(2,1)S(1)} %get-tuple-element.14), channel_id=1, source_target_pairs={{0,1},{1,0},{2,3},{3,2},{4,5},{5,4},{6,7},{7,6},{8,9},{9,8},{10,11... | collective-permute-start | bytes 786440 | tf_op jit(solution)/shard_map/ppermute | solution.py:338
  9.5 8.8 %collective-permute-start.2 = (bf16[4,2,128,128]{3,2,1,0:T(8,128)(2,1)S(1)}, bf16[4,2,128,128]{3,2,1,0:T(8,128)(2,1)S(1)}, u32[]{:S(2)}, u32[]{:S(2)}) collective-permute-start(bf16[4,2,128,128]{3,2,1,0:T(8,128)(2,1)S(1)} %add_convert_fusion.1), channel_id=1, source_target_pairs={{0,2},{1,3},{2,0},{3,1},{4,6},{5,7},{6,4},{7,5},{8,10},{9,11},{10,... | collective-permute-start | bytes 786440 | tf_op jit(solution)/shard_map/ppermute | solution.py:338
  19.2 16.8 %all-to-all-start = ((bf16[4,2,128,128]{3,2,1,0:T(8,128)(2,1)}), bf16[4,2,128,128]{3,2,1,0:T(8,128)(2,1)S(1)}, u32[]{:S(2)}, u32[]{:S(2)}) async-start(bf16[4,2,128,128]{3,2,1,0:T(8,128)(2,1)} %add_convert_fusion), calls=%async_computation | async-start | bytes 524288 | tf_op jit(solution)/shard_map/all_to_all | solution.py:392
  25.0 1.0 %copy-start.8 = (f32[768,128]{1,0:T(8,128)S(1)}, f32[768,128]{1,0:T(8,128)}, u32[]{:S(2)}) copy-start(f32[768,128]{1,0:T(8,128)} %constant.17.clone.kt_ref) | copy-start | bytes 1179652
  26.0 0.9 %copy-start.11 = (f32[128,512]{1,0:T(8,128)S(1)}, f32[128,512]{1,0:T(8,128)}, u32[]{:S(2)}) copy-start(f32[128,512]{1,0:T(8,128)} %constant.18.clone.kwide_ref) | copy-start | bytes 786436
  32.0 1.3 %copy-start.1 = (bf16[512,2048]{1,0:T(8,128)(2,1)}, bf16[512,2048]{1,0:T(8,128)(2,1)S(1)}, u32[]{:S(2)}) copy-start(bf16[512,2048]{1,0:T(8,128)(2,1)S(1)} %get-tuple-element.18.rest_1_) | copy-start | bytes 6291460
  33.3 1.3 %copy-start.3 = (bf16[2048,512]{1,0:T(8,128)(2,1)}, bf16[2048,512]{1,0:T(8,128)(2,1)S(1)}, u32[]{:S(2)}) copy-start(bf16[2048,512]{1,0:T(8,128)(2,1)S(1)} %get-tuple-element.19.rest_2_) | copy-start | bytes 6291460
  34.6 1.3 %copy-start.5 = (bf16[16,512,128]{2,1,0:T(8,128)(2,1)}, bf16[16,512,128]{2,1,0:T(8,128)(2,1)S(1)}, u32[]{:S(2)}) copy-start(bf16[16,512,128]{2,1,0:T(8,128)(2,1)S(1)} %get-tuple-element.20.rest_3_) | copy-start | bytes 6291460
  36.0 1.6 %copy-start.2 = (bf16[512,2048]{1,0:T(8,128)(2,1)S(1)}, bf16[512,2048]{1,0:T(8,128)(2,1)}, u32[]{:S(2)}) copy-start(bf16[512,2048]{1,0:T(8,128)(2,1)} %copy-done.1) | copy-start | bytes 6291460
  37.6 1.6 %copy-start.4 = (bf16[2048,512]{1,0:T(8,128)(2,1)S(1)}, bf16[2048,512]{1,0:T(8,128)(2,1)}, u32[]{:S(2)}) copy-start(bf16[2048,512]{1,0:T(8,128)(2,1)} %copy-done.3) | copy-start | bytes 6291460
  39.2 1.6 %copy-start.6 = (bf16[16,512,128]{2,1,0:T(8,128)(2,1)S(1)}, bf16[16,512,128]{2,1,0:T(8,128)(2,1)}, u32[]{:S(2)}) copy-start(bf16[16,512,128]{2,1,0:T(8,128)(2,1)} %copy-done.5) | copy-start | bytes 6291460
  40.8 0.9 %copy-start.9 = (bf16[2,128,512]{2,1,0:T(8,128)(2,1)S(1)}, bf16[2,128,512]{2,1,0:T(8,128)(2,1)}, u32[]{:S(2)}) copy-start(bf16[2,128,512]{2,1,0:T(8,128)(2,1)} %constant.20.clone.padt_ref) | copy-start | bytes 786436
  41.7 0.9 %copy-start.10 = (bf16[2,512,128]{2,1,0:T(8,128)(2,1)S(1)}, bf16[2,512,128]{2,1,0:T(8,128)(2,1)}, u32[]{:S(2)}) copy-start(bf16[2,512,128]{2,1,0:T(8,128)(2,1)} %constant.19.clone.pad_ref) | copy-start | bytes 786436
  67.6 5.3 %collective-permute-start.3 = (bf16[4,2,128,128]{3,2,1,0:T(8,128)(2,1)S(1)}, bf16[4,2,128,128]{3,2,1,0:T(8,128)(2,1)S(1)}, u32[]{:S(2)}, u32[]{:S(2)}) collective-permute-start(bf16[4,2,128,128]{3,2,1,0:T(8,128)(2,1)S(1)} %all_to_all.10.rest_0_), channel_id=1, source_target_pairs={{0,2},{1,3},{2,0},{3,1},{4,6},{5,7},{6,4},{7,5},{8,10},{9,11},{10,... | collective-permute-start | bytes 786440 | tf_op jit(solution)/shard_map/ppermute | solution.py:338
  68.9 10.5 %collective-permute-start.5 = (bf16[4,2,128,128]{3,2,1,0:T(8,128)(2,1)S(1)}, bf16[4,2,128,128]{3,2,1,0:T(8,128)(2,1)S(1)}, u32[]{:S(2)}, u32[]{:S(2)}) collective-permute-start(bf16[4,2,128,128]{3,2,1,0:T(8,128)(2,1)S(1)} %all_to_all.10.rest_0_), channel_id=1, source_target_pairs={{0,1},{1,0},{2,3},{3,2},{4,5},{5,4},{6,7},{7,6},{8,9},{9,8},{10,11... | collective-permute-start | bytes 786440 | tf_op jit(solution)/shard_map/ppermute | solution.py:338
  72.9 8.6 %collective-permute-start.4 = (bf16[4,2,128,128]{3,2,1,0:T(8,128)(2,1)S(1)}, bf16[4,2,128,128]{3,2,1,0:T(8,128)(2,1)S(1)}, u32[]{:S(2)}, u32[]{:S(2)}) collective-permute-start(bf16[4,2,128,128]{3,2,1,0:T(8,128)(2,1)S(1)} %collective-permute-done.3.rest_1_), channel_id=1, source_target_pairs={{0,1},{1,0},{2,3},{3,2},{4,5},{5,4},{6,7},{7,6},{8,9},{9,8},{10,11... | collective-permute-start | bytes 786440 | tf_op jit(solution)/shard_map/ppermute | solution.py:338
  79.4 2.2 %copy-start = (bf16[2,512,512]{2,1,0:T(8,128)(2,1)S(1)}, bf16[2,512,512]{2,1,0:T(8,128)(2,1)}, u32[]{:S(2)}) copy-start(bf16[2,512,512]{2,1,0:T(8,128)(2,1)} %constant.16.clone.basis_ref) | copy-start | bytes 3145732

commit v4 on v3

--- a/solution.py
+++ b/solution.py
@@ -102,19 +102,14 @@
     return cos_v * taper2, sin_v * taper2
 
 
-def owner_of(j, me):
-    return (j & ~3) | ((j ^ me) & 3)
-
-
-def forward_kernel(sends, me_ref, fo_ref, so_ref, facet_ref, basis_ref, *rest):
-    outs, (facet_buf, basis_buf, spec_ref, sems) = rest[: len(sends)], rest[len(sends) :]
+def forward_kernel(js, me_ref, fo_ref, so_ref, facet_ref, basis_ref, out_ref, spec_ref, *rest):
+    facet_buf, basis_buf, sems = rest
     copies = []
     for k in range(2):
         copies.append(pltpu.make_async_copy(basis_ref.at[k], basis_buf.at[k], sems.at[2 * k]))
         copies.append(pltpu.make_async_copy(facet_ref.at[0, k], facet_buf.at[k], sems.at[2 * k + 1]))
     for copy in copies:
         copy.start()
-    pc, ps = phase_taper(fo_ref)
     for copy in copies:
         copy.wait()
     br, bi = basis_buf[0], basis_buf[1]
@@ -129,10 +124,19 @@
             if c == 0:
                 spec_ref[plane, columns, :F] = part
                 spec_ref[plane, columns, F:] = part[:M]
+    extract([js], [out_ref], me_ref, fo_ref, so_ref, spec_ref)
+
+
+def extract_kernel(sends, me_ref, fo_ref, so_ref, spec_ref, *outs):
+    extract(sends, outs, me_ref, fo_ref, so_ref, spec_ref)
+
+
+def extract(sends, outs, me_ref, fo_ref, so_ref, spec_ref):
+    pc, ps = phase_taper(fo_ref)
     me = me_ref[0]
 
     def block(out_ref, item, j):
-        owner = owner_of(j, me)
+        owner = j ^ me
         sx, sy = so_ref[0, owner], so_ref[1, owner]
         lane = sy // M
         shift = (2 * M - (sy & (M - 1))) & (2 * M - 1)
@@ -164,9 +168,18 @@
             block(ref, item, j)
 
 
-def prepare_kernel(w_ref, to_ref, kt_ref, kwide_ref, screen_ref, kvt_ref, kv_ref, kut_ref):
+def prepare_kernel(w_ref, to_ref, _, *rest):
+    loads = (len(rest) - 6) // 2
+    sources, (screen_ref, kvt_ref, kv_ref, kut_ref) = rest[:loads], rest[loads : loads + 4]
+    targets, zero_ref, sems = rest[loads + 4 : -2], rest[-2], rest[-1]
+    zero_ref[...] = jnp.zeros_like(zero_ref)
+    kt_ref, kwide_ref = targets[-2:]
+    copies = []
+    for k in range(loads - 1, -1, -1):
+        copies.append(pltpu.make_async_copy(sources[k], targets[k], sems.at[k]))
+        copies[-1].start()
     slots = kut_ref.shape[0]
-    w = w_ref[0]
+    w = w_ref[0, 0]
     row = lax.broadcasted_iota(jnp.int32, (SG, 1), 0).astype(F32) - SG / 2.0
     column = lax.broadcasted_iota(jnp.int32, (1, SG), 1).astype(F32) - SG / 2.0
     row2 = row * row * (1.0 / (SG * SG)) + 1.0
@@ -174,6 +187,8 @@
     cos_v, sin_v = cos_sin_turns((jnp.sqrt(row2 + column2) - 1.0) * w)
     screen_ref[0] = cos_v
     screen_ref[1] = sin_v
+    for copy in copies:
+        copy.wait()
     for t in range(slots):
         ou, ov = to_ref[0, t], to_ref[1, t]
         kut_ref[t] = kt_ref[pl.ds(2 * TV - ou, SG), :].astype(BF)
@@ -181,16 +196,18 @@
         kv_ref[t * TV : (t + 1) * TV] = pltpu.roll(kwide_ref[...], ov, 1).astype(BF)
 
 
-def subgrid_kernel(tc_ref, to_ref, got_ref, obs_ref, pad_ref, padt_ref, kern_ref, *rest):
-    (screen_ref, kvt_ref, kv_ref, kut_ref) = rest[:4]
-    (out_ref, coef_ref, model_ref, rows_ref, z_ref, res_ref, sems) = rest[4:]
+def subgrid_kernel(picks, tc_ref, to_ref, *rest):
+    parts = len(picks)
+    sums = rest[:parts]
+    (obs_ref, pad_ref, padt_ref, kern_ref, screen_ref, kvt_ref, kv_ref, kut_ref) = rest[parts : parts + 8]
+    (out_ref, coef_ref, model_ref, rows_ref, z_ref, res_ref, sems) = rest[parts + 8 :]
     slots = obs_ref.shape[0]
-    count = tc_ref[0]
+    count = tc_ref[0, 0]
 
     def total(plane):
-        value = got_ref[0, plane].astype(F32)
-        for item in range(1, got_ref.shape[0]):
-            value = value + got_ref[item, plane].astype(F32)
+        value = sums[0][picks[0], plane].astype(F32)
+        for ref, item in zip(sums[1:], picks[1:]):
+            value = value + ref[item, plane].astype(F32)
         return value.astype(BF)
 
     pr, pi = pad_ref[0], pad_ref[1]
@@ -239,9 +256,8 @@
     screened_i = (sc * ai - ss * ar).astype(BF)
     reduced_r, reduced_i = mul_right(tr, -ti, screened_r, screened_i)
     coef_r, coef_i = mul_left(reduced_r.astype(BF), reduced_i.astype(BF), pr, -pi)
-    for item in range(coef_ref.shape[0]):
-        coef_ref[item, 0] = coef_r.astype(BF)
-        coef_ref[item, 1] = coef_i.astype(BF)
+    coef_ref[0, 0] = coef_r.astype(BF)
+    coef_ref[0, 1] = coef_i.astype(BF)
     for copy in copies:
         copy.wait()
 
@@ -252,7 +268,7 @@
     blank = jnp.zeros((M, M), F32)
 
     def block(in_ref, item, j):
-        owner = owner_of(j, me)
+        owner = j ^ me
         sx, sy = so_ref[0, owner], so_ref[1, owner]
         lane = sy // M
         shift = sy & (M - 1)
@@ -278,8 +294,10 @@
     grid_blocks(pieces, rest[:-2], me_ref, fo_ref, so_ref, rest[-1])
 
 
-def backward_kernel(pieces, me_ref, fo_ref, so_ref, basis_ref, *rest):
-    grid_ref, out_ref, _, out_buf, sems = rest[-5:]
+def backward_kernel(pieces, me_ref, fo_ref, so_ref, basis_hbm, *rest):
+    grid_ref, out_ref, _, basis_ref, out_buf, sems = rest[len(pieces) :]
+    load = pltpu.make_async_copy(basis_hbm, basis_ref, sems.at[4])
+    load.start()
     grid_blocks(pieces, rest[: len(pieces)], me_ref, fo_ref, so_ref, grid_ref)
     columns = F // M
     folded = []
@@ -292,6 +310,7 @@
             top = strip[:M] + strip[F:]
             strips.append(jnp.concatenate([top.astype(BF), strip[M:F].astype(BF)], axis=0))
         folded.append(jnp.concatenate(strips, axis=1))
+    load.wait()
     br, bi = basis_ref[0], basis_ref[1]
     hr, hi = mul_right(br, -bi, *folded)
     hr, hi = hr.astype(BF), hi.astype(BF)
@@ -338,68 +357,125 @@
     return lax.ppermute(value, "facet", [(i, i ^ mask) for i in range(n)])
 
 
+def digit_levels(n):
+    levels, base = [], 1
+    while base < n:
+        radix = 2 if base < 4 or n // base < 4 else 4
+        levels.append((base, radix))
+        base *= radix
+    return levels
+
+
+def reduce_sends(n):
+    levels = digit_levels(n)
+    sends = []
+    for k, (base, radix) in enumerate(levels):
+        for g in range(1, radix):
+            js = [j for j in range(0, n, base) if (j // base) % radix == g]
+            if k + 1 < len(levels):
+                after, width = levels[k + 1]
+                groups = [[j for j in js if (j // after) % width], [j for j in js if not (j // after) % width]]
+            else:
+                groups = [js]
+            sends += [(group, g * base) for group in groups if group]
+    return sends
+
+
+def pick(value, items):
+    step = items[1] - items[0] if len(items) > 1 else 1
+    if items == list(range(items[0], items[0] + step * len(items), step)):
+        if len(items) == value.shape[0]:
+            return value
+        return lax.slice_in_dim(value, items[0], items[-1] + 1, step)
+    return jnp.concatenate([value[i : i + 1] for i in items])
+
+
+def join(pieces):
+    return [j for js, _ in pieces for j in js], jnp.concatenate([value for _, value in pieces])
+
+
 def per_device(facets, facet_offsets, subgrid_offsets, w_terms, tile_count, tile_offsets, observed):
     n = lax.axis_size("facet")
-    far_n = n // 4
     slots = observed.shape[0]
     me = lax.axis_index("facet").astype(jnp.int32).reshape(1)
     corners = far(subgrid_offsets.T)
-    tile_corners = tile_offsets.T
+    tile_corners = far(tile_offsets.T)
     facet_offsets = far(facet_offsets)
-    basis = jnp.asarray(basis_tables())
+    basis = far(jnp.asarray(basis_tables()))
     pad_np = padding_tables(n)
     kern_np = kernel_table()
     kt_np = np.zeros((6 * TV, TV), np.float32)
     kt_np[2 * TV : 4 * TV] = kern_np.astype(np.float32).T
     kwide_np = np.zeros((TV, SG), np.float32)
     kwide_np[:, : 2 * TV] = kern_np.astype(np.float32)
-    columns = [[high * 4 + low for high in range(far_n)] for low in range(4)]
-    quarter = [[high * 4 + low for high in range(far_n)] for low in range(4)]
-
-    own0, own1, own2, own3 = pl.pallas_call(
-        functools.partial(forward_kernel, quarter),
-        out_shape=[held((far_n, 2, M, M))] * 4,
+    grid_shape = (2, F // M + 1, F + M, M)
+
+    sends = reduce_sends(n)
+    first, spec = pl.pallas_call(
+        functools.partial(forward_kernel, sends[0][0]),
+        out_shape=[held((len(sends[0][0]), 2, M, M)), held(grid_shape, F32)],
         in_specs=[SMEM] * 3 + [ANY] * 2,
-        out_specs=[VMEM] * 4,
+        out_specs=[VMEM] * 2,
         scratch_shapes=[
             pltpu.VMEM((2, F, F), BF),
             pltpu.VMEM((2, F, F), BF),
-            pltpu.VMEM((2, F // M + 1, F + M, M), F32),
             pltpu.SemaphoreType.DMA((4,)),
         ],
         compiler_params=params(16),
         name="forward",
-    )(me, facet_offsets, corners, far(facets), far(basis))
-
-    screen, kvt, kv, kut = pl.pallas_call(
-        prepare_kernel,
-        out_shape=[
-            held((2, SG, SG), F32),
-            held((SG, slots * TV)),
-            held((slots * TV, SG)),
-            held((slots, SG, TV)),
-        ],
-        in_specs=[SMEM] * 2 + [VMEM] * 2,
-        out_specs=[VMEM] * 4,
+    )(me, facet_offsets, corners, far(facets), basis)
+    lists = [js for js, _ in sends[1:]] + [[0]]
+    own = pl.pallas_call(
+        functools.partial(extract_kernel, lists),
+        out_shape=[held((len(js), 2, M, M)) for js in lists],
+        in_specs=[SMEM] * 3 + [VMEM],
+        out_specs=[VMEM] * len(lists),
         compiler_params=params(8),
-        name="prepare",
-    )(w_terms, tile_corners, jnp.asarray(kt_np), jnp.asarray(kwide_np))
-
-    def plus(*terms):
-        return sum(term.astype(F32) for term in terms).astype(BF)
-
-    def spread(value):
-        return lax.all_to_all(value, "facet", 0, 0, axis_index_groups=columns, tiled=True)
-
-    got3 = exchange(own3, 1, n)
-    got1 = exchange(own1, 1, n)
-    got2 = exchange(plus(own2, got3), 2, n)
-    got = spread(plus(own0, got1, got2))
-
-    residual, coefficients = pl.pallas_call(
-        subgrid_kernel,
-        out_shape=[pltpu.HBM(observed.shape, BF), held((far_n, 2, M, M))],
-        in_specs=[SMEM] * 2 + [VMEM] * 9,
+        name="extract",
+    )(me, facet_offsets, corners, near(spec))
+
+    arrived = []
+    for (js, mask), value in zip(sends, [first] + list(own)):
+        terms = []
+        for got_js, got in arrived:
+            if set(js) <= set(got_js):
+                terms.append(pick(got, [got_js.index(j) for j in js]))
+            else:
+                assert not set(js) & set(got_js)
+        if terms:
+            total = value.astype(F32)
+            if mask > 2:
+                total = total + prepared[-1]
+            for term in terms:
+                total = total + term.astype(F32)
+            value = total.astype(BF)
+        if mask == 2 and len(js) > 1:
+            loads = [observed, pad_np, pad_np.transpose(0, 2, 1), kern_np, kt_np, kwide_np]
+            prepared = pl.pallas_call(
+                prepare_kernel,
+                out_shape=[
+                    held((2, SG, SG), F32),
+                    held((SG, slots * TV)),
+                    held((slots * TV, SG)),
+                    held((slots, SG, TV)),
+                ]
+                + [held(load.shape, load.dtype) for load in loads]
+                + [held((1, M), F32)],
+                in_specs=[SMEM] * 2 + [VMEM] + [ANY] * len(loads),
+                out_specs=[VMEM] * (5 + len(loads)),
+                scratch_shapes=[pltpu.SemaphoreType.DMA((len(loads),))],
+                compiler_params=params(8),
+                name="prepare",
+            )(w_terms.reshape(1, 1), tile_corners, near(value), *[far(jnp.asarray(load)) for load in loads])
+        got = exchange(value, mask, n)
+        arrived.append(([j ^ mask for j in js], got))
+    last = [(js, got) for js, got in arrived if 0 in js]
+    screen, kvt, kv, kut, tiles, pad, padt, kern = prepared[:8]
+
+    residual, coefficient = pl.pallas_call(
+        functools.partial(subgrid_kernel, [0] + [js.index(0) for js, _ in last]),
+        out_shape=[pltpu.HBM(observed.shape, BF), held((1, 2, M, M))],
+        in_specs=[SMEM] * 2 + [VMEM] * (len(last) + 9),
         out_specs=[ANY, VMEM],
         scratch_shapes=[
             pltpu.VMEM((2 * SG, SG), BF),
@@ -411,53 +487,56 @@
         compiler_params=params(24),
         name="subgrid",
     )(
-        tile_count,
+        tile_count.reshape(1, 1),
         tile_corners,
-        near(got),
-        near(observed),
-        near(jnp.asarray(pad_np)),
-        near(jnp.asarray(pad_np.transpose(0, 2, 1))),
-        near(jnp.asarray(kern_np)),
-        near(screen),
-        near(kvt),
-        near(kv),
-        near(kut),
+        near(own[-1]),
+        *[near(got) for _, got in last],
+        *[near(value) for value in (tiles, pad, padt, kern, screen, kvt, kv, kut)],
     )
 
-    all0 = spread(coefficients)
-    all2 = exchange(all0, 2, n)
-    all1 = exchange(all0, 1, n)
-    all3 = exchange(all2, 1, n)
-    grid_shape = (2, F // M + 1, F + M, M)
+    mine = ([0], coefficient)
+    beside = ([2], exchange(coefficient, 2, n))
+    along = []
+    for base, radix in reversed(digit_levels(n)[2:]):
+        js, value = join([mine] + along) if along else mine
+        along.append(
+            join([([j ^ (g * base) for j in js], exchange(value, g * base, n)) for g in range(1, radix)])
+        )
+    along = join(along) if len(along) > 1 else along[0]
+    early = join([mine, along, beside])
+    early_other = ([j ^ 1 for j in early[0]], exchange(early[1], 1, n))
+    late_js, late_value = [j ^ 2 for j in along[0]], exchange(along[1], 2, n)
     grid = pl.pallas_call(
-        functools.partial(first_grid_kernel, quarter[:1]),
+        functools.partial(first_grid_kernel, [early[0], early_other[0]]),
         out_shape=held(grid_shape, F32),
-        in_specs=[SMEM] * 3 + [VMEM],
+        in_specs=[SMEM] * 3 + [VMEM] * 2,
         out_specs=VMEM,
         compiler_params=params(8),
         name="grid_first",
-    )(me, facet_offsets, corners, near(all0))
+    )(me, facet_offsets, corners, near(early[1]), near(early_other[1]))
+    late_other = ([j ^ 1 for j in late_js], exchange(late_value, 1, n))
     grid = pl.pallas_call(
-        functools.partial(next_grid_kernel, quarter[1:3]),
+        functools.partial(next_grid_kernel, [late_js]),
         out_shape=held(grid_shape, F32),
-        in_specs=[SMEM] * 3 + [VMEM] * 3,
+        in_specs=[SMEM] * 3 + [VMEM] * 2,
         out_specs=VMEM,
         compiler_params=params(8),
         name="grid_next",
-    )(me, facet_offsets, corners, near(all1), near(all2), near(grid))
+    )(me, facet_offsets, corners, near(late_value), near(grid))
     update = pl.pallas_call(
-        functools.partial(backward_kernel, quarter[3:]),
+        functools.partial(backward_kernel, [late_other[0]]),
         out_shape=[pltpu.HBM(facets.shape, BF), held(grid_shape, F32)],
-        in_specs=[SMEM] * 3 + [VMEM] * 3,
+        in_specs=[SMEM] * 3 + [ANY] + [VMEM] * 2,
         out_specs=[ANY, VMEM],
         input_output_aliases={5: 1},
         scratch_shapes=[
             pltpu.VMEM((2, F, F), BF),
-            pltpu.SemaphoreType.DMA((4,)),
+            pltpu.VMEM((2, F, F), BF),
+            pltpu.SemaphoreType.DMA((5,)),
         ],
         compiler_params=params(16),
         name="backward",
-    )(me, facet_offsets, corners, near(basis), near(all3), near(grid))[0]
+    )(me, facet_offsets, corners, basis, near(late_other[1]), near(grid))[0]
     return (residual, update)
 
 

time: 86.8 us -> 66 us (0.76)
  local copies, waits for them, and re-layouts: 12.6 us -> 0.06 us
  blocking collectives: 10.4 us -> 0 us
  starting transfers between devices: 17.7 us -> 21.8 us
  waiting for transfers between devices: 7.41 us -> 6.49 us
    unnamed x28 -> x4, local copies, waits for them, and re-layouts: 12.6 us -> 0.05 us
    all_to_all x1 -> x0, blocking collectives: 10.4 us -> none  [spread(): lax.all_to_all(value, 'facet', 0, 0, axis_index_groups=columns, tiled=True)]
    ppermute x6 -> x14, starting transfers between devices: 13.2 us -> 21.8 us  [exchange(): return lax.ppermute(value, 'facet', [(i, i ^ mask) for i in range(n)])]
    all_to_all x1 -> x0, starting transfers between devices: 4.49 us -> none  [spread(): lax.all_to_all(value, 'facet', 0, 0, axis_index_groups=columns, tiled=True)]
    ppermute x6 -> x14, waiting for transfers between devices: 7.41 us -> 6.49 us  [exchange(): return lax.ppermute(value, 'facet', [(i, i ^ mask) for i in range(n)])]
    pallas_call x5 -> x6, Pallas kernels: 29.9 us -> 30.1 us  [the longest x1 14.6 us: per_device(): pl.pallas_call(functools.partial(subgrid_kernel, [0] + [js.index(0) for j...]
  transfers between devices with their start and end apart: 7 -> 14, of which waited for: 2 -> 4; matrix products, arithmetic and copies ran while one was open for 0% -> 0% of each run, Pallas kernels for 10% -> 15%
where the time goes in v4:
time: 66 us; the launch traced here: 65.6 us
  Pallas kernels  34.9 us (53%)
  starting transfers between devices  21.8 us (33%)
  waiting for transfers between devices  6.49 us (10%)
  between operations  2.24 us (3%)
    ppermute x14, starting transfers between devices, exchange(): return lax.ppermute(value, 'facet', [(i, i ^ mask) for i in range(n)])  21.8 us
    pallas_call x1, Pallas kernels, per_device(): pl.pallas_call(functools.partial(subgrid_kernel, [0] + [js.index(0) for j...  14.6 us
    ppermute x14, waiting for transfers between devices, exchange(): return lax.ppermute(value, 'facet', [(i, i ^ mask) for i in range(n)])  6.49 us
    pallas_call x1, Pallas kernels, per_device(): pl.pallas_call(functools.partial(forward_kernel, sends[0][0]), out_shape=...  5.23 us
    pallas_call x1, Pallas kernels, per_device(): pl.pallas_call(functools.partial(backward_kernel, [late_other[0]]), out_s...  5 us
    pallas_call x1, Pallas kernels, per_device(): pl.pallas_call(prepare_kernel, out_shape=[held((2, SG, SG), F32), held((S...  4.71 us
    pallas_call x1, Pallas kernels, per_device(): pl.pallas_call(functools.partial(extract_kernel, lists), out_shape=[held(...  2.32 us
    pallas_call x1, Pallas kernels, per_device(): pl.pallas_call(functools.partial(first_grid_kernel, [early[0], early_othe...  1.6 us
  transfers between devices with their start and end apart: 14, of which 4 were waited for; matrix products, arithmetic and copies ran while one was open for 0% of the time, Pallas kernels for 15%

profile of v4, /device:TPU:1, one launch (start us, length us, event | category | flops | bytes accessed | tf_op | source)
XLA Modules:
  0.0 65.6 jit_solution(3864739395119406486)
XLA Ops:
  0.6 5.2 %forward.1 = (bf16[4,2,128,128]{3,2,1,0:T(8,128)(2,1)S(1)}, f32[2,5,640,128]{3,2,1,0:T(8,128)S(1)}) custom-call(s32[1]{0:T(128)} %bitcast.2.me_ref, s32[1,2]{1,0:T(1,128)} %fo_ref.9, s32[2,16]{1,0:T(2,128)} %bitcast.9, bf16[1,2,512,512]{3,2,1,0:T(8,128)(2,1)} %facet_ref.1, bf16[2,512,512]{2,1,0:T(8,128)(2,1)} %constant.16.clone.basis_ref.basis_hbm), custom_call_target="tpu_custom_call" | custom-call | tf_op jit(solution)/shard_map/forward/pallas_call | solution.py:414
  5.9 0.1 collective-permute-start.1
  6.0 2.3 %extract.1 = (bf16[4,2,128,128]{3,2,1,0:T(8,128)(2,1)S(1)}, bf16[3,2,128,128]{3,2,1,0:T(8,128)(2,1)S(1)}, bf16[1,2,128,128]{3,2,1,0:T(8,128)(2,1)S(1)}, bf16[1,2...) custom-call(s32[1]{0:T(128)} %bitcast.2.me_ref, ...), custom_call_target="tpu_custom_call" | custom-call | tf_op jit(solution)/shard_map/extract/pallas_call | solution.py:428
  8.3 0.5 collective-permute-start
  9.6 2.3 %collective-permute-start.3 = (bf16[3,2,128,128]{3,2,1,0:T(8,128)(2,1)S(1)}, bf16[3,2,128,128]{3,2,1,0:T(8,128)(2,1)S(1)}, u32[]{:S(2)}, u32[]{:S(2)}) collective-permute-start(bf16[3,2,128,128]{3,2,1,0:T(8,128)(2,1)S(1)} %add_convert_fusion._), channel_id=1, source_target_pairs={{0,2},{1,3},{2,0},{3,1},{4,6},{5,7},{6,4},{7,5},{8,10},{9,11},{10,... | collective-permute-start | bytes 589832 | tf_op jit(solution)/shard_map/ppermute | solution.py:357
  12.0 4.7 %prepare.1 = (f32[2,512,512]{2,1,0:T(8,128)S(1)}, bf16[512,2048]{1,0:T(8,128)(2,1)S(1)}, bf16[2048,512]{1,0:T(8,128)(2,1)S(1)}, bf16[16,512,128]{2,1,0:T(8,128)(...) custom-call(f32[1,1]{1,0:T(1,128)} %bitcast.6.w_ref, ...), custom_call_target="tpu_custom_call" | custom-call | tf_op jit(solution)/shard_map/prepare/pallas_call | solution.py:454
  16.7 0.1 add_convert_fusion.1
  16.8 3.6 %collective-permute-start.6 = (bf16[1,2,128,128]{3,2,1,0:T(8,128)(2,1)S(1)}, bf16[1,2,128,128]{3,2,1,0:T(8,128)(2,1)S(1)}, u32[]{:S(2)}, u32[]{:S(2)}) collective-permute-start(bf16[1,2,128,128]{3,2,1,0:T(8,128)(2,1)S(1)} %get-tuple-element.44), channel_id=1, source_target_pairs={{0,12},{1,13},{2,14},{3,15},{4,8},{5,9},{6,10},{7,11},{8,4},{9,5},... | collective-permute-start | bytes 196616 | tf_op jit(solution)/shard_map/ppermute | solution.py:357
  20.4 0.4 collective-permute-start.4
  21.5 0.6 collective-permute-done.6.rest_5_
  22.1 3.8 %collective-permute-done.5.rest_4_ = bf16[1,2,128,128]{3,2,1,0:T(8,128)(2,1)S(1)} collective-permute-done((bf16[1,2,128,128]{3,2,1,0:T(8,128)(2,1)S(1)}, bf16[1,2,128,128]{3,2,1,0:T(8,128)(2,1)S(1)}, u32[]{:S(2)}, u32[]{:S(2)}) %collective-permute-start.5) | collective-permute-done | bytes 65568 | tf_op jit(solution)/shard_map/ppermute | solution.py:357
  25.9 14.6 %subgrid.1 = (bf16[16,2,128,128]{3,2,1,0:T(8,128)(2,1)}, bf16[1,2,128,128]{3,2,1,0:T(8,128)(2,1)S(1)}) custom-call(s32[1,1]{1,0:T(1,128)} %bitcast.7.tc_ref, s32[2,16]{1,0:T(2,128)} %bitcast.15, bf16[1,2,128,128]{3,2,1,0:T(8,128)(2,1)S(1)} %get-tuple-element.24.rest_0_, bf16[4,2,128,128]{3,2,1,0:T(8,128)(2,1)S(1)} %collective-permute-done.rest_1_, ...), custom_call_target="tpu_custom_call" | custom-call | tf_op jit(solution)/shard_map/subgrid/pallas_call | solution.py:475
  40.4 1.3 %collective-permute-start.12 = (bf16[1,2,128,128]{3,2,1,0:T(8,128)(2,1)S(1)}, bf16[1,2,128,128]{3,2,1,0:T(8,128)(2,1)S(1)}, u32[]{:S(2)}, u32[]{:S(2)}) collective-permute-start(bf16[1,2,128,128]{3,2,1,0:T(8,128)(2,1)S(1)} %get-tuple-element.42), channel_id=1, source_target_pairs={{0,2},{1,3},{2,0},{3,1},{4,6},{5,7},{6,4},{7,5},{8,10},{9,11},{10,... | collective-permute-start | bytes 196616 | tf_op jit(solution)/shard_map/ppermute | solution.py:357
  41.7 0.2 collective-permute-start.9
  41.9 0.4 collective-permute-start.8
  42.3 3.0 %collective-permute-start.7 = (bf16[1,2,128,128]{3,2,1,0:T(8,128)(2,1)S(1)}, bf16[1,2,128,128]{3,2,1,0:T(8,128)(2,1)S(1)}, u32[]{:S(2)}, u32[]{:S(2)}) collective-permute-start(bf16[1,2,128,128]{3,2,1,0:T(8,128)(2,1)S(1)} %get-tuple-element.42), channel_id=1, source_target_pairs={{0,4},{1,5},{2,6},{3,7},{4,0},{5,1},{6,2},{7,3},{8,12},{9,13},{10,... | collective-permute-start | bytes 196616 | tf_op jit(solution)/shard_map/ppermute | solution.py:357
  45.3 1.4 %collective-permute-done.9 = bf16[1,2,128,128]{3,2,1,0:T(8,128)(2,1)S(1)} collective-permute-done((bf16[1,2,128,128]{3,2,1,0:T(8,128)(2,1)S(1)}, bf16[1,2,128,128]{3,2,1,0:T(8,128)(2,1)S(1)}, u32[]{:S(2)}, u32[]{:S(2)}) %collective-permute-start.9) | collective-permute-done | bytes 65568 | tf_op jit(solution)/shard_map/ppermute | solution.py:357
  46.7 0.7 collective-permute-done.7
  47.4 0.3 collective-permute-start.10
  47.8 4.6 %collective-permute-start.13 = (bf16[5,2,128,128]{3,2,1,0:T(8,128)(2,1)S(1)}, bf16[5,2,128,128]{3,2,1,0:T(8,128)(2,1)S(1)}, u32[]{:S(2)}, u32[]{:S(2)}) collective-permute-start(bf16[5,2,128,128]{3,2,1,0:T(8,128)(2,1)S(1)} %constant_dynamic-update-slice_fusion.rest_0_), channel_id=1, source_target_pairs={{0,1},{1,0},{2,3},{3,2},{4,5},{5,4},{6,7},{7,6},{8,9},{9,8},{10,11... | collective-permute-start | bytes 983048 | tf_op jit(solution)/shard_map/ppermute | solution.py:357
  52.4 5.0 %collective-permute-start.11 = (bf16[3,2,128,128]{3,2,1,0:T(8,128)(2,1)S(1)}, bf16[3,2,128,128]{3,2,1,0:T(8,128)(2,1)S(1)}, u32[]{:S(2)}, u32[]{:S(2)}) collective-permute-start(bf16[3,2,128,128]{3,2,1,0:T(8,128)(2,1)S(1)} %collective-permute-done.10.rest_0_), channel_id=1, source_target_pairs={{0,1},{1,0},{2,3},{3,2},{4,5},{5,4},{6,7},{7,6},{8,9},{9,8},{10,11... | collective-permute-start | bytes 589832 | tf_op jit(solution)/shard_map/ppermute | solution.py:357
  57.4 1.6 %grid_first.1.rest_1_ = f32[2,5,640,128]{3,2,1,0:T(8,128)S(1)} custom-call(s32[1]{0:T(128)} %bitcast.2.me_ref, s32[1,2]{1,0:T(1,128)} %fo_ref.9, s32[2,16]{1,0:T(2,128)} %bitcast.11, bf16[5,2,128,128]{3,2,1,0:T(8,128)(2,1)S(1)} %constant_dynamic-update-slice_fusion.rest_0_, bf16[5,2,128,128]{3,2,1,0:T(8,128)(2,1)S(1)} %collective-permute-done.13.rest_1_), custom_call_target="tpu_custom_call" | custom-call | tf_op jit(solution)/shard_map/grid_first/pallas_call | solution.py:509
  59.0 1.4 %grid_next.1.rest_1_ = f32[2,5,640,128]{3,2,1,0:T(8,128)S(1)} custom-call(s32[1]{0:T(128)} %bitcast.2.me_ref, s32[1,2]{1,0:T(1,128)} %fo_ref.9, s32[2,16]{1,0:T(2,128)} %bitcast.12, bf16[3,2,128,128]{3,2,1,0:T(8,128)(2,1)S(1)} %collective-permute-done.10.rest_0_, f32[2,5,640,128]{3,2,1,0:T(8,128)S(1)} %grid_first.1.rest_1_), custom_call_target="tpu_custom_call" | custom-call | tf_op jit(solution)/shard_map/grid_next/pallas_call | solution.py:518
  60.5 5.0 %backward.1 = (bf16[1,2,512,512]{3,2,1,0:T(8,128)(2,1)}, f32[2,5,640,128]{3,2,1,0:T(8,128)S(1)}) custom-call(s32[1]{0:T(128)} %bitcast.2.me_ref, s32[1,2]{1,0:T(1,128)} %fo_ref.9, s32[2,16]{1,0:T(2,128)} %bitcast.13, bf16[2,512,512]{2,1,0:T(8,128)(2,1)} %constant.16.clone.basis_ref.basis_hbm, ...), custom_call_target="tpu_custom_call", output_to_operand_aliasing={{1}: (5, {})} | custom-call | tf_op jit(solution)/shard_map/backward/pallas_call | solution.py:526
  (20 shorter events, 0.3 us)
Async XLA Ops:
  5.9 3.6 %collective-permute-start.1 = (bf16[4,2,128,128]{3,2,1,0:T(8,128)(2,1)S(1)}, bf16[4,2,128,128]{3,2,1,0:T(8,128)(2,1)S(1)}, u32[]{:S(2)}, u32[]{:S(2)}) collective-permute-start(bf16[4,2,128,128]{3,2,1,0:T(8,128)(2,1)S(1)} %get-tuple-element.27), channel_id=1, source_target_pairs={{0,1},{1,0},{2,3},{3,2},{4,5},{5,4},{6,7},{7,6},{8,9},{9,8},{10,11... | collective-permute-start | bytes 786440 | tf_op jit(solution)/shard_map/ppermute | solution.py:357
  8.3 8.4 %collective-permute-start = (bf16[4,2,128,128]{3,2,1,0:T(8,128)(2,1)S(1)}, bf16[4,2,128,128]{3,2,1,0:T(8,128)(2,1)S(1)}, u32[]{:S(2)}, u32[]{:S(2)}) collective-permute-start(bf16[4,2,128,128]{3,2,1,0:T(8,128)(2,1)S(1)} %get-tuple-element.25), channel_id=1, source_target_pairs={{0,1},{1,0},{2,3},{3,2},{4,5},{5,4},{6,7},{7,6},{8,9},{9,8},{10,11... | collective-permute-start | bytes 786440 | tf_op jit(solution)/shard_map/ppermute | solution.py:357
  9.6 7.2 %collective-permute-start.3 = (bf16[3,2,128,128]{3,2,1,0:T(8,128)(2,1)S(1)}, bf16[3,2,128,128]{3,2,1,0:T(8,128)(2,1)S(1)}, u32[]{:S(2)}, u32[]{:S(2)}) collective-permute-start(bf16[3,2,128,128]{3,2,1,0:T(8,128)(2,1)S(1)} %add_convert_fusion._), channel_id=1, source_target_pairs={{0,2},{1,3},{2,0},{3,1},{4,6},{5,7},{6,4},{7,5},{8,10},{9,11},{10,... | collective-permute-start | bytes 589832 | tf_op jit(solution)/shard_map/ppermute | solution.py:357
  11.9 9.5 %collective-permute-start.2 = (bf16[1,2,128,128]{3,2,1,0:T(8,128)(2,1)S(1)}, bf16[1,2,128,128]{3,2,1,0:T(8,128)(2,1)S(1)}, u32[]{:S(2)}, u32[]{:S(2)}) collective-permute-start(bf16[1,2,128,128]{3,2,1,0:T(8,128)(2,1)S(1)} %add_convert_fusion.4), channel_id=1, source_target_pairs={{0,2},{1,3},{2,0},{3,1},{4,6},{5,7},{6,4},{7,5},{8,10},{9,11},{10,... | collective-permute-start | bytes 196616 | tf_op jit(solution)/shard_map/ppermute | solution.py:357
  16.8 5.2 %collective-permute-start.6 = (bf16[1,2,128,128]{3,2,1,0:T(8,128)(2,1)S(1)}, bf16[1,2,128,128]{3,2,1,0:T(8,128)(2,1)S(1)}, u32[]{:S(2)}, u32[]{:S(2)}) collective-permute-start(bf16[1,2,128,128]{3,2,1,0:T(8,128)(2,1)S(1)} %get-tuple-element.44), channel_id=1, source_target_pairs={{0,12},{1,13},{2,14},{3,15},{4,8},{5,9},{6,10},{7,11},{8,4},{9,5},... | collective-permute-start | bytes 196616 | tf_op jit(solution)/shard_map/ppermute | solution.py:357
  20.4 5.4 %collective-permute-start.5 = (bf16[1,2,128,128]{3,2,1,0:T(8,128)(2,1)S(1)}, bf16[1,2,128,128]{3,2,1,0:T(8,128)(2,1)S(1)}, u32[]{:S(2)}, u32[]{:S(2)}) collective-permute-start(bf16[1,2,128,128]{3,2,1,0:T(8,128)(2,1)S(1)} %get-tuple-element.45), channel_id=1, source_target_pairs={{0,8},{1,9},{2,10},{3,11},{4,12},{5,13},{6,14},{7,15},{8,0},{9,1},... | collective-permute-start | bytes 196616 | tf_op jit(solution)/shard_map/ppermute | solution.py:357
  20.4 5.4 %collective-permute-start.4 = (bf16[1,2,128,128]{3,2,1,0:T(8,128)(2,1)S(1)}, bf16[1,2,128,128]{3,2,1,0:T(8,128)(2,1)S(1)}, u32[]{:S(2)}, u32[]{:S(2)}) collective-permute-start(bf16[1,2,128,128]{3,2,1,0:T(8,128)(2,1)S(1)} %get-tuple-element.46), channel_id=1, source_target_pairs={{0,4},{1,5},{2,6},{3,7},{4,0},{5,1},{6,2},{7,3},{8,12},{9,13},{10,... | collective-permute-start | bytes 196616 | tf_op jit(solution)/shard_map/ppermute | solution.py:357
  40.4 7.3 %collective-permute-start.12 = (bf16[1,2,128,128]{3,2,1,0:T(8,128)(2,1)S(1)}, bf16[1,2,128,128]{3,2,1,0:T(8,128)(2,1)S(1)}, u32[]{:S(2)}, u32[]{:S(2)}) collective-permute-start(bf16[1,2,128,128]{3,2,1,0:T(8,128)(2,1)S(1)} %get-tuple-element.42), channel_id=1, source_target_pairs={{0,2},{1,3},{2,0},{3,1},{4,6},{5,7},{6,4},{7,5},{8,10},{9,11},{10,... | collective-permute-start | bytes 196616 | tf_op jit(solution)/shard_map/ppermute | solution.py:357
  41.7 5.0 %collective-permute-start.9 = (bf16[1,2,128,128]{3,2,1,0:T(8,128)(2,1)S(1)}, bf16[1,2,128,128]{3,2,1,0:T(8,128)(2,1)S(1)}, u32[]{:S(2)}, u32[]{:S(2)}) collective-permute-start(bf16[1,2,128,128]{3,2,1,0:T(8,128)(2,1)S(1)} %get-tuple-element.42), channel_id=1, source_target_pairs={{0,12},{1,13},{2,14},{3,15},{4,8},{5,9},{6,10},{7,11},{8,4},{9,5},... | collective-permute-start | bytes 196616 | tf_op jit(solution)/shard_map/ppermute | solution.py:357
  41.9 4.8 %collective-permute-start.8 = (bf16[1,2,128,128]{3,2,1,0:T(8,128)(2,1)S(1)}, bf16[1,2,128,128]{3,2,1,0:T(8,128)(2,1)S(1)}, u32[]{:S(2)}, u32[]{:S(2)}) collective-permute-start(bf16[1,2,128,128]{3,2,1,0:T(8,128)(2,1)S(1)} %get-tuple-element.42), channel_id=1, source_target_pairs={{0,8},{1,9},{2,10},{3,11},{4,12},{5,13},{6,14},{7,15},{8,0},{9,1},... | collective-permute-start | bytes 196616 | tf_op jit(solution)/shard_map/ppermute | solution.py:357
  42.3 5.1 %collective-permute-start.7 = (bf16[1,2,128,128]{3,2,1,0:T(8,128)(2,1)S(1)}, bf16[1,2,128,128]{3,2,1,0:T(8,128)(2,1)S(1)}, u32[]{:S(2)}, u32[]{:S(2)}) collective-permute-start(bf16[1,2,128,128]{3,2,1,0:T(8,128)(2,1)S(1)} %get-tuple-element.42), channel_id=1, source_target_pairs={{0,4},{1,5},{2,6},{3,7},{4,0},{5,1},{6,2},{7,3},{8,12},{9,13},{10,... | collective-permute-start | bytes 196616 | tf_op jit(solution)/shard_map/ppermute | solution.py:357
  47.4 5.0 %collective-permute-start.10 = (bf16[3,2,128,128]{3,2,1,0:T(8,128)(2,1)S(1)}, bf16[3,2,128,128]{3,2,1,0:T(8,128)(2,1)S(1)}, u32[]{:S(2)}, u32[]{:S(2)}) collective-permute-start(bf16[3,2,128,128]{3,2,1,0:T(8,128)(2,1)S(1)} %pad_maximum_fusion), channel_id=1, source_target_pairs={{0,2},{1,3},{2,0},{3,1},{4,6},{5,7},{6,4},{7,5},{8,10},{9,11},{10,... | collective-permute-start | bytes 589832 | tf_op jit(solution)/shard_map/ppermute | solution.py:357
  47.8 9.7 %collective-permute-start.13 = (bf16[5,2,128,128]{3,2,1,0:T(8,128)(2,1)S(1)}, bf16[5,2,128,128]{3,2,1,0:T(8,128)(2,1)S(1)}, u32[]{:S(2)}, u32[]{:S(2)}) collective-permute-start(bf16[5,2,128,128]{3,2,1,0:T(8,128)(2,1)S(1)} %constant_dynamic-update-slice_fusion.rest_0_), channel_id=1, source_target_pairs={{0,1},{1,0},{2,3},{3,2},{4,5},{5,4},{6,7},{7,6},{8,9},{9,8},{10,11... | collective-permute-start | bytes 983048 | tf_op jit(solution)/shard_map/ppermute | solution.py:357
  52.4 8.0 %collective-permute-start.11 = (bf16[3,2,128,128]{3,2,1,0:T(8,128)(2,1)S(1)}, bf16[3,2,128,128]{3,2,1,0:T(8,128)(2,1)S(1)}, u32[]{:S(2)}, u32[]{:S(2)}) collective-permute-start(bf16[3,2,128,128]{3,2,1,0:T(8,128)(2,1)S(1)} %collective-permute-done.10.rest_0_), channel_id=1, source_target_pairs={{0,1},{1,0},{2,3},{3,2},{4,5},{5,4},{6,7},{7,6},{8,9},{9,8},{10,11... | collective-permute-start | bytes 589832 | tf_op jit(solution)/shard_map/ppermute | solution.py:357

commit v5 on v4

--- a/solution.py
+++ b/solution.py
@@ -102,7 +102,20 @@
     return cos_v * taper2, sin_v * taper2
 
 
-def forward_kernel(js, me_ref, fo_ref, so_ref, facet_ref, basis_ref, out_ref, spec_ref, *rest):
+def step_mask(n, step, odd):
+    last = 4 << step >= n
+    return 2 << step if not odd else (2 if last else 4 << step)
+
+
+def position_of(label, other, me, n):
+    who = me ^ other
+    top = n.bit_length() - 3
+    even = label << 1
+    odd = ((label << 2) & (n - 1)) | ((label >> top) << 1)
+    return who ^ jnp.where((who & 1) == 1, odd, even)
+
+
+def forward_kernel(n, labels, me_ref, fo_ref, so_ref, facet_ref, basis_ref, out_ref, spec_ref, *rest):
     facet_buf, basis_buf, sems = rest
     copies = []
     for k in range(2):
@@ -124,19 +137,19 @@
             if c == 0:
                 spec_ref[plane, columns, :F] = part
                 spec_ref[plane, columns, F:] = part[:M]
-    extract([js], [out_ref], me_ref, fo_ref, so_ref, spec_ref)
-
-
-def extract_kernel(sends, me_ref, fo_ref, so_ref, spec_ref, *outs):
-    extract(sends, outs, me_ref, fo_ref, so_ref, spec_ref)
-
-
-def extract(sends, outs, me_ref, fo_ref, so_ref, spec_ref):
+    extract(n, [labels], [out_ref], me_ref, fo_ref, so_ref, spec_ref)
+
+
+def extract_kernel(n, sends, me_ref, fo_ref, so_ref, spec_ref, *outs):
+    extract(n, sends, outs, me_ref, fo_ref, so_ref, spec_ref)
+
+
+def extract(n, sends, outs, me_ref, fo_ref, so_ref, spec_ref):
     pc, ps = phase_taper(fo_ref)
     me = me_ref[0]
 
-    def block(out_ref, item, j):
-        owner = j ^ me
+    def block(out_ref, item, label, other):
+        owner = position_of(label, other, me, n)
         sx, sy = so_ref[0, owner], so_ref[1, owner]
         lane = sy // M
         shift = (2 * M - (sy & (M - 1))) & (2 * M - 1)
@@ -150,35 +163,51 @@
         out_ref[item, 0] = (pc * wr - ps * wi).astype(BF)
         out_ref[item, 1] = (pc * wi + ps * wr).astype(BF)
 
-    for out_ref, js in zip(outs, sends):
-        for_blocks(block, out_ref, js)
-
-
-def for_blocks(block, ref, js):
+    for out_ref, labels in zip(outs, sends):
+        for_blocks(block, out_ref, labels)
+
+
+def for_blocks(block, ref, labels):
+    js, other = labels
     step = js[1] - js[0] if len(js) > 1 else 1
     if len(js) > 1 and js == list(range(js[0], js[0] + step * len(js), step)):
 
         def body(item, carry):
-            block(ref, item, item * step + js[0])
+            block(ref, item, item * step + js[0], other)
             return carry
 
         lax.fori_loop(0, len(js), body, 0)
     else:
         for item, j in enumerate(js):
-            block(ref, item, j)
-
-
-def prepare_kernel(w_ref, to_ref, _, *rest):
-    loads = (len(rest) - 6) // 2
-    sources, (screen_ref, kvt_ref, kv_ref, kut_ref) = rest[:loads], rest[loads : loads + 4]
-    targets, zero_ref, sems = rest[loads + 4 : -2], rest[-2], rest[-1]
+            block(ref, item, j, other)
+
+
+def band_kernel(to_ref, _, kt_hbm, kwide_hbm, kvt_ref, kv_ref, kut_ref, zero_ref, kt_ref, kwide_ref, sems):
+    slots = kut_ref.shape[0]
+    copies = [
+        pltpu.make_async_copy(kt_hbm, kt_ref, sems.at[0]),
+        pltpu.make_async_copy(kwide_hbm, kwide_ref, sems.at[1]),
+    ]
+    for copy in copies:
+        copy.start()
     zero_ref[...] = jnp.zeros_like(zero_ref)
-    kt_ref, kwide_ref = targets[-2:]
-    copies = []
-    for k in range(loads - 1, -1, -1):
-        copies.append(pltpu.make_async_copy(sources[k], targets[k], sems.at[k]))
-        copies[-1].start()
-    slots = kut_ref.shape[0]
+    for copy in copies:
+        copy.wait()
+    for t in range(slots):
+        ou, ov = to_ref[0, t], to_ref[1, t]
+        kut_ref[t] = kt_ref[pl.ds(2 * TV - ou, SG), :].astype(BF)
+        kvt_ref[:, t * TV : (t + 1) * TV] = kt_ref[pl.ds(2 * TV - ov, SG), :].astype(BF)
+        kv_ref[t * TV : (t + 1) * TV] = pltpu.roll(kwide_ref[...], ov, 1).astype(BF)
+
+
+def screen_kernel(w_ref, _, *rest):
+    loads = (len(rest) - 3) // 2
+    sources, screen_ref = rest[:loads], rest[loads]
+    targets, zero_ref, sems = rest[loads + 1 : -2], rest[-2], rest[-1]
+    copies = [pltpu.make_async_copy(sources[k], targets[k], sems.at[k]) for k in range(loads)]
+    for copy in copies:
+        copy.start()
+    zero_ref[...] = jnp.zeros_like(zero_ref)
     w = w_ref[0, 0]
     row = lax.broadcasted_iota(jnp.int32, (SG, 1), 0).astype(F32) - SG / 2.0
     column = lax.broadcasted_iota(jnp.int32, (1, SG), 1).astype(F32) - SG / 2.0
@@ -189,11 +218,6 @@
     screen_ref[1] = sin_v
     for copy in copies:
         copy.wait()
-    for t in range(slots):
-        ou, ov = to_ref[0, t], to_ref[1, t]
-        kut_ref[t] = kt_ref[pl.ds(2 * TV - ou, SG), :].astype(BF)
-        kvt_ref[:, t * TV : (t + 1) * TV] = kt_ref[pl.ds(2 * TV - ov, SG), :].astype(BF)
-        kv_ref[t * TV : (t + 1) * TV] = pltpu.roll(kwide_ref[...], ov, 1).astype(BF)
 
 
 def subgrid_kernel(picks, tc_ref, to_ref, *rest):
@@ -262,13 +286,13 @@
         copy.wait()
 
 
-def grid_blocks(pieces, refs, me_ref, fo_ref, so_ref, grid_ref):
+def grid_blocks(n, pieces, refs, me_ref, fo_ref, so_ref, grid_ref):
     pc, ps = phase_taper(fo_ref)
     me = me_ref[0]
     blank = jnp.zeros((M, M), F32)
 
-    def block(in_ref, item, j):
-        owner = j ^ me
+    def block(in_ref, item, label, other):
+        owner = position_of(label, other, me, n)
         sx, sy = so_ref[0, owner], so_ref[1, owner]
         lane = sy // M
         shift = sy & (M - 1)
@@ -279,26 +303,27 @@
             grid_ref[plane, lane, pl.ds(sx, M), :] += wide[:, :M]
             grid_ref[plane, lane + 1, pl.ds(sx, M), :] += wide[:, M:]
 
-    for in_ref, js in zip(refs, pieces):
-        for_blocks(block, in_ref, js)
-
-
-def first_grid_kernel(pieces, me_ref, fo_ref, so_ref, *rest):
-    grid_ref = rest[-1]
+    for in_ref, labels in zip(refs, pieces):
+        for_blocks(block, in_ref, labels)
+
+
+def first_grid_kernel(n, pieces, me_ref, fo_ref, so_ref, *rest):
+    grid_ref, zero_ref = rest[-2:]
+    zero_ref[...] = jnp.zeros_like(zero_ref)
     grid_ref[...] = jnp.zeros_like(grid_ref)
-    grid_blocks(pieces, rest[:-1], me_ref, fo_ref, so_ref, grid_ref)
-
-
-def next_grid_kernel(pieces, me_ref, fo_ref, so_ref, *rest):
+    grid_blocks(n, pieces, rest[:-2], me_ref, fo_ref, so_ref, grid_ref)
+
+
+def next_grid_kernel(n, pieces, me_ref, fo_ref, so_ref, *rest):
     rest[-1][...] = rest[-2][...]
-    grid_blocks(pieces, rest[:-2], me_ref, fo_ref, so_ref, rest[-1])
-
-
-def backward_kernel(pieces, me_ref, fo_ref, so_ref, basis_hbm, *rest):
+    grid_blocks(n, pieces, rest[:-2], me_ref, fo_ref, so_ref, rest[-1])
+
+
+def backward_kernel(n, pieces, me_ref, fo_ref, so_ref, basis_hbm, *rest):
     grid_ref, out_ref, _, basis_ref, out_buf, sems = rest[len(pieces) :]
     load = pltpu.make_async_copy(basis_hbm, basis_ref, sems.at[4])
     load.start()
-    grid_blocks(pieces, rest[: len(pieces)], me_ref, fo_ref, so_ref, grid_ref)
+    grid_blocks(n, pieces, rest[: len(pieces)], me_ref, fo_ref, so_ref, grid_ref)
     columns = F // M
     folded = []
     for plane in range(2):
@@ -353,32 +378,9 @@
     return pltpu.VMEM(shape, dtype)
 
 
-def exchange(value, mask, n):
-    return lax.ppermute(value, "facet", [(i, i ^ mask) for i in range(n)])
-
-
-def digit_levels(n):
-    levels, base = [], 1
-    while base < n:
-        radix = 2 if base < 4 or n // base < 4 else 4
-        levels.append((base, radix))
-        base *= radix
-    return levels
-
-
-def reduce_sends(n):
-    levels = digit_levels(n)
-    sends = []
-    for k, (base, radix) in enumerate(levels):
-        for g in range(1, radix):
-            js = [j for j in range(0, n, base) if (j // base) % radix == g]
-            if k + 1 < len(levels):
-                after, width = levels[k + 1]
-                groups = [[j for j in js if (j // after) % width], [j for j in js if not (j // after) % width]]
-            else:
-                groups = [js]
-            sends += [(group, g * base) for group in groups if group]
-    return sends
+def exchange(value, step, n):
+    masks = [1, 1] if step < 0 else [step_mask(n, step, odd) for odd in (0, 1)]
+    return lax.ppermute(value, "facet", [(i, i ^ masks[i & 1]) for i in range(n)])
 
 
 def pick(value, items):
@@ -410,10 +412,13 @@
     kwide_np[:, : 2 * TV] = kern_np.astype(np.float32)
     grid_shape = (2, F // M + 1, F + M, M)
 
-    sends = reduce_sends(n)
+    steps = n.bit_length() - 2
+    labels = list(range(n // 2))
+    sends = [(-1, labels[1::2], 1), (-1, labels[::2], 1)]
+    sends += [(k, labels[1 << k :: 2 << k], 0) for k in range(steps)]
     first, spec = pl.pallas_call(
-        functools.partial(forward_kernel, sends[0][0]),
-        out_shape=[held((len(sends[0][0]), 2, M, M)), held(grid_shape, F32)],
+        functools.partial(forward_kernel, n, sends[0][1:]),
+        out_shape=[held((len(sends[0][1]), 2, M, M)), held(grid_shape, F32)],
         in_specs=[SMEM] * 3 + [ANY] * 2,
         out_specs=[VMEM] * 2,
         scratch_shapes=[
@@ -424,53 +429,70 @@
         compiler_params=params(16),
         name="forward",
     )(me, facet_offsets, corners, far(facets), basis)
-    lists = [js for js, _ in sends[1:]] + [[0]]
+    lists = [send[1:] for send in sends[1:]] + [([0], 0)]
     own = pl.pallas_call(
-        functools.partial(extract_kernel, lists),
-        out_shape=[held((len(js), 2, M, M)) for js in lists],
+        functools.partial(extract_kernel, n, lists),
+        out_shape=[held((len(js), 2, M, M)) for js, _ in lists],
         in_specs=[SMEM] * 3 + [VMEM],
         out_specs=[VMEM] * len(lists),
         compiler_params=params(8),
         name="extract",
     )(me, facet_offsets, corners, near(spec))
 
+    def make_bands(after):
+        return pl.pallas_call(
+            band_kernel,
+            out_shape=[
+                held((SG, slots * TV)),
+                held((slots * TV, SG)),
+                held((slots, SG, TV)),
+                held((1, M), F32),
+            ],
+            in_specs=[SMEM, VMEM] + [ANY] * 2,
+            out_specs=[VMEM] * 4,
+            scratch_shapes=[
+                pltpu.VMEM(kt_np.shape, F32),
+                pltpu.VMEM(kwide_np.shape, F32),
+                pltpu.SemaphoreType.DMA((2,)),
+            ],
+            compiler_params=params(8),
+            name="bands",
+        )(tile_corners, near(after), far(jnp.asarray(kt_np)), far(jnp.asarray(kwide_np)))
+
+    def make_screen(after):
+        loads = [observed, pad_np, pad_np.transpose(0, 2, 1), kern_np]
+        return pl.pallas_call(
+            screen_kernel,
+            out_shape=[held((2, SG, SG), F32)]
+            + [held(load.shape, load.dtype) for load in loads]
+            + [held((1, M), F32)],
+            in_specs=[SMEM, VMEM] + [ANY] * len(loads),
+            out_specs=[VMEM] * (2 + len(loads)),
+            scratch_shapes=[pltpu.SemaphoreType.DMA((len(loads),))],
+            compiler_params=params(8),
+            name="screen",
+        )(w_terms.reshape(1, 1), near(after), *[far(jnp.asarray(load)) for load in loads])
+
     arrived = []
-    for (js, mask), value in zip(sends, [first] + list(own)):
-        terms = []
-        for got_js, got in arrived:
-            if set(js) <= set(got_js):
-                terms.append(pick(got, [got_js.index(j) for j in js]))
-            else:
-                assert not set(js) & set(got_js)
-        if terms:
+    token = None
+    for (step, js, _), value in zip(sends, [first] + list(own)):
+        if step >= 0:
             total = value.astype(F32)
-            if mask > 2:
-                total = total + prepared[-1]
-            for term in terms:
-                total = total + term.astype(F32)
+            for got_js, got in arrived:
+                if set(js) <= set(got_js):
+                    total = total + pick(got, [got_js.index(j) for j in js]).astype(F32)
+                else:
+                    assert not set(js) & set(got_js)
+            if token is not None:
+                total = total + token
             value = total.astype(BF)
-        if mask == 2 and len(js) > 1:
-            loads = [observed, pad_np, pad_np.transpose(0, 2, 1), kern_np, kt_np, kwide_np]
-            prepared = pl.pallas_call(
-                prepare_kernel,
-                out_shape=[
-                    held((2, SG, SG), F32),
-                    held((SG, slots * TV)),
-                    held((slots * TV, SG)),
-                    held((slots, SG, TV)),
-                ]
-                + [held(load.shape, load.dtype) for load in loads]
-                + [held((1, M), F32)],
-                in_specs=[SMEM] * 2 + [VMEM] + [ANY] * len(loads),
-                out_specs=[VMEM] * (5 + len(loads)),
-                scratch_shapes=[pltpu.SemaphoreType.DMA((len(loads),))],
-                compiler_params=params(8),
-                name="prepare",
-            )(w_terms.reshape(1, 1), tile_corners, near(value), *[far(jnp.asarray(load)) for load in loads])
-        got = exchange(value, mask, n)
-        arrived.append(([j ^ mask for j in js], got))
+        got = exchange(value, step, n)
+        if step == 0:
+            kvt, kv, kut, token = make_bands(value)
+        if step == 1:
+            screen, tiles, pad, padt, kern, token = make_screen(value)
+        arrived.append((js if step < 0 else [j ^ (1 << step) for j in js], got))
     last = [(js, got) for js, got in arrived if 0 in js]
-    screen, kvt, kv, kut, tiles, pad, padt, kern = prepared[:8]
 
     residual, coefficient = pl.pallas_call(
         functools.partial(subgrid_kernel, [0] + [js.index(0) for js, _ in last]),
@@ -494,37 +516,32 @@
         *[near(value) for value in (tiles, pad, padt, kern, screen, kvt, kv, kut)],
     )
 
-    mine = ([0], coefficient)
-    beside = ([2], exchange(coefficient, 2, n))
-    along = []
-    for base, radix in reversed(digit_levels(n)[2:]):
-        js, value = join([mine] + along) if along else mine
-        along.append(
-            join([([j ^ (g * base) for j in js], exchange(value, g * base, n)) for g in range(1, radix)])
-        )
-    along = join(along) if len(along) > 1 else along[0]
-    early = join([mine, along, beside])
-    early_other = ([j ^ 1 for j in early[0]], exchange(early[1], 1, n))
-    late_js, late_value = [j ^ 2 for j in along[0]], exchange(along[1], 2, n)
-    grid = pl.pallas_call(
-        functools.partial(first_grid_kernel, [early[0], early_other[0]]),
-        out_shape=held(grid_shape, F32),
-        in_specs=[SMEM] * 3 + [VMEM] * 2,
-        out_specs=VMEM,
+    js, value = [0], coefficient
+    for step in range(steps - 1, 0, -1):
+        got = exchange(value, step, n)
+        js, value = js + [j | (1 << step) for j in js], jnp.concatenate([value, got])
+    late_js, late = [j | 1 for j in js], exchange(value, 0, n)
+    other = exchange(value, -1, n)
+    grid, token = pl.pallas_call(
+        functools.partial(first_grid_kernel, n, [(js, 0)]),
+        out_shape=[held(grid_shape, F32), held((1, M), F32)],
+        in_specs=[SMEM] * 3 + [VMEM],
+        out_specs=[VMEM] * 2,
         compiler_params=params(8),
         name="grid_first",
-    )(me, facet_offsets, corners, near(early[1]), near(early_other[1]))
-    late_other = ([j ^ 1 for j in late_js], exchange(late_value, 1, n))
+    )(me, facet_offsets, corners, near(value))
+    late = (late.astype(F32) + token).astype(BF)
+    late_other = exchange(late, -1, n)
     grid = pl.pallas_call(
-        functools.partial(next_grid_kernel, [late_js]),
+        functools.partial(next_grid_kernel, n, [(js, 1), (late_js, 0)]),
         out_shape=held(grid_shape, F32),
-        in_specs=[SMEM] * 3 + [VMEM] * 2,
+        in_specs=[SMEM] * 3 + [VMEM] * 3,
         out_specs=VMEM,
         compiler_params=params(8),
         name="grid_next",
-    )(me, facet_offsets, corners, near(late_value), near(grid))
+    )(me, facet_offsets, corners, near(other), near(late), near(grid))
     update = pl.pallas_call(
-        functools.partial(backward_kernel, [late_other[0]]),
+        functools.partial(backward_kernel, n, [(late_js, 1)]),
         out_shape=[pltpu.HBM(facets.shape, BF), held(grid_shape, F32)],
         in_specs=[SMEM] * 3 + [ANY] + [VMEM] * 2,
         out_specs=[ANY, VMEM],
@@ -536,7 +553,7 @@
         ],
         compiler_params=params(16),
         name="backward",
-    )(me, facet_offsets, corners, basis, near(late_other[1]), near(grid))[0]
+    )(me, facet_offsets, corners, basis, near(late_other), near(grid))[0]
     return (residual, update)
 
 

time: 66 us -> 69.4 us (1.052); the launches traced: 65.6 us -> 68.2 us
  waiting for transfers between devices: 6.49 us -> 10.8 us
  starting transfers between devices: 21.8 us -> 19.4 us
    ppermute x14 -> x10, waiting for transfers between devices: 6.49 us -> 10.8 us  [exchange(): lax.ppermute(value, 'facet', [(i, i ^ masks[i & 1]) for i in range(n)])]
    ppermute x14 -> x10, starting transfers between devices: 21.8 us -> 19.4 us  [exchange(): lax.ppermute(value, 'facet', [(i, i ^ masks[i & 1]) for i in range(n)])]
    pallas_call x6 -> x7, Pallas kernels: 20.3 us -> 20.9 us  [the longest x1 5.31 us: per_device(): pl.pallas_call(functools.partial(backward_kernel, n, [(late_js, 1)]), out...]
  transfers between devices with their start and end apart: 14 -> 10, of which waited for: 4 -> 5; matrix products, arithmetic and copies ran while one was open for 0% -> 0% of each run, Pallas kernels for 15% -> 15%
where the time goes in v5:
time: 69.4 us; the launch traced here: 68.2 us
  Pallas kernels  35.5 us (51%)
  starting transfers between devices  19.4 us (28%)
  waiting for transfers between devices  10.8 us (16%)
  between operations  2.21 us (3%)
    ppermute x10, starting transfers between devices, exchange(): lax.ppermute(value, 'facet', [(i, i ^ masks[i & 1]) for i in range(n)])  19.4 us
    pallas_call x1, Pallas kernels, per_device(): pl.pallas_call(functools.partial(subgrid_kernel, [0] + [js.index(0) for j...  14.6 us
    ppermute x10, waiting for transfers between devices, exchange(): lax.ppermute(value, 'facet', [(i, i ^ masks[i & 1]) for i in range(n)])  10.8 us
    pallas_call x1, Pallas kernels, per_device(): pl.pallas_call(functools.partial(backward_kernel, n, [(late_js, 1)]), out...  5.31 us
    pallas_call x1, Pallas kernels, per_device(): pl.pallas_call(functools.partial(forward_kernel, n, sends[0][1:]), out_sh...  5.24 us
    pallas_call x1, Pallas kernels, make_bands(): pl.pallas_call(band_kernel, out_shape=[held((SG, slots * TV)), held((slot...  3.35 us
    pallas_call x1, Pallas kernels, per_device(): pl.pallas_call(functools.partial(extract_kernel, n, lists), out_shape=[he...  2.6 us
    pallas_call x1, Pallas kernels, make_screen(): pl.pallas_call(screen_kernel, out_shape=[held((2, SG, SG), F32)] + [held(...  1.62 us
  transfers between devices with their start and end apart: 10, of which 5 were waited for; matrix products, arithmetic and copies ran while one was open for 0% of the time, Pallas kernels for 15%

profile of v5, /device:TPU:1, one launch (start us, length us, event | category | flops | bytes accessed | tf_op | source)
XLA Modules:
  0.0 68.2 jit_solution(16858933409652245022)
XLA Ops:
  0.6 5.2 %forward.1 = (bf16[4,2,128,128]{3,2,1,0:T(8,128)(2,1)S(1)}, f32[2,5,640,128]{3,2,1,0:T(8,128)S(1)}) custom-call(s32[1]{0:T(128)} %bitcast.2.me_ref, s32[1,2]{1,0:T(1,128)} %fo_ref.9, s32[2,16]{1,0:T(2,128)} %bitcast.13, bf16[1,2,512,512]{3,2,1,0:T(8,128)(2,1)} %facet_ref.1, bf16[2,512,512]{2,1,0:T(8,128)(2,1)} %constant.16.clone.basis_ref.basis_hbm), custom_call_target="tpu_custom_call" | custom-call | tf_op jit(solution)/shard_map/forward/pallas_call | solution.py:419
  5.9 0.1 collective-permute-start.1
  6.0 2.6 %extract.1 = (bf16[4,2,128,128]{3,2,1,0:T(8,128)(2,1)S(1)}, bf16[4,2,128,128]{3,2,1,0:T(8,128)(2,1)S(1)}, bf16[2,2,128,128]{3,2,1,0:T(8,128)(2,1)S(1)}, bf16[1,2...) custom-call(s32[1]{0:T(128)} %bitcast.2.me_ref, s32[1,2]{1,0:T(1,128)} %fo_ref.9, s32[2,16]{1,0:T(2,128)} %bitcast.14, ...), custom_call_target="tpu_custom_call" | custom-call | tf_op jit(solution)/shard_map/extract/pallas_call | solution.py:433
  8.6 0.5 collective-permute-start
  9.1 0.1 add_convert_fusion.1._
  9.2 2.4 %collective-permute-start.2 = (bf16[4,2,128,128]{3,2,1,0:T(8,128)(2,1)S(1)}, bf16[4,2,128,128]{3,2,1,0:T(8,128)(2,1)S(1)}, u32[]{:S(2)}, u32[]{:S(2)}) collective-permute-start(bf16[4,2,128,128]{3,2,1,0:T(8,128)(2,1)S(1)} %add_convert_fusion.1._), channel_id=1, source_target_pairs={{0,2},{1,5},{2,0},{3,7},{4,6},{5,1},{6,4},{7,3},{8,10},{9,13},{10,... | collective-permute-start | bytes 786440 | tf_op jit(solution)/shard_map/ppermute | solution.py:383
  11.6 3.3 %bands.1 = (bf16[512,2048]{1,0:T(8,128)(2,1)S(1)}, bf16[2048,512]{1,0:T(8,128)(2,1)S(1)}, bf16[16,512,128]{2,1,0:T(8,128)(2,1)S(1)}, f32[1,128]{1,0:T(1,128)S(1)}) custom-call(s32[2,16]{1,0:T(2,128)} %bitcast.18, bf16[4,2,128,128]{3,2,1,0:T(8,128)(2,1)S(1)} %add_convert_fusion.1._, f32[768,128]{1,0:T(8,128)} %constant.17.clone.kt_hbm, ...), custom_call_target="tpu_custom_call" | custom-call | tf_op jit(solution)/shard_map/bands/pallas_call | solution.py:443
  15.0 0.7 %collective-permute-done.2.rest_2_ = bf16[4,2,128,128]{3,2,1,0:T(8,128)(2,1)S(1)} collective-permute-done((bf16[4,2,128,128]{3,2,1,0:T(8,128)(2,1)S(1)}, bf16[4,2,128,128]{3,2,1,0:T(8,128)(2,1)S(1)}, u32[]{:S(2)}, u32[]{:S(2)}) %collective-permute-start.2) | collective-permute-done | bytes 262176 | tf_op jit(solution)/shard_map/ppermute | solution.py:383
  15.7 2.5 %collective-permute-start.3 = (bf16[2,2,128,128]{3,2,1,0:T(8,128)(2,1)S(1)}, bf16[2,2,128,128]{3,2,1,0:T(8,128)(2,1)S(1)}, u32[]{:S(2)}, u32[]{:S(2)}) collective-permute-start(bf16[2,2,128,128]{3,2,1,0:T(8,128)(2,1)S(1)} %add_convert_fusion.2._), channel_id=1, source_target_pairs={{0,4},{1,9},{2,6},{3,11},{4,0},{5,13},{6,2},{7,15},{8,12},{9,1},{1... | collective-permute-start | bytes 393224 | tf_op jit(solution)/shard_map/ppermute | solution.py:383
  18.9 1.6 %screen.1 = (f32[2,512,512]{2,1,0:T(8,128)S(1)}, bf16[16,2,128,128]{3,2,1,0:T(8,128)(2,1)S(1)}, bf16[2,512,128]{2,1,0:T(8,128)(2,1)S(1)}, bf16[2,128,512]{2,1,0:...) custom-call(f32[1,1]{1,0:T(1,128)} %bitcast.8.w_ref, ...), custom_call_target="tpu_custom_call" | custom-call | tf_op jit(solution)/shard_map/screen/pallas_call | solution.py:464
  20.5 1.5 %collective-permute-done.3.rest_3_ = bf16[2,2,128,128]{3,2,1,0:T(8,128)(2,1)S(1)} collective-permute-done((bf16[2,2,128,128]{3,2,1,0:T(8,128)(2,1)S(1)}, bf16[2,2,128,128]{3,2,1,0:T(8,128)(2,1)S(1)}, u32[]{:S(2)}, u32[]{:S(2)}) %collective-permute-start.3) | collective-permute-done | bytes 131104 | tf_op jit(solution)/shard_map/ppermute | solution.py:383
  22.1 1.4 %collective-permute-start.4 = (bf16[1,2,128,128]{3,2,1,0:T(8,128)(2,1)S(1)}, bf16[1,2,128,128]{3,2,1,0:T(8,128)(2,1)S(1)}, u32[]{:S(2)}, u32[]{:S(2)}) collective-permute-start(bf16[1,2,128,128]{3,2,1,0:T(8,128)(2,1)S(1)} %add_convert_fusion.3), channel_id=1, source_target_pairs={{0,8},{1,3},{2,10},{3,1},{4,12},{5,7},{6,14},{7,5},{8,0},{9,11},{1... | collective-permute-start | bytes 196616 | tf_op jit(solution)/shard_map/ppermute | solution.py:383
  24.1 1.2 %collective-permute-done.4.rest_4_ = bf16[1,2,128,128]{3,2,1,0:T(8,128)(2,1)S(1)} collective-permute-done((bf16[1,2,128,128]{3,2,1,0:T(8,128)(2,1)S(1)}, bf16[1,2,128,128]{3,2,1,0:T(8,128)(2,1)S(1)}, u32[]{:S(2)}, u32[]{:S(2)}) %collective-permute-start.4) | collective-permute-done | bytes 65568 | tf_op jit(solution)/shard_map/ppermute | solution.py:383
  25.2 14.6 %subgrid.1 = (bf16[16,2,128,128]{3,2,1,0:T(8,128)(2,1)}, bf16[1,2,128,128]{3,2,1,0:T(8,128)(2,1)S(1)}) custom-call(s32[1,1]{1,0:T(1,128)} %bitcast.9.tc_ref, s32[2,16]{1,0:T(2,128)} %bitcast.19, bf16[1,2,128,128]{3,2,1,0:T(8,128)(2,1)S(1)} %get-tuple-element.25.rest_0_, bf16[4,2,128,128]{3,2,1,0:T(8,128)(2,1)S(1)} %collective-permute-done.rest_1_, ...), custom_call_target="tpu_custom_call" | custom-call | tf_op jit(solution)/shard_map/subgrid/pallas_call | solution.py:497
  39.8 1.4 %collective-permute-start.5 = (bf16[1,2,128,128]{3,2,1,0:T(8,128)(2,1)S(1)}, bf16[1,2,128,128]{3,2,1,0:T(8,128)(2,1)S(1)}, u32[]{:S(2)}, u32[]{:S(2)}) collective-permute-start(bf16[1,2,128,128]{3,2,1,0:T(8,128)(2,1)S(1)} %get-tuple-element.42), channel_id=1, source_target_pairs={{0,8},{1,3},{2,10},{3,1},{4,12},{5,7},{6,14},{7,5},{8,0},{9,11},{1... | collective-permute-start | bytes 196616 | tf_op jit(solution)/shard_map/ppermute | solution.py:383
  41.2 1.8 %collective-permute-done.5 = bf16[1,2,128,128]{3,2,1,0:T(8,128)(2,1)S(1)} collective-permute-done((bf16[1,2,128,128]{3,2,1,0:T(8,128)(2,1)S(1)}, bf16[1,2,128,128]{3,2,1,0:T(8,128)(2,1)S(1)}, u32[]{:S(2)}, u32[]{:S(2)}) %collective-permute-start.5) | collective-permute-done | bytes 65568 | tf_op jit(solution)/shard_map/ppermute | solution.py:383
  43.0 1.6 %collective-permute-start.6 = (bf16[2,2,128,128]{3,2,1,0:T(8,128)(2,1)S(1)}, bf16[2,2,128,128]{3,2,1,0:T(8,128)(2,1)S(1)}, u32[]{:S(2)}, u32[]{:S(2)}) collective-permute-start(bf16[2,2,128,128]{3,2,1,0:T(8,128)(2,1)S(1)} %pad_maximum_fusion), channel_id=1, source_target_pairs={{0,4},{1,9},{2,6},{3,11},{4,0},{5,13},{6,2},{7,15},{8,12},{9,1},{1... | collective-permute-start | bytes 393224 | tf_op jit(solution)/shard_map/ppermute | solution.py:383
  44.7 5.7 %collective-permute-done.6 = bf16[2,2,128,128]{3,2,1,0:T(8,128)(2,1)S(1)} collective-permute-done((bf16[2,2,128,128]{3,2,1,0:T(8,128)(2,1)S(1)}, bf16[2,2,128,128]{3,2,1,0:T(8,128)(2,1)S(1)}, u32[]{:S(2)}, u32[]{:S(2)}) %collective-permute-start.6) | collective-permute-done | bytes 131104 | tf_op jit(solution)/shard_map/ppermute | solution.py:383
  50.4 0.3 collective-permute-start.7
  50.7 5.5 %collective-permute-start.9 = (bf16[4,2,128,128]{3,2,1,0:T(8,128)(2,1)S(1)}, bf16[4,2,128,128]{3,2,1,0:T(8,128)(2,1)S(1)}, u32[]{:S(2)}, u32[]{:S(2)}) collective-permute-start(bf16[4,2,128,128]{3,2,1,0:T(8,128)(2,1)S(1)} %constant_dynamic-update-slice_fusion.rest_0_), channel_id=1, source_target_pairs={{0,1},{1,0},{2,3},{3,2},{4,5},{5,4},{6,7},{7,6},{8,9},{9,8},{10,11... | collective-permute-start | bytes 786440 | tf_op jit(solution)/shard_map/ppermute | solution.py:383
  56.2 1.2 %grid_first.1 = (f32[2,5,640,128]{3,2,1,0:T(8,128)S(1)}, f32[1,128]{1,0:T(1,128)S(1)}) custom-call(s32[1]{0:T(128)} %bitcast.2.me_ref, s32[1,2]{1,0:T(1,128)} %fo_ref.9, s32[2,16]{1,0:T(2,128)} %bitcast.15, bf16[4,2,128,128]{3,2,1,0:T(8,128)(2,1)S(1)} %constant_dynamic-update-slice_fusion.rest_0_), custom_call_target="tpu_custom_call" | custom-call | tf_op jit(solution)/shard_map/grid_first/pallas_call | solution.py:525
  57.5 3.7 %collective-permute-start.8 = (bf16[4,2,128,128]{3,2,1,0:T(8,128)(2,1)S(1)}, bf16[4,2,128,128]{3,2,1,0:T(8,128)(2,1)S(1)}, u32[]{:S(2)}, u32[]{:S(2)}) collective-permute-start(bf16[4,2,128,128]{3,2,1,0:T(8,128)(2,1)S(1)} %add_convert_fusion.rest_1_), channel_id=1, source_target_pairs={{0,1},{1,0},{2,3},{3,2},{4,5},{5,4},{6,7},{7,6},{8,9},{9,8},{10,11... | collective-permute-start | bytes 786440 | tf_op jit(solution)/shard_map/ppermute | solution.py:383
  61.2 1.5 %grid_next.1.rest_1_ = f32[2,5,640,128]{3,2,1,0:T(8,128)S(1)} custom-call(s32[1]{0:T(128)} %bitcast.2.me_ref, s32[1,2]{1,0:T(1,128)} %fo_ref.9, s32[2,16]{1,0:T(2,128)} %bitcast.16, bf16[4,2,128,128]{3,2,1,0:T(8,128)(2,1)S(1)} %collective-permute-done.9.rest_0_, bf16[4,2,128,128]{3,2,1,0:T(8,128)(2,1)S(1)} %add_convert_fusion.rest_1_, ...), custom_call_target="tpu_custom_call" | custom-call | tf_op jit(solution)/shard_map/grid_next/pallas_call | solution.py:535
  62.7 5.3 %backward.1 = (bf16[1,2,512,512]{3,2,1,0:T(8,128)(2,1)}, f32[2,5,640,128]{3,2,1,0:T(8,128)S(1)}) custom-call(s32[1]{0:T(128)} %bitcast.2.me_ref, s32[1,2]{1,0:T(1,128)} %fo_ref.9, s32[2,16]{1,0:T(2,128)} %bitcast.17, bf16[2,512,512]{2,1,0:T(8,128)(2,1)} %constant.16.clone.basis_ref.basis_hbm, ...), custom_call_target="tpu_custom_call", output_to_operand_aliasing={{1}: (5, {})} | custom-call | tf_op jit(solution)/shard_map/backward/pallas_call | solution.py:543
  (12 shorter events, 0.2 us)
Async XLA Ops:
  5.9 3.3 %collective-permute-start.1 = (bf16[4,2,128,128]{3,2,1,0:T(8,128)(2,1)S(1)}, bf16[4,2,128,128]{3,2,1,0:T(8,128)(2,1)S(1)}, u32[]{:S(2)}, u32[]{:S(2)}) collective-permute-start(bf16[4,2,128,128]{3,2,1,0:T(8,128)(2,1)S(1)} %get-tuple-element.28), channel_id=1, source_target_pairs={{0,1},{1,0},{2,3},{3,2},{4,5},{5,4},{6,7},{7,6},{8,9},{9,8},{10,11... | collective-permute-start | bytes 786440 | tf_op jit(solution)/shard_map/ppermute | solution.py:383
  8.6 6.3 %collective-permute-start = (bf16[4,2,128,128]{3,2,1,0:T(8,128)(2,1)S(1)}, bf16[4,2,128,128]{3,2,1,0:T(8,128)(2,1)S(1)}, u32[]{:S(2)}, u32[]{:S(2)}) collective-permute-start(bf16[4,2,128,128]{3,2,1,0:T(8,128)(2,1)S(1)} %get-tuple-element.26), channel_id=1, source_target_pairs={{0,1},{1,0},{2,3},{3,2},{4,5},{5,4},{6,7},{7,6},{8,9},{9,8},{10,11... | collective-permute-start | bytes 786440 | tf_op jit(solution)/shard_map/ppermute | solution.py:383
  9.2 6.4 %collective-permute-start.2 = (bf16[4,2,128,128]{3,2,1,0:T(8,128)(2,1)S(1)}, bf16[4,2,128,128]{3,2,1,0:T(8,128)(2,1)S(1)}, u32[]{:S(2)}, u32[]{:S(2)}) collective-permute-start(bf16[4,2,128,128]{3,2,1,0:T(8,128)(2,1)S(1)} %add_convert_fusion.1._), channel_id=1, source_target_pairs={{0,2},{1,5},{2,0},{3,7},{4,6},{5,1},{6,4},{7,3},{8,10},{9,13},{10,... | collective-permute-start | bytes 786440 | tf_op jit(solution)/shard_map/ppermute | solution.py:383
  15.7 6.3 %collective-permute-start.3 = (bf16[2,2,128,128]{3,2,1,0:T(8,128)(2,1)S(1)}, bf16[2,2,128,128]{3,2,1,0:T(8,128)(2,1)S(1)}, u32[]{:S(2)}, u32[]{:S(2)}) collective-permute-start(bf16[2,2,128,128]{3,2,1,0:T(8,128)(2,1)S(1)} %add_convert_fusion.2._), channel_id=1, source_target_pairs={{0,4},{1,9},{2,6},{3,11},{4,0},{5,13},{6,2},{7,15},{8,12},{9,1},{1... | collective-permute-start | bytes 393224 | tf_op jit(solution)/shard_map/ppermute | solution.py:383
  22.1 3.2 %collective-permute-start.4 = (bf16[1,2,128,128]{3,2,1,0:T(8,128)(2,1)S(1)}, bf16[1,2,128,128]{3,2,1,0:T(8,128)(2,1)S(1)}, u32[]{:S(2)}, u32[]{:S(2)}) collective-permute-start(bf16[1,2,128,128]{3,2,1,0:T(8,128)(2,1)S(1)} %add_convert_fusion.3), channel_id=1, source_target_pairs={{0,8},{1,3},{2,10},{3,1},{4,12},{5,7},{6,14},{7,5},{8,0},{9,11},{1... | collective-permute-start | bytes 196616 | tf_op jit(solution)/shard_map/ppermute | solution.py:383
  39.8 3.2 %collective-permute-start.5 = (bf16[1,2,128,128]{3,2,1,0:T(8,128)(2,1)S(1)}, bf16[1,2,128,128]{3,2,1,0:T(8,128)(2,1)S(1)}, u32[]{:S(2)}, u32[]{:S(2)}) collective-permute-start(bf16[1,2,128,128]{3,2,1,0:T(8,128)(2,1)S(1)} %get-tuple-element.42), channel_id=1, source_target_pairs={{0,8},{1,3},{2,10},{3,1},{4,12},{5,7},{6,14},{7,5},{8,0},{9,11},{1... | collective-permute-start | bytes 196616 | tf_op jit(solution)/shard_map/ppermute | solution.py:383
  43.0 7.4 %collective-permute-start.6 = (bf16[2,2,128,128]{3,2,1,0:T(8,128)(2,1)S(1)}, bf16[2,2,128,128]{3,2,1,0:T(8,128)(2,1)S(1)}, u32[]{:S(2)}, u32[]{:S(2)}) collective-permute-start(bf16[2,2,128,128]{3,2,1,0:T(8,128)(2,1)S(1)} %pad_maximum_fusion), channel_id=1, source_target_pairs={{0,4},{1,9},{2,6},{3,11},{4,0},{5,13},{6,2},{7,15},{8,12},{9,1},{1... | collective-permute-start | bytes 393224 | tf_op jit(solution)/shard_map/ppermute | solution.py:383
  50.4 7.0 %collective-permute-start.7 = (bf16[4,2,128,128]{3,2,1,0:T(8,128)(2,1)S(1)}, bf16[4,2,128,128]{3,2,1,0:T(8,128)(2,1)S(1)}, u32[]{:S(2)}, u32[]{:S(2)}) collective-permute-start(bf16[4,2,128,128]{3,2,1,0:T(8,128)(2,1)S(1)} %constant_dynamic-update-slice_fusion.rest_0_), channel_id=1, source_target_pairs={{0,2},{1,5},{2,0},{3,7},{4,6},{5,1},{6,4},{7,3},{8,10},{9,13},{10,... | collective-permute-start | bytes 786440 | tf_op jit(solution)/shard_map/ppermute | solution.py:383
  50.7 10.5 %collective-permute-start.9 = (bf16[4,2,128,128]{3,2,1,0:T(8,128)(2,1)S(1)}, bf16[4,2,128,128]{3,2,1,0:T(8,128)(2,1)S(1)}, u32[]{:S(2)}, u32[]{:S(2)}) collective-permute-start(bf16[4,2,128,128]{3,2,1,0:T(8,128)(2,1)S(1)} %constant_dynamic-update-slice_fusion.rest_0_), channel_id=1, source_target_pairs={{0,1},{1,0},{2,3},{3,2},{4,5},{5,4},{6,7},{7,6},{8,9},{9,8},{10,11... | collective-permute-start | bytes 786440 | tf_op jit(solution)/shard_map/ppermute | solution.py:383
  57.5 5.2 %collective-permute-start.8 = (bf16[4,2,128,128]{3,2,1,0:T(8,128)(2,1)S(1)}, bf16[4,2,128,128]{3,2,1,0:T(8,128)(2,1)S(1)}, u32[]{:S(2)}, u32[]{:S(2)}) collective-permute-start(bf16[4,2,128,128]{3,2,1,0:T(8,128)(2,1)S(1)} %add_convert_fusion.rest_1_), channel_id=1, source_target_pairs={{0,1},{1,0},{2,3},{3,2},{4,5},{5,4},{6,7},{7,6},{8,9},{9,8},{10,11... | collective-permute-start | bytes 786440 | tf_op jit(solution)/shard_map/ppermute | solution.py:383

commit v6 on v4

--- a/solution.py
+++ b/solution.py
@@ -17,6 +17,7 @@
 BF = jnp.bfloat16
 F32 = jnp.float32
 TWO_PI = 2.0 * math.pi
+OUT_CHUNKS = 4
 
 
 def basis_tables():
@@ -171,7 +172,8 @@
 def prepare_kernel(w_ref, to_ref, _, *rest):
     loads = (len(rest) - 6) // 2
     sources, (screen_ref, kvt_ref, kv_ref, kut_ref) = rest[:loads], rest[loads : loads + 4]
-    targets, zero_ref, sems = rest[loads + 4 : -2], rest[-2], rest[-1]
+    targets = rest[loads + 4 : 2 * loads + 2] + rest[-3:-1]
+    zero_ref, sems = rest[2 * loads + 2], rest[-1]
     zero_ref[...] = jnp.zeros_like(zero_ref)
     kt_ref, kwide_ref = targets[-2:]
     copies = []
@@ -200,7 +202,7 @@
     parts = len(picks)
     sums = rest[:parts]
     (obs_ref, pad_ref, padt_ref, kern_ref, screen_ref, kvt_ref, kv_ref, kut_ref) = rest[parts : parts + 8]
-    (out_ref, coef_ref, model_ref, rows_ref, z_ref, res_ref, sems) = rest[parts + 8 :]
+    (out_ref, coef_ref, model_ref, z_ref, res_ref, sems, *rows_refs) = rest[parts + 8 :]
     slots = obs_ref.shape[0]
     count = tc_ref[0, 0]
 
@@ -224,12 +226,12 @@
     for t0 in range(0, slots, 2):
         pair = dot(model, kvt_ref[:, t0 * TV : (t0 + 2) * TV])
         for t in (t0, t0 + 1):
-            rows_ref[t % rows_ref.shape[0]] = pair[:, (t - t0) * TV : (t - t0 + 1) * TV]
+            rows_refs[t % len(rows_refs)][...] = pair[:, (t - t0) * TV : (t - t0 + 1) * TV]
         for t in (t0, t0 + 1):
-            slot = t % rows_ref.shape[0]
+            rows_ref = rows_refs[t % len(rows_refs)]
             ou = to_ref[0, t]
-            wr = rows_ref[slot, pl.ds(ou, 2 * TV), :]
-            wi = rows_ref[slot, pl.ds(SG + ou, 2 * TV), :]
+            wr = rows_ref[pl.ds(ou, 2 * TV), :]
+            wi = rows_ref[pl.ds(SG + ou, 2 * TV), :]
             window = jnp.concatenate([wr.astype(BF), wi.astype(BF)], axis=1)
             predicted = dot(kern, window)
             live = count > t
@@ -284,19 +286,19 @@
 
 
 def first_grid_kernel(pieces, me_ref, fo_ref, so_ref, *rest):
-    grid_ref = rest[-1]
+    grid_ref, zero_ref = rest[-2:]
+    zero_ref[...] = jnp.zeros_like(zero_ref)
     grid_ref[...] = jnp.zeros_like(grid_ref)
-    grid_blocks(pieces, rest[:-1], me_ref, fo_ref, so_ref, grid_ref)
+    grid_blocks(pieces, rest[:-2], me_ref, fo_ref, so_ref, grid_ref)
 
 
 def next_grid_kernel(pieces, me_ref, fo_ref, so_ref, *rest):
-    rest[-1][...] = rest[-2][...]
-    grid_blocks(pieces, rest[:-2], me_ref, fo_ref, so_ref, rest[-1])
+    grid_blocks(pieces, rest[:-2], me_ref, fo_ref, so_ref, rest[-2])
 
 
 def backward_kernel(pieces, me_ref, fo_ref, so_ref, basis_hbm, *rest):
     grid_ref, out_ref, _, basis_ref, out_buf, sems = rest[len(pieces) :]
-    load = pltpu.make_async_copy(basis_hbm, basis_ref, sems.at[4])
+    load = pltpu.make_async_copy(basis_hbm, basis_ref, sems.at[2 * OUT_CHUNKS])
     load.start()
     grid_blocks(pieces, rest[: len(pieces)], me_ref, fo_ref, so_ref, grid_ref)
     columns = F // M
@@ -314,16 +316,16 @@
     br, bi = basis_ref[0], basis_ref[1]
     hr, hi = mul_right(br, -bi, *folded)
     hr, hi = hr.astype(BF), hi.astype(BF)
-    half = F // 2
+    size = F // OUT_CHUNKS
     copies = []
-    for k in range(2):
-        rows = slice(k * half, (k + 1) * half)
+    for k in range(OUT_CHUNKS):
+        rows = slice(k * size, (k + 1) * size)
         real, imag = mul_left(hr[rows], hi[rows], br, -bi)
         for plane, value in enumerate((real, imag)):
             out_buf[plane, rows] = value.astype(BF)
             copy = pltpu.make_async_copy(
-                out_buf.at[plane, pl.ds(k * half, half)],
-                out_ref.at[0, plane, pl.ds(k * half, half)],
+                out_buf.at[plane, pl.ds(k * size, size)],
+                out_ref.at[0, plane, pl.ds(k * size, size)],
                 sems.at[2 * k + plane],
             )
             copy.start()
@@ -450,7 +452,8 @@
                 total = total + term.astype(F32)
             value = total.astype(BF)
         if mask == 2 and len(js) > 1:
-            loads = [observed, pad_np, pad_np.transpose(0, 2, 1), kern_np, kt_np, kwide_np]
+            loads = [observed, pad_np, pad_np.transpose(0, 2, 1), kern_np]
+            loads += [tile_offsets.T, subgrid_offsets.T, facet_offsets, kt_np, kwide_np]
             prepared = pl.pallas_call(
                 prepare_kernel,
                 out_shape=[
@@ -459,11 +462,15 @@
                     held((slots * TV, SG)),
                     held((slots, SG, TV)),
                 ]
-                + [held(load.shape, load.dtype) for load in loads]
+                + [held(load.shape, load.dtype) for load in loads[:-2]]
                 + [held((1, M), F32)],
                 in_specs=[SMEM] * 2 + [VMEM] + [ANY] * len(loads),
-                out_specs=[VMEM] * (5 + len(loads)),
-                scratch_shapes=[pltpu.SemaphoreType.DMA((len(loads),))],
+                out_specs=[VMEM] * (3 + len(loads)),
+                scratch_shapes=[
+                    pltpu.VMEM(kt_np.shape, F32),
+                    pltpu.VMEM(kwide_np.shape, F32),
+                    pltpu.SemaphoreType.DMA((len(loads),)),
+                ],
                 compiler_params=params(8),
                 name="prepare",
             )(w_terms.reshape(1, 1), tile_corners, near(value), *[far(jnp.asarray(load)) for load in loads])
@@ -471,6 +478,7 @@
         arrived.append(([j ^ mask for j in js], got))
     last = [(js, got) for js, got in arrived if 0 in js]
     screen, kvt, kv, kut, tiles, pad, padt, kern = prepared[:8]
+    tile_corners, corners, facet_offsets = [near(value) for value in prepared[8:11]]
 
     residual, coefficient = pl.pallas_call(
         functools.partial(subgrid_kernel, [0] + [js.index(0) for js, _ in last]),
@@ -479,11 +487,11 @@
         out_specs=[ANY, VMEM],
         scratch_shapes=[
             pltpu.VMEM((2 * SG, SG), BF),
-            pltpu.VMEM((8, 2 * SG, TV), F32),
             pltpu.VMEM((2 * SG, slots * TV), BF),
             pltpu.VMEM(observed.shape, BF),
             pltpu.SemaphoreType.DMA((slots // 4,)),
-        ],
+        ]
+        + [pltpu.VMEM((2 * SG, TV), F32)] * 8,
         compiler_params=params(24),
         name="subgrid",
     )(
@@ -494,35 +502,33 @@
         *[near(value) for value in (tiles, pad, padt, kern, screen, kvt, kv, kut)],
     )
 
-    mine = ([0], coefficient)
-    beside = ([2], exchange(coefficient, 2, n))
-    along = []
+    early = ([0], coefficient)
     for base, radix in reversed(digit_levels(n)[2:]):
-        js, value = join([mine] + along) if along else mine
-        along.append(
-            join([([j ^ (g * base) for j in js], exchange(value, g * base, n)) for g in range(1, radix)])
-        )
-    along = join(along) if len(along) > 1 else along[0]
-    early = join([mine, along, beside])
-    early_other = ([j ^ 1 for j in early[0]], exchange(early[1], 1, n))
-    late_js, late_value = [j ^ 2 for j in along[0]], exchange(along[1], 2, n)
-    grid = pl.pallas_call(
-        functools.partial(first_grid_kernel, [early[0], early_other[0]]),
-        out_shape=held(grid_shape, F32),
-        in_specs=[SMEM] * 3 + [VMEM] * 2,
-        out_specs=VMEM,
+        js, value = early
+        more = [([j ^ (g * base) for j in js], exchange(value, g * base, n)) for g in range(1, radix)]
+        early = join([early] + more)
+    js, value = early
+    late_js, late = [j ^ 2 for j in js], exchange(value, 2, n)
+    other_js, other = [j ^ 1 for j in js], exchange(value, 1, n)
+    grid, token = pl.pallas_call(
+        functools.partial(first_grid_kernel, [js]),
+        out_shape=[held(grid_shape, F32), held((1, M), F32)],
+        in_specs=[SMEM] * 3 + [VMEM],
+        out_specs=[VMEM] * 2,
         compiler_params=params(8),
         name="grid_first",
-    )(me, facet_offsets, corners, near(early[1]), near(early_other[1]))
-    late_other = ([j ^ 1 for j in late_js], exchange(late_value, 1, n))
+    )(me, facet_offsets, corners, near(value))
+    late = (late.astype(F32) + token).astype(BF)
+    late_other = ([j ^ 1 for j in late_js], exchange(late, 1, n))
     grid = pl.pallas_call(
-        functools.partial(next_grid_kernel, [late_js]),
+        functools.partial(next_grid_kernel, [other_js, late_js]),
         out_shape=held(grid_shape, F32),
-        in_specs=[SMEM] * 3 + [VMEM] * 2,
+        in_specs=[SMEM] * 3 + [VMEM] * 3,
         out_specs=VMEM,
+        input_output_aliases={5: 0},
         compiler_params=params(8),
         name="grid_next",
-    )(me, facet_offsets, corners, near(late_value), near(grid))
+    )(me, facet_offsets, corners, near(other), near(late), near(grid))
     update = pl.pallas_call(
         functools.partial(backward_kernel, [late_other[0]]),
         out_shape=[pltpu.HBM(facets.shape, BF), held(grid_shape, F32)],
@@ -532,7 +538,7 @@
         scratch_shapes=[
             pltpu.VMEM((2, F, F), BF),
             pltpu.VMEM((2, F, F), BF),
-            pltpu.SemaphoreType.DMA((5,)),
+            pltpu.SemaphoreType.DMA((2 * OUT_CHUNKS + 1,)),
         ],
         compiler_params=params(16),
         name="backward",

time: 66 us -> 63.6 us (0.964)
  starting transfers between devices: 21.8 us -> 19.5 us
  Pallas kernels: 34.9 us -> 34 us
  waiting for transfers between devices: 6.49 us -> 7.29 us
    ppermute x14 -> x13, starting transfers between devices: 21.8 us -> 19.5 us  [exchange(): return lax.ppermute(value, 'facet', [(i, i ^ mask) for i in range(n)])]
    ppermute x14 -> x13, waiting for transfers between devices: 6.49 us -> 7.29 us  [exchange(): return lax.ppermute(value, 'facet', [(i, i ^ mask) for i in range(n)])]
    pallas_call x1, Pallas kernels: 4.71 us -> 4.02 us  [per_device(): pl.pallas_call(prepare_kernel, out_shape=[held((2, SG, SG), F32), held((S...]
  transfers between devices with their start and end apart: 14 -> 13, of which waited for: 4 -> 5; matrix products, arithmetic and copies ran while one was open for 0% -> 0% of each run, Pallas kernels for 15% -> 15%
where the time goes in v6:
time: 63.6 us; the launch traced here: 63.3 us
  Pallas kernels  34 us (53%)
  starting transfers between devices  19.5 us (31%)
  waiting for transfers between devices  7.29 us (11%)
  between operations  2.23 us (4%)
    ppermute x13, starting transfers between devices, exchange(): return lax.ppermute(value, 'facet', [(i, i ^ mask) for i in range(n)])  19.5 us
    pallas_call x1, Pallas kernels, per_device(): pl.pallas_call(functools.partial(subgrid_kernel, [0] + [js.index(0) for j...  14.4 us
    ppermute x13, waiting for transfers between devices, exchange(): return lax.ppermute(value, 'facet', [(i, i ^ mask) for i in range(n)])  7.29 us
    pallas_call x1, Pallas kernels, per_device(): pl.pallas_call(functools.partial(forward_kernel, sends[0][0]), out_shape=...  5.23 us
    pallas_call x1, Pallas kernels, per_device(): pl.pallas_call(functools.partial(backward_kernel, [late_other[0]]), out_s...  4.87 us
    pallas_call x1, Pallas kernels, per_device(): pl.pallas_call(prepare_kernel, out_shape=[held((2, SG, SG), F32), held((S...  4.02 us
    pallas_call x1, Pallas kernels, per_device(): pl.pallas_call(functools.partial(extract_kernel, lists), out_shape=[held(...  2.32 us
    pallas_call x1, Pallas kernels, per_device(): pl.pallas_call(functools.partial(next_grid_kernel, [other_js, late_js]),...  1.74 us
  transfers between devices with their start and end apart: 13, of which 5 were waited for; matrix products, arithmetic and copies ran while one was open for 0% of the time, Pallas kernels for 15%

profile of v6, /device:TPU:1, one launch (start us, length us, event | category | flops | bytes accessed | tf_op | source)
XLA Modules:
  0.0 63.3 jit_solution(14921144545470235560)
XLA Ops:
  0.6 5.2 %forward.1 = (bf16[4,2,128,128]{3,2,1,0:T(8,128)(2,1)S(1)}, f32[2,5,640,128]{3,2,1,0:T(8,128)S(1)}) custom-call(s32[1]{0:T(128)} %bitcast.3.me_ref, s32[1,2]{1,0:T(1,128)} %rest_6_.1, s32[2,16]{1,0:T(2,128)} %bitcast.11, bf16[1,2,512,512]{3,2,1,0:T(8,128)(2,1)} %facet_ref.1, bf16[2,512,512]{2,1,0:T(8,128)(2,1)} %constant.16.clone.basis_ref.basis_hbm), custom_call_target="tpu_custom_call" | custom-call | tf_op jit(solution)/shard_map/forward/pallas_call | solution.py:416
  5.9 0.1 collective-permute-start
  6.0 2.3 %extract.1 = (bf16[4,2,128,128]{3,2,1,0:T(8,128)(2,1)S(1)}, bf16[3,2,128,128]{3,2,1,0:T(8,128)(2,1)S(1)}, bf16[1,2,128,128]{3,2,1,0:T(8,128)(2,1)S(1)}, bf16[1,2...) custom-call(s32[1]{0:T(128)} %bitcast.3.me_ref, ...), custom_call_target="tpu_custom_call" | custom-call | tf_op jit(solution)/shard_map/extract/pallas_call | solution.py:430
  8.3 0.5 collective-permute-start.1
  9.6 2.3 %collective-permute-start.3 = (bf16[3,2,128,128]{3,2,1,0:T(8,128)(2,1)S(1)}, bf16[3,2,128,128]{3,2,1,0:T(8,128)(2,1)S(1)}, u32[]{:S(2)}, u32[]{:S(2)}) collective-permute-start(bf16[3,2,128,128]{3,2,1,0:T(8,128)(2,1)S(1)} %add_convert_fusion.1._), channel_id=1, source_target_pairs={{0,2},{1,3},{2,0},{3,1},{4,6},{5,7},{6,4},{7,5},{8,10},{9,11},{10,... | collective-permute-start | bytes 589832 | tf_op jit(solution)/shard_map/ppermute | solution.py:359
  12.0 4.0 %prepare.1 = (f32[2,512,512]{2,1,0:T(8,128)S(1)}, bf16[512,2048]{1,0:T(8,128)(2,1)S(1)}, bf16[2048,512]{1,0:T(8,128)(2,1)S(1)}, bf16[16,512,128]{2,1,0:T(8,128)(...) custom-call(f32[1,1]{1,0:T(1,128)} %bitcast.7.w_ref, ...), custom_call_target="tpu_custom_call" | custom-call | tf_op jit(solution)/shard_map/prepare/pallas_call | solution.py:457
  16.0 0.7 %collective-permute-done.3 = bf16[3,2,128,128]{3,2,1,0:T(8,128)(2,1)S(1)} collective-permute-done((bf16[3,2,128,128]{3,2,1,0:T(8,128)(2,1)S(1)}, bf16[3,2,128,128]{3,2,1,0:T(8,128)(2,1)S(1)}, u32[]{:S(2)}, u32[]{:S(2)}) %collective-permute-start.3) | collective-permute-done | bytes 196640 | tf_op jit(solution)/shard_map/ppermute | solution.py:359
  16.7 0.1 add_convert_fusion.2
  16.8 3.3 %collective-permute-start.6 = (bf16[1,2,128,128]{3,2,1,0:T(8,128)(2,1)S(1)}, bf16[1,2,128,128]{3,2,1,0:T(8,128)(2,1)S(1)}, u32[]{:S(2)}, u32[]{:S(2)}) collective-permute-start(bf16[1,2,128,128]{3,2,1,0:T(8,128)(2,1)S(1)} %get-tuple-element.54), channel_id=1, source_target_pairs={{0,12},{1,13},{2,14},{3,15},{4,8},{5,9},{6,10},{7,11},{8,4},{9,5},... | collective-permute-start | bytes 196616 | tf_op jit(solution)/shard_map/ppermute | solution.py:359
  20.1 0.4 collective-permute-start.4
  21.1 0.7 %collective-permute-done.6.rest_5_ = bf16[1,2,128,128]{3,2,1,0:T(8,128)(2,1)S(1)} collective-permute-done((bf16[1,2,128,128]{3,2,1,0:T(8,128)(2,1)S(1)}, bf16[1,2,128,128]{3,2,1,0:T(8,128)(2,1)S(1)}, u32[]{:S(2)}, u32[]{:S(2)}) %collective-permute-start.6) | collective-permute-done | bytes 65568 | tf_op jit(solution)/shard_map/ppermute | solution.py:359
  21.8 3.4 %collective-permute-done.5.rest_4_ = bf16[1,2,128,128]{3,2,1,0:T(8,128)(2,1)S(1)} collective-permute-done((bf16[1,2,128,128]{3,2,1,0:T(8,128)(2,1)S(1)}, bf16[1,2,128,128]{3,2,1,0:T(8,128)(2,1)S(1)}, u32[]{:S(2)}, u32[]{:S(2)}) %collective-permute-start.5) | collective-permute-done | bytes 65568 | tf_op jit(solution)/shard_map/ppermute | solution.py:359
  25.2 14.4 %subgrid.1 = (bf16[16,2,128,128]{3,2,1,0:T(8,128)(2,1)}, bf16[1,2,128,128]{3,2,1,0:T(8,128)(2,1)S(1)}) custom-call(s32[1,1]{1,0:T(1,128)} %bitcast.8.tc_ref, s32[2,16]{1,0:T(2,128)S(1)} %get-tuple-element.31.to_ref, bf16[1,2,128,128]{3,2,1,0:T(8,128)(2,1)S(1)} %get-tuple-element.32.rest_0_, bf16[4,2,128,128]{3,2,1,0:T(8,128)(2,1)S(1)} %collective-permute-done.1.rest_1_, ...), custom_call_target="tpu_custom_call" | custom-call | tf_op jit(solution)/shard_map/subgrid/pallas_call | solution.py:483
  39.7 0.6 collective-permute-start.9
  40.2 0.4 collective-permute-start.8
  40.6 2.7 %collective-permute-start.7 = (bf16[1,2,128,128]{3,2,1,0:T(8,128)(2,1)S(1)}, bf16[1,2,128,128]{3,2,1,0:T(8,128)(2,1)S(1)}, u32[]{:S(2)}, u32[]{:S(2)}) collective-permute-start(bf16[1,2,128,128]{3,2,1,0:T(8,128)(2,1)S(1)} %get-tuple-element.50), channel_id=1, source_target_pairs={{0,4},{1,5},{2,6},{3,7},{4,0},{5,1},{6,2},{7,3},{8,12},{9,13},{10,... | collective-permute-start | bytes 196616 | tf_op jit(solution)/shard_map/ppermute | solution.py:359
  43.3 2.2 %collective-permute-done.7 = bf16[1,2,128,128]{3,2,1,0:T(8,128)(2,1)S(1)} collective-permute-done((bf16[1,2,128,128]{3,2,1,0:T(8,128)(2,1)S(1)}, bf16[1,2,128,128]{3,2,1,0:T(8,128)(2,1)S(1)}, u32[]{:S(2)}, u32[]{:S(2)}) %collective-permute-start.7) | collective-permute-done | bytes 65568 | tf_op jit(solution)/shard_map/ppermute | solution.py:359
  45.5 0.3 collective-permute-done.8
  45.9 1.3 %collective-permute-start.10 = (bf16[4,2,128,128]{3,2,1,0:T(8,128)(2,1)S(1)}, bf16[4,2,128,128]{3,2,1,0:T(8,128)(2,1)S(1)}, u32[]{:S(2)}, u32[]{:S(2)}) collective-permute-start(bf16[4,2,128,128]{3,2,1,0:T(8,128)(2,1)S(1)} %constant_dynamic-update-slice_fusion.rest_0_), channel_id=1, source_target_pairs={{0,2},{1,3},{2,0},{3,1},{4,6},{5,7},{6,4},{7,5},{8,10},{9,11},{10,... | collective-permute-start | bytes 786440 | tf_op jit(solution)/shard_map/ppermute | solution.py:359
  47.1 4.4 %collective-permute-start.12 = (bf16[4,2,128,128]{3,2,1,0:T(8,128)(2,1)S(1)}, bf16[4,2,128,128]{3,2,1,0:T(8,128)(2,1)S(1)}, u32[]{:S(2)}, u32[]{:S(2)}) collective-permute-start(bf16[4,2,128,128]{3,2,1,0:T(8,128)(2,1)S(1)} %constant_dynamic-update-slice_fusion.rest_0_), channel_id=1, source_target_pairs={{0,1},{1,0},{2,3},{3,2},{4,5},{5,4},{6,7},{7,6},{8,9},{9,8},{10,11... | collective-permute-start | bytes 786440 | tf_op jit(solution)/shard_map/ppermute | solution.py:359
  51.5 1.4 %grid_first.1 = (f32[2,5,640,128]{3,2,1,0:T(8,128)S(1)}, f32[1,128]{1,0:T(1,128)S(1)}) custom-call(s32[1]{0:T(128)} %bitcast.3.me_ref, s32[1,2]{1,0:T(1,128)S(1)} %get-tuple-element.48.fo_ref, s32[2,16]{1,0:T(2,128)S(1)} %get-tuple-element.49.so_ref, bf16[4,2,128,128]{3,2,1,0:T(8,128)(2,1)S(1)} %constant_dynamic-update-slice_fusion.rest_0_), custom_call_target="tpu_custom_call" | custom-call | tf_op jit(solution)/shard_map/grid_first/pallas_call | solution.py:513
  53.0 3.5 %collective-permute-start.11 = (bf16[4,2,128,128]{3,2,1,0:T(8,128)(2,1)S(1)}, bf16[4,2,128,128]{3,2,1,0:T(8,128)(2,1)S(1)}, u32[]{:S(2)}, u32[]{:S(2)}) collective-permute-start(bf16[4,2,128,128]{3,2,1,0:T(8,128)(2,1)S(1)} %add_convert_fusion.rest_1_), channel_id=1, source_target_pairs={{0,1},{1,0},{2,3},{3,2},{4,5},{5,4},{6,7},{7,6},{8,9},{9,8},{10,11... | collective-permute-start | bytes 786440 | tf_op jit(solution)/shard_map/ppermute | solution.py:359
  56.5 1.7 %grid_next.1.rest_1_ = f32[2,5,640,128]{3,2,1,0:T(8,128)S(1)} custom-call(s32[1]{0:T(128)} %bitcast.3.me_ref, s32[1,2]{1,0:T(1,128)S(1)} %get-tuple-element.48.fo_ref, s32[2,16]{1,0:T(2,128)S(1)} %get-tuple-element.49.so_ref, bf16[4,2,128,128]{3,2,1,0:T(8,128)(2,1)S(1)} %collective-permute-done.12.rest_0_, ...), custom_call_target="tpu_custom_call", output_to_operand_aliasing={{}: (5, {})} | custom-call | tf_op jit(solution)/shard_map/grid_next/pallas_call | solution.py:523
  58.3 4.9 %backward.1 = (bf16[1,2,512,512]{3,2,1,0:T(8,128)(2,1)}, f32[2,5,640,128]{3,2,1,0:T(8,128)S(1)}) custom-call(s32[1]{0:T(128)} %bitcast.3.me_ref, s32[1,2]{1,0:T(1,128)S(1)} %get-tuple-element.48.fo_ref, s32[2,16]{1,0:T(2,128)S(1)} %get-tuple-element.49.so_ref, ...), custom_call_target="tpu_custom_call", output_to_operand_aliasing={{1}: (5, {})} | custom-call | tf_op jit(solution)/shard_map/backward/pallas_call | solution.py:532
  (17 shorter events, 0.3 us)
Async XLA Ops:
  5.9 3.6 %collective-permute-start = (bf16[4,2,128,128]{3,2,1,0:T(8,128)(2,1)S(1)}, bf16[4,2,128,128]{3,2,1,0:T(8,128)(2,1)S(1)}, u32[]{:S(2)}, u32[]{:S(2)}) collective-permute-start(bf16[4,2,128,128]{3,2,1,0:T(8,128)(2,1)S(1)} %get-tuple-element.30), channel_id=1, source_target_pairs={{0,1},{1,0},{2,3},{3,2},{4,5},{5,4},{6,7},{7,6},{8,9},{9,8},{10,11... | collective-permute-start | bytes 786440 | tf_op jit(solution)/shard_map/ppermute | solution.py:359
  8.3 7.7 %collective-permute-start.1 = (bf16[4,2,128,128]{3,2,1,0:T(8,128)(2,1)S(1)}, bf16[4,2,128,128]{3,2,1,0:T(8,128)(2,1)S(1)}, u32[]{:S(2)}, u32[]{:S(2)}) collective-permute-start(bf16[4,2,128,128]{3,2,1,0:T(8,128)(2,1)S(1)} %get-tuple-element.33), channel_id=1, source_target_pairs={{0,1},{1,0},{2,3},{3,2},{4,5},{5,4},{6,7},{7,6},{8,9},{9,8},{10,11... | collective-permute-start | bytes 786440 | tf_op jit(solution)/shard_map/ppermute | solution.py:359
  9.6 7.2 %collective-permute-start.3 = (bf16[3,2,128,128]{3,2,1,0:T(8,128)(2,1)S(1)}, bf16[3,2,128,128]{3,2,1,0:T(8,128)(2,1)S(1)}, u32[]{:S(2)}, u32[]{:S(2)}) collective-permute-start(bf16[3,2,128,128]{3,2,1,0:T(8,128)(2,1)S(1)} %add_convert_fusion.1._), channel_id=1, source_target_pairs={{0,2},{1,3},{2,0},{3,1},{4,6},{5,7},{6,4},{7,5},{8,10},{9,11},{10,... | collective-permute-start | bytes 589832 | tf_op jit(solution)/shard_map/ppermute | solution.py:359
  11.9 9.2 %collective-permute-start.2 = (bf16[1,2,128,128]{3,2,1,0:T(8,128)(2,1)S(1)}, bf16[1,2,128,128]{3,2,1,0:T(8,128)(2,1)S(1)}, u32[]{:S(2)}, u32[]{:S(2)}) collective-permute-start(bf16[1,2,128,128]{3,2,1,0:T(8,128)(2,1)S(1)} %add_convert_fusion.5), channel_id=1, source_target_pairs={{0,2},{1,3},{2,0},{3,1},{4,6},{5,7},{6,4},{7,5},{8,10},{9,11},{10,... | collective-permute-start | bytes 196616 | tf_op jit(solution)/shard_map/ppermute | solution.py:359
  16.8 5.0 %collective-permute-start.6 = (bf16[1,2,128,128]{3,2,1,0:T(8,128)(2,1)S(1)}, bf16[1,2,128,128]{3,2,1,0:T(8,128)(2,1)S(1)}, u32[]{:S(2)}, u32[]{:S(2)}) collective-permute-start(bf16[1,2,128,128]{3,2,1,0:T(8,128)(2,1)S(1)} %get-tuple-element.54), channel_id=1, source_target_pairs={{0,12},{1,13},{2,14},{3,15},{4,8},{5,9},{6,10},{7,11},{8,4},{9,5},... | collective-permute-start | bytes 196616 | tf_op jit(solution)/shard_map/ppermute | solution.py:359
  20.1 5.1 %collective-permute-start.5 = (bf16[1,2,128,128]{3,2,1,0:T(8,128)(2,1)S(1)}, bf16[1,2,128,128]{3,2,1,0:T(8,128)(2,1)S(1)}, u32[]{:S(2)}, u32[]{:S(2)}) collective-permute-start(bf16[1,2,128,128]{3,2,1,0:T(8,128)(2,1)S(1)} %get-tuple-element.55), channel_id=1, source_target_pairs={{0,8},{1,9},{2,10},{3,11},{4,12},{5,13},{6,14},{7,15},{8,0},{9,1},... | collective-permute-start | bytes 196616 | tf_op jit(solution)/shard_map/ppermute | solution.py:359
  20.1 5.1 %collective-permute-start.4 = (bf16[1,2,128,128]{3,2,1,0:T(8,128)(2,1)S(1)}, bf16[1,2,128,128]{3,2,1,0:T(8,128)(2,1)S(1)}, u32[]{:S(2)}, u32[]{:S(2)}) collective-permute-start(bf16[1,2,128,128]{3,2,1,0:T(8,128)(2,1)S(1)} %get-tuple-element.56), channel_id=1, source_target_pairs={{0,4},{1,5},{2,6},{3,7},{4,0},{5,1},{6,2},{7,3},{8,12},{9,13},{10,... | collective-permute-start | bytes 196616 | tf_op jit(solution)/shard_map/ppermute | solution.py:359
  39.7 6.1 %collective-permute-start.9 = (bf16[1,2,128,128]{3,2,1,0:T(8,128)(2,1)S(1)}, bf16[1,2,128,128]{3,2,1,0:T(8,128)(2,1)S(1)}, u32[]{:S(2)}, u32[]{:S(2)}) collective-permute-start(bf16[1,2,128,128]{3,2,1,0:T(8,128)(2,1)S(1)} %get-tuple-element.50), channel_id=1, source_target_pairs={{0,12},{1,13},{2,14},{3,15},{4,8},{5,9},{6,10},{7,11},{8,4},{9,5},... | collective-permute-start | bytes 196616 | tf_op jit(solution)/shard_map/ppermute | solution.py:359
  40.2 5.6 %collective-permute-start.8 = (bf16[1,2,128,128]{3,2,1,0:T(8,128)(2,1)S(1)}, bf16[1,2,128,128]{3,2,1,0:T(8,128)(2,1)S(1)}, u32[]{:S(2)}, u32[]{:S(2)}) collective-permute-start(bf16[1,2,128,128]{3,2,1,0:T(8,128)(2,1)S(1)} %get-tuple-element.50), channel_id=1, source_target_pairs={{0,8},{1,9},{2,10},{3,11},{4,12},{5,13},{6,14},{7,15},{8,0},{9,1},... | collective-permute-start | bytes 196616 | tf_op jit(solution)/shard_map/ppermute | solution.py:359
  40.6 4.8 %collective-permute-start.7 = (bf16[1,2,128,128]{3,2,1,0:T(8,128)(2,1)S(1)}, bf16[1,2,128,128]{3,2,1,0:T(8,128)(2,1)S(1)}, u32[]{:S(2)}, u32[]{:S(2)}) collective-permute-start(bf16[1,2,128,128]{3,2,1,0:T(8,128)(2,1)S(1)} %get-tuple-element.50), channel_id=1, source_target_pairs={{0,4},{1,5},{2,6},{3,7},{4,0},{5,1},{6,2},{7,3},{8,12},{9,13},{10,... | collective-permute-start | bytes 196616 | tf_op jit(solution)/shard_map/ppermute | solution.py:359
  45.9 7.1 %collective-permute-start.10 = (bf16[4,2,128,128]{3,2,1,0:T(8,128)(2,1)S(1)}, bf16[4,2,128,128]{3,2,1,0:T(8,128)(2,1)S(1)}, u32[]{:S(2)}, u32[]{:S(2)}) collective-permute-start(bf16[4,2,128,128]{3,2,1,0:T(8,128)(2,1)S(1)} %constant_dynamic-update-slice_fusion.rest_0_), channel_id=1, source_target_pairs={{0,2},{1,3},{2,0},{3,1},{4,6},{5,7},{6,4},{7,5},{8,10},{9,11},{10,... | collective-permute-start | bytes 786440 | tf_op jit(solution)/shard_map/ppermute | solution.py:359
  47.1 9.4 %collective-permute-start.12 = (bf16[4,2,128,128]{3,2,1,0:T(8,128)(2,1)S(1)}, bf16[4,2,128,128]{3,2,1,0:T(8,128)(2,1)S(1)}, u32[]{:S(2)}, u32[]{:S(2)}) collective-permute-start(bf16[4,2,128,128]{3,2,1,0:T(8,128)(2,1)S(1)} %constant_dynamic-update-slice_fusion.rest_0_), channel_id=1, source_target_pairs={{0,1},{1,0},{2,3},{3,2},{4,5},{5,4},{6,7},{7,6},{8,9},{9,8},{10,11... | collective-permute-start | bytes 786440 | tf_op jit(solution)/shard_map/ppermute | solution.py:359
  53.0 5.3 %collective-permute-start.11 = (bf16[4,2,128,128]{3,2,1,0:T(8,128)(2,1)S(1)}, bf16[4,2,128,128]{3,2,1,0:T(8,128)(2,1)S(1)}, u32[]{:S(2)}, u32[]{:S(2)}) collective-permute-start(bf16[4,2,128,128]{3,2,1,0:T(8,128)(2,1)S(1)} %add_convert_fusion.rest_1_), channel_id=1, source_target_pairs={{0,1},{1,0},{2,3},{3,2},{4,5},{5,4},{6,7},{7,6},{8,9},{9,8},{10,11... | collective-permute-start | bytes 786440 | tf_op jit(solution)/shard_map/ppermute | solution.py:359

commit v7 on v6

--- a/solution.py
+++ b/solution.py
@@ -103,9 +103,12 @@
     return cos_v * taper2, sin_v * taper2
 
 
-def forward_kernel(js, me_ref, fo_ref, so_ref, facet_ref, basis_ref, out_ref, spec_ref, *rest):
-    facet_buf, basis_buf, sems = rest
-    copies = []
+def forward_kernel(js, me_ref, fo_hbm, so_hbm, facet_ref, basis_ref, out_ref, spec_ref, *rest):
+    facet_buf, basis_buf, fo_ref, so_ref, sems = rest
+    copies = [
+        pltpu.make_async_copy(fo_hbm, fo_ref, sems.at[4]),
+        pltpu.make_async_copy(so_hbm, so_ref, sems.at[5]),
+    ]
     for k in range(2):
         copies.append(pltpu.make_async_copy(basis_ref.at[k], basis_buf.at[k], sems.at[2 * k]))
         copies.append(pltpu.make_async_copy(facet_ref.at[0, k], facet_buf.at[k], sems.at[2 * k + 1]))
@@ -169,18 +172,33 @@
             block(ref, item, j)
 
 
-def prepare_kernel(w_ref, to_ref, _, *rest):
-    loads = (len(rest) - 6) // 2
-    sources, (screen_ref, kvt_ref, kv_ref, kut_ref) = rest[:loads], rest[loads : loads + 4]
-    targets = rest[loads + 4 : 2 * loads + 2] + rest[-3:-1]
-    zero_ref, sems = rest[2 * loads + 2], rest[-1]
+def band_kernel(to_ref, _, kt_hbm, kwide_hbm, kvt_ref, kv_ref, kut_ref, ku_ref, zero_ref, kt_ref, kwide_ref, sems):
+    slots = kut_ref.shape[0]
+    copies = [
+        pltpu.make_async_copy(kt_hbm, kt_ref, sems.at[0]),
+        pltpu.make_async_copy(kwide_hbm, kwide_ref, sems.at[1]),
+    ]
+    for copy in copies:
+        copy.start()
     zero_ref[...] = jnp.zeros_like(zero_ref)
-    kt_ref, kwide_ref = targets[-2:]
-    copies = []
-    for k in range(loads - 1, -1, -1):
-        copies.append(pltpu.make_async_copy(sources[k], targets[k], sems.at[k]))
-        copies[-1].start()
-    slots = kut_ref.shape[0]
+    for copy in copies:
+        copy.wait()
+    for t in range(slots):
+        ou, ov = to_ref[0, t], to_ref[1, t]
+        rows = slice(t * TV, (t + 1) * TV)
+        kut_ref[t] = kt_ref[pl.ds(2 * TV - ou, SG), :].astype(BF)
+        kvt_ref[:, rows] = kt_ref[pl.ds(2 * TV - ov, SG), :].astype(BF)
+        ku_ref[rows] = pltpu.roll(kwide_ref[...], ou, 1).astype(BF)
+        kv_ref[rows] = pltpu.roll(kwide_ref[...], ov, 1).astype(BF)
+
+
+def screen_kernel(w_ref, _, *rest):
+    loads = (len(rest) - 2) // 2
+    sources, screen_ref = rest[:loads], rest[loads]
+    targets, sems = rest[loads + 1 : -1], rest[-1]
+    copies = [pltpu.make_async_copy(sources[k], targets[k], sems.at[k]) for k in range(loads)]
+    for copy in copies:
+        copy.start()
     w = w_ref[0, 0]
     row = lax.broadcasted_iota(jnp.int32, (SG, 1), 0).astype(F32) - SG / 2.0
     column = lax.broadcasted_iota(jnp.int32, (1, SG), 1).astype(F32) - SG / 2.0
@@ -191,18 +209,13 @@
     screen_ref[1] = sin_v
     for copy in copies:
         copy.wait()
-    for t in range(slots):
-        ou, ov = to_ref[0, t], to_ref[1, t]
-        kut_ref[t] = kt_ref[pl.ds(2 * TV - ou, SG), :].astype(BF)
-        kvt_ref[:, t * TV : (t + 1) * TV] = kt_ref[pl.ds(2 * TV - ov, SG), :].astype(BF)
-        kv_ref[t * TV : (t + 1) * TV] = pltpu.roll(kwide_ref[...], ov, 1).astype(BF)
-
-
-def subgrid_kernel(picks, tc_ref, to_ref, *rest):
+
+
+def subgrid_kernel(picks, tc_ref, *rest):
     parts = len(picks)
     sums = rest[:parts]
-    (obs_ref, pad_ref, padt_ref, kern_ref, screen_ref, kvt_ref, kv_ref, kut_ref) = rest[parts : parts + 8]
-    (out_ref, coef_ref, model_ref, z_ref, res_ref, sems, *rows_refs) = rest[parts + 8 :]
+    (obs_ref, pad_ref, padt_ref, screen_ref, kvt_ref, kv_ref, kut_ref, ku_ref) = rest[parts : parts + 8]
+    (out_ref, coef_ref, model_ref, rows_ref, z_ref, res_ref, sems) = rest[parts + 8 :]
     slots = obs_ref.shape[0]
     count = tc_ref[0, 0]
 
@@ -221,35 +234,30 @@
     model_ref[SG:] = (sc * image_i + ss * image_r).astype(BF)
 
     model = model_ref[...]
-    kern = kern_ref[...]
+    for t0 in range(0, slots, 2):
+        pair = dot(model, kvt_ref[:, t0 * TV : (t0 + 2) * TV]).astype(BF)
+        for t in (t0, t0 + 1):
+            lanes = slice((t - t0) * TV, (t - t0 + 1) * TV)
+            rows_ref[:, 2 * t * TV : (2 * t + 1) * TV] = pair[:SG, lanes]
+            rows_ref[:, (2 * t + 1) * TV : (2 * t + 2) * TV] = pair[SG:, lanes]
     copies = []
-    for t0 in range(0, slots, 2):
-        pair = dot(model, kvt_ref[:, t0 * TV : (t0 + 2) * TV])
-        for t in (t0, t0 + 1):
-            rows_refs[t % len(rows_refs)][...] = pair[:, (t - t0) * TV : (t - t0 + 1) * TV]
-        for t in (t0, t0 + 1):
-            rows_ref = rows_refs[t % len(rows_refs)]
-            ou = to_ref[0, t]
-            wr = rows_ref[pl.ds(ou, 2 * TV), :]
-            wi = rows_ref[pl.ds(SG + ou, 2 * TV), :]
-            window = jnp.concatenate([wr.astype(BF), wi.astype(BF)], axis=1)
-            predicted = dot(kern, window)
-            live = count > t
-            res = []
-            for plane in range(2):
-                value = obs_ref[t, plane].astype(F32) - predicted[:, plane * TV : (plane + 1) * TV]
-                res.append(jnp.where(live, value, 0.0).astype(BF))
-                res_ref[t, plane] = res[plane]
-            z = dot(kut_ref[t], jnp.concatenate(res, axis=1)).astype(BF)
-            z_ref[:SG, t * TV : (t + 1) * TV] = z[:, :TV]
-            z_ref[SG:, t * TV : (t + 1) * TV] = z[:, TV:]
-        if t0 % 4 == 2:
+    for t in range(slots):
+        predicted = dot(ku_ref[t * TV : (t + 1) * TV], rows_ref[:, 2 * t * TV : (2 * t + 2) * TV])
+        live = count > t
+        for plane in range(2):
+            value = obs_ref[t, plane].astype(F32) - predicted[:, plane * TV : (plane + 1) * TV]
+            res_ref[t, plane] = jnp.where(live, value, 0.0).astype(BF)
+        if t % 4 == 3:
             copies.append(
                 pltpu.make_async_copy(
-                    res_ref.at[pl.ds(t0 - 2, 4)], out_ref.at[pl.ds(t0 - 2, 4)], sems.at[t0 // 4]
+                    res_ref.at[pl.ds(t - 3, 4)], out_ref.at[pl.ds(t - 3, 4)], sems.at[t // 4]
                 )
             )
             copies[-1].start()
+    for t in range(slots):
+        z = dot(kut_ref[t], jnp.concatenate([res_ref[t, 0], res_ref[t, 1]], axis=1)).astype(BF)
+        z_ref[:SG, t * TV : (t + 1) * TV] = z[:, :TV]
+        z_ref[SG:, t * TV : (t + 1) * TV] = z[:, TV:]
 
     kv = kv_ref[...]
     ar = dot(z_ref[:SG], kv)
@@ -416,12 +424,14 @@
     first, spec = pl.pallas_call(
         functools.partial(forward_kernel, sends[0][0]),
         out_shape=[held((len(sends[0][0]), 2, M, M)), held(grid_shape, F32)],
-        in_specs=[SMEM] * 3 + [ANY] * 2,
+        in_specs=[SMEM] + [ANY] * 4,
         out_specs=[VMEM] * 2,
         scratch_shapes=[
             pltpu.VMEM((2, F, F), BF),
             pltpu.VMEM((2, F, F), BF),
-            pltpu.SemaphoreType.DMA((4,)),
+            pltpu.SMEM(facet_offsets.shape, jnp.int32),
+            pltpu.SMEM(corners.shape, jnp.int32),
+            pltpu.SemaphoreType.DMA((6,)),
         ],
         compiler_params=params(16),
         name="forward",
@@ -436,7 +446,36 @@
         name="extract",
     )(me, facet_offsets, corners, near(spec))
 
+    def make_bands(after):
+        big = held((slots * TV, SG))
+        return pl.pallas_call(
+            band_kernel,
+            out_shape=[held((SG, slots * TV)), big, held((slots, SG, TV)), big, held((1, M), F32)],
+            in_specs=[SMEM, VMEM] + [ANY] * 2,
+            out_specs=[VMEM] * 5,
+            scratch_shapes=[
+                pltpu.VMEM(kt_np.shape, F32),
+                pltpu.VMEM(kwide_np.shape, F32),
+                pltpu.SemaphoreType.DMA((2,)),
+            ],
+            compiler_params=params(8),
+            name="bands",
+        )(tile_corners, near(after), far(jnp.asarray(kt_np)), far(jnp.asarray(kwide_np)))
+
+    def make_screen(after):
+        loads = [observed, pad_np, pad_np.transpose(0, 2, 1), subgrid_offsets.T, facet_offsets]
+        return pl.pallas_call(
+            screen_kernel,
+            out_shape=[held((2, SG, SG), F32)] + [held(load.shape, load.dtype) for load in loads],
+            in_specs=[SMEM, VMEM] + [ANY] * len(loads),
+            out_specs=[VMEM] * (1 + len(loads)),
+            scratch_shapes=[pltpu.SemaphoreType.DMA((len(loads),))],
+            compiler_params=params(8),
+            name="screen",
+        )(w_terms.reshape(1, 1), near(after), *[far(jnp.asarray(load)) for load in loads])
+
     arrived = []
+    token = None
     for (js, mask), value in zip(sends, [first] + list(own)):
         terms = []
         for got_js, got in arrived:
@@ -446,60 +485,37 @@
                 assert not set(js) & set(got_js)
         if terms:
             total = value.astype(F32)
-            if mask > 2:
-                total = total + prepared[-1]
+            if token is not None:
+                total = total + token
             for term in terms:
                 total = total + term.astype(F32)
             value = total.astype(BF)
-        if mask == 2 and len(js) > 1:
-            loads = [observed, pad_np, pad_np.transpose(0, 2, 1), kern_np]
-            loads += [tile_offsets.T, subgrid_offsets.T, facet_offsets, kt_np, kwide_np]
-            prepared = pl.pallas_call(
-                prepare_kernel,
-                out_shape=[
-                    held((2, SG, SG), F32),
-                    held((SG, slots * TV)),
-                    held((slots * TV, SG)),
-                    held((slots, SG, TV)),
-                ]
-                + [held(load.shape, load.dtype) for load in loads[:-2]]
-                + [held((1, M), F32)],
-                in_specs=[SMEM] * 2 + [VMEM] + [ANY] * len(loads),
-                out_specs=[VMEM] * (3 + len(loads)),
-                scratch_shapes=[
-                    pltpu.VMEM(kt_np.shape, F32),
-                    pltpu.VMEM(kwide_np.shape, F32),
-                    pltpu.SemaphoreType.DMA((len(loads),)),
-                ],
-                compiler_params=params(8),
-                name="prepare",
-            )(w_terms.reshape(1, 1), tile_corners, near(value), *[far(jnp.asarray(load)) for load in loads])
-        got = exchange(value, mask, n)
-        arrived.append(([j ^ mask for j in js], got))
+        arrived.append(([j ^ mask for j in js], exchange(value, mask, n)))
+        if mask == 2 and token is None:
+            kvt, kv, kut, ku, token = make_bands(value)
+    screen, tiles, pad, padt, corners, facet_offsets = make_screen(value)
+    corners, facet_offsets = near(corners), near(facet_offsets)
     last = [(js, got) for js, got in arrived if 0 in js]
-    screen, kvt, kv, kut, tiles, pad, padt, kern = prepared[:8]
-    tile_corners, corners, facet_offsets = [near(value) for value in prepared[8:11]]
 
     residual, coefficient = pl.pallas_call(
         functools.partial(subgrid_kernel, [0] + [js.index(0) for js, _ in last]),
         out_shape=[pltpu.HBM(observed.shape, BF), held((1, 2, M, M))],
-        in_specs=[SMEM] * 2 + [VMEM] * (len(last) + 9),
+        in_specs=[SMEM] + [VMEM] * (len(last) + 9),
         out_specs=[ANY, VMEM],
         scratch_shapes=[
             pltpu.VMEM((2 * SG, SG), BF),
+            pltpu.VMEM((SG, 2 * slots * TV), BF),
             pltpu.VMEM((2 * SG, slots * TV), BF),
             pltpu.VMEM(observed.shape, BF),
             pltpu.SemaphoreType.DMA((slots // 4,)),
-        ]
-        + [pltpu.VMEM((2 * SG, TV), F32)] * 8,
+        ],
         compiler_params=params(24),
         name="subgrid",
     )(
         tile_count.reshape(1, 1),
-        tile_corners,
         near(own[-1]),
         *[near(got) for _, got in last],
-        *[near(value) for value in (tiles, pad, padt, kern, screen, kvt, kv, kut)],
+        *[near(value) for value in (tiles, pad, padt, screen, kvt, kv, kut, ku)],
     )
 
     early = ([0], coefficient)

time: 63.6 us -> 57.1 us (0.90)
  Pallas kernels: 34 us -> 28.4 us
  waiting for transfers between devices: 7.29 us -> 6.02 us
    pallas_call x1, Pallas kernels: 14.4 us -> 7.61 us  [per_device(): pl.pallas_call(functools.partial(subgrid_kernel, [0] + [js.index(0) for j...]
    pallas_call x1 -> x2, Pallas kernels: 4.02 us -> 5.85 us  [the longest x1 4.22 us: make_bands(): pl.pallas_call(band_kernel, out_shape=[held((SG, slots * TV)), big, held(...]
    ppermute x13, waiting for transfers between devices: 7.29 us -> 6.02 us  [exchange(): return lax.ppermute(value, 'facet', [(i, i ^ mask) for i in range(n)])]
    pallas_call x1, Pallas kernels: 5.23 us -> 4.55 us  [per_device(): pl.pallas_call(functools.partial(forward_kernel, sends[0][0]), out_shape=...]
  transfers between devices with their start and end apart: 13 -> 13, of which waited for: 5 -> 4; matrix products, arithmetic and copies ran while one was open for 0% -> 0% of each run, Pallas kernels for 15% -> 20%
where the time goes in v7:
time: 57.1 us; the launch traced here: 56.8 us
  Pallas kernels  28.4 us (50%)
  starting transfers between devices  20.1 us (35%)
  waiting for transfers between devices  6.02 us (11%)
  between operations  2.07 us (4%)
    ppermute x13, starting transfers between devices, exchange(): return lax.ppermute(value, 'facet', [(i, i ^ mask) for i in range(n)])  20.1 us
    pallas_call x1, Pallas kernels, per_device(): pl.pallas_call(functools.partial(subgrid_kernel, [0] + [js.index(0) for j...  7.61 us
    ppermute x13, waiting for transfers between devices, exchange(): return lax.ppermute(value, 'facet', [(i, i ^ mask) for i in range(n)])  6.02 us
    pallas_call x1, Pallas kernels, per_device(): pl.pallas_call(functools.partial(backward_kernel, [late_other[0]]), out_s...  4.87 us
    pallas_call x1, Pallas kernels, per_device(): pl.pallas_call(functools.partial(forward_kernel, sends[0][0]), out_shape=...  4.55 us
    pallas_call x1, Pallas kernels, make_bands(): pl.pallas_call(band_kernel, out_shape=[held((SG, slots * TV)), big, held(...  4.22 us
    pallas_call x1, Pallas kernels, per_device(): pl.pallas_call(functools.partial(extract_kernel, lists), out_shape=[held(...  2.32 us
    pallas_call x1, Pallas kernels, per_device(): pl.pallas_call(functools.partial(next_grid_kernel, [other_js, late_js]),...  1.74 us
  transfers between devices with their start and end apart: 13, of which 4 were waited for; matrix products, arithmetic and copies ran while one was open for 0% of the time, Pallas kernels for 20%

profile of v7, /device:TPU:1, one launch (start us, length us, event | category | flops | bytes accessed | tf_op | source)
XLA Modules:
  0.0 56.8 jit_solution(13195135197140405585)
XLA Ops:
  0.6 4.6 %forward.1 = (bf16[4,2,128,128]{3,2,1,0:T(8,128)(2,1)S(1)}, f32[2,5,640,128]{3,2,1,0:T(8,128)S(1)}) custom-call(s32[1]{0:T(128)} %bitcast.1.me_ref, s32[1,2]{1,0:T(1,128)} %rest_4_.1, s32[2,16]{1,0:T(2,128)} %bitcast.11, bf16[1,2,512,512]{3,2,1,0:T(8,128)(2,1)} %facet_ref.1, bf16[2,512,512]{2,1,0:T(8,128)(2,1)} %constant.14.clone.basis_ref.basis_hbm), custom_call_target="tpu_custom_call" | custom-call | tf_op jit(solution)/shard_map/forward/pallas_call | solution.py:424
  5.2 0.1 collective-permute-start.1
  5.3 2.3 %extract.1 = (bf16[4,2,128,128]{3,2,1,0:T(8,128)(2,1)S(1)}, bf16[3,2,128,128]{3,2,1,0:T(8,128)(2,1)S(1)}, bf16[1,2,128,128]{3,2,1,0:T(8,128)(2,1)S(1)}, bf16[1,2...) custom-call(s32[1]{0:T(128)} %bitcast.1.me_ref, ...), custom_call_target="tpu_custom_call" | custom-call | tf_op jit(solution)/shard_map/extract/pallas_call | solution.py:440
  7.6 0.5 collective-permute-start
  8.2 2.3 %collective-permute-start.3 = (bf16[3,2,128,128]{3,2,1,0:T(8,128)(2,1)S(1)}, bf16[3,2,128,128]{3,2,1,0:T(8,128)(2,1)S(1)}, u32[]{:S(2)}, u32[]{:S(2)}) collective-permute-start(bf16[3,2,128,128]{3,2,1,0:T(8,128)(2,1)S(1)} %add_convert_fusion.1._), channel_id=1, source_target_pairs={{0,2},{1,3},{2,0},{3,1},{4,6},{5,7},{6,4},{7,5},{8,10},{9,11},{10,... | collective-permute-start | bytes 589832 | tf_op jit(solution)/shard_map/ppermute | solution.py:367
  10.6 4.2 %bands.1 = (bf16[512,2048]{1,0:T(8,128)(2,1)S(1)}, bf16[2048,512]{1,0:T(8,128)(2,1)S(1)}, bf16[16,512,128]{2,1,0:T(8,128)(2,1)S(1)}, bf16[2048,512]{1,0:T(8,128)(2,1)S(1)}, f32[1,128]{1,0:T(1,128)S(1)}) custom-call(s32[2,16]{1,0:T(2,128)} %bitcast.14, bf16[3,2,128,128]{3,2,1,0:T(8,128)(2,1)S(1)} %add_convert_fusion.1._, f32[768,128]{1,0:T(8,128)} %constant.15.clone.kt_hbm, ...), custom_call_target="tpu_custom_call" | custom-call | tf_op jit(solution)/shard_map/bands/pallas_call | solution.py:451
  14.8 0.6 %collective-permute-done.3 = bf16[3,2,128,128]{3,2,1,0:T(8,128)(2,1)S(1)} collective-permute-done((bf16[3,2,128,128]{3,2,1,0:T(8,128)(2,1)S(1)}, bf16[3,2,128,128]{3,2,1,0:T(8,128)(2,1)S(1)}, u32[]{:S(2)}, u32[]{:S(2)}) %collective-permute-start.3) | collective-permute-done | bytes 196640 | tf_op jit(solution)/shard_map/ppermute | solution.py:367
  15.4 0.1 add_convert_fusion.2
  15.5 2.3 %collective-permute-start.5 = (bf16[1,2,128,128]{3,2,1,0:T(8,128)(2,1)S(1)}, bf16[1,2,128,128]{3,2,1,0:T(8,128)(2,1)S(1)}, u32[]{:S(2)}, u32[]{:S(2)}) collective-permute-start(bf16[1,2,128,128]{3,2,1,0:T(8,128)(2,1)S(1)} %get-tuple-element.53), channel_id=1, source_target_pairs={{0,8},{1,9},{2,10},{3,11},{4,12},{5,13},{6,14},{7,15},{8,0},{9,1},... | collective-permute-start | bytes 196616 | tf_op jit(solution)/shard_map/ppermute | solution.py:367
  17.8 1.3 %collective-permute-start.4 = (bf16[1,2,128,128]{3,2,1,0:T(8,128)(2,1)S(1)}, bf16[1,2,128,128]{3,2,1,0:T(8,128)(2,1)S(1)}, u32[]{:S(2)}, u32[]{:S(2)}) collective-permute-start(bf16[1,2,128,128]{3,2,1,0:T(8,128)(2,1)S(1)} %get-tuple-element.54), channel_id=1, source_target_pairs={{0,4},{1,5},{2,6},{3,7},{4,0},{5,1},{6,2},{7,3},{8,12},{9,13},{10,... | collective-permute-start | bytes 196616 | tf_op jit(solution)/shard_map/ppermute | solution.py:367
  19.1 1.2 %collective-permute-start.2 = (bf16[1,2,128,128]{3,2,1,0:T(8,128)(2,1)S(1)}, bf16[1,2,128,128]{3,2,1,0:T(8,128)(2,1)S(1)}, u32[]{:S(2)}, u32[]{:S(2)}) collective-permute-start(bf16[1,2,128,128]{3,2,1,0:T(8,128)(2,1)S(1)} %get-tuple-element.55), channel_id=1, source_target_pairs={{0,2},{1,3},{2,0},{3,1},{4,6},{5,7},{6,4},{7,5},{8,10},{9,11},{10,... | collective-permute-start | bytes 196616 | tf_op jit(solution)/shard_map/ppermute | solution.py:367
  21.6 1.6 %screen.1 = (f32[2,512,512]{2,1,0:T(8,128)S(1)}, bf16[16,2,128,128]{3,2,1,0:T(8,128)(2,1)S(1)}, bf16[2,512,128]{2,1,0:T(8,128)(2,1)S(1)}, bf16[2,128,512]{2,1,0:...) custom-call(f32[1,1]{1,0:T(1,128)} %bitcast.7.w_ref, bf16[1,2,128,128]{3,2,1,0:T(8,128)(2,1)S(1)} %get-tuple-element.52._, ...), custom_call_target="tpu_custom_call" | custom-call | tf_op jit(solution)/shard_map/screen/pallas_call | solution.py:467
  23.3 1.9 %collective-permute-done.6.rest_5_ = bf16[1,2,128,128]{3,2,1,0:T(8,128)(2,1)S(1)} collective-permute-done((bf16[1,2,128,128]{3,2,1,0:T(8,128)(2,1)S(1)}, bf16[1,2,128,128]{3,2,1,0:T(8,128)(2,1)S(1)}, u32[]{:S(2)}, u32[]{:S(2)}) %collective-permute-start.6) | collective-permute-done | bytes 65568 | tf_op jit(solution)/shard_map/ppermute | solution.py:367
  25.2 7.6 %subgrid.1 = (bf16[16,2,128,128]{3,2,1,0:T(8,128)(2,1)}, bf16[1,2,128,128]{3,2,1,0:T(8,128)(2,1)S(1)}) custom-call(s32[1,1]{1,0:T(1,128)} %bitcast.8.tc_ref, bf16[1,2,128,128]{3,2,1,0:T(8,128)(2,1)S(1)} %get-tuple-element.28.rest_0_, bf16[4,2,128,128]{3,2,1,0:T(8,128)(2,1)S(1)} %collective-permute-done.rest_1_, ...), custom_call_target="tpu_custom_call" | custom-call | tf_op jit(solution)/shard_map/subgrid/pallas_call | solution.py:500
  32.9 1.4 %collective-permute-start.9 = (bf16[1,2,128,128]{3,2,1,0:T(8,128)(2,1)S(1)}, bf16[1,2,128,128]{3,2,1,0:T(8,128)(2,1)S(1)}, u32[]{:S(2)}, u32[]{:S(2)}) collective-permute-start(bf16[1,2,128,128]{3,2,1,0:T(8,128)(2,1)S(1)} %get-tuple-element.48), channel_id=1, source_target_pairs={{0,12},{1,13},{2,14},{3,15},{4,8},{5,9},{6,10},{7,11},{8,4},{9,5},... | collective-permute-start | bytes 196616 | tf_op jit(solution)/shard_map/ppermute | solution.py:367
  34.3 2.2 %collective-permute-start.7 = (bf16[1,2,128,128]{3,2,1,0:T(8,128)(2,1)S(1)}, bf16[1,2,128,128]{3,2,1,0:T(8,128)(2,1)S(1)}, u32[]{:S(2)}, u32[]{:S(2)}) collective-permute-start(bf16[1,2,128,128]{3,2,1,0:T(8,128)(2,1)S(1)} %get-tuple-element.48), channel_id=1, source_target_pairs={{0,4},{1,5},{2,6},{3,7},{4,0},{5,1},{6,2},{7,3},{8,12},{9,13},{10,... | collective-permute-start | bytes 196616 | tf_op jit(solution)/shard_map/ppermute | solution.py:367
  36.5 2.1 %collective-permute-done.7 = bf16[1,2,128,128]{3,2,1,0:T(8,128)(2,1)S(1)} collective-permute-done((bf16[1,2,128,128]{3,2,1,0:T(8,128)(2,1)S(1)}, bf16[1,2,128,128]{3,2,1,0:T(8,128)(2,1)S(1)}, u32[]{:S(2)}, u32[]{:S(2)}) %collective-permute-start.7) | collective-permute-done | bytes 65568 | tf_op jit(solution)/shard_map/ppermute | solution.py:367
  38.6 1.3 %collective-permute-done.8 = bf16[1,2,128,128]{3,2,1,0:T(8,128)(2,1)S(1)} collective-permute-done((bf16[1,2,128,128]{3,2,1,0:T(8,128)(2,1)S(1)}, bf16[1,2,128,128]{3,2,1,0:T(8,128)(2,1)S(1)}, u32[]{:S(2)}, u32[]{:S(2)}) %collective-permute-start.8) | collective-permute-done | bytes 65568 | tf_op jit(solution)/shard_map/ppermute | solution.py:367
  40.0 0.3 collective-permute-start.10
  40.3 3.9 %collective-permute-start.12 = (bf16[4,2,128,128]{3,2,1,0:T(8,128)(2,1)S(1)}, bf16[4,2,128,128]{3,2,1,0:T(8,128)(2,1)S(1)}, u32[]{:S(2)}, u32[]{:S(2)}) collective-permute-start(bf16[4,2,128,128]{3,2,1,0:T(8,128)(2,1)S(1)} %constant_dynamic-update-slice_fusion.rest_0_), channel_id=1, source_target_pairs={{0,1},{1,0},{2,3},{3,2},{4,5},{5,4},{6,7},{7,6},{8,9},{9,8},{10,11... | collective-permute-start | bytes 786440 | tf_op jit(solution)/shard_map/ppermute | solution.py:367
  44.2 1.4 %grid_first.1 = (f32[2,5,640,128]{3,2,1,0:T(8,128)S(1)}, f32[1,128]{1,0:T(1,128)S(1)}) custom-call(s32[1]{0:T(128)} %bitcast.1.me_ref, s32[1,2]{1,0:T(1,128)S(1)} %get-tuple-element.46.fo_ref, s32[2,16]{1,0:T(2,128)S(1)} %get-tuple-element.47.so_ref, bf16[4,2,128,128]{3,2,1,0:T(8,128)(2,1)S(1)} %constant_dynamic-update-slice_fusion.rest_0_), custom_call_target="tpu_custom_call" | custom-call | tf_op jit(solution)/shard_map/grid_first/pallas_call | solution.py:529
  45.7 4.5 %collective-permute-start.11 = (bf16[4,2,128,128]{3,2,1,0:T(8,128)(2,1)S(1)}, bf16[4,2,128,128]{3,2,1,0:T(8,128)(2,1)S(1)}, u32[]{:S(2)}, u32[]{:S(2)}) collective-permute-start(bf16[4,2,128,128]{3,2,1,0:T(8,128)(2,1)S(1)} %add_convert_fusion.rest_1_), channel_id=1, source_target_pairs={{0,1},{1,0},{2,3},{3,2},{4,5},{5,4},{6,7},{7,6},{8,9},{9,8},{10,11... | collective-permute-start | bytes 786440 | tf_op jit(solution)/shard_map/ppermute | solution.py:367
  50.2 1.7 %grid_next.1.rest_1_ = f32[2,5,640,128]{3,2,1,0:T(8,128)S(1)} custom-call(s32[1]{0:T(128)} %bitcast.1.me_ref, s32[1,2]{1,0:T(1,128)S(1)} %get-tuple-element.46.fo_ref, s32[2,16]{1,0:T(2,128)S(1)} %get-tuple-element.47.so_ref, bf16[4,2,128,128]{3,2,1,0:T(8,128)(2,1)S(1)} %collective-permute-done.12.rest_0_, ...), custom_call_target="tpu_custom_call", output_to_operand_aliasing={{}: (5, {})} | custom-call | tf_op jit(solution)/shard_map/grid_next/pallas_call | solution.py:539
  51.9 4.9 %backward.1 = (bf16[1,2,512,512]{3,2,1,0:T(8,128)(2,1)}, f32[2,5,640,128]{3,2,1,0:T(8,128)S(1)}) custom-call(s32[1]{0:T(128)} %bitcast.1.me_ref, s32[1,2]{1,0:T(1,128)S(1)} %get-tuple-element.46.fo_ref, s32[2,16]{1,0:T(2,128)S(1)} %get-tuple-element.47.so_ref, ...), custom_call_target="tpu_custom_call", output_to_operand_aliasing={{1}: (5, {})} | custom-call | tf_op jit(solution)/shard_map/backward/pallas_call | solution.py:548
  (17 shorter events, 0.2 us)
Async XLA Ops:
  5.2 3.0 %collective-permute-start.1 = (bf16[4,2,128,128]{3,2,1,0:T(8,128)(2,1)S(1)}, bf16[4,2,128,128]{3,2,1,0:T(8,128)(2,1)S(1)}, u32[]{:S(2)}, u32[]{:S(2)}) collective-permute-start(bf16[4,2,128,128]{3,2,1,0:T(8,128)(2,1)S(1)} %get-tuple-element.32), channel_id=1, source_target_pairs={{0,1},{1,0},{2,3},{3,2},{4,5},{5,4},{6,7},{7,6},{8,9},{9,8},{10,11... | collective-permute-start | bytes 786440 | tf_op jit(solution)/shard_map/ppermute | solution.py:367
  7.6 7.1 %collective-permute-start = (bf16[4,2,128,128]{3,2,1,0:T(8,128)(2,1)S(1)}, bf16[4,2,128,128]{3,2,1,0:T(8,128)(2,1)S(1)}, u32[]{:S(2)}, u32[]{:S(2)}) collective-permute-start(bf16[4,2,128,128]{3,2,1,0:T(8,128)(2,1)S(1)} %get-tuple-element.29), channel_id=1, source_target_pairs={{0,1},{1,0},{2,3},{3,2},{4,5},{5,4},{6,7},{7,6},{8,9},{9,8},{10,11... | collective-permute-start | bytes 786440 | tf_op jit(solution)/shard_map/ppermute | solution.py:367
  8.2 7.2 %collective-permute-start.3 = (bf16[3,2,128,128]{3,2,1,0:T(8,128)(2,1)S(1)}, bf16[3,2,128,128]{3,2,1,0:T(8,128)(2,1)S(1)}, u32[]{:S(2)}, u32[]{:S(2)}) collective-permute-start(bf16[3,2,128,128]{3,2,1,0:T(8,128)(2,1)S(1)} %add_convert_fusion.1._), channel_id=1, source_target_pairs={{0,2},{1,3},{2,0},{3,1},{4,6},{5,7},{6,4},{7,5},{8,10},{9,11},{10,... | collective-permute-start | bytes 589832 | tf_op jit(solution)/shard_map/ppermute | solution.py:367
  15.5 7.8 %collective-permute-start.5 = (bf16[1,2,128,128]{3,2,1,0:T(8,128)(2,1)S(1)}, bf16[1,2,128,128]{3,2,1,0:T(8,128)(2,1)S(1)}, u32[]{:S(2)}, u32[]{:S(2)}) collective-permute-start(bf16[1,2,128,128]{3,2,1,0:T(8,128)(2,1)S(1)} %get-tuple-element.53), channel_id=1, source_target_pairs={{0,8},{1,9},{2,10},{3,11},{4,12},{5,13},{6,14},{7,15},{8,0},{9,1},... | collective-permute-start | bytes 196616 | tf_op jit(solution)/shard_map/ppermute | solution.py:367
  17.8 5.5 %collective-permute-start.4 = (bf16[1,2,128,128]{3,2,1,0:T(8,128)(2,1)S(1)}, bf16[1,2,128,128]{3,2,1,0:T(8,128)(2,1)S(1)}, u32[]{:S(2)}, u32[]{:S(2)}) collective-permute-start(bf16[1,2,128,128]{3,2,1,0:T(8,128)(2,1)S(1)} %get-tuple-element.54), channel_id=1, source_target_pairs={{0,4},{1,5},{2,6},{3,7},{4,0},{5,1},{6,2},{7,3},{8,12},{9,13},{10,... | collective-permute-start | bytes 196616 | tf_op jit(solution)/shard_map/ppermute | solution.py:367
  19.1 4.2 %collective-permute-start.2 = (bf16[1,2,128,128]{3,2,1,0:T(8,128)(2,1)S(1)}, bf16[1,2,128,128]{3,2,1,0:T(8,128)(2,1)S(1)}, u32[]{:S(2)}, u32[]{:S(2)}) collective-permute-start(bf16[1,2,128,128]{3,2,1,0:T(8,128)(2,1)S(1)} %get-tuple-element.55), channel_id=1, source_target_pairs={{0,2},{1,3},{2,0},{3,1},{4,6},{5,7},{6,4},{7,5},{8,10},{9,11},{10,... | collective-permute-start | bytes 196616 | tf_op jit(solution)/shard_map/ppermute | solution.py:367
  20.3 4.9 %collective-permute-start.6 = (bf16[1,2,128,128]{3,2,1,0:T(8,128)(2,1)S(1)}, bf16[1,2,128,128]{3,2,1,0:T(8,128)(2,1)S(1)}, u32[]{:S(2)}, u32[]{:S(2)}) collective-permute-start(bf16[1,2,128,128]{3,2,1,0:T(8,128)(2,1)S(1)} %get-tuple-element.52._), channel_id=1, source_target_pairs={{0,12},{1,13},{2,14},{3,15},{4,8},{5,9},{6,10},{7,11},{8,4},{9,5},... | collective-permute-start | bytes 196616 | tf_op jit(solution)/shard_map/ppermute | solution.py:367
  32.9 7.1 %collective-permute-start.9 = (bf16[1,2,128,128]{3,2,1,0:T(8,128)(2,1)S(1)}, bf16[1,2,128,128]{3,2,1,0:T(8,128)(2,1)S(1)}, u32[]{:S(2)}, u32[]{:S(2)}) collective-permute-start(bf16[1,2,128,128]{3,2,1,0:T(8,128)(2,1)S(1)} %get-tuple-element.48), channel_id=1, source_target_pairs={{0,12},{1,13},{2,14},{3,15},{4,8},{5,9},{6,10},{7,11},{8,4},{9,5},... | collective-permute-start | bytes 196616 | tf_op jit(solution)/shard_map/ppermute | solution.py:367
  34.3 5.7 %collective-permute-start.8 = (bf16[1,2,128,128]{3,2,1,0:T(8,128)(2,1)S(1)}, bf16[1,2,128,128]{3,2,1,0:T(8,128)(2,1)S(1)}, u32[]{:S(2)}, u32[]{:S(2)}) collective-permute-start(bf16[1,2,128,128]{3,2,1,0:T(8,128)(2,1)S(1)} %get-tuple-element.48), channel_id=1, source_target_pairs={{0,8},{1,9},{2,10},{3,11},{4,12},{5,13},{6,14},{7,15},{8,0},{9,1},... | collective-permute-start | bytes 196616 | tf_op jit(solution)/shard_map/ppermute | solution.py:367
  34.3 4.3 %collective-permute-start.7 = (bf16[1,2,128,128]{3,2,1,0:T(8,128)(2,1)S(1)}, bf16[1,2,128,128]{3,2,1,0:T(8,128)(2,1)S(1)}, u32[]{:S(2)}, u32[]{:S(2)}) collective-permute-start(bf16[1,2,128,128]{3,2,1,0:T(8,128)(2,1)S(1)} %get-tuple-element.48), channel_id=1, source_target_pairs={{0,4},{1,5},{2,6},{3,7},{4,0},{5,1},{6,2},{7,3},{8,12},{9,13},{10,... | collective-permute-start | bytes 196616 | tf_op jit(solution)/shard_map/ppermute | solution.py:367
  40.0 5.6 %collective-permute-start.10 = (bf16[4,2,128,128]{3,2,1,0:T(8,128)(2,1)S(1)}, bf16[4,2,128,128]{3,2,1,0:T(8,128)(2,1)S(1)}, u32[]{:S(2)}, u32[]{:S(2)}) collective-permute-start(bf16[4,2,128,128]{3,2,1,0:T(8,128)(2,1)S(1)} %constant_dynamic-update-slice_fusion.rest_0_), channel_id=1, source_target_pairs={{0,2},{1,3},{2,0},{3,1},{4,6},{5,7},{6,4},{7,5},{8,10},{9,11},{10,... | collective-permute-start | bytes 786440 | tf_op jit(solution)/shard_map/ppermute | solution.py:367
  40.3 9.9 %collective-permute-start.12 = (bf16[4,2,128,128]{3,2,1,0:T(8,128)(2,1)S(1)}, bf16[4,2,128,128]{3,2,1,0:T(8,128)(2,1)S(1)}, u32[]{:S(2)}, u32[]{:S(2)}) collective-permute-start(bf16[4,2,128,128]{3,2,1,0:T(8,128)(2,1)S(1)} %constant_dynamic-update-slice_fusion.rest_0_), channel_id=1, source_target_pairs={{0,1},{1,0},{2,3},{3,2},{4,5},{5,4},{6,7},{7,6},{8,9},{9,8},{10,11... | collective-permute-start | bytes 786440 | tf_op jit(solution)/shard_map/ppermute | solution.py:367
  45.7 6.2 %collective-permute-start.11 = (bf16[4,2,128,128]{3,2,1,0:T(8,128)(2,1)S(1)}, bf16[4,2,128,128]{3,2,1,0:T(8,128)(2,1)S(1)}, u32[]{:S(2)}, u32[]{:S(2)}) collective-permute-start(bf16[4,2,128,128]{3,2,1,0:T(8,128)(2,1)S(1)} %add_convert_fusion.rest_1_), channel_id=1, source_target_pairs={{0,1},{1,0},{2,3},{3,2},{4,5},{5,4},{6,7},{7,6},{8,9},{9,8},{10,11... | collective-permute-start | bytes 786440 | tf_op jit(solution)/shard_map/ppermute | solution.py:367

commit v8 on v7

--- a/solution.py
+++ b/solution.py
@@ -132,6 +132,7 @@
 
 
 def extract_kernel(sends, me_ref, fo_ref, so_ref, spec_ref, *outs):
+    outs = outs[-len(sends) :]
     extract(sends, outs, me_ref, fo_ref, so_ref, spec_ref)
 
 
@@ -293,21 +294,22 @@
         for_blocks(block, in_ref, js)
 
 
-def first_grid_kernel(pieces, me_ref, fo_ref, so_ref, *rest):
-    grid_ref, zero_ref = rest[-2:]
+def first_grid_kernel(pieces, me_ref, fo_ref, so_ref, basis_hbm, *rest):
+    grid_ref, zero_ref, basis_ref, sem = rest[-4:]
+    load = pltpu.make_async_copy(basis_hbm, basis_ref, sem)
+    load.start()
     zero_ref[...] = jnp.zeros_like(zero_ref)
     grid_ref[...] = jnp.zeros_like(grid_ref)
-    grid_blocks(pieces, rest[:-2], me_ref, fo_ref, so_ref, grid_ref)
+    grid_blocks(pieces, rest[:-4], me_ref, fo_ref, so_ref, grid_ref)
+    load.wait()
 
 
 def next_grid_kernel(pieces, me_ref, fo_ref, so_ref, *rest):
     grid_blocks(pieces, rest[:-2], me_ref, fo_ref, so_ref, rest[-2])
 
 
-def backward_kernel(pieces, me_ref, fo_ref, so_ref, basis_hbm, *rest):
-    grid_ref, out_ref, _, basis_ref, out_buf, sems = rest[len(pieces) :]
-    load = pltpu.make_async_copy(basis_hbm, basis_ref, sems.at[2 * OUT_CHUNKS])
-    load.start()
+def backward_kernel(pieces, me_ref, fo_ref, so_ref, basis_ref, *rest):
+    grid_ref, out_ref, _, out_buf, sems = rest[len(pieces) :]
     grid_blocks(pieces, rest[: len(pieces)], me_ref, fo_ref, so_ref, grid_ref)
     columns = F // M
     folded = []
@@ -320,7 +322,6 @@
             top = strip[:M] + strip[F:]
             strips.append(jnp.concatenate([top.astype(BF), strip[M:F].astype(BF)], axis=0))
         folded.append(jnp.concatenate(strips, axis=1))
-    load.wait()
     br, bi = basis_ref[0], basis_ref[1]
     hr, hi = mul_right(br, -bi, *folded)
     hr, hi = hr.astype(BF), hi.astype(BF)
@@ -377,17 +378,12 @@
 
 
 def reduce_sends(n):
-    levels = digit_levels(n)
     sends = []
-    for k, (base, radix) in enumerate(levels):
+    for base, radix in digit_levels(n):
         for g in range(1, radix):
             js = [j for j in range(0, n, base) if (j // base) % radix == g]
-            if k + 1 < len(levels):
-                after, width = levels[k + 1]
-                groups = [[j for j in js if (j // after) % width], [j for j in js if not (j // after) % width]]
-            else:
-                groups = [js]
-            sends += [(group, g * base) for group in groups if group]
+            groups = [js[1::2], js[::2]] if base == 1 else [js]
+            sends += [(group, g * base) for group in groups]
     return sends
 
 
@@ -436,15 +432,15 @@
         compiler_params=params(16),
         name="forward",
     )(me, facet_offsets, corners, far(facets), basis)
-    lists = [js for js, _ in sends[1:]] + [[0]]
-    own = pl.pallas_call(
-        functools.partial(extract_kernel, lists),
-        out_shape=[held((len(js), 2, M, M)) for js in lists],
-        in_specs=[SMEM] * 3 + [VMEM],
-        out_specs=[VMEM] * len(lists),
-        compiler_params=params(8),
-        name="extract",
-    )(me, facet_offsets, corners, near(spec))
+    def make_blocks(lists, after):
+        return pl.pallas_call(
+            functools.partial(extract_kernel, lists),
+            out_shape=[held((len(js), 2, M, M)) for js in lists],
+            in_specs=[SMEM] * 3 + [VMEM] * (1 + len(after)),
+            out_specs=[VMEM] * len(lists),
+            compiler_params=params(8),
+            name="extract",
+        )(me, facet_offsets, corners, near(spec), *[near(value) for value in after])
 
     def make_bands(after):
         big = held((slots * TV, SG))
@@ -475,24 +471,29 @@
         )(w_terms.reshape(1, 1), near(after), *[far(jnp.asarray(load)) for load in loads])
 
     arrived = []
-    token = None
-    for (js, mask), value in zip(sends, [first] + list(own)):
-        terms = []
+
+    def send(js, mask, value, token=None):
+        total = value.astype(F32)
+        if token is not None:
+            total = total + token
         for got_js, got in arrived:
             if set(js) <= set(got_js):
-                terms.append(pick(got, [got_js.index(j) for j in js]))
+                total = total + pick(got, [got_js.index(j) for j in js]).astype(F32)
             else:
                 assert not set(js) & set(got_js)
-        if terms:
-            total = value.astype(F32)
-            if token is not None:
-                total = total + token
-            for term in terms:
-                total = total + term.astype(F32)
-            value = total.astype(BF)
+        value = total.astype(BF)
         arrived.append(([j ^ mask for j in js], exchange(value, mask, n)))
-        if mask == 2 and token is None:
-            kvt, kv, kut, ku, token = make_bands(value)
+        return value
+
+    (urgent, _), (lazy, _), (beside, _) = sends[:3]
+    send(urgent, 1, first)
+    beside_own, lazy_own = make_blocks([beside, lazy], [])
+    value = send(beside, 2, beside_own)
+    send(lazy, 1, lazy_own)
+    own = make_blocks([js for js, _ in sends[3:]] + [[0]], [value])
+    kvt, kv, kut, ku, token = make_bands(value)
+    for (js, mask), value in zip(sends[3:], own):
+        value = send(js, mask, value, token)
     screen, tiles, pad, padt, corners, facet_offsets = make_screen(value)
     corners, facet_offsets = near(corners), near(facet_offsets)
     last = [(js, got) for js, got in arrived if 0 in js]
@@ -522,43 +523,50 @@
     for base, radix in reversed(digit_levels(n)[2:]):
         js, value = early
         more = [([j ^ (g * base) for j in js], exchange(value, g * base, n)) for g in range(1, radix)]
-        early = join([early] + more)
-    js, value = early
-    late_js, late = [j ^ 2 for j in js], exchange(value, 2, n)
-    other_js, other = [j ^ 1 for j in js], exchange(value, 1, n)
-    grid, token = pl.pallas_call(
-        functools.partial(first_grid_kernel, [js]),
-        out_shape=[held(grid_shape, F32), held((1, M), F32)],
-        in_specs=[SMEM] * 3 + [VMEM],
-        out_specs=[VMEM] * 2,
+        early_parts = [join([early, more[0]]), join(more[1:])]
+        early = join(early_parts)
+
+    def hop(part, mask):
+        return [j ^ mask for j in part[0]], exchange(part[1], mask, n)
+
+    a, b = early_parts
+    late_a, late_b = hop(a, 2), hop(b, 2)
+    ready = [a, b, hop(a, 1), hop(b, 1)]
+    grid, token, basis_near = pl.pallas_call(
+        functools.partial(first_grid_kernel, [js for js, _ in ready]),
+        out_shape=[held(grid_shape, F32), held((1, M), F32), held(basis.shape)],
+        in_specs=[SMEM] * 3 + [ANY] + [VMEM] * len(ready),
+        out_specs=[VMEM] * 3,
+        scratch_shapes=[pltpu.SemaphoreType.DMA(())],
         compiler_params=params(8),
         name="grid_first",
-    )(me, facet_offsets, corners, near(value))
-    late = (late.astype(F32) + token).astype(BF)
-    late_other = ([j ^ 1 for j in late_js], exchange(late, 1, n))
+    )(me, facet_offsets, corners, basis, *[near(value) for _, value in ready])
+    late_a_other = hop(late_a, 1)
+    late_b = (late_b[0], (late_b[1].astype(F32) + token).astype(BF))
+    late_b_other = hop(late_b, 1)
+    ready = [late_a, late_a_other, late_b]
     grid = pl.pallas_call(
-        functools.partial(next_grid_kernel, [other_js, late_js]),
+        functools.partial(next_grid_kernel, [js for js, _ in ready]),
         out_shape=held(grid_shape, F32),
-        in_specs=[SMEM] * 3 + [VMEM] * 3,
+        in_specs=[SMEM] * 3 + [VMEM] * (len(ready) + 1),
         out_specs=VMEM,
-        input_output_aliases={5: 0},
+        input_output_aliases={3 + len(ready): 0},
         compiler_params=params(8),
         name="grid_next",
-    )(me, facet_offsets, corners, near(other), near(late), near(grid))
+    )(me, facet_offsets, corners, *[near(value) for _, value in ready], near(grid))
     update = pl.pallas_call(
-        functools.partial(backward_kernel, [late_other[0]]),
+        functools.partial(backward_kernel, [late_b_other[0]]),
         out_shape=[pltpu.HBM(facets.shape, BF), held(grid_shape, F32)],
-        in_specs=[SMEM] * 3 + [ANY] + [VMEM] * 2,
+        in_specs=[SMEM] * 3 + [VMEM] * 3,
         out_specs=[ANY, VMEM],
         input_output_aliases={5: 1},
         scratch_shapes=[
             pltpu.VMEM((2, F, F), BF),
-            pltpu.VMEM((2, F, F), BF),
-            pltpu.SemaphoreType.DMA((2 * OUT_CHUNKS + 1,)),
+            pltpu.SemaphoreType.DMA((2 * OUT_CHUNKS,)),
         ],
         compiler_params=params(16),
         name="backward",
-    )(me, facet_offsets, corners, basis, near(late_other[1]), near(grid))[0]
+    )(me, facet_offsets, corners, near(basis_near), near(late_b_other[1]), near(grid))[0]
     return (residual, update)
 
 

time: 57.1 us -> 56.7 us (level)
  waiting for transfers between devices: 6.02 us -> 5.01 us
    ppermute x13 -> x15, waiting for transfers between devices: 6.02 us -> 5.01 us  [exchange(): return lax.ppermute(value, 'facet', [(i, i ^ mask) for i in range(n)])]
    pallas_call x4 -> x5, Pallas kernels: 10.3 us -> 10.8 us  [the longest x1 4.07 us: per_device(): pl.pallas_call(functools.partial(backward_kernel, [late_b_other[0]]), out...]
    ppermute x13 -> x15, starting transfers between devices: 20.1 us -> 20.1 us  [exchange(): return lax.ppermute(value, 'facet', [(i, i ^ mask) for i in range(n)])]
  transfers between devices with their start and end apart: 13 -> 15, of which waited for: 4 -> 3; matrix products, arithmetic and copies ran while one was open for 0% -> 0% of each run, Pallas kernels for 20% -> 22%
where the time goes in v8:
time: 56.7 us; the launch traced here: 56.4 us
  Pallas kernels  28.8 us (51%)
  starting transfers between devices  20.1 us (35%)
  waiting for transfers between devices  5.01 us (9%)
  between operations  2.25 us (4%)
    ppermute x15, starting transfers between devices, exchange(): return lax.ppermute(value, 'facet', [(i, i ^ mask) for i in range(n)])  20.1 us
    pallas_call x1, Pallas kernels, per_device(): pl.pallas_call(functools.partial(subgrid_kernel, [0] + [js.index(0) for j...  7.61 us
    ppermute x15, waiting for transfers between devices, exchange(): return lax.ppermute(value, 'facet', [(i, i ^ mask) for i in range(n)])  5.01 us
    pallas_call x1, Pallas kernels, per_device(): pl.pallas_call(functools.partial(forward_kernel, sends[0][0]), out_shape=...  4.56 us
    pallas_call x1, Pallas kernels, make_bands(): pl.pallas_call(band_kernel, out_shape=[held((SG, slots * TV)), big, held(...  4.23 us
    pallas_call x1, Pallas kernels, per_device(): pl.pallas_call(functools.partial(backward_kernel, [late_b_other[0]]), out...  4.07 us
    pallas_call x2, Pallas kernels, make_blocks(): pl.pallas_call(functools.partial(extract_kernel, lists), out_shape=[held(...  3.11 us
    pallas_call x1, Pallas kernels, per_device(): pl.pallas_call(functools.partial(first_grid_kernel, [js for js, _ in read...  2.13 us
  transfers between devices with their start and end apart: 15, of which 3 were waited for; matrix products, arithmetic and copies ran while one was open for 0% of the time, Pallas kernels for 22%

profile of v8, /device:TPU:1, one launch (start us, length us, event | category | flops | bytes accessed | tf_op | source)
XLA Modules:
  0.0 56.4 jit_solution(3641818526496616779)
XLA Ops:
  0.6 4.6 %forward.1 = (bf16[4,2,128,128]{3,2,1,0:T(8,128)(2,1)S(1)}, f32[2,5,640,128]{3,2,1,0:T(8,128)S(1)}) custom-call(s32[1]{0:T(128)} %bitcast.1.me_ref, s32[1,2]{1,0:T(1,128)} %rest_4_.1, s32[2,16]{1,0:T(2,128)} %bitcast.11, bf16[1,2,512,512]{3,2,1,0:T(8,128)(2,1)} %facet_ref.1, bf16[2,512,512]{2,1,0:T(8,128)(2,1)} %constant.14.clone.basis_ref.basis_hbm), custom_call_target="tpu_custom_call" | custom-call | tf_op jit(solution)/shard_map/forward/pallas_call | solution.py:420
  5.2 0.1 collective-permute-start
  5.3 2.1 %extract.2 = (bf16[4,2,128,128]{3,2,1,0:T(8,128)(2,1)S(1)}, bf16[4,2,128,128]{3,2,1,0:T(8,128)(2,1)S(1)}) custom-call(s32[1]{0:T(128)} %bitcast.1.me_ref, s32[1,2]{1,0:T(1,128)} %rest_4_.1, s32[2,16]{1,0:T(2,128)} %bitcast.12, f32[2,5,640,128]{3,2,1,0:T(8,128)S(1)} %get-tuple-element.27.spec_ref), custom_call_target="tpu_custom_call" | custom-call | tf_op jit(solution)/shard_map/extract/pallas_call | solution.py:436
  7.4 0.5 collective-permute-start.2
  8.0 2.3 %collective-permute-start.1 = (bf16[4,2,128,128]{3,2,1,0:T(8,128)(2,1)S(1)}, bf16[4,2,128,128]{3,2,1,0:T(8,128)(2,1)S(1)}, u32[]{:S(2)}, u32[]{:S(2)}) collective-permute-start(bf16[4,2,128,128]{3,2,1,0:T(8,128)(2,1)S(1)} %add_convert_fusion.outs_0_._), channel_id=1, source_target_pairs={{0,2},{1,3},{2,0},{3,1},{4,6},{5,7},{6,4},{7,5},{8,10},{9,11},{10,... | collective-permute-start | bytes 786440 | tf_op jit(solution)/shard_map/ppermute | solution.py:368
  10.3 1.1 %extract.3 = (bf16[1,2,128,128]{3,2,1,0:T(8,128)(2,1)S(1)}, bf16[1,2,128,128]{3,2,1,0:T(8,128)(2,1)S(1)}, bf16[1,2,128,128]{3,2,1,0:T(8,128)(2,1)S(1)}, bf16[1,2,128,128]{3,2,1,0:T(8,128)(2,1)S(1)}) custom-call(s32[1]{0:T(128)} %bitcast.1.me_ref, s32[1,2]{1,0:T(1,128)} %rest_4_.1, s32[2,16]{1,0:T(2,128)} %bitcast.13, ...), custom_call_target="tpu_custom_call" | custom-call | tf_op jit(solution)/shard_map/extract/pallas_call | solution.py:436
  11.4 4.2 %bands.1 = (bf16[512,2048]{1,0:T(8,128)(2,1)S(1)}, bf16[2048,512]{1,0:T(8,128)(2,1)S(1)}, bf16[16,512,128]{2,1,0:T(8,128)(2,1)S(1)}, bf16[2048,512]{1,0:T(8,128)(2,1)S(1)}, f32[1,128]{1,0:T(1,128)S(1)}) custom-call(s32[2,16]{1,0:T(2,128)} %bitcast.15, bf16[4,2,128,128]{3,2,1,0:T(8,128)(2,1)S(1)} %add_convert_fusion.outs_0_._, ...), custom_call_target="tpu_custom_call" | custom-call | tf_op jit(solution)/shard_map/bands/pallas_call | solution.py:447
  15.6 0.9 %collective-permute-done.1.rest_1_ = bf16[4,2,128,128]{3,2,1,0:T(8,128)(2,1)S(1)} collective-permute-done((bf16[4,2,128,128]{3,2,1,0:T(8,128)(2,1)S(1)}, bf16[4,2,128,128]{3,2,1,0:T(8,128)(2,1)S(1)}, u32[]{:S(2)}, u32[]{:S(2)}) %collective-permute-start.1) | collective-permute-done | bytes 262176 | tf_op jit(solution)/shard_map/ppermute | solution.py:368
  16.6 2.3 %collective-permute-start.4 = (bf16[1,2,128,128]{3,2,1,0:T(8,128)(2,1)S(1)}, bf16[1,2,128,128]{3,2,1,0:T(8,128)(2,1)S(1)}, u32[]{:S(2)}, u32[]{:S(2)}) collective-permute-start(bf16[1,2,128,128]{3,2,1,0:T(8,128)(2,1)S(1)} %get-tuple-element.53), channel_id=1, source_target_pairs={{0,8},{1,9},{2,10},{3,11},{4,12},{5,13},{6,14},{7,15},{8,0},{9,1},... | collective-permute-start | bytes 196616 | tf_op jit(solution)/shard_map/ppermute | solution.py:368
  18.9 1.3 %collective-permute-start.3 = (bf16[1,2,128,128]{3,2,1,0:T(8,128)(2,1)S(1)}, bf16[1,2,128,128]{3,2,1,0:T(8,128)(2,1)S(1)}, u32[]{:S(2)}, u32[]{:S(2)}) collective-permute-start(bf16[1,2,128,128]{3,2,1,0:T(8,128)(2,1)S(1)} %get-tuple-element.54), channel_id=1, source_target_pairs={{0,4},{1,5},{2,6},{3,7},{4,0},{5,1},{6,2},{7,3},{8,12},{9,13},{10,... | collective-permute-start | bytes 196616 | tf_op jit(solution)/shard_map/ppermute | solution.py:368
  21.6 1.6 %screen.1 = (f32[2,512,512]{2,1,0:T(8,128)S(1)}, bf16[16,2,128,128]{3,2,1,0:T(8,128)(2,1)S(1)}, bf16[2,512,128]{2,1,0:T(8,128)(2,1)S(1)}, bf16[2,128,512]{2,1,0:...) custom-call(f32[1,1]{1,0:T(1,128)} %bitcast.7.w_ref, bf16[1,2,128,128]{3,2,1,0:T(8,128)(2,1)S(1)} %get-tuple-element.52._, ...), custom_call_target="tpu_custom_call" | custom-call | tf_op jit(solution)/shard_map/screen/pallas_call | solution.py:463
  23.2 1.9 %collective-permute-done.5.rest_5_ = bf16[1,2,128,128]{3,2,1,0:T(8,128)(2,1)S(1)} collective-permute-done((bf16[1,2,128,128]{3,2,1,0:T(8,128)(2,1)S(1)}, bf16[1,2,128,128]{3,2,1,0:T(8,128)(2,1)S(1)}, u32[]{:S(2)}, u32[]{:S(2)}) %collective-permute-start.5) | collective-permute-done | bytes 65568 | tf_op jit(solution)/shard_map/ppermute | solution.py:368
  25.2 7.6 %subgrid.1 = (bf16[16,2,128,128]{3,2,1,0:T(8,128)(2,1)}, bf16[1,2,128,128]{3,2,1,0:T(8,128)(2,1)S(1)}) custom-call(s32[1,1]{1,0:T(1,128)} %bitcast.8.tc_ref, bf16[1,2,128,128]{3,2,1,0:T(8,128)(2,1)S(1)} %get-tuple-element.30.rest_0_, bf16[4,2,128,128]{3,2,1,0:T(8,128)(2,1)S(1)} %collective-permute-done.1.rest_1_, ...), custom_call_target="tpu_custom_call" | custom-call | tf_op jit(solution)/shard_map/subgrid/pallas_call | solution.py:501
  32.8 1.4 %collective-permute-start.8 = (bf16[1,2,128,128]{3,2,1,0:T(8,128)(2,1)S(1)}, bf16[1,2,128,128]{3,2,1,0:T(8,128)(2,1)S(1)}, u32[]{:S(2)}, u32[]{:S(2)}) collective-permute-start(bf16[1,2,128,128]{3,2,1,0:T(8,128)(2,1)S(1)} %get-tuple-element.47), channel_id=1, source_target_pairs={{0,12},{1,13},{2,14},{3,15},{4,8},{5,9},{6,10},{7,11},{8,4},{9,5},... | collective-permute-start | bytes 196616 | tf_op jit(solution)/shard_map/ppermute | solution.py:368
  34.2 2.2 %collective-permute-start.6 = (bf16[1,2,128,128]{3,2,1,0:T(8,128)(2,1)S(1)}, bf16[1,2,128,128]{3,2,1,0:T(8,128)(2,1)S(1)}, u32[]{:S(2)}, u32[]{:S(2)}) collective-permute-start(bf16[1,2,128,128]{3,2,1,0:T(8,128)(2,1)S(1)} %get-tuple-element.47), channel_id=1, source_target_pairs={{0,4},{1,5},{2,6},{3,7},{4,0},{5,1},{6,2},{7,3},{8,12},{9,13},{10,... | collective-permute-start | bytes 196616 | tf_op jit(solution)/shard_map/ppermute | solution.py:368
  36.4 2.1 %collective-permute-done.6 = bf16[1,2,128,128]{3,2,1,0:T(8,128)(2,1)S(1)} collective-permute-done((bf16[1,2,128,128]{3,2,1,0:T(8,128)(2,1)S(1)}, bf16[1,2,128,128]{3,2,1,0:T(8,128)(2,1)S(1)}, u32[]{:S(2)}, u32[]{:S(2)}) %collective-permute-start.6) | collective-permute-done | bytes 65568 | tf_op jit(solution)/shard_map/ppermute | solution.py:368
  38.5 1.3 %collective-permute-start.13 = (bf16[2,2,128,128]{3,2,1,0:T(8,128)(2,1)S(1)}, bf16[2,2,128,128]{3,2,1,0:T(8,128)(2,1)S(1)}, u32[]{:S(2)}, u32[]{:S(2)}) collective-permute-start(bf16[2,2,128,128]{3,2,1,0:T(8,128)(2,1)S(1)} %constant_dynamic-update-slice_fusion.rest_0_), channel_id=1, source_target_pairs={{0,2},{1,3},{2,0},{3,1},{4,6},{5,7},{6,4},{7,5},{8,10},{9,11},{10,... | collective-permute-start | bytes 393224 | tf_op jit(solution)/shard_map/ppermute | solution.py:368
  39.8 4.5 %collective-permute-start.9 = (bf16[2,2,128,128]{3,2,1,0:T(8,128)(2,1)S(1)}, bf16[2,2,128,128]{3,2,1,0:T(8,128)(2,1)S(1)}, u32[]{:S(2)}, u32[]{:S(2)}) collective-permute-start(bf16[2,2,128,128]{3,2,1,0:T(8,128)(2,1)S(1)} %constant_dynamic-update-slice_fusion.rest_0_), channel_id=1, source_target_pairs={{0,1},{1,0},{2,3},{3,2},{4,5},{5,4},{6,7},{7,6},{8,9},{9,8},{10,11... | collective-permute-start | bytes 393224 | tf_op jit(solution)/shard_map/ppermute | solution.py:368
  44.4 0.3 collective-permute-start.11
  44.7 3.2 %collective-permute-start.14 = (bf16[2,2,128,128]{3,2,1,0:T(8,128)(2,1)S(1)}, bf16[2,2,128,128]{3,2,1,0:T(8,128)(2,1)S(1)}, u32[]{:S(2)}, u32[]{:S(2)}) collective-permute-start(bf16[2,2,128,128]{3,2,1,0:T(8,128)(2,1)S(1)} %collective-permute-done.13.rest_0_), channel_id=1, source_target_pairs={{0,1},{1,0},{2,3},{3,2},{4,5},{5,4},{6,7},{7,6},{8,9},{9,8},{10,11... | collective-permute-start | bytes 393224 | tf_op jit(solution)/shard_map/ppermute | solution.py:368
  48.0 2.1 %grid_first.1 = (f32[2,5,640,128]{3,2,1,0:T(8,128)S(1)}, f32[1,128]{1,0:T(1,128)S(1)}, bf16[2,512,512]{2,1,0:T(8,128)(2,1)S(1)}) custom-call(s32[1]{0:T(128)} %bitcast.1.me_ref, s32[1,2]{1,0:T(1,128)S(1)} %get-tuple-element.45.fo_ref, s32[2,16]{1,0:T(2,128)S(1)} %get-tuple-element.46.so_ref, bf16[2,512,512]{2,1,0:T(8,128)(2,1)} %constant.14.clone.basis_ref.basis_hbm, ...), custom_call_target="tpu_custom_call" | custom-call | tf_op jit(solution)/shard_map/grid_first/pallas_call | solution.py:535
  50.2 0.5 collective-permute-start.12
  50.7 1.5 %grid_next.1.rest_1_ = f32[2,5,640,128]{3,2,1,0:T(8,128)S(1)} custom-call(s32[1]{0:T(128)} %bitcast.1.me_ref, s32[1,2]{1,0:T(1,128)S(1)} %get-tuple-element.45.fo_ref, s32[2,16]{1,0:T(2,128)S(1)} %get-tuple-element.46.so_ref, bf16[2,2,128,128]{3,2,1,0:T(8,128)(2,1)S(1)} %collective-permute-done.13.rest_0_, ...), custom_call_target="tpu_custom_call", output_to_operand_aliasing={{}: (6, {})} | custom-call | tf_op jit(solution)/shard_map/grid_next/pallas_call | solution.py:548
  52.2 4.1 %backward.1 = (bf16[1,2,512,512]{3,2,1,0:T(8,128)(2,1)}, f32[2,5,640,128]{3,2,1,0:T(8,128)S(1)}) custom-call(s32[1]{0:T(128)} %bitcast.1.me_ref, s32[1,2]{1,0:T(1,128)S(1)} %get-tuple-element.45.fo_ref, s32[2,16]{1,0:T(2,128)S(1)} %get-tuple-element.46.so_ref, bf16[2,512,512]{2,1,0:T(8,128)(2,1)S(1)} %get-tuple-element.48.basis_ref, ...), custom_call_target="tpu_custom_call", output_to_operand_aliasing={{1}: (5, {})} | custom-call | tf_op jit(solution)/shard_map/backward/pallas_call | solution.py:557
  (22 shorter events, 0.4 us)
Async XLA Ops:
  5.2 2.7 %collective-permute-start = (bf16[4,2,128,128]{3,2,1,0:T(8,128)(2,1)S(1)}, bf16[4,2,128,128]{3,2,1,0:T(8,128)(2,1)S(1)}, u32[]{:S(2)}, u32[]{:S(2)}) collective-permute-start(bf16[4,2,128,128]{3,2,1,0:T(8,128)(2,1)S(1)} %get-tuple-element.29), channel_id=1, source_target_pairs={{0,1},{1,0},{2,3},{3,2},{4,5},{5,4},{6,7},{7,6},{8,9},{9,8},{10,11... | collective-permute-start | bytes 786440 | tf_op jit(solution)/shard_map/ppermute | solution.py:368
  7.4 8.2 %collective-permute-start.2 = (bf16[4,2,128,128]{3,2,1,0:T(8,128)(2,1)S(1)}, bf16[4,2,128,128]{3,2,1,0:T(8,128)(2,1)S(1)}, u32[]{:S(2)}, u32[]{:S(2)}) collective-permute-start(bf16[4,2,128,128]{3,2,1,0:T(8,128)(2,1)S(1)} %get-tuple-element.31), channel_id=1, source_target_pairs={{0,1},{1,0},{2,3},{3,2},{4,5},{5,4},{6,7},{7,6},{8,9},{9,8},{10,11... | collective-permute-start | bytes 786440 | tf_op jit(solution)/shard_map/ppermute | solution.py:368
  8.0 8.6 %collective-permute-start.1 = (bf16[4,2,128,128]{3,2,1,0:T(8,128)(2,1)S(1)}, bf16[4,2,128,128]{3,2,1,0:T(8,128)(2,1)S(1)}, u32[]{:S(2)}, u32[]{:S(2)}) collective-permute-start(bf16[4,2,128,128]{3,2,1,0:T(8,128)(2,1)S(1)} %add_convert_fusion.outs_0_._), channel_id=1, source_target_pairs={{0,2},{1,3},{2,0},{3,1},{4,6},{5,7},{6,4},{7,5},{8,10},{9,11},{10,... | collective-permute-start | bytes 786440 | tf_op jit(solution)/shard_map/ppermute | solution.py:368
  16.6 6.6 %collective-permute-start.4 = (bf16[1,2,128,128]{3,2,1,0:T(8,128)(2,1)S(1)}, bf16[1,2,128,128]{3,2,1,0:T(8,128)(2,1)S(1)}, u32[]{:S(2)}, u32[]{:S(2)}) collective-permute-start(bf16[1,2,128,128]{3,2,1,0:T(8,128)(2,1)S(1)} %get-tuple-element.53), channel_id=1, source_target_pairs={{0,8},{1,9},{2,10},{3,11},{4,12},{5,13},{6,14},{7,15},{8,0},{9,1},... | collective-permute-start | bytes 196616 | tf_op jit(solution)/shard_map/ppermute | solution.py:368
  18.9 4.3 %collective-permute-start.3 = (bf16[1,2,128,128]{3,2,1,0:T(8,128)(2,1)S(1)}, bf16[1,2,128,128]{3,2,1,0:T(8,128)(2,1)S(1)}, u32[]{:S(2)}, u32[]{:S(2)}) collective-permute-start(bf16[1,2,128,128]{3,2,1,0:T(8,128)(2,1)S(1)} %get-tuple-element.54), channel_id=1, source_target_pairs={{0,4},{1,5},{2,6},{3,7},{4,0},{5,1},{6,2},{7,3},{8,12},{9,13},{10,... | collective-permute-start | bytes 196616 | tf_op jit(solution)/shard_map/ppermute | solution.py:368
  20.2 4.9 %collective-permute-start.5 = (bf16[1,2,128,128]{3,2,1,0:T(8,128)(2,1)S(1)}, bf16[1,2,128,128]{3,2,1,0:T(8,128)(2,1)S(1)}, u32[]{:S(2)}, u32[]{:S(2)}) collective-permute-start(bf16[1,2,128,128]{3,2,1,0:T(8,128)(2,1)S(1)} %get-tuple-element.52._), channel_id=1, source_target_pairs={{0,12},{1,13},{2,14},{3,15},{4,8},{5,9},{6,10},{7,11},{8,4},{9,5},... | collective-permute-start | bytes 196616 | tf_op jit(solution)/shard_map/ppermute | solution.py:368
  32.8 11.6 %collective-permute-start.8 = (bf16[1,2,128,128]{3,2,1,0:T(8,128)(2,1)S(1)}, bf16[1,2,128,128]{3,2,1,0:T(8,128)(2,1)S(1)}, u32[]{:S(2)}, u32[]{:S(2)}) collective-permute-start(bf16[1,2,128,128]{3,2,1,0:T(8,128)(2,1)S(1)} %get-tuple-element.47), channel_id=1, source_target_pairs={{0,12},{1,13},{2,14},{3,15},{4,8},{5,9},{6,10},{7,11},{8,4},{9,5},... | collective-permute-start | bytes 196616 | tf_op jit(solution)/shard_map/ppermute | solution.py:368
  34.2 10.1 %collective-permute-start.7 = (bf16[1,2,128,128]{3,2,1,0:T(8,128)(2,1)S(1)}, bf16[1,2,128,128]{3,2,1,0:T(8,128)(2,1)S(1)}, u32[]{:S(2)}, u32[]{:S(2)}) collective-permute-start(bf16[1,2,128,128]{3,2,1,0:T(8,128)(2,1)S(1)} %get-tuple-element.47), channel_id=1, source_target_pairs={{0,8},{1,9},{2,10},{3,11},{4,12},{5,13},{6,14},{7,15},{8,0},{9,1},... | collective-permute-start | bytes 196616 | tf_op jit(solution)/shard_map/ppermute | solution.py:368
  34.2 4.3 %collective-permute-start.6 = (bf16[1,2,128,128]{3,2,1,0:T(8,128)(2,1)S(1)}, bf16[1,2,128,128]{3,2,1,0:T(8,128)(2,1)S(1)}, u32[]{:S(2)}, u32[]{:S(2)}) collective-permute-start(bf16[1,2,128,128]{3,2,1,0:T(8,128)(2,1)S(1)} %get-tuple-element.47), channel_id=1, source_target_pairs={{0,4},{1,5},{2,6},{3,7},{4,0},{5,1},{6,2},{7,3},{8,12},{9,13},{10,... | collective-permute-start | bytes 196616 | tf_op jit(solution)/shard_map/ppermute | solution.py:368
  38.5 6.2 %collective-permute-start.13 = (bf16[2,2,128,128]{3,2,1,0:T(8,128)(2,1)S(1)}, bf16[2,2,128,128]{3,2,1,0:T(8,128)(2,1)S(1)}, u32[]{:S(2)}, u32[]{:S(2)}) collective-permute-start(bf16[2,2,128,128]{3,2,1,0:T(8,128)(2,1)S(1)} %constant_dynamic-update-slice_fusion.rest_0_), channel_id=1, source_target_pairs={{0,2},{1,3},{2,0},{3,1},{4,6},{5,7},{6,4},{7,5},{8,10},{9,11},{10,... | collective-permute-start | bytes 393224 | tf_op jit(solution)/shard_map/ppermute | solution.py:368
  39.8 8.2 %collective-permute-start.9 = (bf16[2,2,128,128]{3,2,1,0:T(8,128)(2,1)S(1)}, bf16[2,2,128,128]{3,2,1,0:T(8,128)(2,1)S(1)}, u32[]{:S(2)}, u32[]{:S(2)}) collective-permute-start(bf16[2,2,128,128]{3,2,1,0:T(8,128)(2,1)S(1)} %constant_dynamic-update-slice_fusion.rest_0_), channel_id=1, source_target_pairs={{0,1},{1,0},{2,3},{3,2},{4,5},{5,4},{6,7},{7,6},{8,9},{9,8},{10,11... | collective-permute-start | bytes 393224 | tf_op jit(solution)/shard_map/ppermute | solution.py:368
  44.4 3.6 %collective-permute-start.10 = (bf16[2,2,128,128]{3,2,1,0:T(8,128)(2,1)S(1)}, bf16[2,2,128,128]{3,2,1,0:T(8,128)(2,1)S(1)}, u32[]{:S(2)}, u32[]{:S(2)}) collective-permute-start(bf16[2,2,128,128]{3,2,1,0:T(8,128)(2,1)S(1)} %constant_dynamic-update-slice_fusion.2.rest_1_), channel_id=1, source_target_pairs={{0,1},{1,0},{2,3},{3,2},{4,5},{5,4},{6,7},{7,6},{8,9},{9,8},{10,11... | collective-permute-start | bytes 393224 | tf_op jit(solution)/shard_map/ppermute | solution.py:368
  44.4 5.7 %collective-permute-start.11 = (bf16[2,2,128,128]{3,2,1,0:T(8,128)(2,1)S(1)}, bf16[2,2,128,128]{3,2,1,0:T(8,128)(2,1)S(1)}, u32[]{:S(2)}, u32[]{:S(2)}) collective-permute-start(bf16[2,2,128,128]{3,2,1,0:T(8,128)(2,1)S(1)} %constant_dynamic-update-slice_fusion.2.rest_1_), channel_id=1, source_target_pairs={{0,2},{1,3},{2,0},{3,1},{4,6},{5,7},{6,4},{7,5},{8,10},{9,11},{10,... | collective-permute-start | bytes 393224 | tf_op jit(solution)/shard_map/ppermute | solution.py:368
  44.7 5.9 %collective-permute-start.14 = (bf16[2,2,128,128]{3,2,1,0:T(8,128)(2,1)S(1)}, bf16[2,2,128,128]{3,2,1,0:T(8,128)(2,1)S(1)}, u32[]{:S(2)}, u32[]{:S(2)}) collective-permute-start(bf16[2,2,128,128]{3,2,1,0:T(8,128)(2,1)S(1)} %collective-permute-done.13.rest_0_), channel_id=1, source_target_pairs={{0,1},{1,0},{2,3},{3,2},{4,5},{5,4},{6,7},{7,6},{8,9},{9,8},{10,11... | collective-permute-start | bytes 393224 | tf_op jit(solution)/shard_map/ppermute | solution.py:368
  50.2 2.0 %collective-permute-start.12 = (bf16[2,2,128,128]{3,2,1,0:T(8,128)(2,1)S(1)}, bf16[2,2,128,128]{3,2,1,0:T(8,128)(2,1)S(1)}, u32[]{:S(2)}, u32[]{:S(2)}) collective-permute-start(bf16[2,2,128,128]{3,2,1,0:T(8,128)(2,1)S(1)} %add_convert_fusion.1.rest_2_), channel_id=1, source_target_pairs={{0,1},{1,0},{2,3},{3,2},{4,5},{5,4},{6,7},{7,6},{8,9},{9,8},{10,11... | collective-permute-start | bytes 393224 | tf_op jit(solution)/shard_map/ppermute | solution.py:368

commit v9 on v8

--- a/solution.py
+++ b/solution.py
@@ -74,6 +74,10 @@
 
 def dot(left, right):
     return jnp.dot(left, right, preferred_element_type=F32)
+
+
+def dot_nt(left, right):
+    return lax.dot_general(left, right, (((1,), (1,)), ((), ())), preferred_element_type=F32)
 
 
 def mul_left(left_r, left_i, right_r, right_i):
@@ -114,7 +118,10 @@
         copies.append(pltpu.make_async_copy(facet_ref.at[0, k], facet_buf.at[k], sems.at[2 * k + 1]))
     for copy in copies:
         copy.start()
-    for copy in copies:
+    for copy in copies[:2]:
+        copy.wait()
+    phase = phase_taper(fo_ref)
+    for copy in copies[2:]:
         copy.wait()
     br, bi = basis_buf[0], basis_buf[1]
     hr, hi = mul_left(facet_buf[0], facet_buf[1], br, bi)
@@ -128,16 +135,16 @@
             if c == 0:
                 spec_ref[plane, columns, :F] = part
                 spec_ref[plane, columns, F:] = part[:M]
-    extract([js], [out_ref], me_ref, fo_ref, so_ref, spec_ref)
+    extract([js], [out_ref], me_ref, phase, so_ref, spec_ref)
 
 
 def extract_kernel(sends, me_ref, fo_ref, so_ref, spec_ref, *outs):
     outs = outs[-len(sends) :]
-    extract(sends, outs, me_ref, fo_ref, so_ref, spec_ref)
-
-
-def extract(sends, outs, me_ref, fo_ref, so_ref, spec_ref):
-    pc, ps = phase_taper(fo_ref)
+    extract(sends, outs, me_ref, phase_taper(fo_ref), so_ref, spec_ref)
+
+
+def extract(sends, outs, me_ref, phase, so_ref, spec_ref):
+    pc, ps = phase
     me = me_ref[0]
 
     def block(out_ref, item, j):
@@ -173,7 +180,7 @@
             block(ref, item, j)
 
 
-def band_kernel(to_ref, _, kt_hbm, kwide_hbm, kvt_ref, kv_ref, kut_ref, ku_ref, zero_ref, kt_ref, kwide_ref, sems):
+def band_kernel(to_ref, _, kt_hbm, kwide_hbm, kvt_ref, kut_ref, ku_ref, zero_ref, kt_ref, kwide_ref, sems):
     slots = kut_ref.shape[0]
     copies = [
         pltpu.make_async_copy(kt_hbm, kt_ref, sems.at[0]),
@@ -190,13 +197,13 @@
         kut_ref[t] = kt_ref[pl.ds(2 * TV - ou, SG), :].astype(BF)
         kvt_ref[:, rows] = kt_ref[pl.ds(2 * TV - ov, SG), :].astype(BF)
         ku_ref[rows] = pltpu.roll(kwide_ref[...], ou, 1).astype(BF)
-        kv_ref[rows] = pltpu.roll(kwide_ref[...], ov, 1).astype(BF)
 
 
 def screen_kernel(w_ref, _, *rest):
-    loads = (len(rest) - 2) // 2
+    loads = (len(rest) - 3) // 2
     sources, screen_ref = rest[:loads], rest[loads]
-    targets, sems = rest[loads + 1 : -1], rest[-1]
+    targets, zero_ref, sems = rest[loads + 1 : -2], rest[-2], rest[-1]
+    zero_ref[...] = jnp.zeros_like(zero_ref)
     copies = [pltpu.make_async_copy(sources[k], targets[k], sems.at[k]) for k in range(loads)]
     for copy in copies:
         copy.start()
@@ -215,8 +222,8 @@
 def subgrid_kernel(picks, tc_ref, *rest):
     parts = len(picks)
     sums = rest[:parts]
-    (obs_ref, pad_ref, padt_ref, screen_ref, kvt_ref, kv_ref, kut_ref, ku_ref) = rest[parts : parts + 8]
-    (out_ref, coef_ref, model_ref, rows_ref, z_ref, res_ref, sems) = rest[parts + 8 :]
+    (obs_ref, pad_ref, padt_ref, screen_ref, kvt_ref, kut_ref, ku_ref) = rest[parts : parts + 7]
+    (out_ref, coef_ref, model_ref, rows_ref, z_ref, res_ref, sems) = rest[parts + 7 :]
     slots = obs_ref.shape[0]
     count = tc_ref[0, 0]
 
@@ -260,9 +267,9 @@
         z_ref[:SG, t * TV : (t + 1) * TV] = z[:, :TV]
         z_ref[SG:, t * TV : (t + 1) * TV] = z[:, TV:]
 
-    kv = kv_ref[...]
-    ar = dot(z_ref[:SG], kv)
-    ai = dot(z_ref[SG:], kv)
+    kvt = kvt_ref[...]
+    ar = dot_nt(z_ref[:SG], kvt)
+    ai = dot_nt(z_ref[SG:], kvt)
     screened_r = (sc * ar + ss * ai).astype(BF)
     screened_i = (sc * ai - ss * ar).astype(BF)
     reduced_r, reduced_i = mul_right(tr, -ti, screened_r, screened_i)
@@ -443,12 +450,16 @@
         )(me, facet_offsets, corners, near(spec), *[near(value) for value in after])
 
     def make_bands(after):
-        big = held((slots * TV, SG))
         return pl.pallas_call(
             band_kernel,
-            out_shape=[held((SG, slots * TV)), big, held((slots, SG, TV)), big, held((1, M), F32)],
+            out_shape=[
+                held((SG, slots * TV)),
+                held((slots, SG, TV)),
+                held((slots * TV, SG)),
+                held((1, M), F32),
+            ],
             in_specs=[SMEM, VMEM] + [ANY] * 2,
-            out_specs=[VMEM] * 5,
+            out_specs=[VMEM] * 4,
             scratch_shapes=[
                 pltpu.VMEM(kt_np.shape, F32),
                 pltpu.VMEM(kwide_np.shape, F32),
@@ -462,9 +473,9 @@
         loads = [observed, pad_np, pad_np.transpose(0, 2, 1), subgrid_offsets.T, facet_offsets]
         return pl.pallas_call(
             screen_kernel,
-            out_shape=[held((2, SG, SG), F32)] + [held(load.shape, load.dtype) for load in loads],
+            out_shape=[held((2, SG, SG), F32)] + [held(load.shape, load.dtype) for load in loads] + [held((1, M), F32)],
             in_specs=[SMEM, VMEM] + [ANY] * len(loads),
-            out_specs=[VMEM] * (1 + len(loads)),
+            out_specs=[VMEM] * (2 + len(loads)),
             scratch_shapes=[pltpu.SemaphoreType.DMA((len(loads),))],
             compiler_params=params(8),
             name="screen",
@@ -491,17 +502,17 @@
     value = send(beside, 2, beside_own)
     send(lazy, 1, lazy_own)
     own = make_blocks([js for js, _ in sends[3:]] + [[0]], [value])
-    kvt, kv, kut, ku, token = make_bands(value)
+    kvt, kut, ku, token = make_bands(value)
+    screen, tiles, pad, padt, late_corners, late_facet_offsets, token = make_screen(token)
     for (js, mask), value in zip(sends[3:], own):
         value = send(js, mask, value, token)
-    screen, tiles, pad, padt, corners, facet_offsets = make_screen(value)
-    corners, facet_offsets = near(corners), near(facet_offsets)
+    corners, facet_offsets = near(late_corners), near(late_facet_offsets)
     last = [(js, got) for js, got in arrived if 0 in js]
 
     residual, coefficient = pl.pallas_call(
         functools.partial(subgrid_kernel, [0] + [js.index(0) for js, _ in last]),
         out_shape=[pltpu.HBM(observed.shape, BF), held((1, 2, M, M))],
-        in_specs=[SMEM] + [VMEM] * (len(last) + 9),
+        in_specs=[SMEM] + [VMEM] * (len(last) + 8),
         out_specs=[ANY, VMEM],
         scratch_shapes=[
             pltpu.VMEM((2 * SG, SG), BF),
@@ -516,22 +527,20 @@
         tile_count.reshape(1, 1),
         near(own[-1]),
         *[near(got) for _, got in last],
-        *[near(value) for value in (tiles, pad, padt, screen, kvt, kv, kut, ku)],
+        *[near(value) for value in (tiles, pad, padt, screen, kvt, kut, ku)],
     )
 
     early = ([0], coefficient)
     for base, radix in reversed(digit_levels(n)[2:]):
         js, value = early
         more = [([j ^ (g * base) for j in js], exchange(value, g * base, n)) for g in range(1, radix)]
-        early_parts = [join([early, more[0]]), join(more[1:])]
-        early = join(early_parts)
+        early = join([early] + more)
 
     def hop(part, mask):
         return [j ^ mask for j in part[0]], exchange(part[1], mask, n)
 
-    a, b = early_parts
-    late_a, late_b = hop(a, 2), hop(b, 2)
-    ready = [a, b, hop(a, 1), hop(b, 1)]
+    late = hop(early, 2)
+    ready = [early, hop(early, 1)]
     grid, token, basis_near = pl.pallas_call(
         functools.partial(first_grid_kernel, [js for js, _ in ready]),
         out_shape=[held(grid_shape, F32), held((1, M), F32), held(basis.shape)],
@@ -541,10 +550,9 @@
         compiler_params=params(8),
         name="grid_first",
     )(me, facet_offsets, corners, basis, *[near(value) for _, value in ready])
-    late_a_other = hop(late_a, 1)
-    late_b = (late_b[0], (late_b[1].astype(F32) + token).astype(BF))
-    late_b_other = hop(late_b, 1)
-    ready = [late_a, late_a_other, late_b]
+    late = (late[0], (late[1].astype(F32) + token).astype(BF))
+    late_other = hop(late, 1)
+    ready = [late]
     grid = pl.pallas_call(
         functools.partial(next_grid_kernel, [js for js, _ in ready]),
         out_shape=held(grid_shape, F32),
@@ -555,7 +563,7 @@
         name="grid_next",
     )(me, facet_offsets, corners, *[near(value) for _, value in ready], near(grid))
     update = pl.pallas_call(
-        functools.partial(backward_kernel, [late_b_other[0]]),
+        functools.partial(backward_kernel, [late_other[0]]),
         out_shape=[pltpu.HBM(facets.shape, BF), held(grid_shape, F32)],
         in_specs=[SMEM] * 3 + [VMEM] * 3,
         out_specs=[ANY, VMEM],
@@ -566,7 +574,7 @@
         ],
         compiler_params=params(16),
         name="backward",
-    )(me, facet_offsets, corners, near(basis_near), near(late_b_other[1]), near(grid))[0]
+    )(me, facet_offsets, corners, near(basis_near), near(late_other[1]), near(grid))[0]
     return (residual, update)
 
 

time: 56.7 us -> 58.8 us (1.037)
  waiting for transfers between devices: 5.01 us -> 15.9 us
  starting transfers between devices: 20.1 us -> 12.3 us
  Pallas kernels: 28.8 us -> 27.8 us
    ppermute x15 -> x12, waiting for transfers between devices: 5.01 us -> 15.9 us  [exchange(): return lax.ppermute(value, 'facet', [(i, i ^ mask) for i in range(n)])]
    ppermute x15 -> x12, starting transfers between devices: 20.1 us -> 12.3 us  [exchange(): return lax.ppermute(value, 'facet', [(i, i ^ mask) for i in range(n)])]
  transfers between devices with their start and end apart: 15 -> 12, of which waited for: 3 -> 6; matrix products, arithmetic and copies ran while one was open for 0% -> 0% of each run, Pallas kernels for 22% -> 19%
where the time goes in v9:
time: 58.8 us; the launch traced here: 58.3 us
  Pallas kernels  27.8 us (47%)
  waiting for transfers between devices  15.9 us (27%)
  starting transfers between devices  12.3 us (21%)
  between operations  2.07 us (4%)
    ppermute x12, waiting for transfers between devices, exchange(): return lax.ppermute(value, 'facet', [(i, i ^ mask) for i in range(n)])  15.9 us
    ppermute x12, starting transfers between devices, exchange(): return lax.ppermute(value, 'facet', [(i, i ^ mask) for i in range(n)])  12.3 us
    pallas_call x1, Pallas kernels, per_device(): pl.pallas_call(functools.partial(subgrid_kernel, [0] + [js.index(0) for j...  7.6 us
    pallas_call x1, Pallas kernels, per_device(): pl.pallas_call(functools.partial(forward_kernel, sends[0][0]), out_shape=...  4.54 us
    pallas_call x1, Pallas kernels, per_device(): pl.pallas_call(functools.partial(backward_kernel, [late_other[0]]), out_s...  4.32 us
    pallas_call x1, Pallas kernels, make_bands(): pl.pallas_call(band_kernel, out_shape=[held((SG, slots * TV)), held((slot...  3.41 us
    pallas_call x2, Pallas kernels, make_blocks(): pl.pallas_call(functools.partial(extract_kernel, lists), out_shape=[held(...  3.12 us
    pallas_call x1, Pallas kernels, per_device(): pl.pallas_call(functools.partial(first_grid_kernel, [js for js, _ in read...  1.95 us
  transfers between devices with their start and end apart: 12, of which 6 were waited for; matrix products, arithmetic and copies ran while one was open for 0% of the time, Pallas kernels for 19%

profile of v9, /device:TPU:1, one launch (start us, length us, event | category | flops | bytes accessed | tf_op | source)
XLA Modules:
  0.0 58.3 jit_solution(6351705114995093143)
XLA Ops:
  0.6 4.5 %forward.1 = (bf16[4,2,128,128]{3,2,1,0:T(8,128)(2,1)S(1)}, f32[2,5,640,128]{3,2,1,0:T(8,128)S(1)}) custom-call(s32[1]{0:T(128)} %bitcast.1.me_ref, s32[1,2]{1,0:T(1,128)} %rest_4_.1, s32[2,16]{1,0:T(2,128)} %bitcast.11, bf16[1,2,512,512]{3,2,1,0:T(8,128)(2,1)} %facet_ref.1, bf16[2,512,512]{2,1,0:T(8,128)(2,1)} %constant.14.clone.basis_ref.basis_hbm), custom_call_target="tpu_custom_call" | custom-call | tf_op jit(solution)/shard_map/forward/pallas_call | solution.py:427
  5.2 0.1 collective-permute-start
  5.3 2.1 %extract.2 = (bf16[4,2,128,128]{3,2,1,0:T(8,128)(2,1)S(1)}, bf16[4,2,128,128]{3,2,1,0:T(8,128)(2,1)S(1)}) custom-call(s32[1]{0:T(128)} %bitcast.1.me_ref, s32[1,2]{1,0:T(1,128)} %rest_4_.1, s32[2,16]{1,0:T(2,128)} %bitcast.12, f32[2,5,640,128]{3,2,1,0:T(8,128)S(1)} %get-tuple-element.27.spec_ref), custom_call_target="tpu_custom_call" | custom-call | tf_op jit(solution)/shard_map/extract/pallas_call | solution.py:443
  7.4 0.5 collective-permute-start.2
  8.0 2.3 %collective-permute-start.1 = (bf16[4,2,128,128]{3,2,1,0:T(8,128)(2,1)S(1)}, bf16[4,2,128,128]{3,2,1,0:T(8,128)(2,1)S(1)}, u32[]{:S(2)}, u32[]{:S(2)}) collective-permute-start(bf16[4,2,128,128]{3,2,1,0:T(8,128)(2,1)S(1)} %add_convert_fusion.1.outs_0_._), channel_id=1, source_target_pairs={{0,2},{1,3},{2,0},{3,1},{4,6},{5,7},{6,4},{7,5},{8,10},{9,11},{10,... | collective-permute-start | bytes 786440 | tf_op jit(solution)/shard_map/ppermute | solution.py:375
  10.9 1.1 %extract.3 = (bf16[1,2,128,128]{3,2,1,0:T(8,128)(2,1)S(1)}, bf16[1,2,128,128]{3,2,1,0:T(8,128)(2,1)S(1)}, bf16[1,2,128,128]{3,2,1,0:T(8,128)(2,1)S(1)}, bf16[1,2,128,128]{3,2,1,0:T(8,128)(2,1)S(1)}) custom-call(s32[1]{0:T(128)} %bitcast.1.me_ref, s32[1,2]{1,0:T(1,128)} %rest_4_.1, s32[2,16]{1,0:T(2,128)} %bitcast.13, ...), custom_call_target="tpu_custom_call" | custom-call | tf_op jit(solution)/shard_map/extract/pallas_call | solution.py:443
  12.0 3.4 %bands.1 = (bf16[512,2048]{1,0:T(8,128)(2,1)S(1)}, bf16[16,512,128]{2,1,0:T(8,128)(2,1)S(1)}, bf16[2048,512]{1,0:T(8,128)(2,1)S(1)}, f32[1,128]{1,0:T(1,128)S(1)}) custom-call(s32[2,16]{1,0:T(2,128)} %bitcast.15, bf16[4,2,128,128]{3,2,1,0:T(8,128)(2,1)S(1)} %add_convert_fusion.1.outs_0_._, f32[768,128]{1,0:T(8,128)} %constant.15.clone.kt_hbm, ...), custom_call_target="tpu_custom_call" | custom-call | tf_op jit(solution)/shard_map/bands/pallas_call | solution.py:453
  15.4 1.6 %screen.1 = (f32[2,512,512]{2,1,0:T(8,128)S(1)}, bf16[16,2,128,128]{3,2,1,0:T(8,128)(2,1)S(1)}, bf16[2,512,128]{2,1,0:T(8,128)(2,1)S(1)}, bf16[2,128,512]{2,1,0:...) custom-call(f32[1,1]{1,0:T(1,128)} %bitcast.7.w_ref, ...), custom_call_target="tpu_custom_call" | custom-call | tf_op jit(solution)/shard_map/screen/pallas_call | solution.py:474
  17.2 3.4 %collective-permute-start.5 = (bf16[1,2,128,128]{3,2,1,0:T(8,128)(2,1)S(1)}, bf16[1,2,128,128]{3,2,1,0:T(8,128)(2,1)S(1)}, u32[]{:S(2)}, u32[]{:S(2)}) collective-permute-start(bf16[1,2,128,128]{3,2,1,0:T(8,128)(2,1)S(1)} %get-tuple-element.52), channel_id=1, source_target_pairs={{0,12},{1,13},{2,14},{3,15},{4,8},{5,9},{6,10},{7,11},{8,4},{9,5},... | collective-permute-start | bytes 196616 | tf_op jit(solution)/shard_map/ppermute | solution.py:375
  20.6 0.4 collective-permute-start.3
  21.6 0.7 %collective-permute-done.5.rest_5_ = bf16[1,2,128,128]{3,2,1,0:T(8,128)(2,1)S(1)} collective-permute-done((bf16[1,2,128,128]{3,2,1,0:T(8,128)(2,1)S(1)}, bf16[1,2,128,128]{3,2,1,0:T(8,128)(2,1)S(1)}, u32[]{:S(2)}, u32[]{:S(2)}) %collective-permute-start.5) | collective-permute-done | bytes 65568 | tf_op jit(solution)/shard_map/ppermute | solution.py:375
  22.3 4.1 %collective-permute-done.4.rest_4_ = bf16[1,2,128,128]{3,2,1,0:T(8,128)(2,1)S(1)} collective-permute-done((bf16[1,2,128,128]{3,2,1,0:T(8,128)(2,1)S(1)}, bf16[1,2,128,128]{3,2,1,0:T(8,128)(2,1)S(1)}, u32[]{:S(2)}, u32[]{:S(2)}) %collective-permute-start.4) | collective-permute-done | bytes 65568 | tf_op jit(solution)/shard_map/ppermute | solution.py:375
  26.3 7.6 %subgrid.1 = (bf16[16,2,128,128]{3,2,1,0:T(8,128)(2,1)}, bf16[1,2,128,128]{3,2,1,0:T(8,128)(2,1)S(1)}) custom-call(s32[1,1]{1,0:T(1,128)} %bitcast.8.tc_ref, bf16[1,2,128,128]{3,2,1,0:T(8,128)(2,1)S(1)} %get-tuple-element.30.rest_0_, bf16[4,2,128,128]{3,2,1,0:T(8,128)(2,1)S(1)} %collective-permute-done.1.rest_1_, ...), custom_call_target="tpu_custom_call" | custom-call | tf_op jit(solution)/shard_map/subgrid/pallas_call | solution.py:512
  33.9 1.3 %collective-permute-start.8 = (bf16[1,2,128,128]{3,2,1,0:T(8,128)(2,1)S(1)}, bf16[1,2,128,128]{3,2,1,0:T(8,128)(2,1)S(1)}, u32[]{:S(2)}, u32[]{:S(2)}) collective-permute-start(bf16[1,2,128,128]{3,2,1,0:T(8,128)(2,1)S(1)} %get-tuple-element.47), channel_id=1, source_target_pairs={{0,12},{1,13},{2,14},{3,15},{4,8},{5,9},{6,10},{7,11},{8,4},{9,5},... | collective-permute-start | bytes 196616 | tf_op jit(solution)/shard_map/ppermute | solution.py:375
  35.2 2.3 %collective-permute-start.6 = (bf16[1,2,128,128]{3,2,1,0:T(8,128)(2,1)S(1)}, bf16[1,2,128,128]{3,2,1,0:T(8,128)(2,1)S(1)}, u32[]{:S(2)}, u32[]{:S(2)}) collective-permute-start(bf16[1,2,128,128]{3,2,1,0:T(8,128)(2,1)S(1)} %get-tuple-element.47), channel_id=1, source_target_pairs={{0,4},{1,5},{2,6},{3,7},{4,0},{5,1},{6,2},{7,3},{8,12},{9,13},{10,... | collective-permute-start | bytes 196616 | tf_op jit(solution)/shard_map/ppermute | solution.py:375
  37.6 2.5 %collective-permute-done.6 = bf16[1,2,128,128]{3,2,1,0:T(8,128)(2,1)S(1)} collective-permute-done((bf16[1,2,128,128]{3,2,1,0:T(8,128)(2,1)S(1)}, bf16[1,2,128,128]{3,2,1,0:T(8,128)(2,1)S(1)}, u32[]{:S(2)}, u32[]{:S(2)}) %collective-permute-start.6) | collective-permute-done | bytes 65568 | tf_op jit(solution)/shard_map/ppermute | solution.py:375
  40.1 2.7 %collective-permute-done.7 = bf16[1,2,128,128]{3,2,1,0:T(8,128)(2,1)S(1)} collective-permute-done((bf16[1,2,128,128]{3,2,1,0:T(8,128)(2,1)S(1)}, bf16[1,2,128,128]{3,2,1,0:T(8,128)(2,1)S(1)}, u32[]{:S(2)}, u32[]{:S(2)}) %collective-permute-start.7) | collective-permute-done | bytes 65568 | tf_op jit(solution)/shard_map/ppermute | solution.py:375
  42.9 1.1 %collective-permute-start.9 = (bf16[4,2,128,128]{3,2,1,0:T(8,128)(2,1)S(1)}, bf16[4,2,128,128]{3,2,1,0:T(8,128)(2,1)S(1)}, u32[]{:S(2)}, u32[]{:S(2)}) collective-permute-start(bf16[4,2,128,128]{3,2,1,0:T(8,128)(2,1)S(1)} %constant_dynamic-update-slice_fusion.rest_0_), channel_id=1, source_target_pairs={{0,1},{1,0},{2,3},{3,2},{4,5},{5,4},{6,7},{7,6},{8,9},{9,8},{10,11... | collective-permute-start | bytes 786440 | tf_op jit(solution)/shard_map/ppermute | solution.py:375
  43.9 1.2 %collective-permute-done.9.rest_1_ = bf16[4,2,128,128]{3,2,1,0:T(8,128)(2,1)S(1)} collective-permute-done((bf16[4,2,128,128]{3,2,1,0:T(8,128)(2,1)S(1)}, bf16[4,2,128,128]{3,2,1,0:T(8,128)(2,1)S(1)}, u32[]{:S(2)}, u32[]{:S(2)}) %collective-permute-start.9) | collective-permute-done | bytes 262176 | tf_op jit(solution)/shard_map/ppermute | solution.py:375
  45.1 1.9 %grid_first.1 = (f32[2,5,640,128]{3,2,1,0:T(8,128)S(1)}, f32[1,128]{1,0:T(1,128)S(1)}, bf16[2,512,512]{2,1,0:T(8,128)(2,1)S(1)}) custom-call(s32[1]{0:T(128)} %bitcast.1.me_ref, s32[1,2]{1,0:T(1,128)S(1)} %get-tuple-element.45.fo_ref, s32[2,16]{1,0:T(2,128)S(1)} %get-tuple-element.46.so_ref, bf16[2,512,512]{2,1,0:T(8,128)(2,1)} %constant.14.clone.basis_ref.basis_hbm, ...), custom_call_target="tpu_custom_call" | custom-call | tf_op jit(solution)/shard_map/grid_first/pallas_call | solution.py:544
  47.0 4.8 %collective-permute-done.10 = bf16[4,2,128,128]{3,2,1,0:T(8,128)(2,1)S(1)} collective-permute-done((bf16[4,2,128,128]{3,2,1,0:T(8,128)(2,1)S(1)}, bf16[4,2,128,128]{3,2,1,0:T(8,128)(2,1)S(1)}, u32[]{:S(2)}, u32[]{:S(2)}) %collective-permute-start.10) | collective-permute-done | bytes 262176 | tf_op jit(solution)/shard_map/ppermute | solution.py:375
  51.9 0.9 %collective-permute-start.11 = (bf16[4,2,128,128]{3,2,1,0:T(8,128)(2,1)S(1)}, bf16[4,2,128,128]{3,2,1,0:T(8,128)(2,1)S(1)}, u32[]{:S(2)}, u32[]{:S(2)}) collective-permute-start(bf16[4,2,128,128]{3,2,1,0:T(8,128)(2,1)S(1)} %add_convert_fusion.rest_0_), channel_id=1, source_target_pairs={{0,1},{1,0},{2,3},{3,2},{4,5},{5,4},{6,7},{7,6},{8,9},{9,8},{10,11... | collective-permute-start | bytes 786440 | tf_op jit(solution)/shard_map/ppermute | solution.py:375
  52.8 1.2 %grid_next.1.rest_1_ = f32[2,5,640,128]{3,2,1,0:T(8,128)S(1)} custom-call(s32[1]{0:T(128)} %bitcast.1.me_ref, s32[1,2]{1,0:T(1,128)S(1)} %get-tuple-element.45.fo_ref, s32[2,16]{1,0:T(2,128)S(1)} %get-tuple-element.46.so_ref, bf16[4,2,128,128]{3,2,1,0:T(8,128)(2,1)S(1)} %add_convert_fusion.rest_0_, ...), custom_call_target="tpu_custom_call", output_to_operand_aliasing={{}: (4, {})} | custom-call | tf_op jit(solution)/shard_map/grid_next/pallas_call | solution.py:556
  54.0 4.3 %backward.1 = (bf16[1,2,512,512]{3,2,1,0:T(8,128)(2,1)}, f32[2,5,640,128]{3,2,1,0:T(8,128)S(1)}) custom-call(s32[1]{0:T(128)} %bitcast.1.me_ref, s32[1,2]{1,0:T(1,128)S(1)} %get-tuple-element.45.fo_ref, s32[2,16]{1,0:T(2,128)S(1)} %get-tuple-element.46.so_ref, bf16[2,512,512]{2,1,0:T(8,128)(2,1)S(1)} %get-tuple-element.48.basis_ref, ...), custom_call_target="tpu_custom_call", output_to_operand_aliasing={{1}: (5, {})} | custom-call | tf_op jit(solution)/shard_map/backward/pallas_call | solution.py:565
  (16 shorter events, 0.3 us)
Async XLA Ops:
  5.2 2.7 %collective-permute-start = (bf16[4,2,128,128]{3,2,1,0:T(8,128)(2,1)S(1)}, bf16[4,2,128,128]{3,2,1,0:T(8,128)(2,1)S(1)}, u32[]{:S(2)}, u32[]{:S(2)}) collective-permute-start(bf16[4,2,128,128]{3,2,1,0:T(8,128)(2,1)S(1)} %get-tuple-element.29), channel_id=1, source_target_pairs={{0,1},{1,0},{2,3},{3,2},{4,5},{5,4},{6,7},{7,6},{8,9},{9,8},{10,11... | collective-permute-start | bytes 786440 | tf_op jit(solution)/shard_map/ppermute | solution.py:375
  7.4 9.7 %collective-permute-start.2 = (bf16[4,2,128,128]{3,2,1,0:T(8,128)(2,1)S(1)}, bf16[4,2,128,128]{3,2,1,0:T(8,128)(2,1)S(1)}, u32[]{:S(2)}, u32[]{:S(2)}) collective-permute-start(bf16[4,2,128,128]{3,2,1,0:T(8,128)(2,1)S(1)} %get-tuple-element.31), channel_id=1, source_target_pairs={{0,1},{1,0},{2,3},{3,2},{4,5},{5,4},{6,7},{7,6},{8,9},{9,8},{10,11... | collective-permute-start | bytes 786440 | tf_op jit(solution)/shard_map/ppermute | solution.py:375
  8.0 9.1 %collective-permute-start.1 = (bf16[4,2,128,128]{3,2,1,0:T(8,128)(2,1)S(1)}, bf16[4,2,128,128]{3,2,1,0:T(8,128)(2,1)S(1)}, u32[]{:S(2)}, u32[]{:S(2)}) collective-permute-start(bf16[4,2,128,128]{3,2,1,0:T(8,128)(2,1)S(1)} %add_convert_fusion.1.outs_0_._), channel_id=1, source_target_pairs={{0,2},{1,3},{2,0},{3,1},{4,6},{5,7},{6,4},{7,5},{8,10},{9,11},{10,... | collective-permute-start | bytes 786440 | tf_op jit(solution)/shard_map/ppermute | solution.py:375
  17.2 5.1 %collective-permute-start.5 = (bf16[1,2,128,128]{3,2,1,0:T(8,128)(2,1)S(1)}, bf16[1,2,128,128]{3,2,1,0:T(8,128)(2,1)S(1)}, u32[]{:S(2)}, u32[]{:S(2)}) collective-permute-start(bf16[1,2,128,128]{3,2,1,0:T(8,128)(2,1)S(1)} %get-tuple-element.52), channel_id=1, source_target_pairs={{0,12},{1,13},{2,14},{3,15},{4,8},{5,9},{6,10},{7,11},{8,4},{9,5},... | collective-permute-start | bytes 196616 | tf_op jit(solution)/shard_map/ppermute | solution.py:375
  20.6 5.7 %collective-permute-start.4 = (bf16[1,2,128,128]{3,2,1,0:T(8,128)(2,1)S(1)}, bf16[1,2,128,128]{3,2,1,0:T(8,128)(2,1)S(1)}, u32[]{:S(2)}, u32[]{:S(2)}) collective-permute-start(bf16[1,2,128,128]{3,2,1,0:T(8,128)(2,1)S(1)} %get-tuple-element.53), channel_id=1, source_target_pairs={{0,8},{1,9},{2,10},{3,11},{4,12},{5,13},{6,14},{7,15},{8,0},{9,1},... | collective-permute-start | bytes 196616 | tf_op jit(solution)/shard_map/ppermute | solution.py:375
  20.6 5.7 %collective-permute-start.3 = (bf16[1,2,128,128]{3,2,1,0:T(8,128)(2,1)S(1)}, bf16[1,2,128,128]{3,2,1,0:T(8,128)(2,1)S(1)}, u32[]{:S(2)}, u32[]{:S(2)}) collective-permute-start(bf16[1,2,128,128]{3,2,1,0:T(8,128)(2,1)S(1)} %get-tuple-element.54), channel_id=1, source_target_pairs={{0,4},{1,5},{2,6},{3,7},{4,0},{5,1},{6,2},{7,3},{8,12},{9,13},{10,... | collective-permute-start | bytes 196616 | tf_op jit(solution)/shard_map/ppermute | solution.py:375
  33.9 8.9 %collective-permute-start.8 = (bf16[1,2,128,128]{3,2,1,0:T(8,128)(2,1)S(1)}, bf16[1,2,128,128]{3,2,1,0:T(8,128)(2,1)S(1)}, u32[]{:S(2)}, u32[]{:S(2)}) collective-permute-start(bf16[1,2,128,128]{3,2,1,0:T(8,128)(2,1)S(1)} %get-tuple-element.47), channel_id=1, source_target_pairs={{0,12},{1,13},{2,14},{3,15},{4,8},{5,9},{6,10},{7,11},{8,4},{9,5},... | collective-permute-start | bytes 196616 | tf_op jit(solution)/shard_map/ppermute | solution.py:375
  35.2 7.6 %collective-permute-start.7 = (bf16[1,2,128,128]{3,2,1,0:T(8,128)(2,1)S(1)}, bf16[1,2,128,128]{3,2,1,0:T(8,128)(2,1)S(1)}, u32[]{:S(2)}, u32[]{:S(2)}) collective-permute-start(bf16[1,2,128,128]{3,2,1,0:T(8,128)(2,1)S(1)} %get-tuple-element.47), channel_id=1, source_target_pairs={{0,8},{1,9},{2,10},{3,11},{4,12},{5,13},{6,14},{7,15},{8,0},{9,1},... | collective-permute-start | bytes 196616 | tf_op jit(solution)/shard_map/ppermute | solution.py:375
  35.2 4.8 %collective-permute-start.6 = (bf16[1,2,128,128]{3,2,1,0:T(8,128)(2,1)S(1)}, bf16[1,2,128,128]{3,2,1,0:T(8,128)(2,1)S(1)}, u32[]{:S(2)}, u32[]{:S(2)}) collective-permute-start(bf16[1,2,128,128]{3,2,1,0:T(8,128)(2,1)S(1)} %get-tuple-element.47), channel_id=1, source_target_pairs={{0,4},{1,5},{2,6},{3,7},{4,0},{5,1},{6,2},{7,3},{8,12},{9,13},{10,... | collective-permute-start | bytes 196616 | tf_op jit(solution)/shard_map/ppermute | solution.py:375
  42.9 2.2 %collective-permute-start.9 = (bf16[4,2,128,128]{3,2,1,0:T(8,128)(2,1)S(1)}, bf16[4,2,128,128]{3,2,1,0:T(8,128)(2,1)S(1)}, u32[]{:S(2)}, u32[]{:S(2)}) collective-permute-start(bf16[4,2,128,128]{3,2,1,0:T(8,128)(2,1)S(1)} %constant_dynamic-update-slice_fusion.rest_0_), channel_id=1, source_target_pairs={{0,1},{1,0},{2,3},{3,2},{4,5},{5,4},{6,7},{7,6},{8,9},{9,8},{10,11... | collective-permute-start | bytes 786440 | tf_op jit(solution)/shard_map/ppermute | solution.py:375
  43.9 7.9 %collective-permute-start.10 = (bf16[4,2,128,128]{3,2,1,0:T(8,128)(2,1)S(1)}, bf16[4,2,128,128]{3,2,1,0:T(8,128)(2,1)S(1)}, u32[]{:S(2)}, u32[]{:S(2)}) collective-permute-start(bf16[4,2,128,128]{3,2,1,0:T(8,128)(2,1)S(1)} %constant_dynamic-update-slice_fusion.rest_0_), channel_id=1, source_target_pairs={{0,2},{1,3},{2,0},{3,1},{4,6},{5,7},{6,4},{7,5},{8,10},{9,11},{10,... | collective-permute-start | bytes 786440 | tf_op jit(solution)/shard_map/ppermute | solution.py:375
  51.9 2.1 %collective-permute-start.11 = (bf16[4,2,128,128]{3,2,1,0:T(8,128)(2,1)S(1)}, bf16[4,2,128,128]{3,2,1,0:T(8,128)(2,1)S(1)}, u32[]{:S(2)}, u32[]{:S(2)}) collective-permute-start(bf16[4,2,128,128]{3,2,1,0:T(8,128)(2,1)S(1)} %add_convert_fusion.rest_0_), channel_id=1, source_target_pairs={{0,1},{1,0},{2,3},{3,2},{4,5},{5,4},{6,7},{7,6},{8,9},{9,8},{10,11... | collective-permute-start | bytes 786440 | tf_op jit(solution)/shard_map/ppermute | solution.py:375

commit v10 on v9

--- a/solution.py
+++ b/solution.py
@@ -180,23 +180,27 @@
             block(ref, item, j)
 
 
-def band_kernel(to_ref, _, kt_hbm, kwide_hbm, kvt_ref, kut_ref, ku_ref, zero_ref, kt_ref, kwide_ref, sems):
+def band_kernel(odd, me_ref, to_ref, kt_hbm, kwide_hbm, *rest):
+    kvt_ref, kut_ref, ku_ref, zero_ref, kt_ref, kwide_ref, sems = rest[-7:]
     slots = kut_ref.shape[0]
-    copies = [
-        pltpu.make_async_copy(kt_hbm, kt_ref, sems.at[0]),
-        pltpu.make_async_copy(kwide_hbm, kwide_ref, sems.at[1]),
-    ]
-    for copy in copies:
-        copy.start()
     zero_ref[...] = jnp.zeros_like(zero_ref)
-    for copy in copies:
-        copy.wait()
-    for t in range(slots):
-        ou, ov = to_ref[0, t], to_ref[1, t]
-        rows = slice(t * TV, (t + 1) * TV)
-        kut_ref[t] = kt_ref[pl.ds(2 * TV - ou, SG), :].astype(BF)
-        kvt_ref[:, rows] = kt_ref[pl.ds(2 * TV - ov, SG), :].astype(BF)
-        ku_ref[rows] = pltpu.roll(kwide_ref[...], ou, 1).astype(BF)
+
+    @pl.when((me_ref[0] & 1) == odd)
+    def _():
+        copies = [
+            pltpu.make_async_copy(kt_hbm, kt_ref, sems.at[0]),
+            pltpu.make_async_copy(kwide_hbm, kwide_ref, sems.at[1]),
+        ]
+        for copy in copies:
+            copy.start()
+        for copy in copies:
+            copy.wait()
+        for t in range(slots):
+            ou, ov = to_ref[0, t], to_ref[1, t]
+            rows = slice(t * TV, (t + 1) * TV)
+            kut_ref[t] = kt_ref[pl.ds(2 * TV - ou, SG), :].astype(BF)
+            kvt_ref[:, rows] = kt_ref[pl.ds(2 * TV - ov, SG), :].astype(BF)
+            ku_ref[rows] = pltpu.roll(kwide_ref[...], ou, 1).astype(BF)
 
 
 def screen_kernel(w_ref, _, *rest):
@@ -312,7 +316,9 @@
 
 
 def next_grid_kernel(pieces, me_ref, fo_ref, so_ref, *rest):
-    grid_blocks(pieces, rest[:-2], me_ref, fo_ref, so_ref, rest[-2])
+    grid_ref, _, zero_ref = rest[-3:]
+    zero_ref[...] = jnp.zeros_like(zero_ref)
+    grid_blocks(pieces, rest[:-3], me_ref, fo_ref, so_ref, grid_ref)
 
 
 def backward_kernel(pieces, me_ref, fo_ref, so_ref, basis_ref, *rest):
@@ -387,7 +393,7 @@
 def reduce_sends(n):
     sends = []
     for base, radix in digit_levels(n):
-        for g in range(1, radix):
+        for g in range(radix - 1, 0, -1):
             js = [j for j in range(0, n, base) if (j // base) % radix == g]
             groups = [js[1::2], js[::2]] if base == 1 else [js]
             sends += [(group, g * base) for group in groups]
@@ -449,25 +455,28 @@
             name="extract",
         )(me, facet_offsets, corners, near(spec), *[near(value) for value in after])
 
-    def make_bands(after):
+    def make_bands(odd, bands, after):
+        shapes = [(SG, slots * TV), (slots, SG, TV), (slots * TV, SG)]
         return pl.pallas_call(
-            band_kernel,
-            out_shape=[
-                held((SG, slots * TV)),
-                held((slots, SG, TV)),
-                held((slots * TV, SG)),
-                held((1, M), F32),
-            ],
-            in_specs=[SMEM, VMEM] + [ANY] * 2,
+            functools.partial(band_kernel, odd),
+            out_shape=[held(shape) for shape in shapes] + [held((1, M), F32)],
+            in_specs=[SMEM] * 2 + [ANY] * 2 + [VMEM] * (len(bands) + len(after)),
             out_specs=[VMEM] * 4,
             scratch_shapes=[
                 pltpu.VMEM(kt_np.shape, F32),
                 pltpu.VMEM(kwide_np.shape, F32),
                 pltpu.SemaphoreType.DMA((2,)),
             ],
+            input_output_aliases={4 + k: k for k in range(len(bands))},
             compiler_params=params(8),
             name="bands",
-        )(tile_corners, near(after), far(jnp.asarray(kt_np)), far(jnp.asarray(kwide_np)))
+        )(
+            me,
+            tile_corners,
+            far(jnp.asarray(kt_np)),
+            far(jnp.asarray(kwide_np)),
+            *[near(value) for value in list(bands) + after],
+        )
 
     def make_screen(after):
         loads = [observed, pad_np, pad_np.transpose(0, 2, 1), subgrid_offsets.T, facet_offsets]
@@ -499,13 +508,14 @@
     (urgent, _), (lazy, _), (beside, _) = sends[:3]
     send(urgent, 1, first)
     beside_own, lazy_own = make_blocks([beside, lazy], [])
-    value = send(beside, 2, beside_own)
+    *bands, token = make_bands(0, [], [beside_own])
+    value = send(beside, 2, beside_own, token)
     send(lazy, 1, lazy_own)
     own = make_blocks([js for js, _ in sends[3:]] + [[0]], [value])
-    kvt, kut, ku, token = make_bands(value)
-    screen, tiles, pad, padt, late_corners, late_facet_offsets, token = make_screen(token)
+    screen, tiles, pad, padt, late_corners, late_facet_offsets, token = make_screen(value)
     for (js, mask), value in zip(sends[3:], own):
         value = send(js, mask, value, token)
+    kvt, kut, ku, _ = make_bands(1, bands, [value])
     corners, facet_offsets = near(late_corners), near(late_facet_offsets)
     last = [(js, got) for js, got in arrived if 0 in js]
 
@@ -533,14 +543,26 @@
     early = ([0], coefficient)
     for base, radix in reversed(digit_levels(n)[2:]):
         js, value = early
-        more = [([j ^ (g * base) for j in js], exchange(value, g * base, n)) for g in range(1, radix)]
+        masks = [g * base for g in range(radix - 1, 0, -1)]
+        more = [([j ^ mask for j in js], exchange(value, mask, n)) for mask in masks]
         early = join([early] + more)
 
     def hop(part, mask):
         return [j ^ mask for j in part[0]], exchange(part[1], mask, n)
 
     late = hop(early, 2)
-    ready = [early, hop(early, 1)]
+    ready = [early]
+    def next_grid(ready, grid):
+        return pl.pallas_call(
+            functools.partial(next_grid_kernel, [js for js, _ in ready]),
+            out_shape=[held(grid_shape, F32), held((1, M), F32)],
+            in_specs=[SMEM] * 3 + [VMEM] * (len(ready) + 1),
+            out_specs=[VMEM] * 2,
+            input_output_aliases={3 + len(ready): 0},
+            compiler_params=params(8),
+            name="grid_next",
+        )(me, facet_offsets, corners, *[near(value) for _, value in ready], near(grid))
+
     grid, token, basis_near = pl.pallas_call(
         functools.partial(first_grid_kernel, [js for js, _ in ready]),
         out_shape=[held(grid_shape, F32), held((1, M), F32), held(basis.shape)],
@@ -550,18 +572,10 @@
         compiler_params=params(8),
         name="grid_first",
     )(me, facet_offsets, corners, basis, *[near(value) for _, value in ready])
+    other = hop(early, 1)
     late = (late[0], (late[1].astype(F32) + token).astype(BF))
     late_other = hop(late, 1)
-    ready = [late]
-    grid = pl.pallas_call(
-        functools.partial(next_grid_kernel, [js for js, _ in ready]),
-        out_shape=held(grid_shape, F32),
-        in_specs=[SMEM] * 3 + [VMEM] * (len(ready) + 1),
-        out_specs=VMEM,
-        input_output_aliases={3 + len(ready): 0},
-        compiler_params=params(8),
-        name="grid_next",
-    )(me, facet_offsets, corners, *[near(value) for _, value in ready], near(grid))
+    grid, _ = next_grid([other, late], grid)
     update = pl.pallas_call(
         functools.partial(backward_kernel, [late_other[0]]),
         out_shape=[pltpu.HBM(facets.shape, BF), held(grid_shape, F32)],

time: 58.8 us -> 56.2 us (0.956)
  waiting for transfers between devices: 15.9 us -> 4.04 us
  starting transfers between devices: 12.3 us -> 19.8 us
  Pallas kernels: 27.8 us -> 29.5 us
    ppermute x12, waiting for transfers between devices: 15.9 us -> 4.04 us  [exchange(): return lax.ppermute(value, 'facet', [(i, i ^ mask) for i in range(n)])]
    ppermute x12, starting transfers between devices: 12.3 us -> 19.8 us  [exchange(): return lax.ppermute(value, 'facet', [(i, i ^ mask) for i in range(n)])]
    pallas_call x2 -> x3, Pallas kernels: 4.63 us -> 6.4 us  [the longest x2 4.81 us: make_bands(): pl.pallas_call(functools.partial(band_kernel, odd), out_shape=[held(shape...]
  transfers between devices with their start and end apart: 12 -> 12, of which waited for: 6 -> 3; matrix products, arithmetic and copies ran while one was open for 0% -> 0% of each run, Pallas kernels for 19% -> 24%
where the time goes in v10:
time: 56.2 us; the launch traced here: 55.9 us
  Pallas kernels  29.5 us (52%)
  starting transfers between devices  19.8 us (35%)
  waiting for transfers between devices  4.04 us (7%)
  between operations  2.25 us (4%)
    ppermute x12, starting transfers between devices, exchange(): return lax.ppermute(value, 'facet', [(i, i ^ mask) for i in range(n)])  19.8 us
    pallas_call x1, Pallas kernels, per_device(): pl.pallas_call(functools.partial(subgrid_kernel, [0] + [js.index(0) for j...  7.61 us
    pallas_call x2, Pallas kernels, make_bands(): pl.pallas_call(functools.partial(band_kernel, odd), out_shape=[held(shape...  4.81 us
    pallas_call x1, Pallas kernels, per_device(): pl.pallas_call(functools.partial(forward_kernel, sends[0][0]), out_shape=...  4.54 us
    pallas_call x1, Pallas kernels, per_device(): pl.pallas_call(functools.partial(backward_kernel, [late_other[0]]), out_s...  4.06 us
    ppermute x12, waiting for transfers between devices, exchange(): return lax.ppermute(value, 'facet', [(i, i ^ mask) for i in range(n)])  4.04 us
    pallas_call x2, Pallas kernels, make_blocks(): pl.pallas_call(functools.partial(extract_kernel, lists), out_shape=[held(...  3.12 us
    pallas_call x1, Pallas kernels, per_device(): pl.pallas_call(functools.partial(first_grid_kernel, [js for js, _ in read...  2.11 us
  transfers between devices with their start and end apart: 12, of which 3 were waited for; matrix products, arithmetic and copies ran while one was open for 0% of the time, Pallas kernels for 24%

profile of v10, /device:TPU:1, one launch (start us, length us, event | category | flops | bytes accessed | tf_op | source)
XLA Modules:
  0.0 55.9 jit_solution(17450758983846791181)
XLA Ops:
  0.6 4.5 %forward.1 = (bf16[4,2,128,128]{3,2,1,0:T(8,128)(2,1)S(1)}, f32[2,5,640,128]{3,2,1,0:T(8,128)S(1)}) custom-call(s32[1]{0:T(128)} %bitcast.1.me_ref, s32[1,2]{1,0:T(1,128)} %rest_4_.1, s32[2,16]{1,0:T(2,128)} %bitcast.13, bf16[1,2,512,512]{3,2,1,0:T(8,128)(2,1)} %facet_ref.1, bf16[2,512,512]{2,1,0:T(8,128)(2,1)} %constant.14.clone.basis_ref.basis_hbm), custom_call_target="tpu_custom_call" | custom-call | tf_op jit(solution)/shard_map/forward/pallas_call | solution.py:433
  5.2 0.1 collective-permute-start
  5.3 2.1 %extract.2 = (bf16[4,2,128,128]{3,2,1,0:T(8,128)(2,1)S(1)}, bf16[4,2,128,128]{3,2,1,0:T(8,128)(2,1)S(1)}) custom-call(s32[1]{0:T(128)} %bitcast.1.me_ref, s32[1,2]{1,0:T(1,128)} %rest_4_.1, s32[2,16]{1,0:T(2,128)} %bitcast.14, f32[2,5,640,128]{3,2,1,0:T(8,128)S(1)} %get-tuple-element.31.spec_ref), custom_call_target="tpu_custom_call" | custom-call | tf_op jit(solution)/shard_map/extract/pallas_call | solution.py:449
  7.4 0.5 collective-permute-start.2
  7.9 0.7 %bands.2 = (bf16[512,2048]{1,0:T(8,128)(2,1)S(1)}, bf16[16,512,128]{2,1,0:T(8,128)(2,1)S(1)}, bf16[2048,512]{1,0:T(8,128)(2,1)S(1)}, f32[1,128]{1,0:T(1,128)S(1)}) custom-call(s32[1]{0:T(128)} %bitcast.1.me_ref, s32[2,16]{1,0:T(2,128)} %bitcast.17, f32[768,128]{1,0:T(8,128)} %constant.15.clone.kt_hbm, f32[128,512]{1,0:T(8,128)} %constant.16.clone.kwide_hbm, ...), custom_call_target="tpu_custom_call" | custom-call | tf_op jit(solution)/shard_map/bands/pallas_call | solution.py:460
  8.7 2.3 %collective-permute-start.1 = (bf16[4,2,128,128]{3,2,1,0:T(8,128)(2,1)S(1)}, bf16[4,2,128,128]{3,2,1,0:T(8,128)(2,1)S(1)}, u32[]{:S(2)}, u32[]{:S(2)}) collective-permute-start(bf16[4,2,128,128]{3,2,1,0:T(8,128)(2,1)S(1)} %add_convert_fusion.1.outs_0_._), channel_id=1, source_target_pairs={{0,2},{1,3},{2,0},{3,1},{4,6},{5,7},{6,4},{7,5},{8,10},{9,11},{10,... | collective-permute-start | bytes 786440 | tf_op jit(solution)/shard_map/ppermute | solution.py:381
  11.7 1.1 %extract.3 = (bf16[1,2,128,128]{3,2,1,0:T(8,128)(2,1)S(1)}, bf16[1,2,128,128]{3,2,1,0:T(8,128)(2,1)S(1)}, bf16[1,2,128,128]{3,2,1,0:T(8,128)(2,1)S(1)}, bf16[1,2,128,128]{3,2,1,0:T(8,128)(2,1)S(1)}) custom-call(s32[1]{0:T(128)} %bitcast.1.me_ref, s32[1,2]{1,0:T(1,128)} %rest_4_.1, s32[2,16]{1,0:T(2,128)} %bitcast.15, ...), custom_call_target="tpu_custom_call" | custom-call | tf_op jit(solution)/shard_map/extract/pallas_call | solution.py:449
  12.7 1.6 %screen.1 = (f32[2,512,512]{2,1,0:T(8,128)S(1)}, bf16[16,2,128,128]{3,2,1,0:T(8,128)(2,1)S(1)}, bf16[2,512,128]{2,1,0:T(8,128)(2,1)S(1)}, bf16[2,128,512]{2,1,0:...) custom-call(f32[1,1]{1,0:T(1,128)} %bitcast.8.w_ref, ...), custom_call_target="tpu_custom_call" | custom-call | tf_op jit(solution)/shard_map/screen/pallas_call | solution.py:483
  14.4 0.4 collective-permute-done.1.rest_1_
  14.8 0.1 add_convert_fusion.2
  14.9 3.6 %collective-permute-start.3 = (bf16[1,2,128,128]{3,2,1,0:T(8,128)(2,1)S(1)}, bf16[1,2,128,128]{3,2,1,0:T(8,128)(2,1)S(1)}, u32[]{:S(2)}, u32[]{:S(2)}) collective-permute-start(bf16[1,2,128,128]{3,2,1,0:T(8,128)(2,1)S(1)} %get-tuple-element.62), channel_id=1, source_target_pairs={{0,12},{1,13},{2,14},{3,15},{4,8},{5,9},{6,10},{7,11},{8,4},{9,5},... | collective-permute-start | bytes 196616 | tf_op jit(solution)/shard_map/ppermute | solution.py:381
  18.5 0.4 collective-permute-start.5
  19.5 4.1 %bands.3 = (bf16[512,2048]{1,0:T(8,128)(2,1)S(1)}, bf16[16,512,128]{2,1,0:T(8,128)(2,1)S(1)}, bf16[2048,512]{1,0:T(8,128)(2,1)S(1)}, f32[1,128]{1,0:T(1,128)}) custom-call(s32[1]{0:T(128)} %bitcast.1.me_ref, s32[2,16]{1,0:T(2,128)} %bitcast.18, f32[768,128]{1,0:T(8,128)} %constant.15.clone.kt_hbm, ...), custom_call_target="tpu_custom_call", output_to_operand_aliasing={{0}: (4, {}), {1}: (5, {}), {2}: (6, {})} | custom-call | tf_op jit(solution)/shard_map/bands/pallas_call | solution.py:460
  23.6 7.6 %subgrid.1 = (bf16[16,2,128,128]{3,2,1,0:T(8,128)(2,1)}, bf16[1,2,128,128]{3,2,1,0:T(8,128)(2,1)S(1)}) custom-call(s32[1,1]{1,0:T(1,128)} %bitcast.9.tc_ref, bf16[1,2,128,128]{3,2,1,0:T(8,128)(2,1)S(1)} %get-tuple-element.35.rest_0_, bf16[4,2,128,128]{3,2,1,0:T(8,128)(2,1)S(1)} %collective-permute-done.1.rest_1_, ...), custom_call_target="tpu_custom_call" | custom-call | tf_op jit(solution)/shard_map/subgrid/pallas_call | solution.py:522
  31.3 3.3 %collective-permute-start.6 = (bf16[1,2,128,128]{3,2,1,0:T(8,128)(2,1)S(1)}, bf16[1,2,128,128]{3,2,1,0:T(8,128)(2,1)S(1)}, u32[]{:S(2)}, u32[]{:S(2)}) collective-permute-start(bf16[1,2,128,128]{3,2,1,0:T(8,128)(2,1)S(1)} %get-tuple-element.54), channel_id=1, source_target_pairs={{0,12},{1,13},{2,14},{3,15},{4,8},{5,9},{6,10},{7,11},{8,4},{9,5},... | collective-permute-start | bytes 196616 | tf_op jit(solution)/shard_map/ppermute | solution.py:381
  34.5 0.4 collective-permute-start.8
  34.9 1.4 %collective-permute-done.6 = bf16[1,2,128,128]{3,2,1,0:T(8,128)(2,1)S(1)} collective-permute-done((bf16[1,2,128,128]{3,2,1,0:T(8,128)(2,1)S(1)}, bf16[1,2,128,128]{3,2,1,0:T(8,128)(2,1)S(1)}, u32[]{:S(2)}, u32[]{:S(2)}) %collective-permute-start.6) | collective-permute-done | bytes 65568 | tf_op jit(solution)/shard_map/ppermute | solution.py:381
  36.2 2.3 %collective-permute-done.7 = bf16[1,2,128,128]{3,2,1,0:T(8,128)(2,1)S(1)} collective-permute-done((bf16[1,2,128,128]{3,2,1,0:T(8,128)(2,1)S(1)}, bf16[1,2,128,128]{3,2,1,0:T(8,128)(2,1)S(1)}, u32[]{:S(2)}, u32[]{:S(2)}) %collective-permute-start.7) | collective-permute-done | bytes 65568 | tf_op jit(solution)/shard_map/ppermute | solution.py:381
  38.6 1.3 %collective-permute-start.9 = (bf16[4,2,128,128]{3,2,1,0:T(8,128)(2,1)S(1)}, bf16[4,2,128,128]{3,2,1,0:T(8,128)(2,1)S(1)}, u32[]{:S(2)}, u32[]{:S(2)}) collective-permute-start(bf16[4,2,128,128]{3,2,1,0:T(8,128)(2,1)S(1)} %constant_dynamic-update-slice_fusion.rest_0_), channel_id=1, source_target_pairs={{0,2},{1,3},{2,0},{3,1},{4,6},{5,7},{6,4},{7,5},{8,10},{9,11},{10,... | collective-permute-start | bytes 786440 | tf_op jit(solution)/shard_map/ppermute | solution.py:381
  39.9 5.2 %collective-permute-start.11 = (bf16[4,2,128,128]{3,2,1,0:T(8,128)(2,1)S(1)}, bf16[4,2,128,128]{3,2,1,0:T(8,128)(2,1)S(1)}, u32[]{:S(2)}, u32[]{:S(2)}) collective-permute-start(bf16[4,2,128,128]{3,2,1,0:T(8,128)(2,1)S(1)} %constant_dynamic-update-slice_fusion.rest_0_), channel_id=1, source_target_pairs={{0,1},{1,0},{2,3},{3,2},{4,5},{5,4},{6,7},{7,6},{8,9},{9,8},{10,11... | collective-permute-start | bytes 786440 | tf_op jit(solution)/shard_map/ppermute | solution.py:381
  45.1 2.1 %grid_first.1 = (f32[2,5,640,128]{3,2,1,0:T(8,128)S(1)}, f32[1,128]{1,0:T(1,128)S(1)}, bf16[2,512,512]{2,1,0:T(8,128)(2,1)S(1)}) custom-call(s32[1]{0:T(128)} %bitcast.1.me_ref, s32[1,2]{1,0:T(1,128)S(1)} %get-tuple-element.52.fo_ref, s32[2,16]{1,0:T(2,128)S(1)} %get-tuple-element.53.so_ref, bf16[2,512,512]{2,1,0:T(8,128)(2,1)} %constant.14.clone.basis_ref.basis_hbm, ...), custom_call_target="tpu_custom_call" | custom-call | tf_op jit(solution)/shard_map/grid_first/pallas_call | solution.py:566
  47.3 2.8 %collective-permute-start.10 = (bf16[4,2,128,128]{3,2,1,0:T(8,128)(2,1)S(1)}, bf16[4,2,128,128]{3,2,1,0:T(8,128)(2,1)S(1)}, u32[]{:S(2)}, u32[]{:S(2)}) collective-permute-start(bf16[4,2,128,128]{3,2,1,0:T(8,128)(2,1)S(1)} %add_convert_fusion.rest_1_), channel_id=1, source_target_pairs={{0,1},{1,0},{2,3},{3,2},{4,5},{5,4},{6,7},{7,6},{8,9},{9,8},{10,11... | collective-permute-start | bytes 786440 | tf_op jit(solution)/shard_map/ppermute | solution.py:381
  50.0 1.6 %grid_next.1 = (f32[2,5,640,128]{3,2,1,0:T(8,128)S(1)}, f32[1,128]{1,0:T(1,128)}) custom-call(s32[1]{0:T(128)} %bitcast.1.me_ref, s32[1,2]{1,0:T(1,128)S(1)} %get-tuple-element.52.fo_ref, s32[2,16]{1,0:T(2,128)S(1)} %get-tuple-element.53.so_ref, bf16[4,2,128,128]{3,2,1,0:T(8,128)(2,1)S(1)} %collective-permute-done.11.rest_0_, ...), custom_call_target="tpu_custom_call", output_to_operand_aliasing={{0}: (5, {})} | custom-call | tf_op jit(solution)/shard_map/grid_next/pallas_call | solution.py:556
  51.6 4.1 %backward.1 = (bf16[1,2,512,512]{3,2,1,0:T(8,128)(2,1)}, f32[2,5,640,128]{3,2,1,0:T(8,128)S(1)}) custom-call(s32[1]{0:T(128)} %bitcast.1.me_ref, s32[1,2]{1,0:T(1,128)S(1)} %get-tuple-element.52.fo_ref, s32[2,16]{1,0:T(2,128)S(1)} %get-tuple-element.53.so_ref, bf16[2,512,512]{2,1,0:T(8,128)(2,1)S(1)} %get-tuple-element.55.basis_ref, ...), custom_call_target="tpu_custom_call", output_to_operand_aliasing={{1}: (5, {})} | custom-call | tf_op jit(solution)/shard_map/backward/pallas_call | solution.py:579
  (17 shorter events, 0.2 us)
Async XLA Ops:
  5.2 3.4 %collective-permute-start = (bf16[4,2,128,128]{3,2,1,0:T(8,128)(2,1)S(1)}, bf16[4,2,128,128]{3,2,1,0:T(8,128)(2,1)S(1)}, u32[]{:S(2)}, u32[]{:S(2)}) collective-permute-start(bf16[4,2,128,128]{3,2,1,0:T(8,128)(2,1)S(1)} %get-tuple-element.34), channel_id=1, source_target_pairs={{0,1},{1,0},{2,3},{3,2},{4,5},{5,4},{6,7},{7,6},{8,9},{9,8},{10,11... | collective-permute-start | bytes 786440 | tf_op jit(solution)/shard_map/ppermute | solution.py:381
  7.4 7.0 %collective-permute-start.2 = (bf16[4,2,128,128]{3,2,1,0:T(8,128)(2,1)S(1)}, bf16[4,2,128,128]{3,2,1,0:T(8,128)(2,1)S(1)}, u32[]{:S(2)}, u32[]{:S(2)}) collective-permute-start(bf16[4,2,128,128]{3,2,1,0:T(8,128)(2,1)S(1)} %get-tuple-element.36), channel_id=1, source_target_pairs={{0,1},{1,0},{2,3},{3,2},{4,5},{5,4},{6,7},{7,6},{8,9},{9,8},{10,11... | collective-permute-start | bytes 786440 | tf_op jit(solution)/shard_map/ppermute | solution.py:381
  8.7 6.1 %collective-permute-start.1 = (bf16[4,2,128,128]{3,2,1,0:T(8,128)(2,1)S(1)}, bf16[4,2,128,128]{3,2,1,0:T(8,128)(2,1)S(1)}, u32[]{:S(2)}, u32[]{:S(2)}) collective-permute-start(bf16[4,2,128,128]{3,2,1,0:T(8,128)(2,1)S(1)} %add_convert_fusion.1.outs_0_._), channel_id=1, source_target_pairs={{0,2},{1,3},{2,0},{3,1},{4,6},{5,7},{6,4},{7,5},{8,10},{9,11},{10,... | collective-permute-start | bytes 786440 | tf_op jit(solution)/shard_map/ppermute | solution.py:381
  14.9 8.7 %collective-permute-start.3 = (bf16[1,2,128,128]{3,2,1,0:T(8,128)(2,1)S(1)}, bf16[1,2,128,128]{3,2,1,0:T(8,128)(2,1)S(1)}, u32[]{:S(2)}, u32[]{:S(2)}) collective-permute-start(bf16[1,2,128,128]{3,2,1,0:T(8,128)(2,1)S(1)} %get-tuple-element.62), channel_id=1, source_target_pairs={{0,12},{1,13},{2,14},{3,15},{4,8},{5,9},{6,10},{7,11},{8,4},{9,5},... | collective-permute-start | bytes 196616 | tf_op jit(solution)/shard_map/ppermute | solution.py:381
  18.5 5.1 %collective-permute-start.4 = (bf16[1,2,128,128]{3,2,1,0:T(8,128)(2,1)S(1)}, bf16[1,2,128,128]{3,2,1,0:T(8,128)(2,1)S(1)}, u32[]{:S(2)}, u32[]{:S(2)}) collective-permute-start(bf16[1,2,128,128]{3,2,1,0:T(8,128)(2,1)S(1)} %get-tuple-element.61), channel_id=1, source_target_pairs={{0,8},{1,9},{2,10},{3,11},{4,12},{5,13},{6,14},{7,15},{8,0},{9,1},... | collective-permute-start | bytes 196616 | tf_op jit(solution)/shard_map/ppermute | solution.py:381
  18.5 5.1 %collective-permute-start.5 = (bf16[1,2,128,128]{3,2,1,0:T(8,128)(2,1)S(1)}, bf16[1,2,128,128]{3,2,1,0:T(8,128)(2,1)S(1)}, u32[]{:S(2)}, u32[]{:S(2)}) collective-permute-start(bf16[1,2,128,128]{3,2,1,0:T(8,128)(2,1)S(1)} %get-tuple-element.60.rest_3_), channel_id=1, source_target_pairs={{0,4},{1,5},{2,6},{3,7},{4,0},{5,1},{6,2},{7,3},{8,12},{9,13},{10,... | collective-permute-start | bytes 196616 | tf_op jit(solution)/shard_map/ppermute | solution.py:381
  31.3 5.0 %collective-permute-start.6 = (bf16[1,2,128,128]{3,2,1,0:T(8,128)(2,1)S(1)}, bf16[1,2,128,128]{3,2,1,0:T(8,128)(2,1)S(1)}, u32[]{:S(2)}, u32[]{:S(2)}) collective-permute-start(bf16[1,2,128,128]{3,2,1,0:T(8,128)(2,1)S(1)} %get-tuple-element.54), channel_id=1, source_target_pairs={{0,12},{1,13},{2,14},{3,15},{4,8},{5,9},{6,10},{7,11},{8,4},{9,5},... | collective-permute-start | bytes 196616 | tf_op jit(solution)/shard_map/ppermute | solution.py:381
  34.5 4.0 %collective-permute-start.7 = (bf16[1,2,128,128]{3,2,1,0:T(8,128)(2,1)S(1)}, bf16[1,2,128,128]{3,2,1,0:T(8,128)(2,1)S(1)}, u32[]{:S(2)}, u32[]{:S(2)}) collective-permute-start(bf16[1,2,128,128]{3,2,1,0:T(8,128)(2,1)S(1)} %get-tuple-element.54), channel_id=1, source_target_pairs={{0,8},{1,9},{2,10},{3,11},{4,12},{5,13},{6,14},{7,15},{8,0},{9,1},... | collective-permute-start | bytes 196616 | tf_op jit(solution)/shard_map/ppermute | solution.py:381
  34.5 4.0 %collective-permute-start.8 = (bf16[1,2,128,128]{3,2,1,0:T(8,128)(2,1)S(1)}, bf16[1,2,128,128]{3,2,1,0:T(8,128)(2,1)S(1)}, u32[]{:S(2)}, u32[]{:S(2)}) collective-permute-start(bf16[1,2,128,128]{3,2,1,0:T(8,128)(2,1)S(1)} %get-tuple-element.54), channel_id=1, source_target_pairs={{0,4},{1,5},{2,6},{3,7},{4,0},{5,1},{6,2},{7,3},{8,12},{9,13},{10,... | collective-permute-start | bytes 196616 | tf_op jit(solution)/shard_map/ppermute | solution.py:381
  38.6 8.6 %collective-permute-start.9 = (bf16[4,2,128,128]{3,2,1,0:T(8,128)(2,1)S(1)}, bf16[4,2,128,128]{3,2,1,0:T(8,128)(2,1)S(1)}, u32[]{:S(2)}, u32[]{:S(2)}) collective-permute-start(bf16[4,2,128,128]{3,2,1,0:T(8,128)(2,1)S(1)} %constant_dynamic-update-slice_fusion.rest_0_), channel_id=1, source_target_pairs={{0,2},{1,3},{2,0},{3,1},{4,6},{5,7},{6,4},{7,5},{8,10},{9,11},{10,... | collective-permute-start | bytes 786440 | tf_op jit(solution)/shard_map/ppermute | solution.py:381
  39.9 10.2 %collective-permute-start.11 = (bf16[4,2,128,128]{3,2,1,0:T(8,128)(2,1)S(1)}, bf16[4,2,128,128]{3,2,1,0:T(8,128)(2,1)S(1)}, u32[]{:S(2)}, u32[]{:S(2)}) collective-permute-start(bf16[4,2,128,128]{3,2,1,0:T(8,128)(2,1)S(1)} %constant_dynamic-update-slice_fusion.rest_0_), channel_id=1, source_target_pairs={{0,1},{1,0},{2,3},{3,2},{4,5},{5,4},{6,7},{7,6},{8,9},{9,8},{10,11... | collective-permute-start | bytes 786440 | tf_op jit(solution)/shard_map/ppermute | solution.py:381
  47.3 4.4 %collective-permute-start.10 = (bf16[4,2,128,128]{3,2,1,0:T(8,128)(2,1)S(1)}, bf16[4,2,128,128]{3,2,1,0:T(8,128)(2,1)S(1)}, u32[]{:S(2)}, u32[]{:S(2)}) collective-permute-start(bf16[4,2,128,128]{3,2,1,0:T(8,128)(2,1)S(1)} %add_convert_fusion.rest_1_), channel_id=1, source_target_pairs={{0,1},{1,0},{2,3},{3,2},{4,5},{5,4},{6,7},{7,6},{8,9},{9,8},{10,11... | collective-permute-start | bytes 786440 | tf_op jit(solution)/shard_map/ppermute | solution.py:381

commit v11 on v10

--- a/solution.py
+++ b/solution.py
@@ -180,13 +180,11 @@
             block(ref, item, j)
 
 
-def band_kernel(odd, me_ref, to_ref, kt_hbm, kwide_hbm, *rest):
+def band_kernel(odds, tiles, me_ref, to_ref, kt_hbm, kwide_hbm, *rest):
     kvt_ref, kut_ref, ku_ref, zero_ref, kt_ref, kwide_ref, sems = rest[-7:]
-    slots = kut_ref.shape[0]
     zero_ref[...] = jnp.zeros_like(zero_ref)
 
-    @pl.when((me_ref[0] & 1) == odd)
-    def _():
+    def make():
         copies = [
             pltpu.make_async_copy(kt_hbm, kt_ref, sems.at[0]),
             pltpu.make_async_copy(kwide_hbm, kwide_ref, sems.at[1]),
@@ -195,12 +193,17 @@
             copy.start()
         for copy in copies:
             copy.wait()
-        for t in range(slots):
+        for t in tiles:
             ou, ov = to_ref[0, t], to_ref[1, t]
             rows = slice(t * TV, (t + 1) * TV)
             kut_ref[t] = kt_ref[pl.ds(2 * TV - ou, SG), :].astype(BF)
             kvt_ref[:, rows] = kt_ref[pl.ds(2 * TV - ov, SG), :].astype(BF)
             ku_ref[rows] = pltpu.roll(kwide_ref[...], ou, 1).astype(BF)
+
+    if len(odds) == 2:
+        make()
+    else:
+        pl.when((me_ref[0] & 1) == odds[0])(make)
 
 
 def screen_kernel(w_ref, _, *rest):
@@ -455,10 +458,10 @@
             name="extract",
         )(me, facet_offsets, corners, near(spec), *[near(value) for value in after])
 
-    def make_bands(odd, bands, after):
+    def make_bands(odds, tiles, bands, after):
         shapes = [(SG, slots * TV), (slots, SG, TV), (slots * TV, SG)]
         return pl.pallas_call(
-            functools.partial(band_kernel, odd),
+            functools.partial(band_kernel, odds, tiles),
             out_shape=[held(shape) for shape in shapes] + [held((1, M), F32)],
             in_specs=[SMEM] * 2 + [ANY] * 2 + [VMEM] * (len(bands) + len(after)),
             out_specs=[VMEM] * 4,
@@ -508,14 +511,16 @@
     (urgent, _), (lazy, _), (beside, _) = sends[:3]
     send(urgent, 1, first)
     beside_own, lazy_own = make_blocks([beside, lazy], [])
-    *bands, token = make_bands(0, [], [beside_own])
+    some, others = range(slots // 2), range(slots // 2, slots)
+    *bands, token = make_bands([0], some, [], [beside_own])
     value = send(beside, 2, beside_own, token)
     send(lazy, 1, lazy_own)
     own = make_blocks([js for js, _ in sends[3:]] + [[0]], [value])
     screen, tiles, pad, padt, late_corners, late_facet_offsets, token = make_screen(value)
+    *bands, band_token = make_bands([0, 1], others, bands, [value])
     for (js, mask), value in zip(sends[3:], own):
-        value = send(js, mask, value, token)
-    kvt, kut, ku, _ = make_bands(1, bands, [value])
+        value = send(js, mask, value, token + band_token)
+    kvt, kut, ku, _ = make_bands([1], some, bands, [value])
     corners, facet_offsets = near(late_corners), near(late_facet_offsets)
     last = [(js, got) for js, got in arrived if 0 in js]
 

time: 56.2 us -> 56.6 us (level)
  Pallas kernels: 29.5 us -> 31.3 us
  starting transfers between devices: 19.8 us -> 18 us
    ppermute x12, starting transfers between devices: 19.8 us -> 18 us  [exchange(): return lax.ppermute(value, 'facet', [(i, i ^ mask) for i in range(n)])]
    pallas_call x2 -> x3, Pallas kernels: 4.81 us -> 6.62 us  [make_bands(): pl.pallas_call(functools.partial(band_kernel, odds, tiles), out_shape=[he...]
  transfers between devices with their start and end apart: 12 -> 12, of which waited for: 3 -> 3; matrix products, arithmetic and copies ran while one was open for 0% -> 0% of each run, Pallas kernels for 24% -> 27%
where the time goes in v11:
time: 56.6 us; the launch traced here: 56.3 us
  Pallas kernels  31.3 us (55%)
  starting transfers between devices  18 us (32%)
  waiting for transfers between devices  4.43 us (8%)
  between operations  2.26 us (4%)
    ppermute x12, starting transfers between devices, exchange(): return lax.ppermute(value, 'facet', [(i, i ^ mask) for i in range(n)])  18 us
    pallas_call x1, Pallas kernels, per_device(): pl.pallas_call(functools.partial(subgrid_kernel, [0] + [js.index(0) for j...  7.6 us
    pallas_call x3, Pallas kernels, make_bands(): pl.pallas_call(functools.partial(band_kernel, odds, tiles), out_shape=[he...  6.62 us
    pallas_call x1, Pallas kernels, per_device(): pl.pallas_call(functools.partial(forward_kernel, sends[0][0]), out_shape=...  4.54 us
    ppermute x12, waiting for transfers between devices, exchange(): return lax.ppermute(value, 'facet', [(i, i ^ mask) for i in range(n)])  4.43 us
    pallas_call x1, Pallas kernels, per_device(): pl.pallas_call(functools.partial(backward_kernel, [late_other[0]]), out_s...  4.06 us
    pallas_call x2, Pallas kernels, make_blocks(): pl.pallas_call(functools.partial(extract_kernel, lists), out_shape=[held(...  3.12 us
    pallas_call x1, Pallas kernels, per_device(): pl.pallas_call(functools.partial(first_grid_kernel, [js for js, _ in read...  2.11 us
  transfers between devices with their start and end apart: 12, of which 3 were waited for; matrix products, arithmetic and copies ran while one was open for 0% of the time, Pallas kernels for 27%

profile of v11, /device:TPU:1, one launch (start us, length us, event | category | flops | bytes accessed | tf_op | source)
XLA Modules:
  0.0 56.3 jit_solution(4604707788531950541)
XLA Ops:
  0.6 4.5 %forward.1 = (bf16[4,2,128,128]{3,2,1,0:T(8,128)(2,1)S(1)}, f32[2,5,640,128]{3,2,1,0:T(8,128)S(1)}) custom-call(s32[1]{0:T(128)} %bitcast.1.me_ref, s32[1,2]{1,0:T(1,128)} %rest_4_.1, s32[2,16]{1,0:T(2,128)} %bitcast.13, bf16[1,2,512,512]{3,2,1,0:T(8,128)(2,1)} %facet_ref.1, bf16[2,512,512]{2,1,0:T(8,128)(2,1)} %constant.14.clone.basis_ref.basis_hbm), custom_call_target="tpu_custom_call" | custom-call | tf_op jit(solution)/shard_map/forward/pallas_call | solution.py:436
  5.2 0.1 collective-permute-start
  5.3 2.1 %extract.2 = (bf16[4,2,128,128]{3,2,1,0:T(8,128)(2,1)S(1)}, bf16[4,2,128,128]{3,2,1,0:T(8,128)(2,1)S(1)}) custom-call(s32[1]{0:T(128)} %bitcast.1.me_ref, s32[1,2]{1,0:T(1,128)} %rest_4_.1, s32[2,16]{1,0:T(2,128)} %bitcast.14, f32[2,5,640,128]{3,2,1,0:T(8,128)S(1)} %get-tuple-element.35.spec_ref), custom_call_target="tpu_custom_call" | custom-call | tf_op jit(solution)/shard_map/extract/pallas_call | solution.py:452
  7.4 0.5 collective-permute-start.2
  7.9 0.7 %bands.3 = (bf16[512,2048]{1,0:T(8,128)(2,1)S(1)}, bf16[16,512,128]{2,1,0:T(8,128)(2,1)S(1)}, bf16[2048,512]{1,0:T(8,128)(2,1)S(1)}, f32[1,128]{1,0:T(1,128)S(1)}) custom-call(s32[1]{0:T(128)} %bitcast.1.me_ref, s32[2,16]{1,0:T(2,128)} %bitcast.17, f32[768,128]{1,0:T(8,128)} %constant.15.clone.kt_hbm, f32[128,512]{1,0:T(8,128)} %constant.16.clone.kwide_hbm, ...), custom_call_target="tpu_custom_call" | custom-call | tf_op jit(solution)/shard_map/bands/pallas_call | solution.py:463
  8.7 2.3 %collective-permute-start.1 = (bf16[4,2,128,128]{3,2,1,0:T(8,128)(2,1)S(1)}, bf16[4,2,128,128]{3,2,1,0:T(8,128)(2,1)S(1)}, u32[]{:S(2)}, u32[]{:S(2)}) collective-permute-start(bf16[4,2,128,128]{3,2,1,0:T(8,128)(2,1)S(1)} %add_convert_fusion.1.outs_0_._.rest_3_), channel_id=1, source_target_pairs={{0,2},{1,3},{2,0},{3,1},{4,6},{5,7},{6,4},{7,5},{8,10},{9,11},{10,... | collective-permute-start | bytes 786440 | tf_op jit(solution)/shard_map/ppermute | solution.py:384
  11.7 1.1 %extract.3 = (bf16[1,2,128,128]{3,2,1,0:T(8,128)(2,1)S(1)}, bf16[1,2,128,128]{3,2,1,0:T(8,128)(2,1)S(1)}, bf16[1,2,128,128]{3,2,1,0:T(8,128)(2,1)S(1)}, bf16[1,2,128,128]{3,2,1,0:T(8,128)(2,1)S(1)}) custom-call(s32[1]{0:T(128)} %bitcast.1.me_ref, s32[1,2]{1,0:T(1,128)} %rest_4_.1, s32[2,16]{1,0:T(2,128)} %bitcast.15, ...), custom_call_target="tpu_custom_call" | custom-call | tf_op jit(solution)/shard_map/extract/pallas_call | solution.py:452
  12.7 2.6 %bands.4 = (bf16[512,2048]{1,0:T(8,128)(2,1)S(1)}, bf16[16,512,128]{2,1,0:T(8,128)(2,1)S(1)}, bf16[2048,512]{1,0:T(8,128)(2,1)S(1)}, f32[1,128]{1,0:T(1,128)S(1)}) custom-call(s32[1]{0:T(128)} %bitcast.1.me_ref, s32[2,16]{1,0:T(2,128)} %bitcast.18, f32[768,128]{1,0:T(8,128)} %constant.15.clone.kt_hbm, ...), custom_call_target="tpu_custom_call", output_to_operand_aliasing={{0}: (4, {}), {1}: (5, {}), {2}: (6, {})} | custom-call | tf_op jit(solution)/shard_map/bands/pallas_call | solution.py:463
  15.4 1.6 %screen.1 = (f32[2,512,512]{2,1,0:T(8,128)S(1)}, bf16[16,2,128,128]{3,2,1,0:T(8,128)(2,1)S(1)}, bf16[2,512,128]{2,1,0:T(8,128)(2,1)S(1)}, bf16[2,128,512]{2,1,0:...) custom-call(f32[1,1]{1,0:T(1,128)} %bitcast.9.w_ref, ...), custom_call_target="tpu_custom_call" | custom-call | tf_op jit(solution)/shard_map/screen/pallas_call | solution.py:486
  17.1 3.4 %collective-permute-start.3 = (bf16[1,2,128,128]{3,2,1,0:T(8,128)(2,1)S(1)}, bf16[1,2,128,128]{3,2,1,0:T(8,128)(2,1)S(1)}, u32[]{:S(2)}, u32[]{:S(2)}) collective-permute-start(bf16[1,2,128,128]{3,2,1,0:T(8,128)(2,1)S(1)} %get-tuple-element.70), channel_id=1, source_target_pairs={{0,12},{1,13},{2,14},{3,15},{4,8},{5,9},{6,10},{7,11},{8,4},{9,5},... | collective-permute-start | bytes 196616 | tf_op jit(solution)/shard_map/ppermute | solution.py:384
  20.5 0.4 collective-permute-start.5
  21.5 3.3 %bands.5 = (bf16[512,2048]{1,0:T(8,128)(2,1)S(1)}, bf16[16,512,128]{2,1,0:T(8,128)(2,1)S(1)}, bf16[2048,512]{1,0:T(8,128)(2,1)S(1)}, f32[1,128]{1,0:T(1,128)}) custom-call(s32[1]{0:T(128)} %bitcast.1.me_ref, s32[2,16]{1,0:T(2,128)} %bitcast.19, f32[768,128]{1,0:T(8,128)} %constant.15.clone.kt_hbm, ...), custom_call_target="tpu_custom_call", output_to_operand_aliasing={{0}: (4, {}), {1}: (5, {}), {2}: (6, {})} | custom-call | tf_op jit(solution)/shard_map/bands/pallas_call | solution.py:463
  24.9 1.0 %collective-permute-done.4.rest_4_ = bf16[1,2,128,128]{3,2,1,0:T(8,128)(2,1)S(1)} collective-permute-done((bf16[1,2,128,128]{3,2,1,0:T(8,128)(2,1)S(1)}, bf16[1,2,128,128]{3,2,1,0:T(8,128)(2,1)S(1)}, u32[]{:S(2)}, u32[]{:S(2)}) %collective-permute-start.4) | collective-permute-done | bytes 65568 | tf_op jit(solution)/shard_map/ppermute | solution.py:384
  25.9 7.6 %subgrid.1 = (bf16[16,2,128,128]{3,2,1,0:T(8,128)(2,1)}, bf16[1,2,128,128]{3,2,1,0:T(8,128)(2,1)S(1)}) custom-call(s32[1,1]{1,0:T(1,128)} %bitcast.10.tc_ref, bf16[1,2,128,128]{3,2,1,0:T(8,128)(2,1)S(1)} %get-tuple-element.39.rest_0_, bf16[4,2,128,128]{3,2,1,0:T(8,128)(2,1)S(1)} %collective-permute-done.1.rest_1_, ...), custom_call_target="tpu_custom_call" | custom-call | tf_op jit(solution)/shard_map/subgrid/pallas_call | solution.py:527
  33.5 2.3 %collective-permute-start.6 = (bf16[1,2,128,128]{3,2,1,0:T(8,128)(2,1)S(1)}, bf16[1,2,128,128]{3,2,1,0:T(8,128)(2,1)S(1)}, u32[]{:S(2)}, u32[]{:S(2)}) collective-permute-start(bf16[1,2,128,128]{3,2,1,0:T(8,128)(2,1)S(1)} %get-tuple-element.62), channel_id=1, source_target_pairs={{0,12},{1,13},{2,14},{3,15},{4,8},{5,9},{6,10},{7,11},{8,4},{9,5},... | collective-permute-start | bytes 196616 | tf_op jit(solution)/shard_map/ppermute | solution.py:384
  35.8 1.3 %collective-permute-start.8 = (bf16[1,2,128,128]{3,2,1,0:T(8,128)(2,1)S(1)}, bf16[1,2,128,128]{3,2,1,0:T(8,128)(2,1)S(1)}, u32[]{:S(2)}, u32[]{:S(2)}) collective-permute-start(bf16[1,2,128,128]{3,2,1,0:T(8,128)(2,1)S(1)} %get-tuple-element.62), channel_id=1, source_target_pairs={{0,4},{1,5},{2,6},{3,7},{4,0},{5,1},{6,2},{7,3},{8,12},{9,13},{10,... | collective-permute-start | bytes 196616 | tf_op jit(solution)/shard_map/ppermute | solution.py:384
  37.1 1.4 %collective-permute-done.6 = bf16[1,2,128,128]{3,2,1,0:T(8,128)(2,1)S(1)} collective-permute-done((bf16[1,2,128,128]{3,2,1,0:T(8,128)(2,1)S(1)}, bf16[1,2,128,128]{3,2,1,0:T(8,128)(2,1)S(1)}, u32[]{:S(2)}, u32[]{:S(2)}) %collective-permute-start.6) | collective-permute-done | bytes 65568 | tf_op jit(solution)/shard_map/ppermute | solution.py:384
  38.5 2.0 %collective-permute-done.7 = bf16[1,2,128,128]{3,2,1,0:T(8,128)(2,1)S(1)} collective-permute-done((bf16[1,2,128,128]{3,2,1,0:T(8,128)(2,1)S(1)}, bf16[1,2,128,128]{3,2,1,0:T(8,128)(2,1)S(1)}, u32[]{:S(2)}, u32[]{:S(2)}) %collective-permute-start.7) | collective-permute-done | bytes 65568 | tf_op jit(solution)/shard_map/ppermute | solution.py:384
  40.6 0.3 collective-permute-start.9
  40.9 3.5 %collective-permute-start.11 = (bf16[4,2,128,128]{3,2,1,0:T(8,128)(2,1)S(1)}, bf16[4,2,128,128]{3,2,1,0:T(8,128)(2,1)S(1)}, u32[]{:S(2)}, u32[]{:S(2)}) collective-permute-start(bf16[4,2,128,128]{3,2,1,0:T(8,128)(2,1)S(1)} %constant_dynamic-update-slice_fusion.rest_0_), channel_id=1, source_target_pairs={{0,1},{1,0},{2,3},{3,2},{4,5},{5,4},{6,7},{7,6},{8,9},{9,8},{10,11... | collective-permute-start | bytes 786440 | tf_op jit(solution)/shard_map/ppermute | solution.py:384
  44.4 2.1 %grid_first.1 = (f32[2,5,640,128]{3,2,1,0:T(8,128)S(1)}, f32[1,128]{1,0:T(1,128)S(1)}, bf16[2,512,512]{2,1,0:T(8,128)(2,1)S(1)}) custom-call(s32[1]{0:T(128)} %bitcast.1.me_ref, s32[1,2]{1,0:T(1,128)S(1)} %get-tuple-element.60.fo_ref, s32[2,16]{1,0:T(2,128)S(1)} %get-tuple-element.61.so_ref, bf16[2,512,512]{2,1,0:T(8,128)(2,1)} %constant.14.clone.basis_ref.basis_hbm, ...), custom_call_target="tpu_custom_call" | custom-call | tf_op jit(solution)/shard_map/grid_first/pallas_call | solution.py:571
  46.6 3.8 %collective-permute-start.10 = (bf16[4,2,128,128]{3,2,1,0:T(8,128)(2,1)S(1)}, bf16[4,2,128,128]{3,2,1,0:T(8,128)(2,1)S(1)}, u32[]{:S(2)}, u32[]{:S(2)}) collective-permute-start(bf16[4,2,128,128]{3,2,1,0:T(8,128)(2,1)S(1)} %add_convert_fusion.rest_1_), channel_id=1, source_target_pairs={{0,1},{1,0},{2,3},{3,2},{4,5},{5,4},{6,7},{7,6},{8,9},{9,8},{10,11... | collective-permute-start | bytes 786440 | tf_op jit(solution)/shard_map/ppermute | solution.py:384
  50.4 1.6 %grid_next.1 = (f32[2,5,640,128]{3,2,1,0:T(8,128)S(1)}, f32[1,128]{1,0:T(1,128)}) custom-call(s32[1]{0:T(128)} %bitcast.1.me_ref, s32[1,2]{1,0:T(1,128)S(1)} %get-tuple-element.60.fo_ref, s32[2,16]{1,0:T(2,128)S(1)} %get-tuple-element.61.so_ref, bf16[4,2,128,128]{3,2,1,0:T(8,128)(2,1)S(1)} %collective-permute-done.11.rest_0_, ...), custom_call_target="tpu_custom_call", output_to_operand_aliasing={{0}: (5, {})} | custom-call | tf_op jit(solution)/shard_map/grid_next/pallas_call | solution.py:561
  52.0 4.1 %backward.1 = (bf16[1,2,512,512]{3,2,1,0:T(8,128)(2,1)}, f32[2,5,640,128]{3,2,1,0:T(8,128)S(1)}) custom-call(s32[1]{0:T(128)} %bitcast.1.me_ref, s32[1,2]{1,0:T(1,128)S(1)} %get-tuple-element.60.fo_ref, s32[2,16]{1,0:T(2,128)S(1)} %get-tuple-element.61.so_ref, bf16[2,512,512]{2,1,0:T(8,128)(2,1)S(1)} %get-tuple-element.63.basis_ref, ...), custom_call_target="tpu_custom_call", output_to_operand_aliasing={{1}: (5, {})} | custom-call | tf_op jit(solution)/shard_map/backward/pallas_call | solution.py:584
  (19 shorter events, 0.3 us)
Async XLA Ops:
  5.2 3.4 %collective-permute-start = (bf16[4,2,128,128]{3,2,1,0:T(8,128)(2,1)S(1)}, bf16[4,2,128,128]{3,2,1,0:T(8,128)(2,1)S(1)}, u32[]{:S(2)}, u32[]{:S(2)}) collective-permute-start(bf16[4,2,128,128]{3,2,1,0:T(8,128)(2,1)S(1)} %get-tuple-element.38), channel_id=1, source_target_pairs={{0,1},{1,0},{2,3},{3,2},{4,5},{5,4},{6,7},{7,6},{8,9},{9,8},{10,11... | collective-permute-start | bytes 786440 | tf_op jit(solution)/shard_map/ppermute | solution.py:384
  7.4 9.7 %collective-permute-start.2 = (bf16[4,2,128,128]{3,2,1,0:T(8,128)(2,1)S(1)}, bf16[4,2,128,128]{3,2,1,0:T(8,128)(2,1)S(1)}, u32[]{:S(2)}, u32[]{:S(2)}) collective-permute-start(bf16[4,2,128,128]{3,2,1,0:T(8,128)(2,1)S(1)} %get-tuple-element.40), channel_id=1, source_target_pairs={{0,1},{1,0},{2,3},{3,2},{4,5},{5,4},{6,7},{7,6},{8,9},{9,8},{10,11... | collective-permute-start | bytes 786440 | tf_op jit(solution)/shard_map/ppermute | solution.py:384
  8.7 8.3 %collective-permute-start.1 = (bf16[4,2,128,128]{3,2,1,0:T(8,128)(2,1)S(1)}, bf16[4,2,128,128]{3,2,1,0:T(8,128)(2,1)S(1)}, u32[]{:S(2)}, u32[]{:S(2)}) collective-permute-start(bf16[4,2,128,128]{3,2,1,0:T(8,128)(2,1)S(1)} %add_convert_fusion.1.outs_0_._.rest_3_), channel_id=1, source_target_pairs={{0,2},{1,3},{2,0},{3,1},{4,6},{5,7},{6,4},{7,5},{8,10},{9,11},{10,... | collective-permute-start | bytes 786440 | tf_op jit(solution)/shard_map/ppermute | solution.py:384
  17.1 7.7 %collective-permute-start.3 = (bf16[1,2,128,128]{3,2,1,0:T(8,128)(2,1)S(1)}, bf16[1,2,128,128]{3,2,1,0:T(8,128)(2,1)S(1)}, u32[]{:S(2)}, u32[]{:S(2)}) collective-permute-start(bf16[1,2,128,128]{3,2,1,0:T(8,128)(2,1)S(1)} %get-tuple-element.70), channel_id=1, source_target_pairs={{0,12},{1,13},{2,14},{3,15},{4,8},{5,9},{6,10},{7,11},{8,4},{9,5},... | collective-permute-start | bytes 196616 | tf_op jit(solution)/shard_map/ppermute | solution.py:384
  20.5 5.3 %collective-permute-start.4 = (bf16[1,2,128,128]{3,2,1,0:T(8,128)(2,1)S(1)}, bf16[1,2,128,128]{3,2,1,0:T(8,128)(2,1)S(1)}, u32[]{:S(2)}, u32[]{:S(2)}) collective-permute-start(bf16[1,2,128,128]{3,2,1,0:T(8,128)(2,1)S(1)} %get-tuple-element.69), channel_id=1, source_target_pairs={{0,8},{1,9},{2,10},{3,11},{4,12},{5,13},{6,14},{7,15},{8,0},{9,1},... | collective-permute-start | bytes 196616 | tf_op jit(solution)/shard_map/ppermute | solution.py:384
  20.5 5.3 %collective-permute-start.5 = (bf16[1,2,128,128]{3,2,1,0:T(8,128)(2,1)S(1)}, bf16[1,2,128,128]{3,2,1,0:T(8,128)(2,1)S(1)}, u32[]{:S(2)}, u32[]{:S(2)}) collective-permute-start(bf16[1,2,128,128]{3,2,1,0:T(8,128)(2,1)S(1)} %get-tuple-element.68.rest_3_), channel_id=1, source_target_pairs={{0,4},{1,5},{2,6},{3,7},{4,0},{5,1},{6,2},{7,3},{8,12},{9,13},{10,... | collective-permute-start | bytes 196616 | tf_op jit(solution)/shard_map/ppermute | solution.py:384
  33.5 5.0 %collective-permute-start.6 = (bf16[1,2,128,128]{3,2,1,0:T(8,128)(2,1)S(1)}, bf16[1,2,128,128]{3,2,1,0:T(8,128)(2,1)S(1)}, u32[]{:S(2)}, u32[]{:S(2)}) collective-permute-start(bf16[1,2,128,128]{3,2,1,0:T(8,128)(2,1)S(1)} %get-tuple-element.62), channel_id=1, source_target_pairs={{0,12},{1,13},{2,14},{3,15},{4,8},{5,9},{6,10},{7,11},{8,4},{9,5},... | collective-permute-start | bytes 196616 | tf_op jit(solution)/shard_map/ppermute | solution.py:384
  35.7 4.8 %collective-permute-start.7 = (bf16[1,2,128,128]{3,2,1,0:T(8,128)(2,1)S(1)}, bf16[1,2,128,128]{3,2,1,0:T(8,128)(2,1)S(1)}, u32[]{:S(2)}, u32[]{:S(2)}) collective-permute-start(bf16[1,2,128,128]{3,2,1,0:T(8,128)(2,1)S(1)} %get-tuple-element.62), channel_id=1, source_target_pairs={{0,8},{1,9},{2,10},{3,11},{4,12},{5,13},{6,14},{7,15},{8,0},{9,1},... | collective-permute-start | bytes 196616 | tf_op jit(solution)/shard_map/ppermute | solution.py:384
  35.8 4.8 %collective-permute-start.8 = (bf16[1,2,128,128]{3,2,1,0:T(8,128)(2,1)S(1)}, bf16[1,2,128,128]{3,2,1,0:T(8,128)(2,1)S(1)}, u32[]{:S(2)}, u32[]{:S(2)}) collective-permute-start(bf16[1,2,128,128]{3,2,1,0:T(8,128)(2,1)S(1)} %get-tuple-element.62), channel_id=1, source_target_pairs={{0,4},{1,5},{2,6},{3,7},{4,0},{5,1},{6,2},{7,3},{8,12},{9,13},{10,... | collective-permute-start | bytes 196616 | tf_op jit(solution)/shard_map/ppermute | solution.py:384
  40.6 6.0 %collective-permute-start.9 = (bf16[4,2,128,128]{3,2,1,0:T(8,128)(2,1)S(1)}, bf16[4,2,128,128]{3,2,1,0:T(8,128)(2,1)S(1)}, u32[]{:S(2)}, u32[]{:S(2)}) collective-permute-start(bf16[4,2,128,128]{3,2,1,0:T(8,128)(2,1)S(1)} %constant_dynamic-update-slice_fusion.rest_0_), channel_id=1, source_target_pairs={{0,2},{1,3},{2,0},{3,1},{4,6},{5,7},{6,4},{7,5},{8,10},{9,11},{10,... | collective-permute-start | bytes 786440 | tf_op jit(solution)/shard_map/ppermute | solution.py:384
  40.9 9.6 %collective-permute-start.11 = (bf16[4,2,128,128]{3,2,1,0:T(8,128)(2,1)S(1)}, bf16[4,2,128,128]{3,2,1,0:T(8,128)(2,1)S(1)}, u32[]{:S(2)}, u32[]{:S(2)}) collective-permute-start(bf16[4,2,128,128]{3,2,1,0:T(8,128)(2,1)S(1)} %constant_dynamic-update-slice_fusion.rest_0_), channel_id=1, source_target_pairs={{0,1},{1,0},{2,3},{3,2},{4,5},{5,4},{6,7},{7,6},{8,9},{9,8},{10,11... | collective-permute-start | bytes 786440 | tf_op jit(solution)/shard_map/ppermute | solution.py:384
  46.6 5.4 %collective-permute-start.10 = (bf16[4,2,128,128]{3,2,1,0:T(8,128)(2,1)S(1)}, bf16[4,2,128,128]{3,2,1,0:T(8,128)(2,1)S(1)}, u32[]{:S(2)}, u32[]{:S(2)}) collective-permute-start(bf16[4,2,128,128]{3,2,1,0:T(8,128)(2,1)S(1)} %add_convert_fusion.rest_1_), channel_id=1, source_target_pairs={{0,1},{1,0},{2,3},{3,2},{4,5},{5,4},{6,7},{7,6},{8,9},{9,8},{10,11... | collective-permute-start | bytes 786440 | tf_op jit(solution)/shard_map/ppermute | solution.py:384

commit v12 on v10

--- a/solution.py
+++ b/solution.py
@@ -180,33 +180,29 @@
             block(ref, item, j)
 
 
-def band_kernel(odd, me_ref, to_ref, kt_hbm, kwide_hbm, *rest):
-    kvt_ref, kut_ref, ku_ref, zero_ref, kt_ref, kwide_ref, sems = rest[-7:]
+def band_kernel(odd, me_ref, to_ref, kt_hbm, *rest):
+    kvt_ref, kut_ref, zero_ref, kt_ref, sem = rest[-5:]
     slots = kut_ref.shape[0]
     zero_ref[...] = jnp.zeros_like(zero_ref)
 
     @pl.when((me_ref[0] & 1) == odd)
     def _():
-        copies = [
-            pltpu.make_async_copy(kt_hbm, kt_ref, sems.at[0]),
-            pltpu.make_async_copy(kwide_hbm, kwide_ref, sems.at[1]),
-        ]
-        for copy in copies:
-            copy.start()
-        for copy in copies:
-            copy.wait()
+        load = pltpu.make_async_copy(kt_hbm, kt_ref, sem)
+        load.start()
+        load.wait()
         for t in range(slots):
             ou, ov = to_ref[0, t], to_ref[1, t]
             rows = slice(t * TV, (t + 1) * TV)
             kut_ref[t] = kt_ref[pl.ds(2 * TV - ou, SG), :].astype(BF)
             kvt_ref[:, rows] = kt_ref[pl.ds(2 * TV - ov, SG), :].astype(BF)
-            ku_ref[rows] = pltpu.roll(kwide_ref[...], ou, 1).astype(BF)
-
-
-def screen_kernel(w_ref, _, *rest):
-    loads = (len(rest) - 3) // 2
+
+
+def screen_kernel(w_ref, to_ref, _, kwide_hbm, *rest):
+    loads = (len(rest) - 5) // 2
     sources, screen_ref = rest[:loads], rest[loads]
-    targets, zero_ref, sems = rest[loads + 1 : -2], rest[-2], rest[-1]
+    targets, (zero_ref, ku_ref, kwide_ref, sems) = rest[loads + 1 : -4], rest[-4:]
+    wide_load = pltpu.make_async_copy(kwide_hbm, kwide_ref, sems.at[loads])
+    wide_load.start()
     zero_ref[...] = jnp.zeros_like(zero_ref)
     copies = [pltpu.make_async_copy(sources[k], targets[k], sems.at[k]) for k in range(loads)]
     for copy in copies:
@@ -219,6 +215,9 @@
     cos_v, sin_v = cos_sin_turns((jnp.sqrt(row2 + column2) - 1.0) * w)
     screen_ref[0] = cos_v
     screen_ref[1] = sin_v
+    wide_load.wait()
+    for t in range(ku_ref.shape[0] // TV):
+        ku_ref[t * TV : (t + 1) * TV] = pltpu.roll(kwide_ref[...], to_ref[0, t], 1).astype(BF)
     for copy in copies:
         copy.wait()
 
@@ -456,25 +455,23 @@
         )(me, facet_offsets, corners, near(spec), *[near(value) for value in after])
 
     def make_bands(odd, bands, after):
-        shapes = [(SG, slots * TV), (slots, SG, TV), (slots * TV, SG)]
+        shapes = [(SG, slots * TV), (slots, SG, TV)]
         return pl.pallas_call(
             functools.partial(band_kernel, odd),
             out_shape=[held(shape) for shape in shapes] + [held((1, M), F32)],
-            in_specs=[SMEM] * 2 + [ANY] * 2 + [VMEM] * (len(bands) + len(after)),
-            out_specs=[VMEM] * 4,
+            in_specs=[SMEM] * 2 + [ANY] + [VMEM] * (len(bands) + len(after)),
+            out_specs=[VMEM] * 3,
             scratch_shapes=[
                 pltpu.VMEM(kt_np.shape, F32),
-                pltpu.VMEM(kwide_np.shape, F32),
-                pltpu.SemaphoreType.DMA((2,)),
+                pltpu.SemaphoreType.DMA(()),
             ],
-            input_output_aliases={4 + k: k for k in range(len(bands))},
+            input_output_aliases={3 + k: k for k in range(len(bands))},
             compiler_params=params(8),
             name="bands",
         )(
             me,
             tile_corners,
             far(jnp.asarray(kt_np)),
-            far(jnp.asarray(kwide_np)),
             *[near(value) for value in list(bands) + after],
         )
 
@@ -482,13 +479,20 @@
         loads = [observed, pad_np, pad_np.transpose(0, 2, 1), subgrid_offsets.T, facet_offsets]
         return pl.pallas_call(
             screen_kernel,
-            out_shape=[held((2, SG, SG), F32)] + [held(load.shape, load.dtype) for load in loads] + [held((1, M), F32)],
-            in_specs=[SMEM, VMEM] + [ANY] * len(loads),
-            out_specs=[VMEM] * (2 + len(loads)),
-            scratch_shapes=[pltpu.SemaphoreType.DMA((len(loads),))],
+            out_shape=[held((2, SG, SG), F32)] + [held(load.shape, load.dtype) for load in loads]
+            + [held((1, M), F32), held((slots * TV, SG))],
+            in_specs=[SMEM] * 2 + [VMEM] + [ANY] * (1 + len(loads)),
+            out_specs=[VMEM] * (3 + len(loads)),
+            scratch_shapes=[pltpu.VMEM(kwide_np.shape, F32), pltpu.SemaphoreType.DMA((len(loads) + 1,))],
             compiler_params=params(8),
             name="screen",
-        )(w_terms.reshape(1, 1), near(after), *[far(jnp.asarray(load)) for load in loads])
+        )(
+            w_terms.reshape(1, 1),
+            tile_corners,
+            near(after),
+            far(jnp.asarray(kwide_np)),
+            *[far(jnp.asarray(load)) for load in loads],
+        )
 
     arrived = []
 
@@ -512,10 +516,10 @@
     value = send(beside, 2, beside_own, token)
     send(lazy, 1, lazy_own)
     own = make_blocks([js for js, _ in sends[3:]] + [[0]], [value])
-    screen, tiles, pad, padt, late_corners, late_facet_offsets, token = make_screen(value)
+    screen, tiles, pad, padt, late_corners, late_facet_offsets, token, ku = make_screen(value)
     for (js, mask), value in zip(sends[3:], own):
         value = send(js, mask, value, token)
-    kvt, kut, ku, _ = make_bands(1, bands, [value])
+    kvt, kut, _ = make_bands(1, bands, [value])
     corners, facet_offsets = near(late_corners), near(late_facet_offsets)
     last = [(js, got) for js, got in arrived if 0 in js]
 

time: 56.2 us -> 55.4 us (0.986)
  starting transfers between devices: 19.8 us -> 18 us
  Pallas kernels: 29.5 us -> 30.1 us
    ppermute x12, starting transfers between devices: 19.8 us -> 18 us  [exchange(): return lax.ppermute(value, 'facet', [(i, i ^ mask) for i in range(n)])]
    pallas_call x1, Pallas kernels: 1.64 us -> 3.2 us  [make_screen(): pl.pallas_call(screen_kernel, out_shape=[held((2, SG, SG), F32)] + [held(...]
    pallas_call x2, Pallas kernels: 4.81 us -> 3.84 us  [make_bands(): pl.pallas_call(functools.partial(band_kernel, odd), out_shape=[held(shape...]
  transfers between devices with their start and end apart: 12 -> 12, of which waited for: 3 -> 3; matrix products, arithmetic and copies ran while one was open for 0% -> 0% of each run, Pallas kernels for 24% -> 25%
where the time goes in v12:
time: 55.4 us; the launch traced here: 55.1 us
  Pallas kernels  30.1 us (54%)
  starting transfers between devices  18 us (32%)
  waiting for transfers between devices  4.46 us (8%)
  between operations  2.25 us (4%)
    ppermute x12, starting transfers between devices, exchange(): return lax.ppermute(value, 'facet', [(i, i ^ mask) for i in range(n)])  18 us
    pallas_call x1, Pallas kernels, per_device(): pl.pallas_call(functools.partial(subgrid_kernel, [0] + [js.index(0) for j...  7.6 us
    pallas_call x1, Pallas kernels, per_device(): pl.pallas_call(functools.partial(forward_kernel, sends[0][0]), out_shape=...  4.54 us
    ppermute x12, waiting for transfers between devices, exchange(): return lax.ppermute(value, 'facet', [(i, i ^ mask) for i in range(n)])  4.46 us
    pallas_call x1, Pallas kernels, per_device(): pl.pallas_call(functools.partial(backward_kernel, [late_other[0]]), out_s...  4.06 us
    pallas_call x2, Pallas kernels, make_bands(): pl.pallas_call(functools.partial(band_kernel, odd), out_shape=[held(shape...  3.84 us
    pallas_call x1, Pallas kernels, make_screen(): pl.pallas_call(screen_kernel, out_shape=[held((2, SG, SG), F32)] + [held(...  3.2 us
    pallas_call x2, Pallas kernels, make_blocks(): pl.pallas_call(functools.partial(extract_kernel, lists), out_shape=[held(...  3.11 us
  transfers between devices with their start and end apart: 12, of which 3 were waited for; matrix products, arithmetic and copies ran while one was open for 0% of the time, Pallas kernels for 25%

profile of v12, /device:TPU:1, one launch (start us, length us, event | category | flops | bytes accessed | tf_op | source)
XLA Modules:
  0.0 55.1 jit_solution(15944989512603024938)
XLA Ops:
  0.6 4.5 %forward.1 = (bf16[4,2,128,128]{3,2,1,0:T(8,128)(2,1)S(1)}, f32[2,5,640,128]{3,2,1,0:T(8,128)S(1)}) custom-call(s32[1]{0:T(128)} %bitcast.1.me_ref, s32[1,2]{1,0:T(1,128)} %rest_4_.1, s32[2,16]{1,0:T(2,128)} %bitcast.13, bf16[1,2,512,512]{3,2,1,0:T(8,128)(2,1)} %facet_ref.1, bf16[2,512,512]{2,1,0:T(8,128)(2,1)} %constant.14.clone.basis_ref.basis_hbm), custom_call_target="tpu_custom_call" | custom-call | tf_op jit(solution)/shard_map/forward/pallas_call | solution.py:432
  5.2 0.1 collective-permute-start
  5.3 2.1 %extract.2 = (bf16[4,2,128,128]{3,2,1,0:T(8,128)(2,1)S(1)}, bf16[4,2,128,128]{3,2,1,0:T(8,128)(2,1)S(1)}) custom-call(s32[1]{0:T(128)} %bitcast.1.me_ref, s32[1,2]{1,0:T(1,128)} %rest_4_.1, s32[2,16]{1,0:T(2,128)} %bitcast.14, f32[2,5,640,128]{3,2,1,0:T(8,128)S(1)} %get-tuple-element.30.spec_ref), custom_call_target="tpu_custom_call" | custom-call | tf_op jit(solution)/shard_map/extract/pallas_call | solution.py:448
  7.4 0.5 collective-permute-start.2
  7.9 0.7 %bands.2 = (bf16[512,2048]{1,0:T(8,128)(2,1)S(1)}, bf16[16,512,128]{2,1,0:T(8,128)(2,1)S(1)}, f32[1,128]{1,0:T(1,128)S(1)}) custom-call(s32[1]{0:T(128)} %bitcast.1.me_ref, s32[2,16]{1,0:T(2,128)} %bitcast.17, f32[768,128]{1,0:T(8,128)} %constant.15.clone.kt_hbm, bf16[4,2,128,128]{3,2,1,0:T(8,128)(2,1)S(1)} %get-tuple-element.31.rest_0_), custom_call_target="tpu_custom_call" | custom-call | tf_op jit(solution)/shard_map/bands/pallas_call | solution.py:459
  8.6 0.1 add_convert_fusion.1.outs_0_._
  8.7 2.3 %collective-permute-start.1 = (bf16[4,2,128,128]{3,2,1,0:T(8,128)(2,1)S(1)}, bf16[4,2,128,128]{3,2,1,0:T(8,128)(2,1)S(1)}, u32[]{:S(2)}, u32[]{:S(2)}) collective-permute-start(bf16[4,2,128,128]{3,2,1,0:T(8,128)(2,1)S(1)} %add_convert_fusion.1.outs_0_._), channel_id=1, source_target_pairs={{0,2},{1,3},{2,0},{3,1},{4,6},{5,7},{6,4},{7,5},{8,10},{9,11},{10,... | collective-permute-start | bytes 786440 | tf_op jit(solution)/shard_map/ppermute | solution.py:380
  11.7 1.1 %extract.3 = (bf16[1,2,128,128]{3,2,1,0:T(8,128)(2,1)S(1)}, bf16[1,2,128,128]{3,2,1,0:T(8,128)(2,1)S(1)}, bf16[1,2,128,128]{3,2,1,0:T(8,128)(2,1)S(1)}, bf16[1,2,128,128]{3,2,1,0:T(8,128)(2,1)S(1)}) custom-call(s32[1]{0:T(128)} %bitcast.1.me_ref, s32[1,2]{1,0:T(1,128)} %rest_4_.1, s32[2,16]{1,0:T(2,128)} %bitcast.15, ...), custom_call_target="tpu_custom_call" | custom-call | tf_op jit(solution)/shard_map/extract/pallas_call | solution.py:448
  12.7 3.2 %screen.1 = (f32[2,512,512]{2,1,0:T(8,128)S(1)}, bf16[16,2,128,128]{3,2,1,0:T(8,128)(2,1)S(1)}, bf16[2,512,128]{2,1,0:T(8,128)(2,1)S(1)}, bf16[2,128,512]{2,1,0:...) custom-call(f32[1,1]{1,0:T(1,128)} %bitcast.8.w_ref, ...), custom_call_target="tpu_custom_call" | custom-call | tf_op jit(solution)/shard_map/screen/pallas_call | solution.py:480
  16.0 0.1 add_convert_fusion.2
  16.1 3.4 %collective-permute-start.3 = (bf16[1,2,128,128]{3,2,1,0:T(8,128)(2,1)S(1)}, bf16[1,2,128,128]{3,2,1,0:T(8,128)(2,1)S(1)}, u32[]{:S(2)}, u32[]{:S(2)}) collective-permute-start(bf16[1,2,128,128]{3,2,1,0:T(8,128)(2,1)S(1)} %get-tuple-element.60), channel_id=1, source_target_pairs={{0,12},{1,13},{2,14},{3,15},{4,8},{5,9},{6,10},{7,11},{8,4},{9,5},... | collective-permute-start | bytes 196616 | tf_op jit(solution)/shard_map/ppermute | solution.py:380
  19.5 0.4 collective-permute-start.5
  20.5 3.1 %bands.3 = (bf16[512,2048]{1,0:T(8,128)(2,1)S(1)}, bf16[16,512,128]{2,1,0:T(8,128)(2,1)S(1)}, f32[1,128]{1,0:T(1,128)}) custom-call(s32[1]{0:T(128)} %bitcast.1.me_ref, s32[2,16]{1,0:T(2,128)} %bitcast.19, f32[768,128]{1,0:T(8,128)} %constant.15.clone.kt_hbm, ...), custom_call_target="tpu_custom_call", output_to_operand_aliasing={{0}: (3, {}), {1}: (4, {})} | custom-call | tf_op jit(solution)/shard_map/bands/pallas_call | solution.py:459
  23.6 1.0 %collective-permute-done.4.rest_4_ = bf16[1,2,128,128]{3,2,1,0:T(8,128)(2,1)S(1)} collective-permute-done((bf16[1,2,128,128]{3,2,1,0:T(8,128)(2,1)S(1)}, bf16[1,2,128,128]{3,2,1,0:T(8,128)(2,1)S(1)}, u32[]{:S(2)}, u32[]{:S(2)}) %collective-permute-start.4) | collective-permute-done | bytes 65568 | tf_op jit(solution)/shard_map/ppermute | solution.py:380
  24.7 7.6 %subgrid.1 = (bf16[16,2,128,128]{3,2,1,0:T(8,128)(2,1)}, bf16[1,2,128,128]{3,2,1,0:T(8,128)(2,1)S(1)}) custom-call(s32[1,1]{1,0:T(1,128)} %bitcast.9.tc_ref, bf16[1,2,128,128]{3,2,1,0:T(8,128)(2,1)S(1)} %get-tuple-element.34.rest_0_, bf16[4,2,128,128]{3,2,1,0:T(8,128)(2,1)S(1)} %collective-permute-done.1.rest_1_, ...), custom_call_target="tpu_custom_call" | custom-call | tf_op jit(solution)/shard_map/subgrid/pallas_call | solution.py:526
  32.3 2.3 %collective-permute-start.6 = (bf16[1,2,128,128]{3,2,1,0:T(8,128)(2,1)S(1)}, bf16[1,2,128,128]{3,2,1,0:T(8,128)(2,1)S(1)}, u32[]{:S(2)}, u32[]{:S(2)}) collective-permute-start(bf16[1,2,128,128]{3,2,1,0:T(8,128)(2,1)S(1)} %get-tuple-element.52), channel_id=1, source_target_pairs={{0,12},{1,13},{2,14},{3,15},{4,8},{5,9},{6,10},{7,11},{8,4},{9,5},... | collective-permute-start | bytes 196616 | tf_op jit(solution)/shard_map/ppermute | solution.py:380
  34.5 1.4 %collective-permute-start.8 = (bf16[1,2,128,128]{3,2,1,0:T(8,128)(2,1)S(1)}, bf16[1,2,128,128]{3,2,1,0:T(8,128)(2,1)S(1)}, u32[]{:S(2)}, u32[]{:S(2)}) collective-permute-start(bf16[1,2,128,128]{3,2,1,0:T(8,128)(2,1)S(1)} %get-tuple-element.52), channel_id=1, source_target_pairs={{0,4},{1,5},{2,6},{3,7},{4,0},{5,1},{6,2},{7,3},{8,12},{9,13},{10,... | collective-permute-start | bytes 196616 | tf_op jit(solution)/shard_map/ppermute | solution.py:380
  35.9 1.4 %collective-permute-done.6 = bf16[1,2,128,128]{3,2,1,0:T(8,128)(2,1)S(1)} collective-permute-done((bf16[1,2,128,128]{3,2,1,0:T(8,128)(2,1)S(1)}, bf16[1,2,128,128]{3,2,1,0:T(8,128)(2,1)S(1)}, u32[]{:S(2)}, u32[]{:S(2)}) %collective-permute-start.6) | collective-permute-done | bytes 65568 | tf_op jit(solution)/shard_map/ppermute | solution.py:380
  37.3 2.0 %collective-permute-done.7 = bf16[1,2,128,128]{3,2,1,0:T(8,128)(2,1)S(1)} collective-permute-done((bf16[1,2,128,128]{3,2,1,0:T(8,128)(2,1)S(1)}, bf16[1,2,128,128]{3,2,1,0:T(8,128)(2,1)S(1)}, u32[]{:S(2)}, u32[]{:S(2)}) %collective-permute-start.7) | collective-permute-done | bytes 65568 | tf_op jit(solution)/shard_map/ppermute | solution.py:380
  39.4 4.8 %collective-permute-start.11 = (bf16[4,2,128,128]{3,2,1,0:T(8,128)(2,1)S(1)}, bf16[4,2,128,128]{3,2,1,0:T(8,128)(2,1)S(1)}, u32[]{:S(2)}, u32[]{:S(2)}) collective-permute-start(bf16[4,2,128,128]{3,2,1,0:T(8,128)(2,1)S(1)} %constant_dynamic-update-slice_fusion.rest_0_), channel_id=1, source_target_pairs={{0,1},{1,0},{2,3},{3,2},{4,5},{5,4},{6,7},{7,6},{8,9},{9,8},{10,11... | collective-permute-start | bytes 786440 | tf_op jit(solution)/shard_map/ppermute | solution.py:380
  44.2 2.1 %grid_first.1 = (f32[2,5,640,128]{3,2,1,0:T(8,128)S(1)}, f32[1,128]{1,0:T(1,128)S(1)}, bf16[2,512,512]{2,1,0:T(8,128)(2,1)S(1)}) custom-call(s32[1]{0:T(128)} %bitcast.1.me_ref, s32[1,2]{1,0:T(1,128)S(1)} %get-tuple-element.50.fo_ref, s32[2,16]{1,0:T(2,128)S(1)} %get-tuple-element.51.so_ref, bf16[2,512,512]{2,1,0:T(8,128)(2,1)} %constant.14.clone.basis_ref.basis_hbm, ...), custom_call_target="tpu_custom_call" | custom-call | tf_op jit(solution)/shard_map/grid_first/pallas_call | solution.py:570
  46.4 2.8 %collective-permute-start.10 = (bf16[4,2,128,128]{3,2,1,0:T(8,128)(2,1)S(1)}, bf16[4,2,128,128]{3,2,1,0:T(8,128)(2,1)S(1)}, u32[]{:S(2)}, u32[]{:S(2)}) collective-permute-start(bf16[4,2,128,128]{3,2,1,0:T(8,128)(2,1)S(1)} %add_convert_fusion.rest_1_), channel_id=1, source_target_pairs={{0,1},{1,0},{2,3},{3,2},{4,5},{5,4},{6,7},{7,6},{8,9},{9,8},{10,11... | collective-permute-start | bytes 786440 | tf_op jit(solution)/shard_map/ppermute | solution.py:380
  49.2 1.6 %grid_next.1 = (f32[2,5,640,128]{3,2,1,0:T(8,128)S(1)}, f32[1,128]{1,0:T(1,128)}) custom-call(s32[1]{0:T(128)} %bitcast.1.me_ref, s32[1,2]{1,0:T(1,128)S(1)} %get-tuple-element.50.fo_ref, s32[2,16]{1,0:T(2,128)S(1)} %get-tuple-element.51.so_ref, bf16[4,2,128,128]{3,2,1,0:T(8,128)(2,1)S(1)} %collective-permute-done.11.rest_0_, ...), custom_call_target="tpu_custom_call", output_to_operand_aliasing={{0}: (5, {})} | custom-call | tf_op jit(solution)/shard_map/grid_next/pallas_call | solution.py:560
  50.8 4.1 %backward.1 = (bf16[1,2,512,512]{3,2,1,0:T(8,128)(2,1)}, f32[2,5,640,128]{3,2,1,0:T(8,128)S(1)}) custom-call(s32[1]{0:T(128)} %bitcast.1.me_ref, s32[1,2]{1,0:T(1,128)S(1)} %get-tuple-element.50.fo_ref, s32[2,16]{1,0:T(2,128)S(1)} %get-tuple-element.51.so_ref, bf16[2,512,512]{2,1,0:T(8,128)(2,1)S(1)} %get-tuple-element.53.basis_ref, ...), custom_call_target="tpu_custom_call", output_to_operand_aliasing={{1}: (5, {})} | custom-call | tf_op jit(solution)/shard_map/backward/pallas_call | solution.py:583
  (17 shorter events, 0.2 us)
Async XLA Ops:
  5.2 3.4 %collective-permute-start = (bf16[4,2,128,128]{3,2,1,0:T(8,128)(2,1)S(1)}, bf16[4,2,128,128]{3,2,1,0:T(8,128)(2,1)S(1)}, u32[]{:S(2)}, u32[]{:S(2)}) collective-permute-start(bf16[4,2,128,128]{3,2,1,0:T(8,128)(2,1)S(1)} %get-tuple-element.33), channel_id=1, source_target_pairs={{0,1},{1,0},{2,3},{3,2},{4,5},{5,4},{6,7},{7,6},{8,9},{9,8},{10,11... | collective-permute-start | bytes 786440 | tf_op jit(solution)/shard_map/ppermute | solution.py:380
  7.4 8.6 %collective-permute-start.2 = (bf16[4,2,128,128]{3,2,1,0:T(8,128)(2,1)S(1)}, bf16[4,2,128,128]{3,2,1,0:T(8,128)(2,1)S(1)}, u32[]{:S(2)}, u32[]{:S(2)}) collective-permute-start(bf16[4,2,128,128]{3,2,1,0:T(8,128)(2,1)S(1)} %get-tuple-element.35), channel_id=1, source_target_pairs={{0,1},{1,0},{2,3},{3,2},{4,5},{5,4},{6,7},{7,6},{8,9},{9,8},{10,11... | collective-permute-start | bytes 786440 | tf_op jit(solution)/shard_map/ppermute | solution.py:380
  8.7 7.3 %collective-permute-start.1 = (bf16[4,2,128,128]{3,2,1,0:T(8,128)(2,1)S(1)}, bf16[4,2,128,128]{3,2,1,0:T(8,128)(2,1)S(1)}, u32[]{:S(2)}, u32[]{:S(2)}) collective-permute-start(bf16[4,2,128,128]{3,2,1,0:T(8,128)(2,1)S(1)} %add_convert_fusion.1.outs_0_._), channel_id=1, source_target_pairs={{0,2},{1,3},{2,0},{3,1},{4,6},{5,7},{6,4},{7,5},{8,10},{9,11},{10,... | collective-permute-start | bytes 786440 | tf_op jit(solution)/shard_map/ppermute | solution.py:380
  16.1 7.6 %collective-permute-start.3 = (bf16[1,2,128,128]{3,2,1,0:T(8,128)(2,1)S(1)}, bf16[1,2,128,128]{3,2,1,0:T(8,128)(2,1)S(1)}, u32[]{:S(2)}, u32[]{:S(2)}) collective-permute-start(bf16[1,2,128,128]{3,2,1,0:T(8,128)(2,1)S(1)} %get-tuple-element.60), channel_id=1, source_target_pairs={{0,12},{1,13},{2,14},{3,15},{4,8},{5,9},{6,10},{7,11},{8,4},{9,5},... | collective-permute-start | bytes 196616 | tf_op jit(solution)/shard_map/ppermute | solution.py:380
  19.5 5.2 %collective-permute-start.4 = (bf16[1,2,128,128]{3,2,1,0:T(8,128)(2,1)S(1)}, bf16[1,2,128,128]{3,2,1,0:T(8,128)(2,1)S(1)}, u32[]{:S(2)}, u32[]{:S(2)}) collective-permute-start(bf16[1,2,128,128]{3,2,1,0:T(8,128)(2,1)S(1)} %get-tuple-element.59), channel_id=1, source_target_pairs={{0,8},{1,9},{2,10},{3,11},{4,12},{5,13},{6,14},{7,15},{8,0},{9,1},... | collective-permute-start | bytes 196616 | tf_op jit(solution)/shard_map/ppermute | solution.py:380
  19.5 5.2 %collective-permute-start.5 = (bf16[1,2,128,128]{3,2,1,0:T(8,128)(2,1)S(1)}, bf16[1,2,128,128]{3,2,1,0:T(8,128)(2,1)S(1)}, u32[]{:S(2)}, u32[]{:S(2)}) collective-permute-start(bf16[1,2,128,128]{3,2,1,0:T(8,128)(2,1)S(1)} %get-tuple-element.58.rest_2_), channel_id=1, source_target_pairs={{0,4},{1,5},{2,6},{3,7},{4,0},{5,1},{6,2},{7,3},{8,12},{9,13},{10,... | collective-permute-start | bytes 196616 | tf_op jit(solution)/shard_map/ppermute | solution.py:380
  32.3 5.0 %collective-permute-start.6 = (bf16[1,2,128,128]{3,2,1,0:T(8,128)(2,1)S(1)}, bf16[1,2,128,128]{3,2,1,0:T(8,128)(2,1)S(1)}, u32[]{:S(2)}, u32[]{:S(2)}) collective-permute-start(bf16[1,2,128,128]{3,2,1,0:T(8,128)(2,1)S(1)} %get-tuple-element.52), channel_id=1, source_target_pairs={{0,12},{1,13},{2,14},{3,15},{4,8},{5,9},{6,10},{7,11},{8,4},{9,5},... | collective-permute-start | bytes 196616 | tf_op jit(solution)/shard_map/ppermute | solution.py:380
  34.5 4.8 %collective-permute-start.7 = (bf16[1,2,128,128]{3,2,1,0:T(8,128)(2,1)S(1)}, bf16[1,2,128,128]{3,2,1,0:T(8,128)(2,1)S(1)}, u32[]{:S(2)}, u32[]{:S(2)}) collective-permute-start(bf16[1,2,128,128]{3,2,1,0:T(8,128)(2,1)S(1)} %get-tuple-element.52), channel_id=1, source_target_pairs={{0,8},{1,9},{2,10},{3,11},{4,12},{5,13},{6,14},{7,15},{8,0},{9,1},... | collective-permute-start | bytes 196616 | tf_op jit(solution)/shard_map/ppermute | solution.py:380
  34.5 4.8 %collective-permute-start.8 = (bf16[1,2,128,128]{3,2,1,0:T(8,128)(2,1)S(1)}, bf16[1,2,128,128]{3,2,1,0:T(8,128)(2,1)S(1)}, u32[]{:S(2)}, u32[]{:S(2)}) collective-permute-start(bf16[1,2,128,128]{3,2,1,0:T(8,128)(2,1)S(1)} %get-tuple-element.52), channel_id=1, source_target_pairs={{0,4},{1,5},{2,6},{3,7},{4,0},{5,1},{6,2},{7,3},{8,12},{9,13},{10,... | collective-permute-start | bytes 196616 | tf_op jit(solution)/shard_map/ppermute | solution.py:380
  39.4 7.0 %collective-permute-start.9 = (bf16[4,2,128,128]{3,2,1,0:T(8,128)(2,1)S(1)}, bf16[4,2,128,128]{3,2,1,0:T(8,128)(2,1)S(1)}, u32[]{:S(2)}, u32[]{:S(2)}) collective-permute-start(bf16[4,2,128,128]{3,2,1,0:T(8,128)(2,1)S(1)} %constant_dynamic-update-slice_fusion.rest_0_), channel_id=1, source_target_pairs={{0,2},{1,3},{2,0},{3,1},{4,6},{5,7},{6,4},{7,5},{8,10},{9,11},{10,... | collective-permute-start | bytes 786440 | tf_op jit(solution)/shard_map/ppermute | solution.py:380
  39.4 9.8 %collective-permute-start.11 = (bf16[4,2,128,128]{3,2,1,0:T(8,128)(2,1)S(1)}, bf16[4,2,128,128]{3,2,1,0:T(8,128)(2,1)S(1)}, u32[]{:S(2)}, u32[]{:S(2)}) collective-permute-start(bf16[4,2,128,128]{3,2,1,0:T(8,128)(2,1)S(1)} %constant_dynamic-update-slice_fusion.rest_0_), channel_id=1, source_target_pairs={{0,1},{1,0},{2,3},{3,2},{4,5},{5,4},{6,7},{7,6},{8,9},{9,8},{10,11... | collective-permute-start | bytes 786440 | tf_op jit(solution)/shard_map/ppermute | solution.py:380
  46.4 4.4 %collective-permute-start.10 = (bf16[4,2,128,128]{3,2,1,0:T(8,128)(2,1)S(1)}, bf16[4,2,128,128]{3,2,1,0:T(8,128)(2,1)S(1)}, u32[]{:S(2)}, u32[]{:S(2)}) collective-permute-start(bf16[4,2,128,128]{3,2,1,0:T(8,128)(2,1)S(1)} %add_convert_fusion.rest_1_), channel_id=1, source_target_pairs={{0,1},{1,0},{2,3},{3,2},{4,5},{5,4},{6,7},{7,6},{8,9},{9,8},{10,11... | collective-permute-start | bytes 786440 | tf_op jit(solution)/shard_map/ppermute | solution.py:380

commit v13 on v12

--- a/solution.py
+++ b/solution.py
@@ -17,7 +17,7 @@
 BF = jnp.bfloat16
 F32 = jnp.float32
 TWO_PI = 2.0 * math.pi
-OUT_CHUNKS = 4
+OUT_CHUNKS = 2
 
 
 def basis_tables():

time: 55.4 us -> 55.4 us (level)
  no operation moved by 1% of the time
where the time goes in v13:
time: 55.4 us; the launch traced here: 55 us
  Pallas kernels  30.1 us (54%)
  starting transfers between devices  18 us (32%)
  waiting for transfers between devices  4.46 us (8%)
  between operations  2.25 us (4%)
    ppermute x12, starting transfers between devices, exchange(): return lax.ppermute(value, 'facet', [(i, i ^ mask) for i in range(n)])  18 us
    pallas_call x1, Pallas kernels, per_device(): pl.pallas_call(functools.partial(subgrid_kernel, [0] + [js.index(0) for j...  7.6 us
    pallas_call x1, Pallas kernels, per_device(): pl.pallas_call(functools.partial(forward_kernel, sends[0][0]), out_shape=...  4.54 us
    ppermute x12, waiting for transfers between devices, exchange(): return lax.ppermute(value, 'facet', [(i, i ^ mask) for i in range(n)])  4.46 us
    pallas_call x1, Pallas kernels, per_device(): pl.pallas_call(functools.partial(backward_kernel, [late_other[0]]), out_s...  4.06 us
    pallas_call x2, Pallas kernels, make_bands(): pl.pallas_call(functools.partial(band_kernel, odd), out_shape=[held(shape...  3.84 us
    pallas_call x1, Pallas kernels, make_screen(): pl.pallas_call(screen_kernel, out_shape=[held((2, SG, SG), F32)] + [held(...  3.2 us
    pallas_call x2, Pallas kernels, make_blocks(): pl.pallas_call(functools.partial(extract_kernel, lists), out_shape=[held(...  3.12 us
  transfers between devices with their start and end apart: 12, of which 3 were waited for; matrix products, arithmetic and copies ran while one was open for 0% of the time, Pallas kernels for 25%

profile of v13, /device:TPU:1, one launch (start us, length us, event | category | flops | bytes accessed | tf_op | source)
XLA Modules:
  0.0 55.0 jit_solution(16932805460303207891)
XLA Ops:
  0.6 4.5 %forward.1 = (bf16[4,2,128,128]{3,2,1,0:T(8,128)(2,1)S(1)}, f32[2,5,640,128]{3,2,1,0:T(8,128)S(1)}) custom-call(s32[1]{0:T(128)} %bitcast.1.me_ref, s32[1,2]{1,0:T(1,128)} %rest_4_.1, s32[2,16]{1,0:T(2,128)} %bitcast.13, bf16[1,2,512,512]{3,2,1,0:T(8,128)(2,1)} %facet_ref.1, bf16[2,512,512]{2,1,0:T(8,128)(2,1)} %constant.14.clone.basis_ref.basis_hbm), custom_call_target="tpu_custom_call" | custom-call | tf_op jit(solution)/shard_map/forward/pallas_call | solution.py:432
  5.2 0.1 collective-permute-start
  5.3 2.1 %extract.2 = (bf16[4,2,128,128]{3,2,1,0:T(8,128)(2,1)S(1)}, bf16[4,2,128,128]{3,2,1,0:T(8,128)(2,1)S(1)}) custom-call(s32[1]{0:T(128)} %bitcast.1.me_ref, s32[1,2]{1,0:T(1,128)} %rest_4_.1, s32[2,16]{1,0:T(2,128)} %bitcast.14, f32[2,5,640,128]{3,2,1,0:T(8,128)S(1)} %get-tuple-element.30.spec_ref), custom_call_target="tpu_custom_call" | custom-call | tf_op jit(solution)/shard_map/extract/pallas_call | solution.py:448
  7.4 0.5 collective-permute-start.2
  7.9 0.7 %bands.2 = (bf16[512,2048]{1,0:T(8,128)(2,1)S(1)}, bf16[16,512,128]{2,1,0:T(8,128)(2,1)S(1)}, f32[1,128]{1,0:T(1,128)S(1)}) custom-call(s32[1]{0:T(128)} %bitcast.1.me_ref, s32[2,16]{1,0:T(2,128)} %bitcast.17, f32[768,128]{1,0:T(8,128)} %constant.15.clone.kt_hbm, bf16[4,2,128,128]{3,2,1,0:T(8,128)(2,1)S(1)} %get-tuple-element.31.rest_0_), custom_call_target="tpu_custom_call" | custom-call | tf_op jit(solution)/shard_map/bands/pallas_call | solution.py:459
  8.6 0.1 add_convert_fusion.1.outs_0_._
  8.7 2.3 %collective-permute-start.1 = (bf16[4,2,128,128]{3,2,1,0:T(8,128)(2,1)S(1)}, bf16[4,2,128,128]{3,2,1,0:T(8,128)(2,1)S(1)}, u32[]{:S(2)}, u32[]{:S(2)}) collective-permute-start(bf16[4,2,128,128]{3,2,1,0:T(8,128)(2,1)S(1)} %add_convert_fusion.1.outs_0_._), channel_id=1, source_target_pairs={{0,2},{1,3},{2,0},{3,1},{4,6},{5,7},{6,4},{7,5},{8,10},{9,11},{10,... | collective-permute-start | bytes 786440 | tf_op jit(solution)/shard_map/ppermute | solution.py:380
  11.7 1.1 %extract.3 = (bf16[1,2,128,128]{3,2,1,0:T(8,128)(2,1)S(1)}, bf16[1,2,128,128]{3,2,1,0:T(8,128)(2,1)S(1)}, bf16[1,2,128,128]{3,2,1,0:T(8,128)(2,1)S(1)}, bf16[1,2,128,128]{3,2,1,0:T(8,128)(2,1)S(1)}) custom-call(s32[1]{0:T(128)} %bitcast.1.me_ref, s32[1,2]{1,0:T(1,128)} %rest_4_.1, s32[2,16]{1,0:T(2,128)} %bitcast.15, ...), custom_call_target="tpu_custom_call" | custom-call | tf_op jit(solution)/shard_map/extract/pallas_call | solution.py:448
  12.7 3.2 %screen.1 = (f32[2,512,512]{2,1,0:T(8,128)S(1)}, bf16[16,2,128,128]{3,2,1,0:T(8,128)(2,1)S(1)}, bf16[2,512,128]{2,1,0:T(8,128)(2,1)S(1)}, bf16[2,128,512]{2,1,0:...) custom-call(f32[1,1]{1,0:T(1,128)} %bitcast.8.w_ref, ...), custom_call_target="tpu_custom_call" | custom-call | tf_op jit(solution)/shard_map/screen/pallas_call | solution.py:480
  16.0 0.1 add_convert_fusion.2
  16.1 3.4 %collective-permute-start.3 = (bf16[1,2,128,128]{3,2,1,0:T(8,128)(2,1)S(1)}, bf16[1,2,128,128]{3,2,1,0:T(8,128)(2,1)S(1)}, u32[]{:S(2)}, u32[]{:S(2)}) collective-permute-start(bf16[1,2,128,128]{3,2,1,0:T(8,128)(2,1)S(1)} %get-tuple-element.60), channel_id=1, source_target_pairs={{0,12},{1,13},{2,14},{3,15},{4,8},{5,9},{6,10},{7,11},{8,4},{9,5},... | collective-permute-start | bytes 196616 | tf_op jit(solution)/shard_map/ppermute | solution.py:380
  19.5 0.4 collective-permute-start.5
  20.5 3.1 %bands.3 = (bf16[512,2048]{1,0:T(8,128)(2,1)S(1)}, bf16[16,512,128]{2,1,0:T(8,128)(2,1)S(1)}, f32[1,128]{1,0:T(1,128)}) custom-call(s32[1]{0:T(128)} %bitcast.1.me_ref, s32[2,16]{1,0:T(2,128)} %bitcast.19, f32[768,128]{1,0:T(8,128)} %constant.15.clone.kt_hbm, ...), custom_call_target="tpu_custom_call", output_to_operand_aliasing={{0}: (3, {}), {1}: (4, {})} | custom-call | tf_op jit(solution)/shard_map/bands/pallas_call | solution.py:459
  23.6 1.0 %collective-permute-done.4.rest_4_ = bf16[1,2,128,128]{3,2,1,0:T(8,128)(2,1)S(1)} collective-permute-done((bf16[1,2,128,128]{3,2,1,0:T(8,128)(2,1)S(1)}, bf16[1,2,128,128]{3,2,1,0:T(8,128)(2,1)S(1)}, u32[]{:S(2)}, u32[]{:S(2)}) %collective-permute-start.4) | collective-permute-done | bytes 65568 | tf_op jit(solution)/shard_map/ppermute | solution.py:380
  24.7 7.6 %subgrid.1 = (bf16[16,2,128,128]{3,2,1,0:T(8,128)(2,1)}, bf16[1,2,128,128]{3,2,1,0:T(8,128)(2,1)S(1)}) custom-call(s32[1,1]{1,0:T(1,128)} %bitcast.9.tc_ref, bf16[1,2,128,128]{3,2,1,0:T(8,128)(2,1)S(1)} %get-tuple-element.34.rest_0_, bf16[4,2,128,128]{3,2,1,0:T(8,128)(2,1)S(1)} %collective-permute-done.1.rest_1_, ...), custom_call_target="tpu_custom_call" | custom-call | tf_op jit(solution)/shard_map/subgrid/pallas_call | solution.py:526
  32.3 2.2 %collective-permute-start.6 = (bf16[1,2,128,128]{3,2,1,0:T(8,128)(2,1)S(1)}, bf16[1,2,128,128]{3,2,1,0:T(8,128)(2,1)S(1)}, u32[]{:S(2)}, u32[]{:S(2)}) collective-permute-start(bf16[1,2,128,128]{3,2,1,0:T(8,128)(2,1)S(1)} %get-tuple-element.52), channel_id=1, source_target_pairs={{0,12},{1,13},{2,14},{3,15},{4,8},{5,9},{6,10},{7,11},{8,4},{9,5},... | collective-permute-start | bytes 196616 | tf_op jit(solution)/shard_map/ppermute | solution.py:380
  34.5 1.4 %collective-permute-start.8 = (bf16[1,2,128,128]{3,2,1,0:T(8,128)(2,1)S(1)}, bf16[1,2,128,128]{3,2,1,0:T(8,128)(2,1)S(1)}, u32[]{:S(2)}, u32[]{:S(2)}) collective-permute-start(bf16[1,2,128,128]{3,2,1,0:T(8,128)(2,1)S(1)} %get-tuple-element.52), channel_id=1, source_target_pairs={{0,4},{1,5},{2,6},{3,7},{4,0},{5,1},{6,2},{7,3},{8,12},{9,13},{10,... | collective-permute-start | bytes 196616 | tf_op jit(solution)/shard_map/ppermute | solution.py:380
  35.9 1.4 %collective-permute-done.6 = bf16[1,2,128,128]{3,2,1,0:T(8,128)(2,1)S(1)} collective-permute-done((bf16[1,2,128,128]{3,2,1,0:T(8,128)(2,1)S(1)}, bf16[1,2,128,128]{3,2,1,0:T(8,128)(2,1)S(1)}, u32[]{:S(2)}, u32[]{:S(2)}) %collective-permute-start.6) | collective-permute-done | bytes 65568 | tf_op jit(solution)/shard_map/ppermute | solution.py:380
  37.3 2.0 %collective-permute-done.7 = bf16[1,2,128,128]{3,2,1,0:T(8,128)(2,1)S(1)} collective-permute-done((bf16[1,2,128,128]{3,2,1,0:T(8,128)(2,1)S(1)}, bf16[1,2,128,128]{3,2,1,0:T(8,128)(2,1)S(1)}, u32[]{:S(2)}, u32[]{:S(2)}) %collective-permute-start.7) | collective-permute-done | bytes 65568 | tf_op jit(solution)/shard_map/ppermute | solution.py:380
  39.4 4.8 %collective-permute-start.11 = (bf16[4,2,128,128]{3,2,1,0:T(8,128)(2,1)S(1)}, bf16[4,2,128,128]{3,2,1,0:T(8,128)(2,1)S(1)}, u32[]{:S(2)}, u32[]{:S(2)}) collective-permute-start(bf16[4,2,128,128]{3,2,1,0:T(8,128)(2,1)S(1)} %constant_dynamic-update-slice_fusion.rest_0_), channel_id=1, source_target_pairs={{0,1},{1,0},{2,3},{3,2},{4,5},{5,4},{6,7},{7,6},{8,9},{9,8},{10,11... | collective-permute-start | bytes 786440 | tf_op jit(solution)/shard_map/ppermute | solution.py:380
  44.2 2.1 %grid_first.1 = (f32[2,5,640,128]{3,2,1,0:T(8,128)S(1)}, f32[1,128]{1,0:T(1,128)S(1)}, bf16[2,512,512]{2,1,0:T(8,128)(2,1)S(1)}) custom-call(s32[1]{0:T(128)} %bitcast.1.me_ref, s32[1,2]{1,0:T(1,128)S(1)} %get-tuple-element.50.fo_ref, s32[2,16]{1,0:T(2,128)S(1)} %get-tuple-element.51.so_ref, bf16[2,512,512]{2,1,0:T(8,128)(2,1)} %constant.14.clone.basis_ref.basis_hbm, ...), custom_call_target="tpu_custom_call" | custom-call | tf_op jit(solution)/shard_map/grid_first/pallas_call | solution.py:570
  46.4 2.8 %collective-permute-start.10 = (bf16[4,2,128,128]{3,2,1,0:T(8,128)(2,1)S(1)}, bf16[4,2,128,128]{3,2,1,0:T(8,128)(2,1)S(1)}, u32[]{:S(2)}, u32[]{:S(2)}) collective-permute-start(bf16[4,2,128,128]{3,2,1,0:T(8,128)(2,1)S(1)} %add_convert_fusion.rest_1_), channel_id=1, source_target_pairs={{0,1},{1,0},{2,3},{3,2},{4,5},{5,4},{6,7},{7,6},{8,9},{9,8},{10,11... | collective-permute-start | bytes 786440 | tf_op jit(solution)/shard_map/ppermute | solution.py:380
  49.2 1.6 %grid_next.1 = (f32[2,5,640,128]{3,2,1,0:T(8,128)S(1)}, f32[1,128]{1,0:T(1,128)}) custom-call(s32[1]{0:T(128)} %bitcast.1.me_ref, s32[1,2]{1,0:T(1,128)S(1)} %get-tuple-element.50.fo_ref, s32[2,16]{1,0:T(2,128)S(1)} %get-tuple-element.51.so_ref, bf16[4,2,128,128]{3,2,1,0:T(8,128)(2,1)S(1)} %collective-permute-done.11.rest_0_, ...), custom_call_target="tpu_custom_call", output_to_operand_aliasing={{0}: (5, {})} | custom-call | tf_op jit(solution)/shard_map/grid_next/pallas_call | solution.py:560
  50.8 4.1 %backward.1 = (bf16[1,2,512,512]{3,2,1,0:T(8,128)(2,1)}, f32[2,5,640,128]{3,2,1,0:T(8,128)S(1)}) custom-call(s32[1]{0:T(128)} %bitcast.1.me_ref, s32[1,2]{1,0:T(1,128)S(1)} %get-tuple-element.50.fo_ref, s32[2,16]{1,0:T(2,128)S(1)} %get-tuple-element.51.so_ref, bf16[2,512,512]{2,1,0:T(8,128)(2,1)S(1)} %get-tuple-element.53.basis_ref, ...), custom_call_target="tpu_custom_call", output_to_operand_aliasing={{1}: (5, {})} | custom-call | tf_op jit(solution)/shard_map/backward/pallas_call | solution.py:583
  (17 shorter events, 0.2 us)
Async XLA Ops:
  5.2 3.4 %collective-permute-start = (bf16[4,2,128,128]{3,2,1,0:T(8,128)(2,1)S(1)}, bf16[4,2,128,128]{3,2,1,0:T(8,128)(2,1)S(1)}, u32[]{:S(2)}, u32[]{:S(2)}) collective-permute-start(bf16[4,2,128,128]{3,2,1,0:T(8,128)(2,1)S(1)} %get-tuple-element.33), channel_id=1, source_target_pairs={{0,1},{1,0},{2,3},{3,2},{4,5},{5,4},{6,7},{7,6},{8,9},{9,8},{10,11... | collective-permute-start | bytes 786440 | tf_op jit(solution)/shard_map/ppermute | solution.py:380
  7.4 8.6 %collective-permute-start.2 = (bf16[4,2,128,128]{3,2,1,0:T(8,128)(2,1)S(1)}, bf16[4,2,128,128]{3,2,1,0:T(8,128)(2,1)S(1)}, u32[]{:S(2)}, u32[]{:S(2)}) collective-permute-start(bf16[4,2,128,128]{3,2,1,0:T(8,128)(2,1)S(1)} %get-tuple-element.35), channel_id=1, source_target_pairs={{0,1},{1,0},{2,3},{3,2},{4,5},{5,4},{6,7},{7,6},{8,9},{9,8},{10,11... | collective-permute-start | bytes 786440 | tf_op jit(solution)/shard_map/ppermute | solution.py:380
  8.7 7.3 %collective-permute-start.1 = (bf16[4,2,128,128]{3,2,1,0:T(8,128)(2,1)S(1)}, bf16[4,2,128,128]{3,2,1,0:T(8,128)(2,1)S(1)}, u32[]{:S(2)}, u32[]{:S(2)}) collective-permute-start(bf16[4,2,128,128]{3,2,1,0:T(8,128)(2,1)S(1)} %add_convert_fusion.1.outs_0_._), channel_id=1, source_target_pairs={{0,2},{1,3},{2,0},{3,1},{4,6},{5,7},{6,4},{7,5},{8,10},{9,11},{10,... | collective-permute-start | bytes 786440 | tf_op jit(solution)/shard_map/ppermute | solution.py:380
  16.1 7.6 %collective-permute-start.3 = (bf16[1,2,128,128]{3,2,1,0:T(8,128)(2,1)S(1)}, bf16[1,2,128,128]{3,2,1,0:T(8,128)(2,1)S(1)}, u32[]{:S(2)}, u32[]{:S(2)}) collective-permute-start(bf16[1,2,128,128]{3,2,1,0:T(8,128)(2,1)S(1)} %get-tuple-element.60), channel_id=1, source_target_pairs={{0,12},{1,13},{2,14},{3,15},{4,8},{5,9},{6,10},{7,11},{8,4},{9,5},... | collective-permute-start | bytes 196616 | tf_op jit(solution)/shard_map/ppermute | solution.py:380
  19.5 5.2 %collective-permute-start.4 = (bf16[1,2,128,128]{3,2,1,0:T(8,128)(2,1)S(1)}, bf16[1,2,128,128]{3,2,1,0:T(8,128)(2,1)S(1)}, u32[]{:S(2)}, u32[]{:S(2)}) collective-permute-start(bf16[1,2,128,128]{3,2,1,0:T(8,128)(2,1)S(1)} %get-tuple-element.59), channel_id=1, source_target_pairs={{0,8},{1,9},{2,10},{3,11},{4,12},{5,13},{6,14},{7,15},{8,0},{9,1},... | collective-permute-start | bytes 196616 | tf_op jit(solution)/shard_map/ppermute | solution.py:380
  19.5 5.2 %collective-permute-start.5 = (bf16[1,2,128,128]{3,2,1,0:T(8,128)(2,1)S(1)}, bf16[1,2,128,128]{3,2,1,0:T(8,128)(2,1)S(1)}, u32[]{:S(2)}, u32[]{:S(2)}) collective-permute-start(bf16[1,2,128,128]{3,2,1,0:T(8,128)(2,1)S(1)} %get-tuple-element.58.rest_2_), channel_id=1, source_target_pairs={{0,4},{1,5},{2,6},{3,7},{4,0},{5,1},{6,2},{7,3},{8,12},{9,13},{10,... | collective-permute-start | bytes 196616 | tf_op jit(solution)/shard_map/ppermute | solution.py:380
  32.3 5.0 %collective-permute-start.6 = (bf16[1,2,128,128]{3,2,1,0:T(8,128)(2,1)S(1)}, bf16[1,2,128,128]{3,2,1,0:T(8,128)(2,1)S(1)}, u32[]{:S(2)}, u32[]{:S(2)}) collective-permute-start(bf16[1,2,128,128]{3,2,1,0:T(8,128)(2,1)S(1)} %get-tuple-element.52), channel_id=1, source_target_pairs={{0,12},{1,13},{2,14},{3,15},{4,8},{5,9},{6,10},{7,11},{8,4},{9,5},... | collective-permute-start | bytes 196616 | tf_op jit(solution)/shard_map/ppermute | solution.py:380
  34.5 4.8 %collective-permute-start.7 = (bf16[1,2,128,128]{3,2,1,0:T(8,128)(2,1)S(1)}, bf16[1,2,128,128]{3,2,1,0:T(8,128)(2,1)S(1)}, u32[]{:S(2)}, u32[]{:S(2)}) collective-permute-start(bf16[1,2,128,128]{3,2,1,0:T(8,128)(2,1)S(1)} %get-tuple-element.52), channel_id=1, source_target_pairs={{0,8},{1,9},{2,10},{3,11},{4,12},{5,13},{6,14},{7,15},{8,0},{9,1},... | collective-permute-start | bytes 196616 | tf_op jit(solution)/shard_map/ppermute | solution.py:380
  34.5 4.8 %collective-permute-start.8 = (bf16[1,2,128,128]{3,2,1,0:T(8,128)(2,1)S(1)}, bf16[1,2,128,128]{3,2,1,0:T(8,128)(2,1)S(1)}, u32[]{:S(2)}, u32[]{:S(2)}) collective-permute-start(bf16[1,2,128,128]{3,2,1,0:T(8,128)(2,1)S(1)} %get-tuple-element.52), channel_id=1, source_target_pairs={{0,4},{1,5},{2,6},{3,7},{4,0},{5,1},{6,2},{7,3},{8,12},{9,13},{10,... | collective-permute-start | bytes 196616 | tf_op jit(solution)/shard_map/ppermute | solution.py:380
  39.4 7.0 %collective-permute-start.9 = (bf16[4,2,128,128]{3,2,1,0:T(8,128)(2,1)S(1)}, bf16[4,2,128,128]{3,2,1,0:T(8,128)(2,1)S(1)}, u32[]{:S(2)}, u32[]{:S(2)}) collective-permute-start(bf16[4,2,128,128]{3,2,1,0:T(8,128)(2,1)S(1)} %constant_dynamic-update-slice_fusion.rest_0_), channel_id=1, source_target_pairs={{0,2},{1,3},{2,0},{3,1},{4,6},{5,7},{6,4},{7,5},{8,10},{9,11},{10,... | collective-permute-start | bytes 786440 | tf_op jit(solution)/shard_map/ppermute | solution.py:380
  39.4 9.8 %collective-permute-start.11 = (bf16[4,2,128,128]{3,2,1,0:T(8,128)(2,1)S(1)}, bf16[4,2,128,128]{3,2,1,0:T(8,128)(2,1)S(1)}, u32[]{:S(2)}, u32[]{:S(2)}) collective-permute-start(bf16[4,2,128,128]{3,2,1,0:T(8,128)(2,1)S(1)} %constant_dynamic-update-slice_fusion.rest_0_), channel_id=1, source_target_pairs={{0,1},{1,0},{2,3},{3,2},{4,5},{5,4},{6,7},{7,6},{8,9},{9,8},{10,11... | collective-permute-start | bytes 786440 | tf_op jit(solution)/shard_map/ppermute | solution.py:380
  46.4 4.4 %collective-permute-start.10 = (bf16[4,2,128,128]{3,2,1,0:T(8,128)(2,1)S(1)}, bf16[4,2,128,128]{3,2,1,0:T(8,128)(2,1)S(1)}, u32[]{:S(2)}, u32[]{:S(2)}) collective-permute-start(bf16[4,2,128,128]{3,2,1,0:T(8,128)(2,1)S(1)} %add_convert_fusion.rest_1_), channel_id=1, source_target_pairs={{0,1},{1,0},{2,3},{3,2},{4,5},{5,4},{6,7},{7,6},{8,9},{9,8},{10,11... | collective-permute-start | bytes 786440 | tf_op jit(solution)/shard_map/ppermute | solution.py:380
